TPU v7x, 32 devices: a whole 2x2x4 slice. The times are simulated.
32 devices in a mesh: dp: 8 (over z, x), tensor: 4 (over y, core).
Axes of the slice: x: 2, y: 2, z: 4, core: 2. Of those that a mesh axis runs over, the one named last changes fastest.
Arguments:
- inputs: bfloat16 [12288, 1280], P(('dp', 'tensor')), may hold values from -6 to 6
- lengths: int32 [8], P('dp'), may hold values from 1153 to 1536, as said below
- cotangent: bfloat16 [12288, 1280], P(('dp', 'tensor')), may hold values from -6 to 6
- w_qkv: float32 [1280, 3, 1280], P('dp', None, 'tensor')
- w_out: float32 [1280, 1280], P('dp', 'tensor')
- w_up: float32 [1280, 5120], P('dp', 'tensor')
- w_down: float32 [1280, 5120], P('dp', 'tensor')
- vectors: float32 [1280, 6], P('dp')
- bias_qkv: float32 [1280, 2], P(('tensor', 'dp')), may hold values from -1.8 to 1.8
- bias_up: float32 [5120], P(('tensor', 'dp')), may hold values from -1.8 to 1.8
- mom_qkv: float32 [1280, 3, 1280], P('dp', None, 'tensor'), may hold values from -665.1075 to 665.1075
- mom_out: float32 [1280, 1280], P('dp', 'tensor'), may hold values from -133.0215 to 133.0215
- mom_up: float32 [1280, 5120], P('dp', 'tensor'), may hold values from -199.53226 to 199.53226
- mom_down: float32 [1280, 5120], P('dp', 'tensor'), may hold values from -399.0645 to 399.0645
- mom_vectors: float32 [1280, 6], P('dp'), may hold values from -665.1075 to 665.1075
- mom_bias_qkv: float32 [1280, 2], P(('tensor', 'dp')), may hold values from -665.1075 to 665.1075
- mom_bias_up: float32 [5120], P(('tensor', 'dp')), may hold values from -199.53226 to 199.53226
Outputs:
- output: float32 [12288, 1280], P(('dp', 'tensor'))
- input_grad: float32 [12288, 1280], P(('dp', 'tensor'))
- new_w_qkv: float32 [1280, 3, 1280], P('dp', None, 'tensor')
- new_w_out: float32 [1280, 1280], P('dp', 'tensor')
- new_w_up: float32 [1280, 5120], P('dp', 'tensor')
- new_w_down: float32 [1280, 5120], P('dp', 'tensor')
- new_vectors: float32 [1280, 6], P('dp')
- new_bias_qkv: float32 [1280, 2], P(('tensor', 'dp'))
- new_bias_up: float32 [5120], P(('tensor', 'dp'))
- new_mom_qkv: float32 [1280, 3, 1280], P('dp', None, 'tensor')
- new_mom_out: float32 [1280, 1280], P('dp', 'tensor')
- new_mom_up: float32 [1280, 5120], P('dp', 'tensor')
- new_mom_down: float32 [1280, 5120], P('dp', 'tensor')
- new_mom_vectors: float32 [1280, 6], P('dp')
- new_mom_bias_qkv: float32 [1280, 2], P(('tensor', 'dp'))
- new_mom_bias_up: float32 [5120], P(('tensor', 'dp'))
Inputs may be any that keep to these rules, and one draw needn't show every extreme that they name: `lengths`: frames of a clip at positions below its length are keys; every clip is longer than three quarters of 1536, and one clip has exactly 1536.
All inputs are finite; a program needn't handle non-finite values.
Results may differ from a plain program's by a relative error of at most 0.018.
The roundings to bfloat16 on the way count: a program that leaves them out, or rounds other values in their place, can miss the bound.
Values may be sent and summed in bfloat16 or wider, within the bound.
No kernel may reach another device: no remote copies, remote signals or barrier semaphores. Data moves between devices by JAX's collectives and lax.ppermute only.
A program may use at most 256 MiB of HBM per device.

v0:
```python
from functools import partial
import math

import jax
import jax.numpy as jnp
from jax import lax
from jax.sharding import PartitionSpec as P

HD = 80
SWEEPS = 5


HIGHEST = lax.Precision.HIGHEST
NORM_EPS = 1e-05
POLAR_EPS = 1e-07
MASKED = -1e30
QUINTIC_A = 3.4445
QUINTIC_B = -4.775
QUINTIC_C = 2.0315
MUON_DECAY = 0.95
VEC_DECAY = 0.9
VEC_RATE = 0.1
STEP_QKV = 0.5 * math.sqrt(3.0)
STEP_OUT = 2.0
STEP_UP = 1.0
STEP_DOWN = 0.5


def layer_norm(values, gain, shift):
    center = values - jnp.mean(values, axis=-1, keepdims=True)
    spread = jnp.mean(center * center, axis=-1, keepdims=True)
    return center * lax.rsqrt(spread + NORM_EPS) * gain + shift


def matmul_plain(left, right):
    return jnp.dot(left, right, preferred_element_type=jnp.float32)


def matmul_left_t(left, right):
    return lax.dot_general(
        left, right, (((0,), (0,)), ((), ())), preferred_element_type=jnp.float32
    )


def matmul_right_t(left, right):
    return lax.dot_general(
        left, right, (((1,), (1,)), ((), ())), preferred_element_type=jnp.float32
    )


def gram_matrix(block):
    return lax.dot_general(
        block,
        block,
        (((1,), (1,)), ((), ())),
        precision=HIGHEST,
        preferred_element_type=jnp.float32,
    )


def tensor_total(first, second, third, fourth):
    return lax.psum((first, second, third, fourth), "tensor")


def quintic(iterate, gram):
    polynomial = QUINTIC_B * gram + QUINTIC_C * jnp.dot(gram, gram, precision=HIGHEST)
    return QUINTIC_A * iterate + jnp.dot(polynomial, iterate, precision=HIGHEST)


def local(
    inputs,
    lengths,
    cotangent,
    w_qkv,
    w_out,
    w_up,
    w_down,
    vectors,
    bias_qkv,
    bias_up,
    mom_qkv,
    mom_out,
    mom_up,
    mom_down,
    mom_vectors,
    mom_bias_qkv,
    mom_bias_up,
):
    tensor_size = lax.axis_size("tensor")
    tok_dev = inputs.shape[0]
    frames = tok_dev * tensor_size
    tokens = frames * lax.axis_size("dp")
    model_width = inputs.shape[1]
    local_width = w_qkv.shape[2]
    heads_here = local_width // HD
    q_block = min(512, frames)
    score_scale = 1.0 / math.sqrt(HD)
    wq_full, wo_full, wu_full, wd_full, vec_full, bq_full, bu_full = (
        lax.all_gather(w_qkv.astype(jnp.bfloat16), "dp", axis=0, tiled=True),
        lax.all_gather(w_out.astype(jnp.bfloat16), "dp", axis=0, tiled=True),
        lax.all_gather(w_up.astype(jnp.bfloat16), "dp", axis=0, tiled=True),
        lax.all_gather(w_down.astype(jnp.bfloat16), "dp", axis=0, tiled=True),
        lax.all_gather(vectors.astype(jnp.bfloat16), "dp", axis=0, tiled=True),
        lax.all_gather(bias_qkv.astype(jnp.bfloat16), "dp", axis=0, tiled=True),
        lax.all_gather(bias_up.astype(jnp.bfloat16), "dp", axis=0, tiled=True),
    )
    vec_vals = vec_full.astype(jnp.float32)
    bias_vals = bq_full.astype(jnp.float32)
    wq_flat = wq_full.reshape(model_width, 3 * local_width)
    x_float = inputs.astype(jnp.float32)
    attn_in = layer_norm(x_float, vec_vals[:, 0], vec_vals[:, 1]).astype(jnp.bfloat16)
    attn_in_full = lax.all_gather(attn_in, "tensor", axis=0, tiled=True)
    projected = matmul_plain(attn_in_full, wq_flat).reshape(frames, 3, local_width)
    bias_rows = jnp.stack([bias_vals[:, 0], jnp.zeros_like(bias_vals[:, 0]), bias_vals[:, 1]])
    qkv_rows = (projected + bias_rows).astype(jnp.bfloat16)
    queries = qkv_rows[:, 0].reshape(frames, heads_here, HD)
    key_side = qkv_rows[:, 1].reshape(frames, heads_here, HD)
    value_side = qkv_rows[:, 2].reshape(frames, heads_here, HD)
    key_valid = (jnp.arange(frames) < lengths[0])[None, None, :]

    def block_logits(q_part):
        scores = jnp.einsum("qhd,khd->hqk", q_part, key_side, preferred_element_type=jnp.float32)
        return jnp.where(key_valid, scores * score_scale, MASKED)

    offsets = list(range(0, frames, q_block))
    attn_parts = []
    lse_parts = []
    for offset in offsets:
        logits = block_logits(queries[offset : offset + q_block])
        row_max = jnp.max(logits, axis=-1, keepdims=True)
        powers = jnp.exp(logits - row_max)
        totals = jnp.sum(powers, axis=-1, keepdims=True)
        prob_low = (powers / totals).astype(jnp.bfloat16)
        part_out = jnp.einsum(
            "hqk,khd->qhd", prob_low, value_side, preferred_element_type=jnp.float32
        )
        attn_parts.append(part_out.astype(jnp.bfloat16))
        lse_parts.append(row_max + jnp.log(totals))
    attended = jnp.concatenate(attn_parts, axis=0).reshape(frames, local_width)
    attn_part = matmul_right_t(attended, wo_full)
    attn_sum = lax.psum_scatter(
        attn_part.astype(jnp.bfloat16), "tensor", scatter_dimension=0, tiled=True
    ).astype(jnp.float32)
    residual = x_float + attn_sum + vec_vals[:, 2]
    mlp_in = layer_norm(residual, vec_vals[:, 3], vec_vals[:, 4]).astype(jnp.bfloat16)
    mlp_in_full = lax.all_gather(mlp_in, "tensor", axis=0, tiled=True)
    pre_act = matmul_plain(mlp_in_full, wu_full) + bu_full.astype(jnp.float32)
    hidden = jax.nn.gelu(pre_act, approximate=False).astype(jnp.bfloat16)
    mlp_part = matmul_right_t(hidden, wd_full)
    mlp_sum = lax.psum_scatter(
        mlp_part.astype(jnp.bfloat16), "tensor", scatter_dimension=0, tiled=True
    ).astype(jnp.float32)
    output = residual + mlp_sum + vec_vals[:, 5]
    cot_float = cotangent.astype(jnp.float32)
    cot_full = lax.all_gather(cotangent, "tensor", axis=0, tiled=True)
    grad_wd = matmul_left_t(cot_full, hidden)
    d_hidden = matmul_plain(cot_full, wd_full)
    gelu_value, gelu_back = jax.vjp(partial(jax.nn.gelu, approximate=False), pre_act)
    d_pre = gelu_back(d_hidden)[0].astype(jnp.bfloat16)
    grad_wu = matmul_left_t(mlp_in_full, d_pre)
    grad_bu = jnp.sum(d_pre.astype(jnp.float32), axis=0)
    mlp_in_back = matmul_right_t(d_pre, wu_full)
    d_mlp_in = lax.psum_scatter(
        mlp_in_back.astype(jnp.bfloat16), "tensor", scatter_dimension=0, tiled=True
    ).astype(jnp.float32)
    norm_value, norm_back = jax.vjp(layer_norm, residual, vec_vals[:, 3], vec_vals[:, 4])
    d_from_norm, grad_gain_two, grad_shift_two = norm_back(d_mlp_in)
    d_residual = d_from_norm + cot_float
    grad_bias_down = jnp.sum(cot_float, axis=0)
    grad_bias_out = jnp.sum(d_residual, axis=0)
    d_out_full = lax.all_gather(d_residual.astype(jnp.bfloat16), "tensor", axis=0, tiled=True)
    grad_wo = matmul_left_t(d_out_full, attended)
    d_att = matmul_plain(d_out_full, wo_full).astype(jnp.bfloat16).reshape(frames, heads_here, HD)
    d_key = jnp.zeros((frames, heads_here, HD), jnp.float32)
    d_value = jnp.zeros((frames, heads_here, HD), jnp.float32)
    d_query_parts = []
    for block_index, offset in enumerate(offsets):
        q_part = queries[offset : offset + q_block]
        logits = block_logits(q_part)
        prob_vals = jnp.exp(logits - lse_parts[block_index])
        prob_low = prob_vals.astype(jnp.bfloat16)
        d_att_part = d_att[offset : offset + q_block]
        d_value = d_value + jnp.einsum(
            "hqk,qhd->khd", prob_low, d_att_part, preferred_element_type=jnp.float32
        )
        d_probs = jnp.einsum(
            "qhd,khd->hqk", d_att_part, value_side, preferred_element_type=jnp.float32
        )
        inner = jnp.sum(prob_vals * d_probs, axis=-1, keepdims=True)
        d_scores = (score_scale * (prob_vals * (d_probs - inner))).astype(jnp.bfloat16)
        d_query_parts.append(
            jnp.einsum("hqk,khd->qhd", d_scores, key_side, preferred_element_type=jnp.float32)
        )
        d_key = d_key + jnp.einsum(
            "hqk,qhd->khd", d_scores, q_part, preferred_element_type=jnp.float32
        )
    d_query = jnp.concatenate(d_query_parts, axis=0)
    d_qkv = (
        jnp.stack([d_query, d_key, d_value], axis=1)
        .astype(jnp.bfloat16)
        .reshape(frames, 3 * local_width)
    )
    grad_wq = matmul_left_t(attn_in_full, d_qkv).reshape(model_width, 3, local_width)
    part_sums = jnp.sum(d_qkv.astype(jnp.float32), axis=0).reshape(3, local_width)
    grad_bq = jnp.stack([part_sums[0], part_sums[2]], axis=1)
    attn_in_back = matmul_right_t(d_qkv, wq_flat)
    d_attn_in = lax.psum_scatter(
        attn_in_back.astype(jnp.bfloat16), "tensor", scatter_dimension=0, tiled=True
    ).astype(jnp.float32)
    first_value, first_back = jax.vjp(layer_norm, x_float, vec_vals[:, 0], vec_vals[:, 1])
    d_input, grad_gain_one, grad_shift_one = first_back(d_attn_in)
    input_grad = d_input + d_residual
    grad_vec = jnp.stack(
        [
            grad_gain_one,
            grad_shift_one,
            grad_bias_out,
            grad_gain_two,
            grad_shift_two,
            grad_bias_down,
        ],
        axis=1,
    )
    own_wq, own_wo, own_wu, own_wd, own_vec, own_bq, own_bu = (
        lax.psum_scatter(grad_wq, "dp", scatter_dimension=0, tiled=True),
        lax.psum_scatter(grad_wo, "dp", scatter_dimension=0, tiled=True),
        lax.psum_scatter(grad_wu, "dp", scatter_dimension=0, tiled=True),
        lax.psum_scatter(grad_wd, "dp", scatter_dimension=0, tiled=True),
        lax.psum_scatter(grad_vec, "dp", scatter_dimension=0, tiled=True),
        lax.psum_scatter(grad_bq, "dp", scatter_dimension=0, tiled=True),
        lax.psum_scatter(grad_bu, "dp", scatter_dimension=0, tiled=True),
    )
    vec_grad = lax.psum(own_vec, "tensor")
    gradients = (own_wq.reshape(own_wq.shape[0], -1), own_wo, own_wu, own_wd)
    moments = (mom_qkv.reshape(mom_qkv.shape[0], -1), mom_out, mom_up, mom_down)
    new_moments = [MUON_DECAY * moment + gradient for gradient, moment in zip(gradients, moments)]
    updates = [gradient + MUON_DECAY * moment for gradient, moment in zip(gradients, new_moments)]
    first_grams = tensor_total(
        gram_matrix(updates[0]),
        gram_matrix(updates[1]),
        gram_matrix(updates[2]),
        gram_matrix(updates[3]),
    )
    factors = [1.0 / (jnp.sqrt(jnp.trace(gram)) + POLAR_EPS) for gram in first_grams]
    iterates = [update * factor for update, factor in zip(updates, factors)]
    grams = [gram * factor * factor for gram, factor in zip(first_grams, factors)]
    for sweep_index in range(SWEEPS):
        if sweep_index > 0:
            grams = tensor_total(
                gram_matrix(iterates[0]),
                gram_matrix(iterates[1]),
                gram_matrix(iterates[2]),
                gram_matrix(iterates[3]),
            )
        iterates = [quintic(iterate, gram) for iterate, gram in zip(iterates, grams)]
    new_w_qkv = w_qkv - STEP_QKV * iterates[0].reshape(w_qkv.shape)
    new_w_out = w_out - STEP_OUT * iterates[1]
    new_w_up = w_up - STEP_UP * iterates[2]
    new_w_down = w_down - STEP_DOWN * iterates[3]
    vec_rate = VEC_RATE / math.sqrt(tokens)
    new_mom_vectors = VEC_DECAY * mom_vectors + vec_grad
    new_mom_bias_qkv = VEC_DECAY * mom_bias_qkv + own_bq
    new_mom_bias_up = VEC_DECAY * mom_bias_up + own_bu
    new_vectors = vectors - vec_rate * new_mom_vectors
    new_bias_qkv = bias_qkv - vec_rate * new_mom_bias_qkv
    new_bias_up = bias_up - vec_rate * new_mom_bias_up
    return (
        output,
        input_grad,
        new_w_qkv,
        new_w_out,
        new_w_up,
        new_w_down,
        new_vectors,
        new_bias_qkv,
        new_bias_up,
        new_moments[0].reshape(mom_qkv.shape),
        new_moments[1],
        new_moments[2],
        new_moments[3],
        new_mom_vectors,
        new_mom_bias_qkv,
        new_mom_bias_up,
    )


def solution(mesh):
    in_specs = (
        P(("dp", "tensor"), None),
        P("dp"),
        P(("dp", "tensor"), None),
        P("dp", None, "tensor"),
        P("dp", "tensor"),
        P("dp", "tensor"),
        P("dp", "tensor"),
        P("dp", None),
        P(("tensor", "dp"), None),
        P(("tensor", "dp")),
        P("dp", None, "tensor"),
        P("dp", "tensor"),
        P("dp", "tensor"),
        P("dp", "tensor"),
        P("dp", None),
        P(("tensor", "dp"), None),
        P(("tensor", "dp")),
    )
    out_specs = (
        P(("dp", "tensor"), None),
        P(("dp", "tensor"), None),
        P("dp", None, "tensor"),
        P("dp", "tensor"),
        P("dp", "tensor"),
        P("dp", "tensor"),
        P("dp", None),
        P(("tensor", "dp"), None),
        P(("tensor", "dp")),
        P("dp", None, "tensor"),
        P("dp", "tensor"),
        P("dp", "tensor"),
        P("dp", "tensor"),
        P("dp", None),
        P(("tensor", "dp"), None),
        P(("tensor", "dp")),
    )
    return jax.shard_map(local, mesh=mesh, in_specs=in_specs, out_specs=out_specs, check_vma=False)
```

profile of v0, /device:TPU:0, one launch (start us, length us, event | category | flops | bytes accessed | tf_op | source)
XLA Modules:
  0.0 1363.8 jit_solution(8041395495115766762)
XLA Ops:
  9.9 32.4 %all-gather = bf16[8,160,6]{1,2,0:T(8,128)(2,1)S(1)} all-gather(bf16[1,160,6]{1,2,0:T(8,128)(2,1)S(1)} %convert_bitcast_fusion), channel_id=1, replica_groups=mesh['dp'=8,'tensor'=4] {'dp'}, dimensions={0}, use_global_device_ids=true | all-gather | bytes 17280 | tf_op jit(solution)/shard_map/all_gather | solution.py:103
  50.1 20.4 %all-gather.1 = bf16[8,40,2]{1,2,0:T(2,128)(2,1)S(1)} all-gather(bf16[1,40,2]{1,2,0:T(2,128)(2,1)S(1)} %convert_bitcast_fusion.1), channel_id=1, replica_groups=mesh['dp'=8,'tensor'=4] {'dp'}, dimensions={0}, use_global_device_ids=true | all-gather | bytes 1440 | tf_op jit(solution)/shard_map/all_gather | solution.py:104
  71.7 34.2 %all_gather.37 = bf16[1280,320]{1,0:T(8,128)(2,1)} all-gather(bf16[160,320]{1,0:T(8,128)(2,1)S(1)} %convert_element_type.165), channel_id=1, replica_groups=mesh['dp'=8,'tensor'=4] {'dp'}, dimensions={0}, use_global_device_ids=true | all-gather | bytes 921600 | tf_op jit(solution)/shard_map/all_gather | solution.py:100
  109.8 7.2 add_convert_fusion.1
  120.3 7.1 fusion.208
  132.8 6.4 fusion.6
  139.2 6.5 fusion.120
  159.5 39.4 %reduce-scatter.13.cloned.1.call-done = bf16[384,1280]{1,0:T(8,128)(2,1)} async-done(((bf16[1536,1280]{1,0:T(8,128)(2,1)}), bf16[384,1280]{1,0:T(8,128)(2,1)}) %reduce-scatter.13.cloned.1.call-update) | async-done | bytes 983056 | tf_op jit(solution)/shard_map/reduce_scatter | solution.py:141
  208.2 21.6 %all-reduce = bf16[1280]{0:T(1024)(128)(2,1)S(1)} all-reduce(bf16[1280]{0:T(1024)(128)(2,1)S(1)} %dynamic-update-slice), channel_id=1, replica_groups=mesh['dp'=8,'tensor'=4] {'dp'}, use_global_device_ids=true, to_apply=%add | all-reduce | flops 1280 | bytes 5120
  229.8 34.2 %all-gather.16.cloned.1.call-done = bf16[1280,1280]{1,0:T(8,128)(2,1)} async-done(((bf16[160,1280]{1,0:T(8,128)(2,1)}), bf16[1280,1280]{1,0:T(8,128)(2,1)}) %all-gather.16.cloned.1.call-update) | async-done | bytes 3276816 | tf_op jit(solution)/shard_map/all_gather | solution.py:101
  264.0 33.7 %all-gather.14.cloned.1.call-done = bf16[1536,1280]{1,0:T(8,128)(2,1)} async-done(((bf16[384,1280]{1,0:T(8,128)(2,1)}), bf16[1536,1280]{1,0:T(8,128)(2,1)}) %all-gather.14.cloned.1.call-update) | async-done | bytes 3932176 | tf_op jit(solution)/shard_map/all_gather | solution.py:146
  297.7 10.0 convolution_add_fusion
  307.6 54.9 %all-gather.18.cloned.1.call-done = bf16[1280,1280]{1,0:T(8,128)(2,1)} async-done(((bf16[160,1280]{1,0:T(8,128)(2,1)}), bf16[1280,1280]{1,0:T(8,128)(2,1)}) %all-gather.18.cloned.1.call-update) | async-done | bytes 3276816 | tf_op jit(solution)/shard_map/all_gather | solution.py:102
  362.5 33.2 %all-gather.20.cloned.1.call-done = bf16[1536,1280]{1,0:T(8,128)(2,1)} async-done(((bf16[384,1280]{1,0:T(8,128)(2,1)}), bf16[1536,1280]{1,0:T(8,128)(2,1)}) %all-gather.20.cloned.1.call-update) | async-done | bytes 3932176 | tf_op jit(solution)/shard_map/all_gather | solution.py:155
  395.8 27.4 %convert_reduce_fusion = (f32[1280]{0:T(1024)}, bf16[1536,1280]{1,0:T(8,128)(2,1)S(1)}, f32[1536,1280]{1,0:T(8,128)}) fusion(f32[1536,1280]{1,0:T(8,128)} %convolution_add_fusion, bf16[1536,1280]{1,0:T(8,128)(2,1)} %all-gather.20.cloned.1.call-done, bf16[1280,1280]{1,0:T(8,128)(2,1)} %all-gather.18.cloned.1.call-done), kind=kOutput, calls=%fused_computation.34 | convolution fusion | flops 5178653696 | bytes 26874880 | tf_op jit(solution)/shard_map/dot_general | solution.py:36
  425.1 6.8 convolution_convert_fusion.1
  432.0 6.6 multiply_convert_fusion.3
  440.8 9.1 convolution_convert_fusion.2
  450.1 24.9 %reduce-scatter.17.cloned.1.call-done = bf16[384,1280]{1,0:T(8,128)(2,1)} async-done(((bf16[1536,1280]{1,0:T(8,128)(2,1)}), bf16[384,1280]{1,0:T(8,128)(2,1)}) %reduce-scatter.17.cloned.1.call-update) | async-done | bytes 983056 | tf_op jit(solution)/shard_map/reduce_scatter | solution.py:163
  479.3 41.1 %reduce-scatter.15.cloned.1.call-done = bf16[384,1280]{1,0:T(8,128)(2,1)} async-done(((bf16[1536,1280]{1,0:T(8,128)(2,1)}), bf16[384,1280]{1,0:T(8,128)(2,1)}) %reduce-scatter.15.cloned.1.call-update) | async-done | bytes 983056 | tf_op jit(solution)/shard_map/reduce_scatter | solution.py:150
  527.2 10.1 fusion.221
  537.5 10.1 convolution_bitcast_fusion
  547.7 12.6 all-gather.22.cloned.1.call-done
  564.9 6.3 fusion.209
  571.2 27.5 %fusion.106 = bf16[512,4,80]{0,2,1:T(8,128)(2,1)} fusion(bf16[1536,4,80]{0,2,1:T(8,128)(2,1)S(1)} %bitcast.229, f32[4,512,1536]{2,1,0:T(8,128)} %fusion.209, f32[4,512,1536]{2,1,0:T(8,128)} %get-tuple-element.136, f32[4,512]{1,0:T(4,128)S(1)} %log_add_fusion.2), kind=kOutput, calls=%fused_computation.141 | convolution fusion | flops 525340160 | bytes 26484736 | tf_op jit(solution)/shard_map/hqk,khd->qhd/dot_general | solution.py:192
  598.7 7.3 fusion.210
  606.0 26.9 %fusion.109 = bf16[512,4,80]{0,2,1:T(8,128)(2,1)} fusion(bf16[1536,4,80]{0,2,1:T(8,128)(2,1)S(1)} %bitcast.230, f32[4,512,1536]{2,1,0:T(8,128)} %fusion.210, f32[4,512,1536]{2,1,0:T(8,128)} %copy-done.1, f32[4,512]{1,0:T(4,128)S(1)} %log_add_fusion.1), kind=kOutput, calls=%fused_computation.142 | convolution fusion | flops 525340160 | bytes 26484736 | tf_op jit(solution)/shard_map/hqk,khd->qhd/dot_general | solution.py:192
  632.9 7.3 fusion.211
  640.1 27.1 %fusion.112 = bf16[512,4,80]{0,2,1:T(8,128)(2,1)} fusion(bf16[1536,4,80]{0,2,1:T(8,128)(2,1)S(1)} %bitcast.231, f32[4,512,1536]{2,1,0:T(8,128)} %fusion.211, f32[4,512,1536]{2,1,0:T(8,128)} %copy-done, f32[4,512]{1,0:T(4,128)S(1)} %log_add_fusion), kind=kOutput, calls=%fused_computation.143 | convolution fusion | flops 525340160 | bytes 26484736 | tf_op jit(solution)/shard_map/hqk,khd->qhd/dot_general | solution.py:192
  667.3 23.2 %fusion.41 = f32[4,80,1536]{2,1,0:T(8,128)} fusion(bf16[512,4,80]{0,2,1:T(8,128)(2,1)S(1)} %bitcast.246, f32[4,512,1536]{2,1,0:T(8,128)} %fusion.210, f32[4,512,1536]{2,1,0:T(8,128)} %copy-done.1, f32[4,512]{1,0:T(4,128)S(1)} %log_add_fusion.1), kind=kOutput, calls=%fused_computation.63 | convolution fusion | flops 525340160 | bytes 27467776 | tf_op jit(solution)/shard_map/hqk,qhd->khd/dot_general | solution.py:194
  690.5 24.2 %fusion.70 = f32[4,80,1536]{2,1,0:T(8,128)} fusion(f32[4,80,1536]{2,1,0:T(8,128)} %fusion.41, bf16[512,4,80]{0,2,1:T(8,128)(2,1)S(1)} %bitcast.244, f32[4,512,1536]{2,1,0:T(8,128)} %fusion.209, f32[4,512,1536]{2,1,0:T(8,128)} %get-tuple-element.136, f32[4,512]{1,0:T(4,128)S(1)} %log_add_fusion.2), kind=kOutput, calls=%fused_computation.99 | convolution fusion | flops 525831680 | bytes 29433856 | tf_op jit(solution)/shard_map/hqk,qhd->khd/dot_general | solution.py:194
  714.7 24.4 %fusion.76 = bf16[1536,1,4,80]{0,3,2,1:T(8,128)(2,1)} fusion(f32[4,80,1536]{2,1,0:T(8,128)} %fusion.70, bf16[512,4,80]{0,2,1:T(8,128)(2,1)S(1)} %bitcast.242, f32[4,512,1536]{2,1,0:T(8,128)} %fusion.211, f32[4,512,1536]{2,1,0:T(8,128)} %copy-done, f32[4,512]{1,0:T(4,128)S(1)} %log_add_fusion), kind=kOutput, calls=%fused_computation.101 | convolution fusion | flops 526323200 | bytes 28450816 | tf_op jit(solution)/shard_map/hqk,qhd->khd/dot_general | solution.py:194
  746.1 6.1 fusion.24
  752.2 6.2 fusion.26
  763.4 5.9 convolution_convert_fusion
  769.4 10.1 fusion.63
  786.7 23.7 %reduce-scatter.27.cloned.1.call-done = f32[160,1280]{1,0:T(8,128)} async-done(((f32[1280,1280]{1,0:T(8,128)}), f32[160,1280]{1,0:T(8,128)}) %reduce-scatter.27.cloned.1.call-update) | async-done | bytes 819216 | tf_op jit(solution)/shard_map/reduce_scatter | solution.py:228
  815.4 35.6 %all-reduce.3 = (f32[320,2]{0,1:T(2,128)S(1)}, f32[1280]{0:T(1024)S(1)}) all-reduce(f32[320,2]{0,1:T(2,128)S(1)} %pad_maximum_fusion.2, f32[1280]{0:T(1024)S(1)} %copy-done.74), channel_id=11, replica_groups=mesh['dp'=8,'tensor'=4] {'dp'}, use_global_device_ids=true, to_apply=%region_58.59.clone | all-reduce | flops 1920 | bytes 15360
  852.2 27.9 %reduce-scatter.23.cloned.1.call-done = f32[160,320]{1,0:T(8,128)} async-done(((f32[1280,320]{1,0:T(8,128)}), f32[160,320]{1,0:T(8,128)}) %reduce-scatter.23.cloned.1.call-update) | async-done | bytes 204816 | tf_op jit(solution)/shard_map/reduce_scatter | solution.py:226
  883.5 40.9 %reduce-scatter.19.cloned.1.call-done = bf16[384,1280]{1,0:T(8,128)(2,1)} async-done(((bf16[1536,1280]{1,0:T(8,128)(2,1)}), bf16[384,1280]{1,0:T(8,128)(2,1)}) %reduce-scatter.19.cloned.1.call-update) | async-done | bytes 983056 | tf_op jit(solution)/shard_map/reduce_scatter | solution.py:207
  926.7 113.4 %reduce-scatter.21.cloned.1.call-done = f32[160,3,320]{2,0,1:T(8,128)} async-done(((f32[1280,3,320]{2,0,1:T(8,128)}), f32[160,3,320]{2,0,1:T(8,128)}) %reduce-scatter.21.cloned.1.call-update) | async-done | bytes 614416 | tf_op jit(solution)/shard_map/reduce_scatter | solution.py:225
  1056.3 23.4 %all-reduce.23.cloned.1.call-done = (f32[160,160]{1,0:T(8,128)}, f32[160,160]{1,0:T(8,128)}, f32[160,160]{1,0:T(8,128)}, f32[160,160]{1,0:T(8,128)}) async-done(((f32[160,160]{1,0:T(8,128)}, f32[160,160]{1,0:T(8,128)}, f32[160,160]{1,0:T(8,128)}, f32[160,160]{1,0:T(8,128)}), (f32[160,160]{1,0:T(8,128)}, f32[160,160]{1,0:T(8,128)}, f32[160,160]{1,0:T(8,128)}, ...) | async-done | bytes 409616 | tf_op jit(solution)/shard_map/psum | solution.py:62
  1111.3 27.4 %all-reduce.21.cloned.1.call-done = (f32[160,160]{1,0:T(8,128)}, f32[160,160]{1,0:T(8,128)}, f32[160,160]{1,0:T(8,128)}, f32[160,160]{1,0:T(8,128)}) async-done(((f32[160,160]{1,0:T(8,128)}, f32[160,160]{1,0:T(8,128)}, f32[160,160]{1,0:T(8,128)}, f32[160,160]{1,0:T(8,128)}), (f32[160,160]{1,0:T(8,128)}, f32[160,160]{1,0:T(8,128)}, f32[160,160]{1,0:T(8,128)}, ...) | async-done | bytes 409616 | tf_op jit(solution)/shard_map/psum | solution.py:62
  1153.5 33.3 %all-reduce.19.cloned.1.call-done = (f32[160,160]{1,0:T(8,128)}, f32[160,160]{1,0:T(8,128)}, f32[160,160]{1,0:T(8,128)}, f32[160,160]{1,0:T(8,128)}) async-done(((f32[160,160]{1,0:T(8,128)}, f32[160,160]{1,0:T(8,128)}, f32[160,160]{1,0:T(8,128)}, f32[160,160]{1,0:T(8,128)}), (f32[160,160]{1,0:T(8,128)}, f32[160,160]{1,0:T(8,128)}, f32[160,160]{1,0:T(8,128)}, ...) | async-done | bytes 409616 | tf_op jit(solution)/shard_map/psum | solution.py:62
  1207.3 45.1 %reduce-scatter.29.cloned.1.call-done = f32[160,6]{1,0:T(8,128)} async-done(((f32[1280,6]{1,0:T(8,128)}), f32[160,6]{1,0:T(8,128)}) %reduce-scatter.29.cloned.1.call-update) | async-done | bytes 3856
  1253.3 6.0 psum.167
  1259.4 29.3 %all-reduce.17.cloned.1.call-done = (f32[160,160]{1,0:T(8,128)}, f32[160,160]{1,0:T(8,128)}, f32[160,160]{1,0:T(8,128)}, f32[160,160]{1,0:T(8,128)}) async-done(((f32[160,160]{1,0:T(8,128)}, f32[160,160]{1,0:T(8,128)}, f32[160,160]{1,0:T(8,128)}, f32[160,160]{1,0:T(8,128)}), (f32[160,160]{1,0:T(8,128)}, f32[160,160]{1,0:T(8,128)}, f32[160,160]{1,0:T(8,128)}, ...) | async-done | bytes 409616 | tf_op jit(solution)/shard_map/psum | solution.py:62
  1304.7 33.7 %all-reduce.15.cloned.1.call-done = (f32[160,160]{1,0:T(8,128)}, f32[160,160]{1,0:T(8,128)}, f32[160,160]{1,0:T(8,128)}, f32[160,160]{1,0:T(8,128)}) async-done(((f32[160,160]{1,0:T(8,128)}, f32[160,160]{1,0:T(8,128)}, f32[160,160]{1,0:T(8,128)}, f32[160,160]{1,0:T(8,128)}), (f32[160,160]{1,0:T(8,128)}, f32[160,160]{1,0:T(8,128)}, f32[160,160]{1,0:T(8,128)}, ...) | async-done | bytes 409616 | tf_op jit(solution)/shard_map/psum | solution.py:62
  (370 shorter events, 210.4 us)
Async XLA Ops:
  7.2 98.7 %all-gather.12.cloned.1.call-start = ((), (), s32[]{:S(2)}) async-start(), calls=%async_computation.10 | async-start | bytes 3317760 | tf_op jit(solution)/shard_map/all_gather | solution.py:99
  9.1 100.7 %all-gather.10.cloned.1.call-start = ((), (), s32[]{:S(2)}) async-start(), calls=%async_computation.9 | async-start | bytes 4915200 | tf_op jit(solution)/shard_map/all_gather | solution.py:112
  48.7 150.2 %reduce-scatter.13.cloned.1.call-start = ((), (), s32[]{:S(2)}) async-start(), calls=%async_computation.11 | async-start | bytes 4915200 | tf_op jit(solution)/shard_map/reduce_scatter | solution.py:141
  118.0 27.6 %copy-start.4 = (bf16[1536,1,320]{0,2,1:T(8,128)(2,1)}, bf16[1536,1,320]{0,2,1:T(8,128)(2,1)S(1)}, u32[]{:S(2)}) copy-start(bf16[1536,1,320]{0,2,1:T(8,128)(2,1)S(1)} %get-tuple-element.116) | copy-start | bytes 2949124
  154.4 44.5 %copy-start.2 = (bf16[384,1280]{1,0:T(8,128)(2,1)S(1)}, bf16[384,1280]{1,0:T(8,128)(2,1)}, u32[]{:S(2)}) copy-start(bf16[384,1280]{1,0:T(8,128)(2,1)} %param.17) | copy-start | bytes 2949124
  158.5 48.2 %copy-start.79 = (f32[160]{0:T(256)S(1)}, f32[160]{0:T(256)}, u32[]{:S(2)}) copy-start(f32[160]{0:T(256)} %param.26) | copy-start | bytes 1924
  158.5 48.2 %copy-start.76 = (u32[32]{0:T(128)S(1)}, u32[32]{0:T(128)}, u32[]{:S(2)}) copy-start(u32[32]{0:T(128)} %constant.126) | copy-start | bytes 388
  158.5 105.5 %all-gather.16.cloned.1.call-start = ((), (), s32[]{:S(2)}) async-start(), calls=%async_computation.13 | async-start | bytes 3686400 | tf_op jit(solution)/shard_map/all_gather | solution.py:101
  159.4 45.6 %copy-start.24 = (f32[160,1280]{1,0:T(8,128)S(1)}, f32[160,1280]{1,0:T(8,128)}, u32[]{:S(2)}) copy-start(f32[160,1280]{1,0:T(8,128)} %param.23) | copy-start | bytes 2457604
  159.4 138.3 %all-gather.14.cloned.1.call-start = ((), (), s32[]{:S(2)}) async-start(), calls=%async_computation.12 | async-start | bytes 4915200 | tf_op jit(solution)/shard_map/all_gather | solution.py:146
  205.0 157.5 %all-gather.18.cloned.1.call-start = ((), (), s32[]{:S(2)}) async-start(), calls=%async_computation.14 | async-start | bytes 3686400 | tf_op jit(solution)/shard_map/all_gather | solution.py:102
  205.9 189.9 %all-gather.20.cloned.1.call-start = ((), (), s32[]{:S(2)}) async-start(), calls=%async_computation.16 | async-start | bytes 4915200 | tf_op jit(solution)/shard_map/all_gather | solution.py:155
  206.6 268.3 %reduce-scatter.17.cloned.1.call-start = ((), (), s32[]{:S(2)}) async-start(), calls=%async_computation.17 | async-start | bytes 4915200 | tf_op jit(solution)/shard_map/reduce_scatter | solution.py:163
  395.8 29.3 %copy-start.82 = (bf16[1280,1280]{1,0:T(8,128)(2,1)S(1)}, bf16[1280,1280]{1,0:T(8,128)(2,1)}, u32[]{:S(2)}) copy-start(bf16[1280,1280]{1,0:T(8,128)(2,1)} %all-gather.16.cloned.1.call-done) | copy-start | bytes 9830404
  431.9 88.5 %reduce-scatter.15.cloned.1.call-start = ((), (), s32[]{:S(2)}) async-start(), calls=%async_computation.15 | async-start | bytes 4915200 | tf_op jit(solution)/shard_map/reduce_scatter | solution.py:150
  440.8 34.2 %copy-start.3 = (bf16[384,1280]{1,0:T(8,128)(2,1)S(1)}, bf16[384,1280]{1,0:T(8,128)(2,1)}, u32[]{:S(2)}) copy-start(bf16[384,1280]{1,0:T(8,128)(2,1)} %reduce-scatter.13.cloned.1.call-done) | copy-start | bytes 2949124
  449.8 70.6 %copy-start.69 = (f32[1280]{0:T(1024)S(1)}, f32[1280]{0:T(1024)}, u32[]{:S(2)}) copy-start(f32[1280]{0:T(1024)} %get-tuple-element.72) | copy-start | bytes 15364
  449.8 110.5 %all-gather.22.cloned.1.call-start = ((), (), s32[]{:S(2)}) async-start(), calls=%async_computation.18 | async-start | bytes 4915200 | tf_op jit(solution)/shard_map/all_gather | solution.py:171
  527.2 255.0 %reduce-scatter.25.cloned.1.call-start = ((), (), s32[]{:S(2)}) async-start(), calls=%async_computation.22 | async-start | bytes 7372800 | tf_op jit(solution)/shard_map/reduce_scatter | solution.py:227
  537.4 273.0 %reduce-scatter.27.cloned.1.call-start = ((), (), s32[]{:S(2)}) async-start(), calls=%async_computation.23 | async-start | bytes 7372800 | tf_op jit(solution)/shard_map/reduce_scatter | solution.py:228
  547.6 332.5 %reduce-scatter.23.cloned.1.call-start = ((), (), s32[]{:S(2)}) async-start(), calls=%async_computation.21 | async-start | bytes 2211840 | tf_op jit(solution)/shard_map/reduce_scatter | solution.py:226
  745.0 179.4 %reduce-scatter.19.cloned.1.call-start = ((), (), s32[]{:S(2)}) async-start(), calls=%async_computation.19 | async-start | bytes 4915200 | tf_op jit(solution)/shard_map/reduce_scatter | solution.py:207
  769.3 270.8 %reduce-scatter.21.cloned.1.call-start = ((), (), s32[]{:S(2)}) async-start(), calls=%async_computation.20 | async-start | bytes 6635520 | tf_op jit(solution)/shard_map/reduce_scatter | solution.py:225
  779.4 35.9 %copy-start.74 = (f32[1280]{0:T(1024)S(1)}, f32[1280]{0:T(1024)}, u32[]{:S(2)}) copy-start(f32[1280]{0:T(1024)} %get-tuple-element.104) | copy-start | bytes 15364
  779.4 71.5 %copy-start.77 = (f32[40,2]{0,1:T(2,128)S(1)}, f32[40,2]{0,1:T(2,128)}, u32[]{:S(2)}) copy-start(f32[40,2]{0,1:T(2,128)} %param.25) | copy-start | bytes 964
  779.4 71.5 %copy-start.78 = (f32[40,2]{0,1:T(2,128)S(1)}, f32[40,2]{0,1:T(2,128)}, u32[]{:S(2)}) copy-start(f32[40,2]{0,1:T(2,128)} %param.32) | copy-start | bytes 964
  779.4 72.1 %copy-start.80 = (f32[160]{0:T(256)S(1)}, f32[160]{0:T(256)}, u32[]{:S(2)}) copy-start(f32[160]{0:T(256)} %param.26) | copy-start | bytes 1924
  779.5 72.1 %copy-start.81 = (f32[160]{0:T(256)S(1)}, f32[160]{0:T(256)}, u32[]{:S(2)}) copy-start(f32[160]{0:T(256)} %param.33) | copy-start | bytes 1924
  779.5 144.9 %copy-start.53 = (f32[1280]{0:T(1024)S(1)}, f32[1280]{0:T(1024)}, u32[]{:S(2)}) copy-start(f32[1280]{0:T(1024)} %copy-done.52) | copy-start | bytes 15364
  779.5 144.8 %copy-start.61 = (f32[384]{0:T(512)S(1)}, f32[384]{0:T(512)}, u32[]{:S(2)}) copy-start(f32[384]{0:T(512)} %copy-done.60) | copy-start | bytes 4612
  779.5 300.2 %all-reduce.23.cloned.1.call-start = ((), (), s32[]{:S(2)}) async-start(), calls=%async_computation.29 | async-start | bytes 1310720 | tf_op jit(solution)/shard_map/psum | solution.py:62
  783.4 309.5 %copy-start.16 = (f32[160,1280]{1,0:T(8,128)}, f32[160,1280]{1,0:T(8,128)S(1)}, u32[]{:S(2)}) copy-start(f32[160,1280]{1,0:T(8,128)S(1)} %multiply_add_fusion.3) | copy-start | bytes 2457604
  783.4 262.2 %copy-start.71 = (f32[384]{0:T(512)S(1)}, f32[384]{0:T(512)}, u32[]{:S(2)}) copy-start(f32[384]{0:T(512)} %copy-done.70) | copy-start | bytes 4612
  811.9 284.8 %copy-start.17 = (f32[160,1280]{1,0:T(8,128)}, f32[160,1280]{1,0:T(8,128)S(1)}, u32[]{:S(2)}) copy-start(f32[160,1280]{1,0:T(8,128)S(1)} %multiply_add_fusion.1) | copy-start | bytes 2457604
  881.2 45.5 %copy-start.32 = (f32[160,320]{1,0:T(8,128)}, f32[160,320]{1,0:T(8,128)S(1)}, u32[]{:S(2)}) copy-start(f32[160,320]{1,0:T(8,128)S(1)} %multiply_add_fusion.9) | copy-start | bytes 614404
  1042.4 49.1 %copy-start.26 = (f32[160,3,320]{2,0,1:T(8,128)}, f32[160,3,320]{2,0,1:T(8,128)S(1)}, u32[]{:S(2)}) copy-start(f32[160,3,320]{2,0,1:T(8,128)S(1)} %get-tuple-element.124) | copy-start | bytes 1843204
  1045.6 93.1 %all-reduce.21.cloned.1.call-start = ((), (), s32[]{:S(2)}) async-start(), calls=%async_computation.28 | async-start | bytes 1310720 | tf_op jit(solution)/shard_map/psum | solution.py:62
  1104.4 82.4 %all-reduce.19.cloned.1.call-start = ((), (), s32[]{:S(2)}) async-start(), calls=%async_computation.27 | async-start | bytes 1310720 | tf_op jit(solution)/shard_map/psum | solution.py:62
  1109.4 43.1 %copy-start.75 = (f32[384]{0:T(512)S(1)}, f32[384]{0:T(512)}, u32[]{:S(2)}) copy-start(f32[384]{0:T(512)} %get-tuple-element.67) | copy-start | bytes 4612
  1152.4 51.7 %copy-start.7 = (f32[384,1280]{1,0:T(8,128)S(1)}, f32[384,1280]{1,0:T(8,128)}, u32[]{:S(2)}) copy-start(f32[384,1280]{1,0:T(8,128)} %copy-done.6) | copy-start | bytes 5898244
  1152.4 51.7 %copy-start.72 = (f32[384]{0:T(512)S(1)}, f32[384]{0:T(512)}, u32[]{:S(2)}) copy-start(f32[384]{0:T(512)} %multiply_multiply_fusion.5) | copy-start | bytes 4612
  1152.4 99.9 %reduce-scatter.29.cloned.1.call-start = ((), (), s32[]{:S(2)}) async-start(), calls=%async_computation.24 | async-start | bytes 737280
  1153.2 135.5 %all-reduce.17.cloned.1.call-start = ((), (), s32[]{:S(2)}) async-start(), calls=%async_computation.26 | async-start | bytes 1310720 | tf_op jit(solution)/shard_map/psum | solution.py:62
  1204.1 134.4 %all-reduce.15.cloned.1.call-start = ((), (), s32[]{:S(2)}) async-start(), calls=%async_computation.25 | async-start | bytes 1310720 | tf_op jit(solution)/shard_map/psum | solution.py:62
  1207.3 94.5 %copy-start.10 = (f32[160,1280]{1,0:T(8,128)S(1)}, f32[160,1280]{1,0:T(8,128)}, u32[]{:S(2)}) copy-start(f32[160,1280]{1,0:T(8,128)} %copy-done.9) | copy-start | bytes 2457604
  1207.3 96.8 %copy-start.66 = (f32[160,6]{0,1:T(8,128)S(1)}, f32[160,6]{0,1:T(8,128)}, u32[]{:S(2)}) copy-start(f32[160,6]{0,1:T(8,128)} %param.24) | copy-start | bytes 11524
  1207.3 96.8 %copy-start.73 = (f32[160,6]{0,1:T(8,128)S(1)}, f32[160,6]{0,1:T(8,128)}, u32[]{:S(2)}) copy-start(f32[160,6]{0,1:T(8,128)} %param.31) | copy-start | bytes 11524
  1297.7 45.2 %copy-start.22 = (f32[160,320]{1,0:T(8,128)S(1)}, f32[160,320]{1,0:T(8,128)}, u32[]{:S(2)}) copy-start(f32[160,320]{1,0:T(8,128)} %copy-done.21) | copy-start | bytes 614404
  (60 other events, 588.4 us)
Sparse Core Ops, SparseCore 0:
  10.8 63.7 all-gather.11
  76.7 30.8 all-gather.9
  158.6 40.1 reduce-scatter.12
  201.7 62.2 all-gather.15
  266.1 31.5 all-gather.13
  300.5 61.9 all-gather.17
  364.2 31.5 all-gather.19
  432.0 42.8 reduce-scatter.16
  477.5 42.8 reduce-scatter.14
  527.3 32.9 all-gather.21
  564.4 121.6 reduce-scatter.24
  689.5 120.8 reduce-scatter.26
  814.3 65.7 reduce-scatter.22
  882.5 41.7 reduce-scatter.18
  928.3 111.8 reduce-scatter.20
  1045.7 33.9 all-reduce.22
  1104.5 34.1 all-reduce.20
  1152.5 34.1 all-reduce.18
  1190.4 61.9 reduce-scatter.28
  1255.3 33.2 all-reduce.16
  1304.2 34.1 all-reduce.14
where the time goes:
time: 1380 us; the launch traced here: 1360 us
  waiting for transfers between devices  674 us (49%)
  matrix products  413 us (30%)
  blocking collectives  150 us (11%)
  other arithmetic  67.3 us (5%)
  local copies, waits for them, and re-layouts  36.8 us (3%)
  between operations  21.7 us (2%)
    psum x5, waiting for transfers between devices, tensor_total(): return lax.psum((first, second, third, fourth), 'tensor')  147 us
    reduce_scatter x1, waiting for transfers between devices, local(): lax.psum_scatter(grad_wq, 'dp', scatter_dimension=0, tiled=True)  113 us
    dot_general x3, matrix products, local(): jnp.einsum('hqk,khd->qhd', d_scores, key_side, preferred_element_type=jnp...  81.6 us
    dot_general x3, matrix products, local(): jnp.einsum('hqk,qhd->khd', d_scores, q_part, preferred_element_type=jnp.f...  71.9 us
    unnamed x2, blocking collectives  57.1 us
    all_gather x1, waiting for transfers between devices, local(): lax.all_gather(w_down.astype(jnp.bfloat16), 'dp', axis=0, tiled=True)  54.9 us
    dot_general x4, matrix products, matmul_plain(): return jnp.dot(left, right, preferred_element_type=jnp.float32)  48.2 us
    unnamed x22, waiting for transfers between devices  46.7 us
  transfers between devices with their start and end apart: 21, of which 18 were waited for; matrix products, arithmetic and copies ran while one was open for 25% of the time, Pallas kernels for 0%

commit v1 on v0

v1 whole, which is shorter than its diff:
```python
from functools import partial
import math

import jax
import jax.numpy as jnp
from jax import lax
from jax.experimental import pallas as pl
from jax.experimental.pallas import tpu as pltpu
from jax.sharding import PartitionSpec as P

HD = 80
SWEEPS = 5
LANES = 128
WINDOW = 256
BIAS_LANE = WINDOW - 1
VMEM_LIMIT = 58 * 1024 * 1024

HIGHEST = lax.Precision.HIGHEST
NORM_EPS = 1e-05
POLAR_EPS = 1e-07
MASKED = -1e30
QUINTIC_A = 3.4445
QUINTIC_B = -4.775
QUINTIC_C = 2.0315
MUON_DECAY = 0.95
VEC_DECAY = 0.9
VEC_RATE = 0.1
STEP_QKV = 0.5 * math.sqrt(3.0)
STEP_OUT = 2.0
STEP_UP = 1.0
STEP_DOWN = 0.5
LOG2E = math.log2(math.e)
SCORE_SCALE = 1.0 / math.sqrt(HD)
F32 = jnp.float32
BF16 = jnp.bfloat16
LITTLE = pl.CostEstimate(flops=1_000_000, bytes_accessed=100_000, transcendentals=0)
NN = (((1,), (0,)), ((), ()))
NT = (((1,), (1,)), ((), ()))
TN = (((0,), (0,)), ((), ()))


def mm(left, right, dims=NN):
    return lax.dot_general(left, right, dims, preferred_element_type=F32)


def norm_parts(values):
    center = values - jnp.mean(values, axis=-1, keepdims=True)
    spread = jnp.mean(center * center, axis=-1, keepdims=True)
    scale = lax.rsqrt(spread + NORM_EPS)
    return center * scale, scale


def norm_back(grad, gain, unit, scale):
    inner = grad * gain
    mean_grad = jnp.mean(inner, axis=-1, keepdims=True)
    mean_unit = jnp.mean(inner * unit, axis=-1, keepdims=True)
    return scale * (inner - mean_grad - unit * mean_unit)


def params(*semantics):
    return pltpu.CompilerParams(
        dimension_semantics=semantics or None, vmem_limit_bytes=VMEM_LIMIT
    )


def swap(value, axis, mask):
    size = lax.axis_size(axis)
    return lax.ppermute(value, axis, [(i, i ^ mask) for i in range(size)])


def tensor_slots(own):
    near = swap(own, "tensor", 1)
    far = swap(own, "tensor", 2)
    return [own, near, far, swap(far, "tensor", 1)]


def tensor_gather(own):
    return jnp.concatenate(tensor_slots(own), axis=0)


def tensor_sum(value):
    value = value + swap(value, "tensor", 1)
    return value + swap(value, "tensor", 2)


def pair_sum(own, sent):
    arrived = swap(sent, "tensor", 1)
    return (own.astype(F32) + arrived.astype(F32)).astype(BF16)


def near_swap(sent):
    rows = sent.shape[0] // 2
    return jnp.concatenate(
        [swap(sent[:rows], "tensor", 1), swap(sent[rows:], "tensor", 1)], axis=0
    )


def after(value, *others):
    return lax.optimization_barrier((value, *others))[0]


def qkv_body(x_ref, vec_ref, w_ref, bias_ref, attn_ref, qkv_ref):
    unit, _ = norm_parts(x_ref[...].astype(F32))
    attn_in = (unit * vec_ref[0:1, :] + vec_ref[1:2, :]).astype(BF16)
    attn_ref[...] = attn_in
    qkv_ref[...] = (mm(attn_in, w_ref[...]) + bias_ref[0:1, :]).astype(BF16)


def qkv_call(x_rows, vec_rows, weight, bias, block):
    rows, width = x_rows.shape
    columns = weight.shape[1]
    return pl.pallas_call(
        qkv_body,
        grid=(rows // block,),
        in_specs=[
            pl.BlockSpec((block, width), lambda i: (i, 0)),
            pl.BlockSpec(vec_rows.shape, lambda i: (0, 0)),
            pl.BlockSpec(weight.shape, lambda i: (0, 0)),
            pl.BlockSpec(bias.shape, lambda i: (0, 0)),
        ],
        out_specs=[
            pl.BlockSpec((block, width), lambda i: (i, 0)),
            pl.BlockSpec((block, columns), lambda i: (i, 0)),
        ],
        out_shape=[
            jax.ShapeDtypeStruct((rows, width), BF16),
            jax.ShapeDtypeStruct((rows, columns), BF16),
        ],
        compiler_params=params("arbitrary"),
        cost_estimate=LITTLE,
        name="norm_qkv",
    )(x_rows, vec_rows, weight, bias)


def rows_body(dims, x_ref, w_ref, out_ref):
    out_ref[...] = mm(x_ref[...], w_ref[...], dims).astype(out_ref.dtype)


def rows_mm(x_rows, weight, dims, kind, block, first=0, count=None):
    rows, depth = x_rows.shape
    count = rows if count is None else count
    columns = weight.shape[1 - dims[0][1][0]]
    base = first // block
    return pl.pallas_call(
        partial(rows_body, dims),
        grid=(count // block,),
        in_specs=[
            pl.BlockSpec((block, depth), lambda i: (i + base, 0)),
            pl.BlockSpec(weight.shape, lambda i: (0, 0)),
        ],
        out_specs=pl.BlockSpec((block, columns), lambda i: (i, 0)),
        out_shape=jax.ShapeDtypeStruct((count, columns), kind),
        compiler_params=params("arbitrary"),
        cost_estimate=LITTLE,
        name="rows_product",
    )(x_rows, weight)


def sum_body(steps, *refs):
    lefts, (right_ref, out_ref, total) = refs[:-3], refs[-3:]
    step = pl.program_id(0)
    for index, left_ref in enumerate(lefts):

        @pl.when(step // steps == index)
        def _():
            term = mm(left_ref[...], right_ref[...], TN)
            if index:
                total[...] += term
            else:

                @pl.when(step == 0)
                def _():
                    total[...] = term

                @pl.when(step > 0)
                def _():
                    total[...] += term

    @pl.when(step == pl.num_programs(0) - 1)
    def _():
        out_ref[...] = total[...].astype(BF16)


def sum_mm(lefts, right, block):
    rows, width = lefts[0].shape
    columns = right.shape[1]
    steps = rows // block

    def spot(index):
        return lambda i: (jnp.clip(i - index * steps, 0, steps - 1), 0)

    return pl.pallas_call(
        partial(sum_body, steps),
        grid=(steps * len(lefts),),
        in_specs=[pl.BlockSpec((block, width), spot(index)) for index in range(len(lefts))]
        + [pl.BlockSpec((block, columns), lambda i: (i, 0))],
        out_specs=pl.BlockSpec((width, columns), lambda i: (0, 0)),
        out_shape=jax.ShapeDtypeStruct((width, columns), BF16),
        scratch_shapes=[pltpu.VMEM((width, columns), F32)],
        compiler_params=params("arbitrary"),
        cost_estimate=LITTLE,
        name="sum_product",
    )(*lefts, right)


def head_place(head):
    start = 0 if head * HD + HD <= BIAS_LANE else LANES
    return start, head * HD - start


def lane_mask(rows, head):
    _, offset = head_place(head)
    lane = lax.broadcasted_iota(jnp.int32, (rows, WINDOW), 1)
    return (lane >= offset) & (lane < offset + HD), lane == BIAS_LANE


def window(value, head):
    start, _ = head_place(head)
    return value[:, start : start + WINDOW].astype(F32)


def key_columns(qkv_ref):
    third = (qkv_ref.shape[1] + LANES) // 3
    return qkv_ref[:, third : 2 * third]


def value_columns(qkv_ref):
    third = (qkv_ref.shape[1] + LANES) // 3
    tail = qkv_ref[:, qkv_ref.shape[1] - third :].astype(F32)
    return pltpu.roll(tail, third - LANES // 2, 1)


def fill_keys(qkv_ref, bias_ref, keys_out, heads):
    columns = key_columns(qkv_ref)
    for head in range(heads):
        inside, last = lane_mask(columns.shape[0], head)
        picked = jnp.where(inside, window(columns, head), 0.0)
        keys_out[head] = jnp.where(last, bias_ref[...], picked).astype(BF16)


def join_windows(parts):
    low, high = None, None
    for head, part in enumerate(parts):
        if head_place(head)[0] == 0:
            low = part if low is None else low + part
        else:
            high = part if high is None else high + part
    return jnp.concatenate(
        [low[:, :LANES], low[:, LANES:] + high[:, :LANES], high[:, LANES:]], axis=1
    )


def attn_body(heads, q_ref, qkv_ref, bias_ref, wo_ref, *rest):
    att_ref, part_ref, lse_ref, keys, vals = rest[-5:]
    block = q_ref.shape[0]
    frames = qkv_ref.shape[0]

    @pl.when(pl.program_id(0) == 0)
    def _():
        fill_keys(qkv_ref, bias_ref, keys, heads)
        columns = value_columns(qkv_ref)
        for head in range(heads):
            inside, _ = lane_mask(frames, head)
            vals[head] = jnp.where(inside, window(columns, head), 0.0).astype(BF16)

    log_scale = SCORE_SCALE * LOG2E
    outs = []
    lane = lax.broadcasted_iota(jnp.int32, (block, LANES), 1)
    lse_cols = jnp.zeros((block, LANES), F32)
    for head in range(heads):
        _, last = lane_mask(block, head)
        query = jnp.where(last, 1.0, window(q_ref, head)).astype(BF16)
        scores = mm(query, keys[head], NT)
        row_max = jnp.max(scores, axis=1, keepdims=True)
        powers = jnp.exp2((scores - row_max) * log_scale)
        totals = jnp.sum(powers, axis=1, keepdims=True)
        outs.append(mm(powers.astype(BF16), vals[head]) * (1.0 / totals))
        lse_cols = jnp.where(lane == head, row_max * log_scale + jnp.log2(totals), lse_cols)
    attended = join_windows(outs).astype(BF16)
    att_ref[...] = attended
    lse_ref[...] = jnp.transpose(lse_cols)[:8]
    part_ref[...] = mm(attended, wo_ref[...], NT).astype(BF16)


def attn_call(heads, qkv, key_bias, wo, block, first, count, earlier=None):
    frames = qkv.shape[0]
    part_width = wo.shape[1]
    width = wo.shape[0]
    held = [] if earlier is None else list(earlier)
    base = first // block
    return pl.pallas_call(
        partial(attn_body, heads),
        grid=(count // block,),
        in_specs=[
            pl.BlockSpec((block, part_width), lambda i: (i + base, 0)),
            pl.BlockSpec(qkv.shape, lambda i: (0, 0)),
            pl.BlockSpec(key_bias.shape, lambda i: (0, 0)),
            pl.BlockSpec(wo.shape, lambda i: (0, 0)),
        ]
        + [pl.BlockSpec(memory_space=pl.ANY)] * len(held),
        out_specs=[
            pl.BlockSpec((block, part_width), lambda i: (i + base, 0)),
            pl.BlockSpec((block, width), lambda i: (i, 0)),
            pl.BlockSpec((8, block), lambda i: (0, i + base)),
        ],
        out_shape=[
            jax.ShapeDtypeStruct((frames, part_width), BF16),
            jax.ShapeDtypeStruct((count, width), BF16),
            jax.ShapeDtypeStruct((8, frames), F32),
        ],
        scratch_shapes=[
            pltpu.VMEM((heads, frames, WINDOW), BF16),
            pltpu.VMEM((heads, frames, WINDOW), BF16),
        ],
        input_output_aliases={} if earlier is None else {4: 0, 5: 2},
        compiler_params=params("arbitrary"),
        cost_estimate=LITTLE,
        name="attn_fwd",
    )(qkv, qkv, key_bias, wo, *held)


def attn_back_body(heads, last_part, first, dout_ref, wo_ref, att_ref, q_ref, qkv_ref, bias_ref, lse_ref, *rest):
    if last_part:
        dkey_in, dval_in, sums_in, _, dqkv_ref, sums_ref, keys, vals, d_query, d_key, d_val, packed, sems = rest
    else:
        dqkv_ref, sums_ref, d_key, d_val, keys, vals, d_query, sems = rest
    step = pl.program_id(0)
    block, part_width = q_ref.shape
    count = d_query.shape[0]

    @pl.when(step == 0)
    def _():
        fill_keys(qkv_ref, bias_ref, keys, heads)
        vals[...] = value_columns(qkv_ref).astype(BF16)
        if last_part:
            d_key[...] = dkey_in[...]
            d_val[...] = dval_in[...]
            sums_ref[...] = sums_in[...]
        else:
            d_key[...] = jnp.zeros_like(d_key)
            d_val[...] = jnp.zeros_like(d_val)
            sums_ref[...] = jnp.zeros_like(sums_ref)

    log_scale = SCORE_SCALE * LOG2E
    d_att = mm(dout_ref[...], wo_ref[...]).astype(BF16)
    inner_cols = jnp.transpose(d_att.astype(F32) * att_ref[...].astype(F32))
    outs = []
    for head in range(heads):
        start, _ = head_place(head)
        inside, last = lane_mask(block, head)
        q_window = window(q_ref, head)
        query = jnp.where(last, 1.0, q_window).astype(BF16)
        q_only = jnp.where(inside, q_window, 0.0).astype(BF16)
        d_only = jnp.where(inside, window(d_att, head), 0.0).astype(BF16)
        inner = jnp.sum(inner_cols[head * HD : head * HD + HD], axis=0, keepdims=True)
        scores = mm(keys[head], query, NT)
        probs = jnp.exp2(scores * log_scale - lse_ref[head : head + 1, :])
        d_probs = mm(vals[:, start : start + WINDOW], d_only, NT)
        d_scores = (probs * (d_probs - inner)).astype(BF16)
        d_val[:, start : start + WINDOW] += mm(probs.astype(BF16), d_only)
        d_key[:, start : start + WINDOW] += mm(d_scores, q_only)
        outs.append(mm(d_scores, keys[head], TN))
    low = (join_windows(outs) * SCORE_SCALE).astype(BF16)
    d_query[pl.ds(pl.multiple_of(step * block, block), block), :] = low
    sums_ref[0:1, :] += jnp.sum(low.astype(F32), axis=0, keepdims=True)

    @pl.when(step == pl.num_programs(0) - 1)
    def _():
        copies = [
            pltpu.make_async_copy(
                d_query, dqkv_ref.at[pl.ds(first, count), pl.ds(0, part_width)], sems.at[0]
            )
        ]
        copies[0].start()
        if last_part:
            key_low = d_key[...] * SCORE_SCALE
            value_low = d_val[...]
            sums_ref[1:2, :] = jnp.sum(value_low.astype(BF16).astype(F32), axis=0, keepdims=True)
            value_low = pltpu.roll(value_low, LANES // 2, 1)
            whole = part_width - LANES
            packed[:, :whole] = key_low[:, :whole].astype(BF16)
            packed[:, whole:part_width] = (key_low[:, whole:] + value_low[:, :LANES]).astype(BF16)
            packed[:, part_width:] = value_low[:, LANES:].astype(BF16)
            copies.append(
                pltpu.make_async_copy(
                    packed,
                    dqkv_ref.at[pl.ds(0, packed.shape[0]), pl.ds(part_width, packed.shape[1])],
                    sems.at[1],
                )
            )
            copies[1].start()
        for copy in copies:
            copy.wait()


def attn_back_call(heads, d_out, wo, attended, qkv, key_bias, lse, block, first, earlier=None):
    count, width = d_out.shape
    frames = qkv.shape[0]
    part_width = wo.shape[1]
    base = first // block
    last_part = earlier is not None
    whole = pl.BlockSpec((frames, part_width), lambda i: (0, 0))
    sums_spec = pl.BlockSpec((8, part_width), lambda i: (0, 0))
    anywhere = pl.BlockSpec(memory_space=pl.ANY)
    out_shape = [
        jax.ShapeDtypeStruct(qkv.shape, BF16),
        jax.ShapeDtypeStruct((8, part_width), F32),
    ]
    out_specs = [anywhere, sums_spec]
    scratch = [
        pltpu.VMEM((heads, frames, WINDOW), BF16),
        pltpu.VMEM((frames, part_width), BF16),
        pltpu.VMEM((count, part_width), BF16),
    ]
    held = []
    if last_part:
        d_qkv, sums, d_key, d_val = earlier
        held = [d_key, d_val, sums, d_qkv]
        scratch += [pltpu.VMEM((frames, part_width), F32)] * 2
        scratch += [pltpu.VMEM((frames, qkv.shape[1] - part_width), BF16)]
    else:
        out_shape += [jax.ShapeDtypeStruct((frames, part_width), F32)] * 2
        out_specs += [whole, whole]
    return pl.pallas_call(
        partial(attn_back_body, heads, last_part, first),
        grid=(count // block,),
        in_specs=[
            pl.BlockSpec((block, width), lambda i: (i, 0)),
            pl.BlockSpec(wo.shape, lambda i: (0, 0)),
            pl.BlockSpec((block, part_width), lambda i: (i + base, 0)),
            pl.BlockSpec((block, part_width), lambda i: (i + base, 0)),
            pl.BlockSpec(qkv.shape, lambda i: (0, 0)),
            pl.BlockSpec(key_bias.shape, lambda i: (0, 0)),
            pl.BlockSpec((8, block), lambda i: (0, i + base)),
        ]
        + [whole, whole, sums_spec, anywhere][: len(held)],
        out_specs=out_specs,
        out_shape=out_shape,
        scratch_shapes=scratch + [pltpu.SemaphoreType.DMA((2,))],
        input_output_aliases={10: 0} if last_part else {},
        compiler_params=params("arbitrary"),
        cost_estimate=LITTLE,
        name="attn_bwd",
    )(d_out, wo, attended, qkv, qkv, key_bias, lse, *held)


def gelu_parts(values):
    size = jnp.abs(values)
    bell = jnp.exp2(values * values * (-0.5 * LOG2E))
    inv = 1.0 / (1.0 + (0.3275911 * math.sqrt(0.5)) * size)
    tail = inv * (
        0.5 * 0.254829592
        + inv
        * (
            0.5 * -0.284496736
            + inv * (0.5 * 1.421413741 + inv * (0.5 * -1.453152027 + inv * (0.5 * 1.061405429)))
        )
    )
    tail = tail * bell
    share = jnp.where(values < 0.0, tail, 1.0 - tail)
    return share, share + values * bell * (1.0 / math.sqrt(2.0 * math.pi))


def mlp_body(chunk, in_ref, w_ref, bias_ref, dhid_ref, *rest):
    hid_ref, dpre_ref, part_ref, sums_ref = rest[-4:]

    @pl.when(pl.program_id(0) == 0)
    def _():
        sums_ref[...] = jnp.zeros_like(sums_ref)

    for start in range(0, w_ref.shape[1], chunk):
        cols = slice(start, start + chunk)
        pre = mm(in_ref[...], w_ref[:, cols]) + bias_ref[0:1, cols]
        share, slope = gelu_parts(pre)
        hid_ref[:, cols] = (pre * share).astype(BF16)
        d_pre = (dhid_ref[:, cols] * slope).astype(BF16)
        dpre_ref[:, cols] = d_pre
        sums_ref[0:1, cols] += jnp.sum(d_pre.astype(F32), axis=0, keepdims=True)
    part_ref[...] = mm(dpre_ref[...], w_ref[...], NT).astype(BF16)


def mlp_call(mlp_in, weight, bias, d_hidden, block, first, frames, earlier=None):
    count, width = mlp_in.shape
    hidden_width = weight.shape[1]
    held = [] if earlier is None else list(earlier)
    base = first // block
    return pl.pallas_call(
        partial(mlp_body, min(256, hidden_width)),
        grid=(count // block,),
        in_specs=[
            pl.BlockSpec((block, width), lambda i: (i, 0)),
            pl.BlockSpec(weight.shape, lambda i: (0, 0)),
            pl.BlockSpec(bias.shape, lambda i: (0, 0)),
            pl.BlockSpec((block, hidden_width), lambda i: (i + base, 0)),
        ]
        + [pl.BlockSpec(memory_space=pl.ANY)] * len(held),
        out_specs=[
            pl.BlockSpec((block, hidden_width), lambda i: (i + base, 0)),
            pl.BlockSpec((block, hidden_width), lambda i: (i + base, 0)),
            pl.BlockSpec((block, width), lambda i: (i, 0)),
            pl.BlockSpec((8, hidden_width), lambda i: (0, 0)),
        ],
        out_shape=[
            jax.ShapeDtypeStruct((frames, hidden_width), BF16),
            jax.ShapeDtypeStruct((frames, hidden_width), BF16),
            jax.ShapeDtypeStruct((count, width), BF16),
            jax.ShapeDtypeStruct((8, hidden_width), F32),
        ],
        input_output_aliases={} if earlier is None else {4: 0, 5: 1},
        compiler_params=params("arbitrary"),
        cost_estimate=LITTLE,
        name="mlp_up",
    )(mlp_in, weight, bias, d_hidden, *held)


def residual_body(x_ref, mine_ref, near_ref, far_ref, vec_ref, res_ref, in_ref):
    total = mine_ref[...].astype(F32) + near_ref[...].astype(F32) + far_ref[...].astype(F32)
    residual = x_ref[...].astype(F32) + total + vec_ref[2:3, :]
    res_ref[...] = residual
    unit, _ = norm_parts(residual)
    in_ref[...] = (unit * vec_ref[3:4, :] + vec_ref[4:5, :]).astype(BF16)


def second_back_body(
    res_ref, mine_ref, near_ref, far_ref, cot_ref, vec_ref, dres_ref, low_ref, sums_ref
):
    @pl.when(pl.program_id(0) == 0)
    def _():
        sums_ref[...] = jnp.zeros_like(sums_ref)

    grad = mine_ref[...].astype(F32) + near_ref[...].astype(F32) + far_ref[...].astype(F32)
    unit, scale = norm_parts(res_ref[...])
    cot = cot_ref[...].astype(F32)
    d_res = norm_back(grad, vec_ref[3:4, :], unit, scale) + cot
    dres_ref[...] = d_res
    low_ref[...] = d_res.astype(BF16)
    sums_ref[2:3, :] += jnp.sum(d_res, axis=0, keepdims=True)
    sums_ref[3:4, :] += jnp.sum(grad * unit, axis=0, keepdims=True)
    sums_ref[4:5, :] += jnp.sum(grad, axis=0, keepdims=True)
    sums_ref[5:6, :] += jnp.sum(cot, axis=0, keepdims=True)


def first_back_body(x_ref, mine_ref, near_ref, far_ref, dres_ref, vec_ref, out_ref, sums_ref):
    @pl.when(pl.program_id(0) == 0)
    def _():
        sums_ref[...] = jnp.zeros_like(sums_ref)

    grad = mine_ref[...].astype(F32) + near_ref[...].astype(F32) + far_ref[...].astype(F32)
    unit, scale = norm_parts(x_ref[...].astype(F32))
    out_ref[...] = norm_back(grad, vec_ref[0:1, :], unit, scale) + dres_ref[...]
    sums_ref[0:1, :] += jnp.sum(grad * unit, axis=0, keepdims=True)
    sums_ref[1:2, :] += jnp.sum(grad, axis=0, keepdims=True)


def row_call(body, rows_in, vec_rows, out_types, with_sums, block, name):
    rows, width = rows_in[0].shape
    row_spec = pl.BlockSpec((block, width), lambda i: (i, 0))
    whole = pl.BlockSpec((8, width), lambda i: (0, 0))
    return pl.pallas_call(
        body,
        grid=(rows // block,),
        in_specs=[row_spec] * len(rows_in) + [whole],
        out_specs=[row_spec] * len(out_types) + [whole] * with_sums,
        out_shape=[jax.ShapeDtypeStruct((rows, width), kind) for kind in out_types]
        + [jax.ShapeDtypeStruct((8, width), F32)] * with_sums,
        compiler_params=params("arbitrary"),
        name=name,
    )(*rows_in, vec_rows)


def polar_factors(grams, eye):
    def high(left, right):
        return jnp.dot(left, right, precision=HIGHEST, preferred_element_type=F32)

    scales = [1.0 / (jnp.sqrt(jnp.sum(gram * eye, keepdims=True)) + POLAR_EPS) for gram in grams]
    grams = [gram * scale * scale for gram, scale in zip(grams, scales)]
    factors = None
    for sweep in range(SWEEPS):
        squares = [high(gram, gram) for gram in grams]
        steps = [
            QUINTIC_A * eye + QUINTIC_B * gram + QUINTIC_C * square
            for gram, square in zip(grams, squares)
        ]
        if sweep < SWEEPS - 1:
            halves = [high(step, gram) for step, gram in zip(steps, grams)]
        if factors is None:
            factors = steps
        else:
            factors = [high(step, factor) for step, factor in zip(steps, factors)]
        if sweep < SWEEPS - 1:
            grams = [high(step, part) for step, part in zip(steps, halves)]
    return [factor * scale for factor, scale in zip(factors, scales)]


def polar_body(gram_ref, out_ref):
    count, rows, _ = gram_ref.shape
    row = lax.broadcasted_iota(jnp.int32, (rows, rows), 0)
    col = lax.broadcasted_iota(jnp.int32, (rows, rows), 1)
    eye = jnp.where(row == col, 1.0, 0.0)
    for index, factor in enumerate(polar_factors([gram_ref[i] for i in range(count)], eye)):
        out_ref[index] = factor


def polar_call(grams):
    count, rows, _ = grams.shape
    if rows % 32:
        return jnp.stack(polar_factors([grams[i] for i in range(count)], jnp.eye(rows, dtype=F32)))
    return pl.pallas_call(
        polar_body,
        out_shape=jax.ShapeDtypeStruct(grams.shape, F32),
        compiler_params=params(),
        name="polar",
    )(grams)


def gram_of(update):
    return lax.dot_general(update, update, NT, precision=HIGHEST, preferred_element_type=F32)


def momentum(moment, gradient):
    moved = MUON_DECAY * moment + gradient
    return moved, gradient + MUON_DECAY * moved


def applied(weight, factor, update, rate):
    return weight - rate * jnp.dot(factor, update, precision=HIGHEST)


def place_body(splits, me_ref, *refs):
    slots, outs = refs[:8], refs[8:]
    rows = slots[0].shape[0]
    for mask, slot in enumerate(slots):
        start = pl.multiple_of((me_ref[0] ^ mask) * rows, rows)
        for (low, high), out in zip(splits, outs):
            out[pl.ds(start, rows), :] = slot[:, low:high]


def place_rows(slots, splits):
    rows = slots[0].shape[0]
    return pl.pallas_call(
        partial(place_body, splits),
        in_specs=[pl.BlockSpec(memory_space=pltpu.SMEM)]
        + [pl.BlockSpec(memory_space=pltpu.VMEM)] * 8,
        out_specs=[pl.BlockSpec(memory_space=pltpu.VMEM)] * len(splits),
        out_shape=[
            jax.ShapeDtypeStruct((8 * rows, high - low), slots[0].dtype) for low, high in splits
        ],
        compiler_params=params(),
        cost_estimate=LITTLE,
        name="place_rows",
    )(lax.axis_index("dp").astype(jnp.int32)[None], *slots)


def dp_slots(own):
    slots = {0: own}
    for mask in (4, 6, 2):
        slots[mask] = swap(own, "dp", mask)
    for mask in (0, 2, 4, 6):
        slots[mask + 1] = swap(slots[mask], "dp", 1)
    return [slots[mask] for mask in range(8)]


def dp_send(own):
    if lax.axis_size("dp") != 8:
        return [lax.all_gather(own, "dp", axis=0, tiled=True)]
    return dp_slots(own)


def dp_place(slots, splits):
    if len(slots) == 1:
        return [slots[0][:, low:high] for low, high in splits]
    return place_rows(slots, splits)


def dp_scatter(part):
    size = lax.axis_size("dp")
    if size != 8:
        return dp_scatter_plain(part), []
    rows = part.shape[0] // size
    me = lax.axis_index("dp")

    def block(mask):
        return lax.dynamic_slice(part, ((me ^ mask) * rows, 0), (rows, part.shape[1]))

    total, arrivals = None, []
    for mask in (4, 6, 2, 0):
        arrived = swap(block(mask + 1), "dp", 1)
        arrivals.append(arrived)
        pair = block(mask).astype(F32) + arrived.astype(F32)
        if mask:
            pair = swap(pair.astype(BF16), "dp", mask).astype(F32)
        total = pair if total is None else total + pair
    return total, arrivals


def dp_scatter_plain(part):
    return lax.psum_scatter(part, "dp", scatter_dimension=0, tiled=True).astype(F32)


def dp_sum(value):
    if lax.axis_size("dp") != 8:
        return lax.psum(value, "dp")
    for mask in (1, 2, 4):
        value = value + swap(value, "dp", mask)
    return value


def local(
    inputs,
    lengths,
    cotangent,
    w_qkv,
    w_out,
    w_up,
    w_down,
    vectors,
    bias_qkv,
    bias_up,
    mom_qkv,
    mom_out,
    mom_up,
    mom_down,
    mom_vectors,
    mom_bias_qkv,
    mom_bias_up,
):
    dp_size = lax.axis_size("dp")
    tensor_size = lax.axis_size("tensor")
    dp_index = lax.axis_index("dp")
    tok = inputs.shape[0]
    frames = tok * tensor_size
    tokens = frames * dp_size
    half = 2 * tok
    width = inputs.shape[1]
    own_rows = w_qkv.shape[0]
    head_width = w_qkv.shape[2]
    heads = head_width // HD
    padded = -(-head_width // LANES) * LANES
    extra = padded - head_width
    own_bias = bias_qkv.shape[0]

    w_parts = w_qkv.astype(BF16)
    small = jnp.concatenate(
        [
            vectors.astype(BF16),
            bias_up.astype(BF16)[:, None],
            jnp.pad(bias_qkv.astype(BF16), ((0, own_rows - own_bias), (0, 0))),
        ],
        axis=1,
    )
    small = jnp.pad(small, ((0, 0), (0, extra - small.shape[1])))
    packed = 3 * head_width + extra
    w_cols = jnp.concatenate(
        [
            w_parts[:, 0],
            small,
            w_parts[:, 1],
            w_parts[:, 2],
            jnp.pad(w_out.astype(BF16), ((0, 0), (0, extra))),
        ],
        axis=1,
    )
    wd = lax.all_gather(w_down.astype(BF16), "dp", axis=0, tiled=True)
    x_rows = tensor_gather(inputs)
    cot_rows = tensor_gather(cotangent)
    first_slots = dp_send(w_cols)
    wq, wo = dp_place(first_slots, ((0, packed), (packed, packed + padded)))
    x_rows, cot_rows, wq, wo = lax.optimization_barrier((x_rows, cot_rows, wq, wo))
    w_up_low = after(w_up.astype(BF16), *first_slots)
    up_slots = dp_send(w_up_low)
    smalls = jnp.transpose(wq[:, head_width : head_width + 16].astype(F32))
    vec_rows = smalls[:8]
    bu = smalls[6:7]
    bq = smalls[7:9].reshape(2, dp_size, own_rows)[:, :, :own_bias].reshape(2, head_width)
    qkv_bias = jnp.concatenate(
        [bq[0:1], jnp.zeros((1, padded), F32), bq[1:2]], axis=1
    )

    me = lax.axis_index("tensor")
    place = jnp.concatenate([(me ^ s) * tok + jnp.arange(tok, dtype=jnp.int32) for s in range(4)])
    key_bias = jnp.where(place < lengths[0], 0.0, MASKED).astype(F32)[:, None]

    attn_in, qkv = qkv_call(x_rows, vec_rows, wq, qkv_bias, tok)
    att, part_three, lse = attn_call(heads, qkv, key_bias, wo, tok, 3 * tok, tok)
    att, part_two, lse = attn_call(heads, qkv, key_bias, wo, tok, 2 * tok, tok, (att, lse))
    total = pair_sum(part_two, part_three)
    far = swap(total, "tensor", 2)
    att, part_mine, lse = attn_call(
        heads, after(qkv, total, *up_slots[0:8:2]), key_bias, wo, tok, 0, half, (att, lse)
    )
    near = near_swap(part_mine[tok:])
    row_block = tok // 3
    residual, mlp_in = row_call(
        residual_body, (inputs, part_mine[:tok], near, after(far, wd)), vec_rows, (F32, BF16), 0, row_block, "residual"
    )

    near = swap(mlp_in, "tensor", 1)
    far = swap(mlp_in, "tensor", 2)
    block = tok * 2 // 3
    d_hidden = rows_mm(after(cot_rows, mlp_in), wd, NN, F32, block)
    parts = {}
    (wu,) = dp_place([*up_slots[:-1], after(up_slots[-1], d_hidden)], ((0, w_up.shape[1]),))
    in_mine = jnp.concatenate([mlp_in, near], axis=0)
    hidden, d_pre, part_mine, bu_sums = mlp_call(in_mine, wu, bu, d_hidden, block, 0, frames)
    parts[0], parts[1] = part_mine[:tok], part_mine[tok:]
    far = after(far, part_mine)
    slots = [mlp_in, near, far, swap(far, "tensor", 1)]
    for index in (3, 2):
        hidden, d_pre, parts[index], sums = mlp_call(
            slots[index], wu, bu, d_hidden, tok // 2, index * tok, frames, (hidden, d_pre)
        )
        bu_sums = bu_sums + sums
    total = pair_sum(parts[2], parts[3])
    far = swap(total, "tensor", 2)
    near = near_swap(parts[1])
    hidden_later, d_pre_later = lax.optimization_barrier((hidden, d_pre, total))[:2]
    raw_wd = sum_mm([cot_rows], hidden_later, half)
    in_rows = jnp.concatenate([in_mine, *slots[2:]], axis=0)
    raw_wu = sum_mm([in_rows], d_pre_later, half)
    near = after(near, raw_wd, raw_wu)
    grad_wd = dp_scatter_plain(raw_wd)
    grad_wu = dp_scatter_plain(raw_wu)
    d_residual, d_out, sums_two = row_call(
        second_back_body,
        (residual, parts[0], near, far, cotangent),
        vec_rows,
        (F32, BF16),
        1,
        row_block,
        "second_back",
    )
    near = swap(d_out, "tensor", 1)
    far = swap(d_out, "tensor", 2)
    out_mine = jnp.concatenate([d_out, near], axis=0)
    carried = attn_back_call(heads, out_mine, wo, att, qkv, key_bias, lse, block, 0)
    far = after(far, carried[1])
    out_far = jnp.concatenate([far, swap(far, "tensor", 1)], axis=0)
    d_qkv, bias_sums = attn_back_call(
        heads, out_far, wo, att, qkv, key_bias, lse, block, half, carried
    )
    raw_wo = sum_mm([out_mine, out_far], att, half)
    raw_wq = sum_mm([attn_in], d_qkv, half)
    grad_first, arrivals = dp_scatter(jnp.concatenate([raw_wq, raw_wo], axis=1))
    grad_wq, grad_wo = grad_first[:, :packed], grad_first[:, packed : packed + head_width]
    d_qkv, hidden = lax.optimization_barrier((d_qkv, hidden, raw_wq, raw_wo))[:2]
    first_far = rows_mm(d_qkv, wq, NT, BF16, tok, half, half)
    far = swap(pair_sum(first_far[:tok], first_far[tok:]), "tensor", 2)
    first_mine = rows_mm(d_qkv, wq, NT, BF16, tok, 0, half)
    near = swap(first_mine[tok:], "tensor", 1)
    hidden = after(hidden, *arrivals[:3])
    down_far = rows_mm(hidden, wd, NT, BF16, tok, half, half)
    output_far = swap(pair_sum(down_far[:tok], down_far[tok:]), "tensor", 2)
    down_mine = rows_mm(hidden, wd, NT, BF16, tok, 0, half)
    output_near = swap(down_mine[tok:], "tensor", 1)
    output = (
        residual
        + (down_mine[:tok].astype(F32) + output_near.astype(F32) + output_far.astype(F32))
        + vec_rows[5]
    )
    input_grad, sums_one = row_call(
        first_back_body,
        (inputs, first_mine[:tok], near, far, d_residual),
        vec_rows,
        (F32,),
        1,
        row_block,
        "first_back",
    )

    vec_sums = tensor_sum(sums_one + sums_two)
    rows_of = jnp.concatenate(
        [
            vec_sums[:6],
            bu_sums[0:1],
            jnp.pad(bias_sums[:2], ((0, 0), (0, width - padded))),
        ],
        axis=0,
    )
    rows_of = dp_sum(rows_of)
    own_cols = lax.dynamic_slice(rows_of, (0, dp_index * own_rows), (7, own_rows))
    vec_grad = jnp.transpose(own_cols[:6])
    bu_grad = own_cols[6]
    bq_grad = jnp.transpose(
        lax.dynamic_slice(rows_of, (7, dp_index * own_bias), (2, own_bias))
    )

    mom_down_new, update_down = momentum(mom_down, grad_wd)
    mom_up_new, update_up = momentum(mom_up, grad_wu)
    mom_out_new, update_out = momentum(mom_out, grad_wo)
    spots = (0, padded, padded + head_width)
    grad_parts = jnp.stack([grad_wq[:, spot : spot + head_width] for spot in spots], axis=1)
    mom_qkv_new, update_qkv = momentum(mom_qkv, grad_parts)
    flat = jnp.concatenate(
        [update_qkv[:, 0], jnp.zeros((own_rows, extra), F32), update_qkv[:, 1], update_qkv[:, 2]], axis=1
    )
    updates = (update_down, update_up, update_out, flat)
    factors = polar_call(tensor_sum(jnp.stack([gram_of(update) for update in updates])))
    new_w_down = applied(w_down, factors[0], update_down, STEP_DOWN)
    new_w_up = applied(w_up, factors[1], update_up, STEP_UP)
    new_w_out = applied(w_out, factors[2], update_out, STEP_OUT)
    polar_qkv = jnp.dot(factors[3], flat, precision=HIGHEST)
    new_w_qkv = w_qkv - STEP_QKV * jnp.stack(
        [polar_qkv[:, spot : spot + head_width] for spot in spots], axis=1
    )

    vec_rate = VEC_RATE / math.sqrt(tokens)
    new_mom_vectors = VEC_DECAY * mom_vectors + vec_grad
    new_mom_bias_qkv = VEC_DECAY * mom_bias_qkv + bq_grad
    new_mom_bias_up = VEC_DECAY * mom_bias_up + bu_grad
    new_vectors = vectors - vec_rate * new_mom_vectors
    new_bias_qkv = bias_qkv - vec_rate * new_mom_bias_qkv
    new_bias_up = bias_up - vec_rate * new_mom_bias_up
    return (
        output,
        input_grad,
        new_w_qkv,
        new_w_out,
        new_w_up,
        new_w_down,
        new_vectors,
        new_bias_qkv,
        new_bias_up,
        mom_qkv_new,
        mom_out_new,
        mom_up_new,
        mom_down_new,
        new_mom_vectors,
        new_mom_bias_qkv,
        new_mom_bias_up,
    )


def solution(mesh):
    in_specs = (
        P(("dp", "tensor"), None),
        P("dp"),
        P(("dp", "tensor"), None),
        P("dp", None, "tensor"),
        P("dp", "tensor"),
        P("dp", "tensor"),
        P("dp", "tensor"),
        P("dp", None),
        P(("tensor", "dp"), None),
        P(("tensor", "dp")),
        P("dp", None, "tensor"),
        P("dp", "tensor"),
        P("dp", "tensor"),
        P("dp", "tensor"),
        P("dp", None),
        P(("tensor", "dp"), None),
        P(("tensor", "dp")),
    )
    out_specs = (
        P(("dp", "tensor"), None),
        P(("dp", "tensor"), None),
        P("dp", None, "tensor"),
        P("dp", "tensor"),
        P("dp", "tensor"),
        P("dp", "tensor"),
        P("dp", None),
        P(("tensor", "dp"), None),
        P(("tensor", "dp")),
        P("dp", None, "tensor"),
        P("dp", "tensor"),
        P("dp", "tensor"),
        P("dp", "tensor"),
        P("dp", None),
        P(("tensor", "dp"), None),
        P(("tensor", "dp")),
    )
    return jax.shard_map(local, mesh=mesh, in_specs=in_specs, out_specs=out_specs, check_vma=False)
```

time: 1380 us -> 598 us (0.43)
  waiting for transfers between devices: 674 us -> 204 us
  matrix products: 413 us -> 13.6 us
  Pallas kernels: 0 us -> 222 us
  blocking collectives: 150 us -> 0 us
  starting transfers between devices: 1.55 us -> 58.9 us
  other arithmetic: 67.3 us -> 45.8 us
    dot_general x90 -> x8, matrix products: 413 us -> 13.6 us  [the longest x4 5.94 us: gram_of(): lax.dot_general(update, update, NT, precision=HIGHEST, preferred_element_...]
    reduce_scatter x8 -> x2, waiting for transfers between devices: 311 us -> 0.02 us  [dp_scatter_plain(): lax.psum_scatter(part, 'dp', scatter_dimension=0, tiled=True).astype(F32)]
    pallas_call x0 -> x24, Pallas kernels: none -> 222 us  [the longest x2 45.5 us: attn_back_call(): pl.pallas_call(partial(attn_back_body, heads, last_part, first), grid=(co...]
    ppermute x0 -> x54, waiting for transfers between devices: none -> 204 us  [swap(): return lax.ppermute(value, axis, [(i, i ^ mask) for i in range(size)])]
    all_gather x7 -> x1, waiting for transfers between devices: 169 us -> 0.01 us  [local(): wd = lax.all_gather(w_down.astype(BF16), 'dp', axis=0, tiled=True)]
    psum x5 -> x0, waiting for transfers between devices: 147 us -> none  [tensor_total(): return lax.psum((first, second, third, fourth), 'tensor')]
    all_gather x3 -> x0, blocking collectives: 87 us -> none  [the longest x1 34.2 us: local(): lax.all_gather(w_out.astype(jnp.bfloat16), 'dp', axis=0, tiled=True)]
    ppermute x0 -> x54, starting transfers between devices: none -> 58.8 us  [swap(): return lax.ppermute(value, axis, [(i, i ^ mask) for i in range(size)])]
  transfers between devices with their start and end apart: 21 -> 57, of which waited for: 18 -> 30; matrix products, arithmetic and copies ran while one was open for 25% -> 12% of each run, Pallas kernels for 0% -> 32%
where the time goes in v1:
time: 598 us; the launch traced here: 593 us
  Pallas kernels  222 us (37%)
  waiting for transfers between devices  204 us (34%)
  starting transfers between devices  58.9 us (10%)
  other arithmetic  45.8 us (8%)
  local copies, waits for them, and re-layouts  33.3 us (6%)
  between operations  15.5 us (3%)
  matrix products  13.6 us (2%)
    ppermute x54, waiting for transfers between devices, swap(): return lax.ppermute(value, axis, [(i, i ^ mask) for i in range(size)])  204 us
    ppermute x54, starting transfers between devices, swap(): return lax.ppermute(value, axis, [(i, i ^ mask) for i in range(size)])  58.8 us
    pallas_call x2, Pallas kernels, attn_back_call(): pl.pallas_call(partial(attn_back_body, heads, last_part, first), grid=(co...  45.5 us
    pallas_call x4, Pallas kernels, sum_mm(): pl.pallas_call(partial(sum_body, steps), grid=(steps * len(lefts),), in_s...  37.5 us
    pallas_call x5, Pallas kernels, rows_mm(): pl.pallas_call(partial(rows_body, dims), grid=(count // block,), in_specs...  33.9 us
    pallas_call x3, Pallas kernels, attn_call(): pl.pallas_call(partial(attn_body, heads), grid=(count // block,), in_spec...  30.6 us
    pallas_call x3, Pallas kernels, mlp_call(): pl.pallas_call(partial(mlp_body, min(256, hidden_width)), grid=(count //...  28.3 us
    pallas_call x3, Pallas kernels, row_call(): pl.pallas_call(body, grid=(rows // block,), in_specs=[row_spec] * len(row...  16.7 us
  transfers between devices with their start and end apart: 57, of which 30 were waited for; matrix products, arithmetic and copies ran while one was open for 12% of the time, Pallas kernels for 32%

profile of v1, /device:TPU:0, one launch (start us, length us, event | category | flops | bytes accessed | tf_op | source)
XLA Modules:
  0.0 593.0 jit_solution(9907564163628632103)
XLA Ops:
  23.1 5.9 collective-permute-done.6.refs_1_
  31.1 7.8 %collective-permute-done.7.refs_2_ = bf16[160,1408]{1,0:T(8,128)(2,1)} collective-permute-done((bf16[160,1408]{1,0:T(8,128)(2,1)S(1)}, bf16[160,1408]{1,0:T(8,128)(2,1)}, u32[]{:S(2)}, u32[]{:S(2)}) %collective-permute-start.7) | collective-permute-done | bytes 450592 | tf_op jit(solution)/shard_map/ppermute | solution.py:68
  38.9 20.8 %collective-permute-done.9.refs_4_ = bf16[160,1408]{1,0:T(8,128)(2,1)} collective-permute-done((bf16[160,1408]{1,0:T(8,128)(2,1)S(1)}, bf16[160,1408]{1,0:T(8,128)(2,1)}, u32[]{:S(2)}, u32[]{:S(2)}) %collective-permute-start.9) | collective-permute-done | bytes 450592 | tf_op jit(solution)/shard_map/ppermute | solution.py:68
  62.9 5.4 collective-permute-done.8.refs_3_
  68.4 6.4 %collective-permute-done.10.refs_5_ = bf16[160,1408]{1,0:T(8,128)(2,1)} collective-permute-done((bf16[160,1408]{1,0:T(8,128)(2,1)}, bf16[160,1408]{1,0:T(8,128)(2,1)}, u32[]{:S(2)}, u32[]{:S(2)}) %collective-permute-start.10) | collective-permute-done | bytes 450592 | tf_op jit(solution)/shard_map/ppermute | solution.py:68
  75.8 18.1 %collective-permute-done.12.refs_7_ = bf16[160,1408]{1,0:T(8,128)(2,1)} collective-permute-done((bf16[160,1408]{1,0:T(8,128)(2,1)}, bf16[160,1408]{1,0:T(8,128)(2,1)}, u32[]{:S(2)}, u32[]{:S(2)}) %collective-permute-start.12) | collective-permute-done | bytes 450592 | tf_op jit(solution)/shard_map/ppermute | solution.py:68
  93.9 4.1 place_rows.2
  98.0 3.3 pad_maximum_fusion.x_ref
  101.3 3.8 pad_maximum_fusion.1.x_ref.refs_0_
  110.2 10.0 %norm_qkv.1 = (bf16[1536,1280]{1,0:T(8,128)(2,1)}, bf16[1536,1024]{1,0:T(8,128)(2,1)}) custom-call(bf16[1536,1280]{1,0:T(8,128)(2,1)} %pad_maximum_fusion.x_ref, f32[8,1280]{1,0:T(8,128)} %slice.198.vec_ref, bf16[1280,1024]{1,0:T(8,128)(2,1)} %get-tuple-element.74.w_ref, f32[1,1024]{1,0:T(1,128)} %pad_maximum_fusion.11.bias_ref), custom_call_target="tpu_custom_call" | custom-call | flops 1000000 | bytes 100000 | tf_op jit(solution)/shard_map/norm_qkv/pallas_call | solution.py:112
  120.1 8.3 %attn_fwd.3 = (bf16[1536,384]{1,0:T(8,128)(2,1)}, bf16[384,1280]{1,0:T(8,128)(2,1)}, f32[8,1536]{1,0:T(8,128)}) custom-call(bf16[1536,1024]{1,0:T(8,128)(2,1)} %get-tuple-element.82.q_ref.qkv_ref, bf16[1536,1024]{1,0:T(8,128)(2,1)} %get-tuple-element.82.q_ref.qkv_ref, f32[1536,1]{1,0:T(8,128)} %broadcast_select_fusion.bias_ref, ...), custom_call_target="tpu_custom_call" | custom-call | flops 1000000 | bytes 100000 | tf_op jit(solution)/shard_map/attn_fwd/pallas_call | solution.py:291
  128.5 19.4 %collective-permute-start.14 = (bf16[160,1280]{1,0:T(8,128)(2,1)S(1)}, bf16[160,1280]{1,0:T(8,128)(2,1)S(1)}, u32[]{:S(2)}, u32[]{:S(2)}) collective-permute-start(bf16[160,1280]{1,0:T(8,128)(2,1)S(1)} %convert_element_type.131.refs_0_), channel_id=1, source_target_pairs={{0,8},{4,12},{8,0},{12,4},{16,24},{20,28},{24,16},{28,20},{1,9},{5... | collective-permute-start | bytes 1228808 | tf_op jit(solution)/shard_map/ppermute | solution.py:68
  150.3 8.2 %attn_fwd.4 = (bf16[1536,384]{1,0:T(8,128)(2,1)}, bf16[384,1280]{1,0:T(8,128)(2,1)}, f32[8,1536]{1,0:T(8,128)}) custom-call(bf16[1536,1024]{1,0:T(8,128)(2,1)} %get-tuple-element.82.q_ref.qkv_ref, bf16[1536,1024]{1,0:T(8,128)(2,1)} %get-tuple-element.82.q_ref.qkv_ref, ...), custom_call_target="tpu_custom_call", output_to_operand_aliasing={{0}: (4, {}), {2}: (5, {})} | custom-call | flops 1000000 | bytes 100000 | tf_op jit(solution)/shard_map/attn_fwd/pallas_call | solution.py:291
  160.5 5.8 collective-permute-done.14.refs_2_
  166.3 12.3 %collective-permute-done.15.refs_4_ = bf16[160,1280]{1,0:T(8,128)(2,1)S(1)} collective-permute-done((bf16[160,1280]{1,0:T(8,128)(2,1)S(1)}, bf16[160,1280]{1,0:T(8,128)(2,1)S(1)}, u32[]{:S(2)}, u32[]{:S(2)}) %collective-permute-start.15) | collective-permute-done | bytes 409632 | tf_op jit(solution)/shard_map/ppermute | solution.py:68
  178.7 14.1 %attn_fwd.5 = (bf16[1536,384]{1,0:T(8,128)(2,1)}, bf16[768,1280]{1,0:T(8,128)(2,1)}, f32[8,1536]{1,0:T(8,128)}) custom-call(bf16[1536,1024]{1,0:T(8,128)(2,1)} %get-tuple-element.82.q_ref.qkv_ref, bf16[1536,1024]{1,0:T(8,128)(2,1)} %get-tuple-element.82.q_ref.qkv_ref, ...), custom_call_target="tpu_custom_call", output_to_operand_aliasing={{0}: (4, {}), {2}: (5, {})} | custom-call | flops 1000000 | bytes 100000 | tf_op jit(solution)/shard_map/attn_fwd/pallas_call | solution.py:291
  198.8 4.7 residual.1
  206.7 9.2 %collective-permute-done.24.refs_7_ = bf16[160,1280]{1,0:T(8,128)(2,1)S(1)} collective-permute-done((bf16[160,1280]{1,0:T(8,128)(2,1)S(1)}, bf16[160,1280]{1,0:T(8,128)(2,1)S(1)}, u32[]{:S(2)}, u32[]{:S(2)}) %collective-permute-start.24) | collective-permute-done | bytes 409632 | tf_op jit(solution)/shard_map/ppermute | solution.py:68
  217.0 10.6 %rows_product.5.dhid_ref = f32[1536,1280]{1,0:T(8,128)} custom-call(bf16[1536,1280]{1,0:T(8,128)(2,1)} %pad_maximum_fusion.1.x_ref.refs_0_, bf16[1280,1280]{1,0:T(8,128)(2,1)} %all-gather.2.cloned.1.call-done.w_ref), custom_call_target="tpu_custom_call" | custom-call | flops 1000000 | bytes 100000 | tf_op jit(solution)/shard_map/rows_product/pallas_call | solution.py:144
  227.6 5.8 collective-permute-done.22.refs_3_
  233.4 8.3 %collective-permute-done.23.refs_5_ = bf16[160,1280]{1,0:T(8,128)(2,1)S(1)} collective-permute-done((bf16[160,1280]{1,0:T(8,128)(2,1)S(1)}, bf16[160,1280]{1,0:T(8,128)(2,1)S(1)}, u32[]{:S(2)}, u32[]{:S(2)}) %collective-permute-start.23) | collective-permute-done | bytes 409632 | tf_op jit(solution)/shard_map/ppermute | solution.py:68
  242.5 3.8 place_rows.3.w_ref
  247.7 12.2 %mlp_up.3 = (bf16[1536,1280]{1,0:T(8,128)(2,1)}, bf16[1536,1280]{1,0:T(8,128)(2,1)}, bf16[768,1280]{1,0:T(8,128)(2,1)}, f32[8,1280]{1,0:T(8,128)}) custom-call(bf16[768,1280]{1,0:T(8,128)(2,1)} %pad_maximum_fusion.3.in_ref, bf16[1280,1280]{1,0:T(8,128)(2,1)} %place_rows.3.w_ref, f32[1,1280]{1,0:T(1,128)} %get-tuple-element.161.bias_ref, ...), custom_call_target="tpu_custom_call" | custom-call | flops 1000000 | bytes 100000 | tf_op jit(solution)/shard_map/mlp_up/pallas_call | solution.py:487
  263.5 8.1 %mlp_up.4 = (bf16[1536,1280]{1,0:T(8,128)(2,1)}, bf16[1536,1280]{1,0:T(8,128)(2,1)}, bf16[384,1280]{1,0:T(8,128)(2,1)}, f32[8,1280]{1,0:T(8,128)}) custom-call(bf16[384,1280]{1,0:T(8,128)(2,1)} %copy-done.15, bf16[1280,1280]{1,0:T(8,128)(2,1)} %place_rows.3.w_ref, ...), custom_call_target="tpu_custom_call", output_to_operand_aliasing={{0}: (4, {}), {1}: (5, {})} | custom-call | flops 1000000 | bytes 100000 | tf_op jit(solution)/shard_map/mlp_up/pallas_call | solution.py:487
  271.8 8.0 %mlp_up.5 = (bf16[1536,1280]{1,0:T(8,128)(2,1)}, bf16[1536,1280]{1,0:T(8,128)(2,1)}, bf16[384,1280]{1,0:T(8,128)(2,1)}, f32[8,1280]{1,0:T(8,128)}) custom-call(bf16[384,1280]{1,0:T(8,128)(2,1)} %copy-done.13, bf16[1280,1280]{1,0:T(8,128)(2,1)} %place_rows.3.w_ref, ...), custom_call_target="tpu_custom_call", output_to_operand_aliasing={{0}: (4, {}), {1}: (5, {})} | custom-call | flops 1000000 | bytes 100000 | tf_op jit(solution)/shard_map/mlp_up/pallas_call | solution.py:487
  284.4 10.8 %sum_product.5 = bf16[1280,1280]{1,0:T(8,128)(2,1)} custom-call(bf16[1536,1280]{1,0:T(8,128)(2,1)} %pad_maximum_fusion.2.refs_0_, bf16[1536,1280]{1,0:T(8,128)(2,1)} %get-tuple-element.103.refs_1_), custom_call_target="tpu_custom_call" | custom-call | flops 1000000 | bytes 100000 | tf_op jit(solution)/shard_map/sum_product/pallas_call | solution.py:192
  300.5 11.0 %sum_product.4 = bf16[1280,1280]{1,0:T(8,128)(2,1)} custom-call(bf16[1536,1280]{1,0:T(8,128)(2,1)} %pad_maximum_fusion.1.x_ref.refs_0_, bf16[1536,1280]{1,0:T(8,128)(2,1)} %get-tuple-element.116.refs_1_.x_ref), custom_call_target="tpu_custom_call" | custom-call | flops 1000000 | bytes 100000 | tf_op jit(solution)/shard_map/sum_product/pallas_call | solution.py:192
  311.5 8.0 %collective-permute-done.30.far_ref = bf16[384,1280]{1,0:T(8,128)(2,1)} collective-permute-done((bf16[384,1280]{1,0:T(8,128)(2,1)S(1)}, bf16[384,1280]{1,0:T(8,128)(2,1)}, u32[]{:S(2)}, u32[]{:S(2)}) %collective-permute-start.30) | collective-permute-done | bytes 983072 | tf_op jit(solution)/shard_map/ppermute | solution.py:68
  319.5 6.2 %second_back.1 = (f32[384,1280]{1,0:T(8,128)}, bf16[384,1280]{1,0:T(8,128)(2,1)}, f32[8,1280]{1,0:T(8,128)}) custom-call(f32[384,1280]{1,0:T(8,128)} %get-tuple-element.87.res_ref, bf16[384,1280]{1,0:T(8,128)(2,1)} %slice.163.mine_ref, bf16[384,1280]{1,0:T(8,128)(2,1)} %pad_maximum_fusion.5.near_ref, bf16[384,1280]{1,0:T(8,128)(2,1)} %collective-permute-done.30.far_ref, ...), custom_call_target="tpu_custom_call" | custom-call | tf_op jit(solution)/shard_map/second_back/pallas_call | solution.py:559
  329.9 22.3 %attn_bwd.2 = (bf16[1536,1024]{1,0:T(8,128)(2,1)}, f32[8,384]{1,0:T(8,128)}, f32[1536,384]{1,0:T(8,128)}, f32[1536,384]{1,0:T(8,128)}) custom-call(bf16[768,1280]{1,0:T(8,128)(2,1)} %copy-done.3, bf16[1280,384]{1,0:T(8,128)(2,1)} %get-tuple-element.76.wo_ref, bf16[1536,384]{1,0:T(8,128)(2,1)} %get-tuple-element.106.att_ref.refs_2_, ...), custom_call_target="tpu_custom_call" | custom-call | flops 1000000 | bytes 100000 | tf_op jit(solution)/shard_map/attn_bwd/pallas_call | solution.py:424
  356.2 6.1 %sum_product.7 = bf16[1280,384]{1,0:T(8,128)(2,1)} custom-call(bf16[768,1280]{1,0:T(8,128)(2,1)} %copy-done.3, bf16[768,1280]{1,0:T(8,128)(2,1)} %copy-done.4, bf16[1536,384]{1,0:T(8,128)(2,1)} %get-tuple-element.106.att_ref.refs_2_), custom_call_target="tpu_custom_call" | custom-call | flops 1000000 | bytes 100000 | tf_op jit(solution)/shard_map/sum_product/pallas_call | solution.py:192
  362.2 23.3 %attn_bwd.3 = (bf16[1536,1024]{1,0:T(8,128)(2,1)}, f32[8,384]{1,0:T(8,128)}) custom-call(bf16[768,1280]{1,0:T(8,128)(2,1)} %copy-done.4, bf16[1280,384]{1,0:T(8,128)(2,1)} %get-tuple-element.76.wo_ref, bf16[1536,384]{1,0:T(8,128)(2,1)} %get-tuple-element.106.att_ref.refs_2_, ...), custom_call_target="tpu_custom_call", output_to_operand_aliasing={{0}: (10, {})} | custom-call | flops 1000000 | bytes 100000 | tf_op jit(solution)/shard_map/attn_bwd/pallas_call | solution.py:424
  385.5 9.6 %sum_product.6 = bf16[1280,1024]{1,0:T(8,128)(2,1)} custom-call(bf16[1536,1280]{1,0:T(8,128)(2,1)} %get-tuple-element.114.refs_0_, bf16[1536,1024]{1,0:T(8,128)(2,1)} %get-tuple-element.117.refs_1_.x_ref), custom_call_target="tpu_custom_call" | custom-call | flops 1000000 | bytes 100000 | tf_op jit(solution)/shard_map/sum_product/pallas_call | solution.py:192
  399.8 5.4 rows_product.9
  407.4 5.4 rows_product.8
  418.5 10.8 %collective-permute-done.35 = bf16[160,1408]{1,0:T(8,128)(2,1)} collective-permute-done((bf16[160,1408]{1,0:T(8,128)(2,1)}, bf16[160,1408]{1,0:T(8,128)(2,1)}, u32[]{:S(2)}, u32[]{:S(2)}) %collective-permute-start.35) | collective-permute-done | bytes 450592 | tf_op jit(solution)/shard_map/ppermute | solution.py:68
  429.3 14.0 %collective-permute-done.36 = bf16[160,1408]{1,0:T(8,128)(2,1)} collective-permute-done((bf16[160,1408]{1,0:T(8,128)(2,1)}, bf16[160,1408]{1,0:T(8,128)(2,1)}, u32[]{:S(2)}, u32[]{:S(2)}) %collective-permute-start.36) | collective-permute-done | bytes 450592 | tf_op jit(solution)/shard_map/ppermute | solution.py:68
  445.8 4.0 collective-permute-start.45
  455.8 6.2 %rows_product.7 = bf16[768,1280]{1,0:T(8,128)(2,1)} custom-call(bf16[1536,1280]{1,0:T(8,128)(2,1)} %get-tuple-element.116.refs_1_.x_ref, bf16[1280,1280]{1,0:T(8,128)(2,1)} %all-gather.2.cloned.1.call-done.w_ref), custom_call_target="tpu_custom_call" | custom-call | flops 1000000 | bytes 100000 | tf_op jit(solution)/shard_map/rows_product/pallas_call | solution.py:144
  464.2 6.2 %rows_product.6 = bf16[768,1280]{1,0:T(8,128)(2,1)} custom-call(bf16[1536,1280]{1,0:T(8,128)(2,1)} %get-tuple-element.116.refs_1_.x_ref, bf16[1280,1280]{1,0:T(8,128)(2,1)} %all-gather.2.cloned.1.call-done.w_ref), custom_call_target="tpu_custom_call" | custom-call | flops 1000000 | bytes 100000 | tf_op jit(solution)/shard_map/rows_product/pallas_call | solution.py:144
  472.6 6.0 %collective-permute-done.45 = bf16[160,1408]{1,0:T(8,128)(2,1)} collective-permute-done((bf16[160,1408]{1,0:T(8,128)(2,1)}, bf16[160,1408]{1,0:T(8,128)(2,1)}, u32[]{:S(2)}, u32[]{:S(2)}) %collective-permute-start.45) | collective-permute-done | bytes 450592 | tf_op jit(solution)/shard_map/ppermute | solution.py:68
  478.6 7.7 %collective-permute-done.44 = bf16[160,1408]{1,0:T(8,128)(2,1)} collective-permute-done((bf16[160,1408]{1,0:T(8,128)(2,1)}, bf16[160,1408]{1,0:T(8,128)(2,1)}, u32[]{:S(2)}, u32[]{:S(2)}) %collective-permute-start.44) | collective-permute-done | bytes 450592 | tf_op jit(solution)/shard_map/ppermute | solution.py:68
  486.4 16.0 %collective-permute-done.43 = bf16[160,1408]{1,0:T(8,128)(2,1)} collective-permute-done((bf16[160,1408]{1,0:T(8,128)(2,1)}, bf16[160,1408]{1,0:T(8,128)(2,1)}, u32[]{:S(2)}, u32[]{:S(2)}) %collective-permute-start.43) | collective-permute-done | bytes 450592 | tf_op jit(solution)/shard_map/ppermute | solution.py:68
  505.1 5.8 first_back.1
  522.1 4.0 collective-permute-done.52
  544.1 10.7 %collective-permute-done.39 = bf16[384,1280]{1,0:T(8,128)(2,1)} collective-permute-done((bf16[384,1280]{1,0:T(8,128)(2,1)}, bf16[384,1280]{1,0:T(8,128)(2,1)}, u32[]{:S(2)}, u32[]{:S(2)}) %collective-permute-start.39) | collective-permute-done | bytes 983072 | tf_op jit(solution)/shard_map/ppermute | solution.py:68
  558.1 6.4 %collective-permute-done.48 = f32[4,160,160]{2,1,0:T(8,128)S(1)} collective-permute-done((f32[4,160,160]{2,1,0:T(8,128)S(1)}, f32[4,160,160]{2,1,0:T(8,128)S(1)}, u32[]{:S(2)}, u32[]{:S(2)}) %collective-permute-start.48) | collective-permute-done | bytes 409632 | tf_op jit(solution)/shard_map/ppermute | solution.py:68
  565.4 12.0 %polar.1 = f32[4,160,160]{2,1,0:T(8,128)} custom-call(f32[4,160,160]{2,1,0:T(8,128)} %fusion.36.gram_ref), custom_call_target="tpu_custom_call" | custom-call | tf_op jit(solution)/shard_map/polar/pallas_call | solution.py:608
  (309 shorter events, 135.3 us)
Async XLA Ops:
  7.2 190.6 %all-gather.2.cloned.1.call-start = ((), (), s32[]{:S(2)}) async-start(), calls=%async_computation.2 | async-start | bytes 3686400 | tf_op jit(solution)/shard_map/all_gather | solution.py:763
  7.2 54.5 %collective-permute-start.1 = (bf16[384,1280]{1,0:T(8,128)(2,1)}, bf16[384,1280]{1,0:T(8,128)(2,1)S(1)}, u32[]{:S(2)}, u32[]{:S(2)}) collective-permute-start(bf16[384,1280]{1,0:T(8,128)(2,1)} %x_ref.3), channel_id=1, source_target_pairs={{0,2},{1,3},{2,0},{3,1},{4,6},{5,7},{6,4},{7,5},{8,10},{9,11},{10,... | collective-permute-start | bytes 2949128 | tf_op jit(solution)/shard_map/ppermute | solution.py:68
  17.1 11.9 %collective-permute-start.6 = (bf16[160,1408]{1,0:T(8,128)(2,1)S(1)}, bf16[160,1408]{1,0:T(8,128)(2,1)S(1)}, u32[]{:S(2)}, u32[]{:S(2)}) collective-permute-start(bf16[160,1408]{1,0:T(8,128)(2,1)S(1)} %concatenate.64.refs_0_), channel_id=1, source_target_pairs={{0,4},{4,0},{8,12},{12,8},{16,20},{20,16},{24,28},{28,24},{1,5},{5... | collective-permute-start | bytes 1351688 | tf_op jit(solution)/shard_map/ppermute | solution.py:68
  18.7 20.2 %collective-permute-start.7 = (bf16[160,1408]{1,0:T(8,128)(2,1)S(1)}, bf16[160,1408]{1,0:T(8,128)(2,1)}, u32[]{:S(2)}, u32[]{:S(2)}) collective-permute-start(bf16[160,1408]{1,0:T(8,128)(2,1)S(1)} %concatenate.64.refs_0_), channel_id=1, source_target_pairs={{0,8},{4,12},{8,0},{12,4},{16,24},{20,28},{24,16},{28,20},{1,9},{5... | collective-permute-start | bytes 1351688 | tf_op jit(solution)/shard_map/ppermute | solution.py:68
  20.3 39.5 %collective-permute-start.9 = (bf16[160,1408]{1,0:T(8,128)(2,1)S(1)}, bf16[160,1408]{1,0:T(8,128)(2,1)}, u32[]{:S(2)}, u32[]{:S(2)}) collective-permute-start(bf16[160,1408]{1,0:T(8,128)(2,1)S(1)} %concatenate.64.refs_0_), channel_id=1, source_target_pairs={{0,16},{4,20},{8,24},{12,28},{16,0},{20,4},{24,8},{28,12},{1,17},{... | collective-permute-start | bytes 1351688 | tf_op jit(solution)/shard_map/ppermute | solution.py:68
  22.9 36.9 %collective-permute-start.11 = (bf16[160,1408]{1,0:T(8,128)(2,1)S(1)}, bf16[160,1408]{1,0:T(8,128)(2,1)}, u32[]{:S(2)}, u32[]{:S(2)}) collective-permute-start(bf16[160,1408]{1,0:T(8,128)(2,1)S(1)} %concatenate.64.refs_0_), channel_id=1, source_target_pairs={{0,24},{4,28},{8,16},{12,20},{16,8},{20,12},{24,0},{28,4},{1,25},{... | collective-permute-start | bytes 1351688 | tf_op jit(solution)/shard_map/ppermute | solution.py:68
  29.8 44.9 %collective-permute-start.4 = (bf16[384,1280]{1,0:T(8,128)(2,1)}, bf16[384,1280]{1,0:T(8,128)(2,1)}, u32[]{:S(2)}, u32[]{:S(2)}) collective-permute-start(bf16[384,1280]{1,0:T(8,128)(2,1)} %cot_ref.1), channel_id=1, source_target_pairs={{0,2},{1,3},{2,0},{3,1},{4,6},{5,7},{6,4},{7,5},{8,10},{9,11},{10,... | collective-permute-start | bytes 2949128 | tf_op jit(solution)/shard_map/ppermute | solution.py:68
  31.1 501.5 %reduce-scatter.5.cloned.1.call-start = ((), (), s32[]{:S(2)}) async-start(), calls=%async_computation.4 | async-start | bytes 3686400 | tf_op jit(solution)/shard_map/reduce_scatter | solution.py:697
  38.9 59.0 %collective-permute-start = (bf16[384,1280]{1,0:T(8,128)(2,1)S(1)}, bf16[384,1280]{1,0:T(8,128)(2,1)}, u32[]{:S(2)}, u32[]{:S(2)}) collective-permute-start(bf16[384,1280]{1,0:T(8,128)(2,1)S(1)} %copy-done.5), channel_id=1, source_target_pairs={{0,1},{1,0},{2,3},{3,2},{4,5},{5,4},{6,7},{7,6},{8,9},{9,8},{10,11... | collective-permute-start | bytes 2949128 | tf_op jit(solution)/shard_map/ppermute | solution.py:68
  59.7 8.6 %collective-permute-start.8 = (bf16[160,1408]{1,0:T(8,128)(2,1)}, bf16[160,1408]{1,0:T(8,128)(2,1)S(1)}, u32[]{:S(2)}, u32[]{:S(2)}) collective-permute-start(bf16[160,1408]{1,0:T(8,128)(2,1)} %collective-permute-done.7.refs_2_), channel_id=1, source_target_pairs={{0,4},{4,0},{8,12},{12,8},{16,20},{20,16},{24,28},{28,24},{1,5},{5... | collective-permute-start | bytes 1351688 | tf_op jit(solution)/shard_map/ppermute | solution.py:68
  59.8 15.0 %collective-permute-start.10 = (bf16[160,1408]{1,0:T(8,128)(2,1)}, bf16[160,1408]{1,0:T(8,128)(2,1)}, u32[]{:S(2)}, u32[]{:S(2)}) collective-permute-start(bf16[160,1408]{1,0:T(8,128)(2,1)} %collective-permute-done.9.refs_4_), channel_id=1, source_target_pairs={{0,4},{4,0},{8,12},{12,8},{16,20},{20,16},{24,28},{28,24},{1,5},{5... | collective-permute-start | bytes 1351688 | tf_op jit(solution)/shard_map/ppermute | solution.py:68
  61.8 36.2 %collective-permute-start.2 = (bf16[384,1280]{1,0:T(8,128)(2,1)S(1)}, bf16[384,1280]{1,0:T(8,128)(2,1)}, u32[]{:S(2)}, u32[]{:S(2)}) collective-permute-start(bf16[384,1280]{1,0:T(8,128)(2,1)S(1)} %collective-permute-done.1), channel_id=1, source_target_pairs={{0,1},{1,0},{2,3},{3,2},{4,5},{5,4},{6,7},{7,6},{8,9},{9,8},{10,11... | collective-permute-start | bytes 2949128 | tf_op jit(solution)/shard_map/ppermute | solution.py:68
  68.3 33.0 %collective-permute-start.3 = (bf16[384,1280]{1,0:T(8,128)(2,1)}, bf16[384,1280]{1,0:T(8,128)(2,1)}, u32[]{:S(2)}, u32[]{:S(2)}) collective-permute-start(bf16[384,1280]{1,0:T(8,128)(2,1)} %cot_ref.1), channel_id=1, source_target_pairs={{0,1},{1,0},{2,3},{3,2},{4,5},{5,4},{6,7},{7,6},{8,9},{9,8},{10,11... | collective-permute-start | bytes 2949128 | tf_op jit(solution)/shard_map/ppermute | solution.py:68
  74.7 19.2 %collective-permute-start.12 = (bf16[160,1408]{1,0:T(8,128)(2,1)}, bf16[160,1408]{1,0:T(8,128)(2,1)}, u32[]{:S(2)}, u32[]{:S(2)}) collective-permute-start(bf16[160,1408]{1,0:T(8,128)(2,1)} %collective-permute-done.11.refs_6_), channel_id=1, source_target_pairs={{0,4},{4,0},{8,12},{12,8},{16,20},{20,16},{24,28},{28,24},{1,5},{5... | collective-permute-start | bytes 1351688 | tf_op jit(solution)/shard_map/ppermute | solution.py:68
  74.7 26.6 %collective-permute-start.5 = (bf16[384,1280]{1,0:T(8,128)(2,1)}, bf16[384,1280]{1,0:T(8,128)(2,1)}, u32[]{:S(2)}, u32[]{:S(2)}) collective-permute-start(bf16[384,1280]{1,0:T(8,128)(2,1)} %collective-permute-done.4), channel_id=1, source_target_pairs={{0,1},{1,0},{2,3},{3,2},{4,5},{5,4},{6,7},{7,6},{8,9},{9,8},{10,11... | collective-permute-start | bytes 2949128 | tf_op jit(solution)/shard_map/ppermute | solution.py:68
  128.4 30.1 %collective-permute-start.13 = (bf16[384,1280]{1,0:T(8,128)(2,1)}, bf16[384,1280]{1,0:T(8,128)(2,1)S(1)}, u32[]{:S(2)}, u32[]{:S(2)}) collective-permute-start(bf16[384,1280]{1,0:T(8,128)(2,1)} %get-tuple-element.80), channel_id=1, source_target_pairs={{0,1},{1,0},{2,3},{3,2},{4,5},{5,4},{6,7},{7,6},{8,9},{9,8},{10,11... | collective-permute-start | bytes 2949128 | tf_op jit(solution)/shard_map/ppermute | solution.py:68
  128.5 37.8 %collective-permute-start.14 = (bf16[160,1280]{1,0:T(8,128)(2,1)S(1)}, bf16[160,1280]{1,0:T(8,128)(2,1)S(1)}, u32[]{:S(2)}, u32[]{:S(2)}) collective-permute-start(bf16[160,1280]{1,0:T(8,128)(2,1)S(1)} %convert_element_type.131.refs_0_), channel_id=1, source_target_pairs={{0,8},{4,12},{8,0},{12,4},{16,24},{20,28},{24,16},{28,20},{1,9},{5... | collective-permute-start | bytes 1228808 | tf_op jit(solution)/shard_map/ppermute | solution.py:68
  147.8 30.8 %collective-permute-start.15 = (bf16[160,1280]{1,0:T(8,128)(2,1)S(1)}, bf16[160,1280]{1,0:T(8,128)(2,1)S(1)}, u32[]{:S(2)}, u32[]{:S(2)}) collective-permute-start(bf16[160,1280]{1,0:T(8,128)(2,1)S(1)} %convert_element_type.131.refs_0_), channel_id=1, source_target_pairs={{0,16},{4,20},{8,24},{12,28},{16,0},{20,4},{24,8},{28,12},{1,17},{... | collective-permute-start | bytes 1228808 | tf_op jit(solution)/shard_map/ppermute | solution.py:68
  148.9 29.8 %collective-permute-start.16 = (bf16[160,1280]{1,0:T(8,128)(2,1)S(1)}, bf16[160,1280]{1,0:T(8,128)(2,1)S(1)}, u32[]{:S(2)}, u32[]{:S(2)}) collective-permute-start(bf16[160,1280]{1,0:T(8,128)(2,1)S(1)} %convert_element_type.131.refs_0_), channel_id=1, source_target_pairs={{0,24},{4,28},{8,16},{12,20},{16,8},{20,12},{24,0},{28,4},{1,25},{... | collective-permute-start | bytes 1228808 | tf_op jit(solution)/shard_map/ppermute | solution.py:68
  159.9 37.9 %collective-permute-start.19 = (bf16[384,1280]{1,0:T(8,128)(2,1)S(1)}, bf16[384,1280]{1,0:T(8,128)(2,1)S(1)}, u32[]{:S(2)}, u32[]{:S(2)}) collective-permute-start(bf16[384,1280]{1,0:T(8,128)(2,1)S(1)} %add_convert_fusion.3), channel_id=1, source_target_pairs={{0,2},{1,3},{2,0},{3,1},{4,6},{5,7},{6,4},{7,5},{8,10},{9,11},{10,... | collective-permute-start | bytes 2949128 | tf_op jit(solution)/shard_map/ppermute | solution.py:68
  203.5 42.8 %collective-permute-start.20 = (bf16[384,1280]{1,0:T(8,128)(2,1)}, bf16[384,1280]{1,0:T(8,128)(2,1)S(1)}, u32[]{:S(2)}, u32[]{:S(2)}) collective-permute-start(bf16[384,1280]{1,0:T(8,128)(2,1)} %get-tuple-element.88), channel_id=1, source_target_pairs={{0,1},{1,0},{2,3},{3,2},{4,5},{5,4},{6,7},{7,6},{8,9},{9,8},{10,11... | collective-permute-start | bytes 2949128 | tf_op jit(solution)/shard_map/ppermute | solution.py:68
  203.6 12.3 %collective-permute-start.24 = (bf16[160,1280]{1,0:T(8,128)(2,1)S(1)}, bf16[160,1280]{1,0:T(8,128)(2,1)S(1)}, u32[]{:S(2)}, u32[]{:S(2)}) collective-permute-start(bf16[160,1280]{1,0:T(8,128)(2,1)S(1)} %collective-permute-done.16.refs_6_), channel_id=1, source_target_pairs={{0,4},{4,0},{8,12},{12,8},{16,20},{20,16},{24,28},{28,24},{1,5},{5... | collective-permute-start | bytes 1228808 | tf_op jit(solution)/shard_map/ppermute | solution.py:68
  204.1 55.8 %collective-permute-start.27 = (bf16[384,1280]{1,0:T(8,128)(2,1)}, bf16[384,1280]{1,0:T(8,128)(2,1)S(1)}, u32[]{:S(2)}, u32[]{:S(2)}) collective-permute-start(bf16[384,1280]{1,0:T(8,128)(2,1)} %get-tuple-element.88), channel_id=1, source_target_pairs={{0,2},{1,3},{2,0},{3,1},{4,6},{5,7},{6,4},{7,5},{8,10},{9,11},{10,... | collective-permute-start | bytes 2949128 | tf_op jit(solution)/shard_map/ppermute | solution.py:68
  204.6 23.0 %collective-permute-start.21 = (bf16[160,1280]{1,0:T(8,128)(2,1)S(1)}, bf16[160,1280]{1,0:T(8,128)(2,1)S(1)}, u32[]{:S(2)}, u32[]{:S(2)}) collective-permute-start(bf16[160,1280]{1,0:T(8,128)(2,1)S(1)} %convert_element_type.131.refs_0_), channel_id=1, source_target_pairs={{0,4},{4,0},{8,12},{12,8},{16,20},{20,16},{24,28},{28,24},{1,5},{5... | collective-permute-start | bytes 1228808 | tf_op jit(solution)/shard_map/ppermute | solution.py:68
  206.1 27.3 %collective-permute-start.22 = (bf16[160,1280]{1,0:T(8,128)(2,1)S(1)}, bf16[160,1280]{1,0:T(8,128)(2,1)S(1)}, u32[]{:S(2)}, u32[]{:S(2)}) collective-permute-start(bf16[160,1280]{1,0:T(8,128)(2,1)S(1)} %collective-permute-done.14.refs_2_), channel_id=1, source_target_pairs={{0,4},{4,0},{8,12},{12,8},{16,20},{20,16},{24,28},{28,24},{1,5},{5... | collective-permute-start | bytes 1228808 | tf_op jit(solution)/shard_map/ppermute | solution.py:68
  215.9 25.9 %collective-permute-start.23 = (bf16[160,1280]{1,0:T(8,128)(2,1)S(1)}, bf16[160,1280]{1,0:T(8,128)(2,1)S(1)}, u32[]{:S(2)}, u32[]{:S(2)}) collective-permute-start(bf16[160,1280]{1,0:T(8,128)(2,1)S(1)} %collective-permute-done.15.refs_4_), channel_id=1, source_target_pairs={{0,4},{4,0},{8,12},{12,8},{16,20},{20,16},{24,28},{28,24},{1,5},{5... | collective-permute-start | bytes 1228808 | tf_op jit(solution)/shard_map/ppermute | solution.py:68
  271.6 10.4 %collective-permute-start.29 = (bf16[384,1280]{1,0:T(8,128)(2,1)}, bf16[384,1280]{1,0:T(8,128)(2,1)S(1)}, u32[]{:S(2)}, u32[]{:S(2)}) collective-permute-start(bf16[384,1280]{1,0:T(8,128)(2,1)} %get-tuple-element.101), channel_id=1, source_target_pairs={{0,1},{1,0},{2,3},{3,2},{4,5},{5,4},{6,7},{7,6},{8,9},{9,8},{10,11... | collective-permute-start | bytes 2949128 | tf_op jit(solution)/shard_map/ppermute | solution.py:68
  295.2 240.9 %reduce-scatter.3.cloned.1.call-start = ((), (), s32[]{:S(2)}) async-start(), calls=%async_computation.3 | async-start | bytes 3686400 | tf_op jit(solution)/shard_map/reduce_scatter | solution.py:697
  295.3 24.2 %collective-permute-start.30 = (bf16[384,1280]{1,0:T(8,128)(2,1)S(1)}, bf16[384,1280]{1,0:T(8,128)(2,1)}, u32[]{:S(2)}, u32[]{:S(2)}) collective-permute-start(bf16[384,1280]{1,0:T(8,128)(2,1)S(1)} %add_convert_fusion.2), channel_id=1, source_target_pairs={{0,2},{1,3},{2,0},{3,1},{4,6},{5,7},{6,4},{7,5},{8,10},{9,11},{10,... | collective-permute-start | bytes 2949128 | tf_op jit(solution)/shard_map/ppermute | solution.py:68
  325.8 26.4 %collective-permute-start.31 = (bf16[384,1280]{1,0:T(8,128)(2,1)}, bf16[384,1280]{1,0:T(8,128)(2,1)S(1)}, u32[]{:S(2)}, u32[]{:S(2)}) collective-permute-start(bf16[384,1280]{1,0:T(8,128)(2,1)} %get-tuple-element.105), channel_id=1, source_target_pairs={{0,2},{1,3},{2,0},{3,1},{4,6},{5,7},{6,4},{7,5},{8,10},{9,11},{10,... | collective-permute-start | bytes 2949128 | tf_op jit(solution)/shard_map/ppermute | solution.py:68
  397.5 18.9 %collective-permute-start.34 = (bf16[160,1408]{1,0:T(8,128)(2,1)S(1)}, bf16[160,1408]{1,0:T(8,128)(2,1)}, u32[]{:S(2)}, u32[]{:S(2)}) collective-permute-start(bf16[160,1408]{1,0:T(8,128)(2,1)S(1)} %get-tuple-element.138), channel_id=1, source_target_pairs={{0,4},{4,0},{8,12},{12,8},{16,20},{20,16},{24,28},{28,24},{1,5},{5... | collective-permute-start | bytes 1351688 | tf_op jit(solution)/shard_map/ppermute | solution.py:68
  397.7 31.5 %collective-permute-start.35 = (bf16[160,1408]{1,0:T(8,128)(2,1)}, bf16[160,1408]{1,0:T(8,128)(2,1)}, u32[]{:S(2)}, u32[]{:S(2)}) collective-permute-start(bf16[160,1408]{1,0:T(8,128)(2,1)} %get-tuple-element.139), channel_id=1, source_target_pairs={{0,4},{4,0},{8,12},{12,8},{16,20},{20,16},{24,28},{28,24},{1,5},{5... | collective-permute-start | bytes 1351688 | tf_op jit(solution)/shard_map/ppermute | solution.py:68
  399.6 43.7 %collective-permute-start.36 = (bf16[160,1408]{1,0:T(8,128)(2,1)}, bf16[160,1408]{1,0:T(8,128)(2,1)}, u32[]{:S(2)}, u32[]{:S(2)}) collective-permute-start(bf16[160,1408]{1,0:T(8,128)(2,1)} %get-tuple-element.140), channel_id=1, source_target_pairs={{0,4},{4,0},{8,12},{12,8},{16,20},{20,16},{24,28},{28,24},{1,5},{5... | collective-permute-start | bytes 1351688 | tf_op jit(solution)/shard_map/ppermute | solution.py:68
  407.4 44.9 %collective-permute-start.41 = (bf16[384,1280]{1,0:T(8,128)(2,1)}, bf16[384,1280]{1,0:T(8,128)(2,1)S(1)}, u32[]{:S(2)}, u32[]{:S(2)}) collective-permute-start(bf16[384,1280]{1,0:T(8,128)(2,1)} %slice.211), channel_id=1, source_target_pairs={{0,1},{1,0},{2,3},{3,2},{4,5},{5,4},{6,7},{7,6},{8,9},{9,8},{10,11... | collective-permute-start | bytes 2949128 | tf_op jit(solution)/shard_map/ppermute | solution.py:68
  416.0 88.2 %collective-permute-start.40 = (bf16[384,1280]{1,0:T(8,128)(2,1)}, bf16[384,1280]{1,0:T(8,128)(2,1)S(1)}, u32[]{:S(2)}, u32[]{:S(2)}) collective-permute-start(bf16[384,1280]{1,0:T(8,128)(2,1)} %get-tuple-element.141), channel_id=1, source_target_pairs={{0,1},{1,0},{2,3},{3,2},{4,5},{5,4},{6,7},{7,6},{8,9},{9,8},{10,11... | collective-permute-start | bytes 2949128 | tf_op jit(solution)/shard_map/ppermute | solution.py:68
  416.5 37.1 %collective-permute-start.46 = (bf16[160,1408]{1,0:T(8,128)(2,1)S(1)}, bf16[160,1408]{1,0:T(8,128)(2,1)S(1)}, u32[]{:S(2)}, u32[]{:S(2)}) collective-permute-start(bf16[160,1408]{1,0:T(8,128)(2,1)S(1)} %copy-done.42), channel_id=1, source_target_pairs={{0,4},{4,0},{8,12},{12,8},{16,20},{20,16},{24,28},{28,24},{1,5},{5... | collective-permute-start | bytes 1351688 | tf_op jit(solution)/shard_map/ppermute | solution.py:68
  445.8 32.8 %collective-permute-start.45 = (bf16[160,1408]{1,0:T(8,128)(2,1)}, bf16[160,1408]{1,0:T(8,128)(2,1)}, u32[]{:S(2)}, u32[]{:S(2)}) collective-permute-start(bf16[160,1408]{1,0:T(8,128)(2,1)} %get-tuple-element.136), channel_id=1, source_target_pairs={{0,8},{4,12},{8,0},{12,4},{16,24},{20,28},{24,16},{28,20},{1,9},{5... | collective-permute-start | bytes 1351688 | tf_op jit(solution)/shard_map/ppermute | solution.py:68
  449.9 36.5 %collective-permute-start.44 = (bf16[160,1408]{1,0:T(8,128)(2,1)}, bf16[160,1408]{1,0:T(8,128)(2,1)}, u32[]{:S(2)}, u32[]{:S(2)}) collective-permute-start(bf16[160,1408]{1,0:T(8,128)(2,1)} %get-tuple-element.135), channel_id=1, source_target_pairs={{0,24},{4,28},{8,16},{12,20},{16,8},{20,12},{24,0},{28,4},{1,25},{... | collective-permute-start | bytes 1351688 | tf_op jit(solution)/shard_map/ppermute | solution.py:68
  452.3 50.1 %collective-permute-start.43 = (bf16[160,1408]{1,0:T(8,128)(2,1)}, bf16[160,1408]{1,0:T(8,128)(2,1)}, u32[]{:S(2)}, u32[]{:S(2)}) collective-permute-start(bf16[160,1408]{1,0:T(8,128)(2,1)} %get-tuple-element.134), channel_id=1, source_target_pairs={{0,16},{4,20},{8,24},{12,28},{16,0},{20,4},{24,8},{28,12},{1,17},{... | collective-permute-start | bytes 1351688 | tf_op jit(solution)/shard_map/ppermute | solution.py:68
  453.6 50.6 %collective-permute-start.42 = (bf16[384,1280]{1,0:T(8,128)(2,1)}, bf16[384,1280]{1,0:T(8,128)(2,1)}, u32[]{:S(2)}, u32[]{:S(2)}) collective-permute-start(bf16[384,1280]{1,0:T(8,128)(2,1)} %add_convert_fusion), channel_id=1, source_target_pairs={{0,2},{1,3},{2,0},{3,1},{4,6},{5,7},{6,4},{7,5},{8,10},{9,11},{10,... | collective-permute-start | bytes 2949128 | tf_op jit(solution)/shard_map/ppermute | solution.py:68
  478.6 48.7 %collective-permute-start.38 = (bf16[384,1280]{1,0:T(8,128)(2,1)}, bf16[384,1280]{1,0:T(8,128)(2,1)}, u32[]{:S(2)}, u32[]{:S(2)}) collective-permute-start(bf16[384,1280]{1,0:T(8,128)(2,1)} %slice.206), channel_id=1, source_target_pairs={{0,1},{1,0},{2,3},{3,2},{4,5},{5,4},{6,7},{7,6},{8,9},{9,8},{10,11... | collective-permute-start | bytes 2949128 | tf_op jit(solution)/shard_map/ppermute | solution.py:68
  486.4 57.8 %collective-permute-start.37 = (bf16[384,1280]{1,0:T(8,128)(2,1)}, bf16[384,1280]{1,0:T(8,128)(2,1)}, u32[]{:S(2)}, u32[]{:S(2)}) collective-permute-start(bf16[384,1280]{1,0:T(8,128)(2,1)} %slice.204), channel_id=1, source_target_pairs={{0,1},{1,0},{2,3},{3,2},{4,5},{5,4},{6,7},{7,6},{8,9},{9,8},{10,11... | collective-permute-start | bytes 2949128 | tf_op jit(solution)/shard_map/ppermute | solution.py:68
  513.0 4.0 collective-permute-start.50
  517.0 4.5 collective-permute-start.51
  521.6 4.5 collective-permute-start.52
  526.1 5.8 collective-permute-start.53
  529.8 25.0 %collective-permute-start.39 = (bf16[384,1280]{1,0:T(8,128)(2,1)}, bf16[384,1280]{1,0:T(8,128)(2,1)}, u32[]{:S(2)}, u32[]{:S(2)}) collective-permute-start(bf16[384,1280]{1,0:T(8,128)(2,1)} %add_convert_fusion.1), channel_id=1, source_target_pairs={{0,2},{1,3},{2,0},{3,1},{4,6},{5,7},{6,4},{7,5},{8,10},{9,11},{10,... | collective-permute-start | bytes 2949128 | tf_op jit(solution)/shard_map/ppermute | solution.py:68
  542.3 22.1 %collective-permute-start.48 = (f32[4,160,160]{2,1,0:T(8,128)S(1)}, f32[4,160,160]{2,1,0:T(8,128)S(1)}, u32[]{:S(2)}, u32[]{:S(2)}) collective-permute-start(f32[4,160,160]{2,1,0:T(8,128)S(1)} %fusion.30), channel_id=1, source_target_pairs={{0,2},{1,3},{2,0},{3,1},{4,6},{5,7},{6,4},{7,5},{8,10},{9,11},{10,... | collective-permute-start | bytes 1228808 | tf_op jit(solution)/shard_map/ppermute | solution.py:68
  (69 other events, 979.9 us)
Sparse Core Ops, SparseCore 0:
  31.2 90.0 all-gather.1
  295.4 81.4 reduce-scatter.4
  380.9 99.5 reduce-scatter.2

commit v2 on v1

--- a/solution.py
+++ b/solution.py
@@ -88,15 +88,12 @@
     return (own.astype(F32) + arrived.astype(F32)).astype(BF16)
 
 
-def near_swap(sent):
-    rows = sent.shape[0] // 2
-    return jnp.concatenate(
-        [swap(sent[:rows], "tensor", 1), swap(sent[rows:], "tensor", 1)], axis=0
-    )
-
-
 def after(value, *others):
     return lax.optimization_barrier((value, *others))[0]
+
+
+def tie(values, *others):
+    return list(lax.optimization_barrier((*values, *others))[: len(values)])
 
 
 def qkv_body(x_ref, vec_ref, w_ref, bias_ref, attn_ref, qkv_ref):
@@ -132,75 +129,57 @@
     )(x_rows, vec_rows, weight, bias)
 
 
-def rows_body(dims, x_ref, w_ref, out_ref):
-    out_ref[...] = mm(x_ref[...], w_ref[...], dims).astype(out_ref.dtype)
-
-
-def rows_mm(x_rows, weight, dims, kind, block, first=0, count=None):
-    rows, depth = x_rows.shape
-    count = rows if count is None else count
-    columns = weight.shape[1 - dims[0][1][0]]
-    base = first // block
+PIECES = 4
+
+
+def part_shapes(emits, rows, width):
+    shapes = []
+    for kind in emits:
+        count = PIECES if kind == "pieces" else 1
+        shapes += [jax.ShapeDtypeStruct((rows // count, width), BF16)] * count
+    return shapes, [pl.BlockSpec(shape.shape, lambda i: (0, 0)) for shape in shapes]
+
+
+def part_store(emits, refs, value):
+    spot = 0
+    for index, kind in enumerate(emits):
+        count = PIECES if kind == "pieces" else 1
+        group = refs[spot : spot + count]
+        spot += count
+
+        @pl.when(pl.program_id(0) == index)
+        def _():
+            rows = value.shape[0] // count
+            for piece, ref in enumerate(group):
+                ref[...] = value[piece * rows : piece * rows + rows].astype(BF16)
+
+
+def swap_all(values, axis, mask):
+    return [swap(value, axis, mask) for value in values]
+
+
+def pair_body(own_ref, *rest):
+    pieces, out_ref = rest[:-1], rest[-1]
+    for index, piece in enumerate(pieces):
+
+        @pl.when(pl.program_id(0) == index)
+        def _():
+            out_ref[...] = (own_ref[...].astype(F32) + piece[...].astype(F32)).astype(BF16)
+
+
+def pair_pieces(own, pieces):
+    rows, width = own.shape
+    spec = pl.BlockSpec((rows // PIECES, width), lambda i: (i, 0))
     return pl.pallas_call(
-        partial(rows_body, dims),
-        grid=(count // block,),
-        in_specs=[
-            pl.BlockSpec((block, depth), lambda i: (i + base, 0)),
-            pl.BlockSpec(weight.shape, lambda i: (0, 0)),
-        ],
-        out_specs=pl.BlockSpec((block, columns), lambda i: (i, 0)),
-        out_shape=jax.ShapeDtypeStruct((count, columns), kind),
+        pair_body,
+        grid=(PIECES,),
+        in_specs=[spec] + [pl.BlockSpec(pieces[0].shape, lambda i: (0, 0))] * PIECES,
+        out_specs=spec,
+        out_shape=jax.ShapeDtypeStruct(own.shape, BF16),
         compiler_params=params("arbitrary"),
         cost_estimate=LITTLE,
-        name="rows_product",
-    )(x_rows, weight)
-
-
-def sum_body(steps, *refs):
-    lefts, (right_ref, out_ref, total) = refs[:-3], refs[-3:]
-    step = pl.program_id(0)
-    for index, left_ref in enumerate(lefts):
-
-        @pl.when(step // steps == index)
-        def _():
-            term = mm(left_ref[...], right_ref[...], TN)
-            if index:
-                total[...] += term
-            else:
-
-                @pl.when(step == 0)
-                def _():
-                    total[...] = term
-
-                @pl.when(step > 0)
-                def _():
-                    total[...] += term
-
-    @pl.when(step == pl.num_programs(0) - 1)
-    def _():
-        out_ref[...] = total[...].astype(BF16)
-
-
-def sum_mm(lefts, right, block):
-    rows, width = lefts[0].shape
-    columns = right.shape[1]
-    steps = rows // block
-
-    def spot(index):
-        return lambda i: (jnp.clip(i - index * steps, 0, steps - 1), 0)
-
-    return pl.pallas_call(
-        partial(sum_body, steps),
-        grid=(steps * len(lefts),),
-        in_specs=[pl.BlockSpec((block, width), spot(index)) for index in range(len(lefts))]
-        + [pl.BlockSpec((block, columns), lambda i: (i, 0))],
-        out_specs=pl.BlockSpec((width, columns), lambda i: (0, 0)),
-        out_shape=jax.ShapeDtypeStruct((width, columns), BF16),
-        scratch_shapes=[pltpu.VMEM((width, columns), F32)],
-        compiler_params=params("arbitrary"),
-        cost_estimate=LITTLE,
-        name="sum_product",
-    )(*lefts, right)
+        name="pair_sum",
+    )(own, *pieces)
 
 
 def head_place(head):
@@ -250,8 +229,8 @@
     )
 
 
-def attn_body(heads, q_ref, qkv_ref, bias_ref, wo_ref, *rest):
-    att_ref, part_ref, lse_ref, keys, vals = rest[-5:]
+def attn_body(heads, emits, skip, q_ref, qkv_ref, bias_ref, wo_ref, *rest):
+    (att_ref, lse_ref), parts, (keys, vals) = rest[skip : skip + 2], rest[skip + 2 : -2], rest[-2:]
     block = q_ref.shape[0]
     frames = qkv_ref.shape[0]
 
@@ -279,17 +258,19 @@
     attended = join_windows(outs).astype(BF16)
     att_ref[...] = attended
     lse_ref[...] = jnp.transpose(lse_cols)[:8]
-    part_ref[...] = mm(attended, wo_ref[...], NT).astype(BF16)
-
-
-def attn_call(heads, qkv, key_bias, wo, block, first, count, earlier=None):
+    part_store(emits, parts, mm(attended, wo_ref[...], NT))
+
+
+def attn_call(heads, emits, qkv, key_bias, wo, block, first, earlier=None):
+    count = block * len(emits)
     frames = qkv.shape[0]
     part_width = wo.shape[1]
     width = wo.shape[0]
     held = [] if earlier is None else list(earlier)
     base = first // block
+    shapes, specs = part_shapes(emits, block, width)
     return pl.pallas_call(
-        partial(attn_body, heads),
+        partial(attn_body, heads, emits, len(held)),
         grid=(count // block,),
         in_specs=[
             pl.BlockSpec((block, part_width), lambda i: (i + base, 0)),
@@ -300,19 +281,19 @@
         + [pl.BlockSpec(memory_space=pl.ANY)] * len(held),
         out_specs=[
             pl.BlockSpec((block, part_width), lambda i: (i + base, 0)),
-            pl.BlockSpec((block, width), lambda i: (i, 0)),
             pl.BlockSpec((8, block), lambda i: (0, i + base)),
-        ],
+        ]
+        + specs,
         out_shape=[
             jax.ShapeDtypeStruct((frames, part_width), BF16),
-            jax.ShapeDtypeStruct((count, width), BF16),
             jax.ShapeDtypeStruct((8, frames), F32),
-        ],
+        ]
+        + shapes,
         scratch_shapes=[
             pltpu.VMEM((heads, frames, WINDOW), BF16),
             pltpu.VMEM((heads, frames, WINDOW), BF16),
         ],
-        input_output_aliases={} if earlier is None else {4: 0, 5: 2},
+        input_output_aliases={} if earlier is None else {4: 0, 5: 1},
         compiler_params=params("arbitrary"),
         cost_estimate=LITTLE,
         name="attn_fwd",
@@ -461,8 +442,15 @@
     return share, share + values * bell * (1.0 / math.sqrt(2.0 * math.pi))
 
 
-def mlp_body(chunk, in_ref, w_ref, bias_ref, dhid_ref, *rest):
-    hid_ref, dpre_ref, part_ref, sums_ref = rest[-4:]
+def mlp_body(chunk, emits, skip, *refs):
+    slot_refs, (w_ref, bias_ref, dhid_ref) = refs[: len(emits)], refs[len(emits) : len(emits) + 3]
+    outs = refs[len(emits) + 3 + skip :]
+    hid_ref, dpre_ref, sums_ref, parts, in_ref = *outs[:3], outs[3:-1], outs[-1]
+    for index, slot_ref in enumerate(slot_refs):
+
+        @pl.when(pl.program_id(0) == index)
+        def _():
+            in_ref[...] = slot_ref[...]
 
     @pl.when(pl.program_id(0) == 0)
     def _():
@@ -476,19 +464,21 @@
         d_pre = (dhid_ref[:, cols] * slope).astype(BF16)
         dpre_ref[:, cols] = d_pre
         sums_ref[0:1, cols] += jnp.sum(d_pre.astype(F32), axis=0, keepdims=True)
-    part_ref[...] = mm(dpre_ref[...], w_ref[...], NT).astype(BF16)
-
-
-def mlp_call(mlp_in, weight, bias, d_hidden, block, first, frames, earlier=None):
-    count, width = mlp_in.shape
+    part_store(emits, parts, mm(dpre_ref[...], w_ref[...], NT))
+
+
+def mlp_call(emits, slots, weight, bias, d_hidden, first, frames, earlier=None):
+    block, width = slots[0].shape
+    count = block * len(slots)
     hidden_width = weight.shape[1]
     held = [] if earlier is None else list(earlier)
     base = first // block
+    shapes, specs = part_shapes(emits, block, width)
     return pl.pallas_call(
-        partial(mlp_body, min(256, hidden_width)),
+        partial(mlp_body, min(256, hidden_width), emits, len(held)),
         grid=(count // block,),
-        in_specs=[
-            pl.BlockSpec((block, width), lambda i: (i, 0)),
+        in_specs=[pl.BlockSpec((block, width), lambda i: (0, 0))] * len(slots)
+        + [
             pl.BlockSpec(weight.shape, lambda i: (0, 0)),
             pl.BlockSpec(bias.shape, lambda i: (0, 0)),
             pl.BlockSpec((block, hidden_width), lambda i: (i + base, 0)),
@@ -497,23 +487,26 @@
         out_specs=[
             pl.BlockSpec((block, hidden_width), lambda i: (i + base, 0)),
             pl.BlockSpec((block, hidden_width), lambda i: (i + base, 0)),
-            pl.BlockSpec((block, width), lambda i: (i, 0)),
             pl.BlockSpec((8, hidden_width), lambda i: (0, 0)),
-        ],
+        ]
+        + specs,
         out_shape=[
             jax.ShapeDtypeStruct((frames, hidden_width), BF16),
             jax.ShapeDtypeStruct((frames, hidden_width), BF16),
-            jax.ShapeDtypeStruct((count, width), BF16),
             jax.ShapeDtypeStruct((8, hidden_width), F32),
-        ],
-        input_output_aliases={} if earlier is None else {4: 0, 5: 1},
+        ]
+        + shapes,
+        scratch_shapes=[pltpu.VMEM((block, width), BF16)],
+        input_output_aliases=(
+            {} if earlier is None else {len(slots) + 3: 0, len(slots) + 4: 1}
+        ),
         compiler_params=params("arbitrary"),
         cost_estimate=LITTLE,
         name="mlp_up",
-    )(mlp_in, weight, bias, d_hidden, *held)
-
-
-def residual_body(x_ref, mine_ref, near_ref, far_ref, vec_ref, res_ref, in_ref):
+    )(*slots, weight, bias, d_hidden, *held)
+
+
+def residual_body(x_ref, mine_ref, far_ref, near_ref, vec_ref, res_ref, in_ref):
     total = mine_ref[...].astype(F32) + near_ref[...].astype(F32) + far_ref[...].astype(F32)
     residual = x_ref[...].astype(F32) + total + vec_ref[2:3, :]
     res_ref[...] = residual
@@ -522,7 +515,7 @@
 
 
 def second_back_body(
-    res_ref, mine_ref, near_ref, far_ref, cot_ref, vec_ref, dres_ref, low_ref, sums_ref
+    res_ref, mine_ref, far_ref, cot_ref, near_ref, vec_ref, dres_ref, low_ref, sums_ref
 ):
     @pl.when(pl.program_id(0) == 0)
     def _():
@@ -540,7 +533,7 @@
     sums_ref[5:6, :] += jnp.sum(cot, axis=0, keepdims=True)
 
 
-def first_back_body(x_ref, mine_ref, near_ref, far_ref, dres_ref, vec_ref, out_ref, sums_ref):
+def first_back_body(x_ref, mine_ref, far_ref, dres_ref, near_ref, vec_ref, out_ref, sums_ref):
     @pl.when(pl.program_id(0) == 0)
     def _():
         sums_ref[...] = jnp.zeros_like(sums_ref)
@@ -552,20 +545,37 @@
     sums_ref[1:2, :] += jnp.sum(grad, axis=0, keepdims=True)
 
 
-def row_call(body, rows_in, vec_rows, out_types, with_sums, block, name):
+def row_body(body, count, *refs):
+    row_refs, pieces, vec_ref = refs[:count], refs[count : count + PIECES], refs[count + PIECES]
+    near_ref = refs[-1]
+    for index, piece in enumerate(pieces):
+
+        @pl.when(pl.program_id(0) == index)
+        def _():
+            near_ref[...] = piece[...]
+
+    body(*row_refs, near_ref, vec_ref, *refs[count + PIECES + 1 : -1])
+
+
+def row_call(body, rows_in, near, vec_rows, out_types, with_sums, name):
     rows, width = rows_in[0].shape
+    block = rows // PIECES
     row_spec = pl.BlockSpec((block, width), lambda i: (i, 0))
     whole = pl.BlockSpec((8, width), lambda i: (0, 0))
     return pl.pallas_call(
-        body,
-        grid=(rows // block,),
-        in_specs=[row_spec] * len(rows_in) + [whole],
+        partial(row_body, body, len(rows_in)),
+        grid=(PIECES,),
+        in_specs=[row_spec] * len(rows_in)
+        + [pl.BlockSpec((block, width), lambda i: (0, 0))] * PIECES
+        + [whole],
         out_specs=[row_spec] * len(out_types) + [whole] * with_sums,
         out_shape=[jax.ShapeDtypeStruct((rows, width), kind) for kind in out_types]
         + [jax.ShapeDtypeStruct((8, width), F32)] * with_sums,
+        scratch_shapes=[pltpu.VMEM((block, width), BF16)],
         compiler_params=params("arbitrary"),
+        cost_estimate=LITTLE,
         name=name,
-    )(*rows_in, vec_rows)
+    )(*rows_in, *near, vec_rows)
 
 
 def polar_factors(grams, eye):
@@ -651,19 +661,23 @@
     )(lax.axis_index("dp").astype(jnp.int32)[None], *slots)
 
 
-def dp_slots(own):
-    slots = {0: own}
-    for mask in (4, 6, 2):
-        slots[mask] = swap(own, "dp", mask)
-    for mask in (0, 2, 4, 6):
-        slots[mask + 1] = swap(slots[mask], "dp", 1)
-    return [slots[mask] for mask in range(8)]
-
-
-def dp_send(own):
+def dp_slots(own, ordered=False):
+    line = {mask: swap(own, "dp", mask) for mask in (6, 2, 4)}
+    slots = [own, swap(own, "dp", 1)] + [None] * 6
+    for mask in (6, 2, 4):
+        arrived = line[mask]
+        if ordered:
+            held = [slots[1]] if mask == 2 else [slots[3], slots[7]] if mask == 4 else []
+            arrived = after(arrived, *held)
+        slots[mask] = arrived
+        slots[mask + 1] = swap(arrived, "dp", 1)
+    return slots
+
+
+def dp_send(own, ordered=False):
     if lax.axis_size("dp") != 8:
         return [lax.all_gather(own, "dp", axis=0, tiled=True)]
-    return dp_slots(own)
+    return dp_slots(own, ordered)
 
 
 def dp_place(slots, splits):
@@ -672,29 +686,42 @@
     return place_rows(slots, splits)
 
 
-def dp_scatter(part):
+LINE = (4, 6, 2, 0)
+
+
+def dp_cross(part):
     size = lax.axis_size("dp")
     if size != 8:
-        return dp_scatter_plain(part), []
+        return [], [dp_scatter_plain(part)]
     rows = part.shape[0] // size
     me = lax.axis_index("dp")
 
     def block(mask):
         return lax.dynamic_slice(part, ((me ^ mask) * rows, 0), (rows, part.shape[1]))
 
-    total, arrivals = None, []
-    for mask in (4, 6, 2, 0):
-        arrived = swap(block(mask + 1), "dp", 1)
-        arrivals.append(arrived)
-        pair = block(mask).astype(F32) + arrived.astype(F32)
-        if mask:
-            pair = swap(pair.astype(BF16), "dp", mask).astype(F32)
-        total = pair if total is None else total + pair
-    return total, arrivals
+    return [block(mask) for mask in LINE], [swap(block(mask + 1), "dp", 1) for mask in LINE]
+
+
+def dp_line(owns, arrivals):
+    if not owns:
+        return arrivals
+    sums, pair = [], None
+    for mask, own, arrived in zip(LINE, owns, arrivals):
+        arrived = arrived if pair is None else after(arrived, pair)
+        pair = own.astype(F32) + arrived.astype(F32)
+        sums.append(swap(pair.astype(BF16), "dp", mask) if mask else pair)
+    return sums
+
+
+def dp_total(sums):
+    total = sums[-1].astype(F32)
+    for value in sums[:-1]:
+        total = total + value.astype(F32)
+    return total
 
 
 def dp_scatter_plain(part):
-    return lax.psum_scatter(part, "dp", scatter_dimension=0, tiled=True).astype(F32)
+    return lax.psum_scatter(part, "dp", scatter_dimension=0, tiled=True)
 
 
 def dp_sum(value):
@@ -760,12 +787,16 @@
         ],
         axis=1,
     )
-    wd = lax.all_gather(w_down.astype(BF16), "dp", axis=0, tiled=True)
-    x_rows = tensor_gather(inputs)
+    first_slots = dp_send(w_cols, True)
+    x_far = after(swap(inputs, "tensor", 2), *first_slots[2:7:4])
+    x_rows = jnp.concatenate(
+        [inputs, swap(inputs, "tensor", 1), x_far, swap(x_far, "tensor", 1)], axis=0
+    )
+    first_slots[-1], x_rows = tie([first_slots[-1], x_rows])
     cot_rows = tensor_gather(cotangent)
-    first_slots = dp_send(w_cols)
     wq, wo = dp_place(first_slots, ((0, packed), (packed, packed + padded)))
-    x_rows, cot_rows, wq, wo = lax.optimization_barrier((x_rows, cot_rows, wq, wo))
+    w_down_low = after(w_down.astype(BF16), *first_slots)
+    wd = lax.all_gather(w_down_low, "dp", axis=0, tiled=True)
     w_up_low = after(w_up.astype(BF16), *first_slots)
     up_slots = dp_send(w_up_low)
     smalls = jnp.transpose(wq[:, head_width : head_width + 16].astype(F32))
@@ -781,77 +812,96 @@
     key_bias = jnp.where(place < lengths[0], 0.0, MASKED).astype(F32)[:, None]
 
     attn_in, qkv = qkv_call(x_rows, vec_rows, wq, qkv_bias, tok)
-    att, part_three, lse = attn_call(heads, qkv, key_bias, wo, tok, 3 * tok, tok)
-    att, part_two, lse = attn_call(heads, qkv, key_bias, wo, tok, 2 * tok, tok, (att, lse))
-    total = pair_sum(part_two, part_three)
+    up_line = up_slots[4:8:2] + up_slots[2:3] if len(up_slots) == 8 else up_slots * 3
+    att, lse, *sent = attn_call(
+        heads, ("pieces",), after(qkv, up_line[0]), key_bias, wo, tok, 3 * tok
+    )
+    att, lse, part_two = attn_call(
+        heads, ("own",), after(qkv, up_line[1]), key_bias, wo, tok, 2 * tok, (att, lse)
+    )
+    total = pair_pieces(part_two, swap_all(sent, "tensor", 1))
     far = swap(total, "tensor", 2)
-    att, part_mine, lse = attn_call(
-        heads, after(qkv, total, *up_slots[0:8:2]), key_bias, wo, tok, 0, half, (att, lse)
-    )
-    near = near_swap(part_mine[tok:])
-    row_block = tok // 3
+    att, lse, mine, *sent = attn_call(
+        heads,
+        ("own", "pieces"),
+        after(qkv, total, up_line[2]),
+        key_bias,
+        wo,
+        tok,
+        0,
+        (att, lse),
+    )
+    near = swap_all(sent, "tensor", 1)
     residual, mlp_in = row_call(
-        residual_body, (inputs, part_mine[:tok], near, after(far, wd)), vec_rows, (F32, BF16), 0, row_block, "residual"
+        residual_body, (inputs, mine, far), near, vec_rows, (F32, BF16), 0, "residual"
     )
 
     near = swap(mlp_in, "tensor", 1)
     far = swap(mlp_in, "tensor", 2)
-    block = tok * 2 // 3
-    d_hidden = rows_mm(after(cot_rows, mlp_in), wd, NN, F32, block)
-    parts = {}
+    d_hidden = mm(after(cot_rows, mlp_in), wd)
     (wu,) = dp_place([*up_slots[:-1], after(up_slots[-1], d_hidden)], ((0, w_up.shape[1]),))
-    in_mine = jnp.concatenate([mlp_in, near], axis=0)
-    hidden, d_pre, part_mine, bu_sums = mlp_call(in_mine, wu, bu, d_hidden, block, 0, frames)
-    parts[0], parts[1] = part_mine[:tok], part_mine[tok:]
-    far = after(far, part_mine)
+    hidden, d_pre, bu_sums, mine, *sent = mlp_call(
+        ("own", "pieces"), [mlp_in, near], wu, bu, d_hidden, 0, frames
+    )
+    near_parts = swap_all(sent, "tensor", 1)
+    far = after(far, mine)
     slots = [mlp_in, near, far, swap(far, "tensor", 1)]
-    for index in (3, 2):
-        hidden, d_pre, parts[index], sums = mlp_call(
-            slots[index], wu, bu, d_hidden, tok // 2, index * tok, frames, (hidden, d_pre)
-        )
-        bu_sums = bu_sums + sums
-    total = pair_sum(parts[2], parts[3])
+    hidden, d_pre, sums, *sent = mlp_call(
+        ("pieces",), slots[3:], wu, bu, d_hidden, 3 * tok, frames, (hidden, d_pre)
+    )
+    bu_sums = bu_sums + sums
+    hidden, d_pre, sums, part_two = mlp_call(
+        ("own",), slots[2:3], wu, bu, d_hidden, 2 * tok, frames, (hidden, d_pre)
+    )
+    bu_sums = bu_sums + sums
+    total = pair_pieces(part_two, swap_all(sent, "tensor", 1))
     far = swap(total, "tensor", 2)
-    near = near_swap(parts[1])
-    hidden_later, d_pre_later = lax.optimization_barrier((hidden, d_pre, total))[:2]
-    raw_wd = sum_mm([cot_rows], hidden_later, half)
-    in_rows = jnp.concatenate([in_mine, *slots[2:]], axis=0)
-    raw_wu = sum_mm([in_rows], d_pre_later, half)
-    near = after(near, raw_wd, raw_wu)
-    grad_wd = dp_scatter_plain(raw_wd)
-    grad_wu = dp_scatter_plain(raw_wu)
+    hidden_later, d_pre_later = tie([hidden, d_pre], total)
+    raw_wd = mm(cot_rows, hidden_later, TN).astype(BF16)
+    raw_wu = mm(jnp.concatenate(slots, axis=0), after(d_pre_later, raw_wd), TN).astype(BF16)
+    near_parts = tie(near_parts, raw_wd, raw_wu)
+    grad_wd, grad_wu = dp_scatter_plain(raw_wd), dp_scatter_plain(raw_wu)
     d_residual, d_out, sums_two = row_call(
         second_back_body,
-        (residual, parts[0], near, far, cotangent),
+        (residual, mine, far, cotangent),
+        near_parts,
         vec_rows,
         (F32, BF16),
         1,
-        row_block,
         "second_back",
     )
+    block = tok * 2 // 3
     near = swap(d_out, "tensor", 1)
     far = swap(d_out, "tensor", 2)
     out_mine = jnp.concatenate([d_out, near], axis=0)
-    carried = attn_back_call(heads, out_mine, wo, att, qkv, key_bias, lse, block, 0)
+    carried = attn_back_call(
+        heads, out_mine, wo, att, qkv, key_bias, lse, block, 0
+    )
     far = after(far, carried[1])
     out_far = jnp.concatenate([far, swap(far, "tensor", 1)], axis=0)
+    raw_wo = (mm(out_mine, att[:half], TN) + mm(out_far, att[half:], TN)).astype(BF16)
+    out_later = after(out_far, raw_wo)
     d_qkv, bias_sums = attn_back_call(
-        heads, out_far, wo, att, qkv, key_bias, lse, block, half, carried
-    )
-    raw_wo = sum_mm([out_mine, out_far], att, half)
-    raw_wq = sum_mm([attn_in], d_qkv, half)
-    grad_first, arrivals = dp_scatter(jnp.concatenate([raw_wq, raw_wo], axis=1))
-    grad_wq, grad_wo = grad_first[:, :packed], grad_first[:, packed : packed + head_width]
-    d_qkv, hidden = lax.optimization_barrier((d_qkv, hidden, raw_wq, raw_wo))[:2]
-    first_far = rows_mm(d_qkv, wq, NT, BF16, tok, half, half)
+        heads, out_later, wo, att, qkv, key_bias, lse, block, half, carried
+    )
+    raw_wq = mm(attn_in, d_qkv, TN).astype(BF16)
+    d_qkv, raw_wq, raw_wo = tie([d_qkv, raw_wq, raw_wo])
+    raw_first = jnp.concatenate([raw_wq, raw_wo], axis=1)
+    owns, crossed = dp_cross(raw_first)
+    first_far = mm(d_qkv[half:], wq, NT).astype(BF16)
     far = swap(pair_sum(first_far[:tok], first_far[tok:]), "tensor", 2)
-    first_mine = rows_mm(d_qkv, wq, NT, BF16, tok, 0, half)
-    near = swap(first_mine[tok:], "tensor", 1)
-    hidden = after(hidden, *arrivals[:3])
-    down_far = rows_mm(hidden, wd, NT, BF16, tok, half, half)
+    first_mine = mm(after(d_qkv[:half], first_far, crossed[0]), wq, NT).astype(BF16)
+    hidden = after(hidden, first_mine)
+    down_far = mm(hidden[half:], wd, NT).astype(BF16)
     output_far = swap(pair_sum(down_far[:tok], down_far[tok:]), "tensor", 2)
-    down_mine = rows_mm(hidden, wd, NT, BF16, tok, 0, half)
+    down_mine = mm(hidden[:half], wd, NT).astype(BF16)
     output_near = swap(down_mine[tok:], "tensor", 1)
+    quarter = tok // PIECES
+    sent = [first_mine[tok + k * quarter : tok + k * quarter + quarter] for k in range(PIECES)]
+    near = swap_all(sent, "tensor", 1)
+    lined = dp_line(owns, crossed)
+    grad_wd = after(grad_wd, first_mine, lined[0], far)
+    grad_wu = after(grad_wu, *lined[:2], output_far, output_near)
     output = (
         residual
         + (down_mine[:tok].astype(F32) + output_near.astype(F32) + output_far.astype(F32))
@@ -859,11 +909,11 @@
     )
     input_grad, sums_one = row_call(
         first_back_body,
-        (inputs, first_mine[:tok], near, far, d_residual),
+        (inputs, first_mine[:tok], far, d_residual),
+        near,
         vec_rows,
         (F32,),
         1,
-        row_block,
         "first_back",
     )
 
@@ -884,8 +934,14 @@
         lax.dynamic_slice(rows_of, (7, dp_index * own_bias), (2, own_bias))
     )
 
-    mom_down_new, update_down = momentum(mom_down, grad_wd)
-    mom_up_new, update_up = momentum(mom_up, grad_wu)
+    mom_down_new, update_down = momentum(mom_down, grad_wd.astype(F32))
+    mom_up_new, update_up = momentum(mom_up, grad_wu.astype(F32))
+    early = polar_call(tensor_sum(gram_of(update_down)[None]))
+    new_w_down = applied(w_down, early[0], update_down, STEP_DOWN)
+    gram_up = gram_of(update_up)
+    lined = tie(lined, new_w_down, gram_up, input_grad)
+    grad_first = dp_total(lined)
+    grad_wq, grad_wo = grad_first[:, :packed], grad_first[:, packed : packed + head_width]
     mom_out_new, update_out = momentum(mom_out, grad_wo)
     spots = (0, padded, padded + head_width)
     grad_parts = jnp.stack([grad_wq[:, spot : spot + head_width] for spot in spots], axis=1)
@@ -893,12 +949,11 @@
     flat = jnp.concatenate(
         [update_qkv[:, 0], jnp.zeros((own_rows, extra), F32), update_qkv[:, 1], update_qkv[:, 2]], axis=1
     )
-    updates = (update_down, update_up, update_out, flat)
-    factors = polar_call(tensor_sum(jnp.stack([gram_of(update) for update in updates])))
-    new_w_down = applied(w_down, factors[0], update_down, STEP_DOWN)
-    new_w_up = applied(w_up, factors[1], update_up, STEP_UP)
-    new_w_out = applied(w_out, factors[2], update_out, STEP_OUT)
-    polar_qkv = jnp.dot(factors[3], flat, precision=HIGHEST)
+    late = tensor_sum(jnp.stack([gram_of(update_out), gram_of(flat), gram_up]))
+    late = polar_call(after(late, vec_sums))
+    new_w_out = applied(w_out, late[0], update_out, STEP_OUT)
+    new_w_up = applied(w_up, late[2], update_up, STEP_UP)
+    polar_qkv = jnp.dot(late[1], flat, precision=HIGHEST)
     new_w_qkv = w_qkv - STEP_QKV * jnp.stack(
         [polar_qkv[:, spot : spot + head_width] for spot in spots], axis=1
     )

time: 598 us -> 563 us (0.941)
  Pallas kernels: 222 us -> 166 us
  matrix products: 13.6 us -> 64.8 us
  starting transfers between devices: 58.9 us -> 43.5 us
  other arithmetic: 45.8 us -> 37.6 us
  local copies, waits for them, and re-layouts: 33.3 us -> 26.8 us
    pallas_call x18 -> x11, Pallas kernels: 147 us -> 86.8 us  [the longest x3 30.5 us: attn_call(): pl.pallas_call(partial(attn_body, heads, emits, len(held)), grid=(count /...]
    dot_general x1 -> x11, matrix products: 2.02 us -> 51.7 us  [the longest x10 49.8 us: mm(): return lax.dot_general(left, right, dims, preferred_element_type=F32)]
    ppermute x54 -> x69, starting transfers between devices: 58.8 us -> 43.4 us  [swap(): return lax.ppermute(value, axis, [(i, i ^ mask) for i in range(size)])]
    concatenate x7 -> x1, other arithmetic: 15.1 us -> 3.49 us  [local(): jnp.concatenate([inputs, swap(inputs, 'tensor', 1), x_far, swap(x_far, 't...]
    slice x5 -> x3, local copies, waits for them, and re-layouts: 7.72 us -> 1.22 us  [the longest x1 1.04 us: local(): first_mine[:tok]]
    pallas_call x1 -> x2, Pallas kernels: 12 us -> 15.7 us  [polar_call(): pl.pallas_call(polar_body, out_shape=jax.ShapeDtypeStruct(grams.shape, F3...]
    unnamed x122 -> x142, local copies, waits for them, and re-layouts: 10.4 us -> 13.6 us
    ppermute x54 -> x69, waiting for transfers between devices: 204 us -> 204 us  [swap(): return lax.ppermute(value, axis, [(i, i ^ mask) for i in range(size)])]
  transfers between devices with their start and end apart: 57 -> 72, of which waited for: 30 -> 23; matrix products, arithmetic and copies ran while one was open for 12% -> 18% of each run, Pallas kernels for 32% -> 26%
where the time goes in v2:
time: 563 us; the launch traced here: 558 us
  waiting for transfers between devices  204 us (36%)
  Pallas kernels  166 us (29%)
  matrix products  64.8 us (12%)
  starting transfers between devices  43.5 us (8%)
  other arithmetic  37.6 us (7%)
  local copies, waits for them, and re-layouts  26.8 us (5%)
  between operations  15.8 us (3%)
    ppermute x69, waiting for transfers between devices, swap(): return lax.ppermute(value, axis, [(i, i ^ mask) for i in range(size)])  204 us
    dot_general x10, matrix products, mm(): return lax.dot_general(left, right, dims, preferred_element_type=F32)  49.8 us
    pallas_call x2, Pallas kernels, attn_back_call(): pl.pallas_call(partial(attn_back_body, heads, last_part, first), grid=(co...  45.8 us
    ppermute x69, starting transfers between devices, swap(): return lax.ppermute(value, axis, [(i, i ^ mask) for i in range(size)])  43.4 us
    pallas_call x3, Pallas kernels, attn_call(): pl.pallas_call(partial(attn_body, heads, emits, len(held)), grid=(count /...  30.5 us
    pallas_call x3, Pallas kernels, mlp_call(): pl.pallas_call(partial(mlp_body, min(256, hidden_width), emits, len(held)...  30.3 us
    pallas_call x3, Pallas kernels, row_call(): pl.pallas_call(partial(row_body, body, len(rows_in)), grid=(PIECES,), in_...  17.8 us
    pallas_call x2, Pallas kernels, polar_call(): pl.pallas_call(polar_body, out_shape=jax.ShapeDtypeStruct(grams.shape, F3...  15.7 us
  transfers between devices with their start and end apart: 72, of which 23 were waited for; matrix products, arithmetic and copies ran while one was open for 18% of the time, Pallas kernels for 26%

profile of v2, /device:TPU:0, one launch (start us, length us, event | category | flops | bytes accessed | tf_op | source)
XLA Modules:
  0.0 558.2 jit_solution(1765101299282948273)
XLA Ops:
  7.2 3.0 collective-permute-start.3
  20.6 6.8 %collective-permute-done.4.refs_2_ = bf16[160,1408]{1,0:T(8,128)(2,1)} collective-permute-done((bf16[160,1408]{1,0:T(8,128)(2,1)S(1)}, bf16[160,1408]{1,0:T(8,128)(2,1)}, u32[]{:S(2)}, u32[]{:S(2)}) %collective-permute-start.4) | collective-permute-done | bytes 450592 | tf_op jit(solution)/shard_map/ppermute | solution.py:68
  28.1 10.6 %collective-permute-done.refs_6_ = bf16[160,1408]{1,0:T(8,128)(2,1)} collective-permute-done((bf16[160,1408]{1,0:T(8,128)(2,1)S(1)}, bf16[160,1408]{1,0:T(8,128)(2,1)}, u32[]{:S(2)}, u32[]{:S(2)}) %collective-permute-start) | collective-permute-done | bytes 450592 | tf_op jit(solution)/shard_map/ppermute | solution.py:68
  38.7 3.0 collective-permute-start.8
  44.6 17.9 %collective-permute-done.8.refs_4_ = bf16[160,1408]{1,0:T(8,128)(2,1)} collective-permute-done((bf16[160,1408]{1,0:T(8,128)(2,1)S(1)}, bf16[160,1408]{1,0:T(8,128)(2,1)}, u32[]{:S(2)}, u32[]{:S(2)}) %collective-permute-start.8) | collective-permute-done | bytes 450592 | tf_op jit(solution)/shard_map/ppermute | solution.py:68
  64.7 3.5 pad_maximum_fusion.x_ref
  68.2 7.9 %collective-permute-done.9.refs_5_ = bf16[160,1408]{1,0:T(8,128)(2,1)} collective-permute-done((bf16[160,1408]{1,0:T(8,128)(2,1)}, bf16[160,1408]{1,0:T(8,128)(2,1)}, u32[]{:S(2)}, u32[]{:S(2)}) %collective-permute-start.9) | collective-permute-done | bytes 450592 | tf_op jit(solution)/shard_map/ppermute | solution.py:68
  80.4 4.2 place_rows.2
  84.6 4.7 copy.58
  92.9 9.7 %norm_qkv.1 = (bf16[1536,1280]{1,0:T(8,128)(2,1)}, bf16[1536,1024]{1,0:T(8,128)(2,1)}) custom-call(bf16[1536,1280]{1,0:T(8,128)(2,1)} %pad_maximum_fusion.x_ref, f32[8,1280]{1,0:T(8,128)} %slice.200.vec_ref.refs_7_.refs_8_, bf16[1280,1024]{1,0:T(8,128)(2,1)} %get-tuple-element.110.w_ref, f32[1,1024]{1,0:T(1,128)} %pad_maximum_fusion.6.bias_ref), custom_call_target="tpu_custom_call" | custom-call | flops 1000000 | bytes 100000 | tf_op jit(solution)/shard_map/norm_qkv/pallas_call | solution.py:109
  102.6 48.2 %collective-permute-done.11.refs_4_ = bf16[160,1280]{1,0:T(8,128)(2,1)} collective-permute-done((bf16[160,1280]{1,0:T(8,128)(2,1)S(1)}, bf16[160,1280]{1,0:T(8,128)(2,1)}, u32[]{:S(2)}, u32[]{:S(2)}) %collective-permute-start.11) | collective-permute-done | bytes 409632 | tf_op jit(solution)/shard_map/ppermute | solution.py:68
  150.8 8.2 %attn_fwd.3 = (bf16[1536,384]{1,0:T(8,128)(2,1)}, f32[8,1536]{1,0:T(8,128)}, bf16[96,1280]{1,0:T(8,128)(2,1)}, bf16[96,1280]{1,0:T(8,128)(2,1)}, bf16[96,1280]{1,0:T(8,128)(2,1)}, /*index=5*/bf16[96,1280]{1,0:T(8,128)(2,1)}) custom-call(bf16[1536,1024]{1,0:T(8,128)(2,1)} %get-tuple-element.123.q_ref.qkv_ref, ...), custom_call_target="tpu_custom_call" | custom-call | flops 1000000 | bytes 100000 | tf_op jit(solution)/shard_map/attn_fwd/pallas_call | solution.py:272
  162.5 8.2 %attn_fwd.4 = (bf16[1536,384]{1,0:T(8,128)(2,1)}, f32[8,1536]{1,0:T(8,128)}, bf16[384,1280]{1,0:T(8,128)(2,1)}) custom-call(bf16[1536,1024]{1,0:T(8,128)(2,1)} %get-tuple-element.123.q_ref.qkv_ref, bf16[1536,1024]{1,0:T(8,128)(2,1)} %get-tuple-element.123.q_ref.qkv_ref, ...), custom_call_target="tpu_custom_call", output_to_operand_aliasing={{0}: (4, {}), {1}: (5, {})} | custom-call | flops 1000000 | bytes 100000 | tf_op jit(solution)/shard_map/attn_fwd/pallas_call | solution.py:272
  171.5 4.4 pair_sum.2
  179.6 14.2 %attn_fwd.5 = (bf16[1536,384]{1,0:T(8,128)(2,1)}, f32[8,1536]{1,0:T(8,128)}, bf16[384,1280]{1,0:T(8,128)(2,1)}, bf16[96,1280]{1,0:T(8,128)(2,1)}, bf16[96,1280]{...) custom-call(bf16[1536,1024]{1,0:T(8,128)(2,1)} %get-tuple-element.12, ...), custom_call_target="tpu_custom_call", output_to_operand_aliasing={{0}: (4, {}), {1}: (5, {})} | custom-call | flops 1000000 | bytes 100000 | tf_op jit(solution)/shard_map/attn_fwd/pallas_call | solution.py:272
  202.4 4.9 residual.1
  208.0 9.9 %fusion.43.refs_4_.refs_3_ = f32[1536,1280]{1,0:T(8,128)} fusion(bf16[1536,1280]{1,0:T(8,128)(2,1)} %constant_dynamic-update-slice_fusion, bf16[1280,1280]{1,0:T(8,128)(2,1)} %all-gather.2.cloned.1.call-done), kind=kOutput, calls=%fused_computation.126 | convolution fusion | flops 5033164800 | bytes 15073280 | tf_op jit(solution)/shard_map/dot_general | solution.py:43
  217.9 7.1 %collective-permute-done.25.refs_3_ = bf16[160,1280]{1,0:T(8,128)(2,1)} collective-permute-done((bf16[160,1280]{1,0:T(8,128)(2,1)}, bf16[160,1280]{1,0:T(8,128)(2,1)}, u32[]{:S(2)}, u32[]{:S(2)}) %collective-permute-start.25) | collective-permute-done | bytes 409632 | tf_op jit(solution)/shard_map/ppermute | solution.py:68
  225.0 8.4 %collective-permute-done.26.refs_5_ = bf16[160,1280]{1,0:T(8,128)(2,1)} collective-permute-done((bf16[160,1280]{1,0:T(8,128)(2,1)}, bf16[160,1280]{1,0:T(8,128)(2,1)}, u32[]{:S(2)}, u32[]{:S(2)}) %collective-permute-start.26) | collective-permute-done | bytes 409632 | tf_op jit(solution)/shard_map/ppermute | solution.py:68
  233.4 3.8 place_rows.3.refs_2_.refs_1_
  238.2 14.2 %mlp_up.3 = (bf16[1536,1280]{1,0:T(8,128)(2,1)}, bf16[1536,1280]{1,0:T(8,128)(2,1)}, f32[8,1280]{1,0:T(8,128)}, bf16[384,1280]{1,0:T(8,128)(2,1)}, bf16[96,1280]...) custom-call(bf16[384,1280]{1,0:T(8,128)(2,1)} %get-tuple-element.132.refs_0_, ...), custom_call_target="tpu_custom_call" | custom-call | flops 1000000 | bytes 100000 | tf_op jit(solution)/shard_map/mlp_up/pallas_call | solution.py:477
  252.4 2.6 collective-permute-done.31.refs_0_
  256.0 8.0 %mlp_up.4 = (bf16[1536,1280]{1,0:T(8,128)(2,1)}, bf16[1536,1280]{1,0:T(8,128)(2,1)}, f32[8,1280]{1,0:T(8,128)}, bf16[96,1280]{1,0:T(8,128)(2,1)}, bf16[96,1280]{...) custom-call(bf16[384,1280]{1,0:T(8,128)(2,1)} %copy-done.29, ...), custom_call_target="tpu_custom_call", output_to_operand_aliasing={{0}: (4, {}), {1}: (5, {})} | custom-call | flops 1000000 | bytes 100000 | tf_op jit(solution)/shard_map/mlp_up/pallas_call | solution.py:477
  265.0 8.2 %mlp_up.5 = (bf16[1536,1280]{1,0:T(8,128)(2,1)}, bf16[1536,1280]{1,0:T(8,128)(2,1)}, f32[8,1280]{1,0:T(8,128)}, bf16[384,1280]{1,0:T(8,128)(2,1)}) custom-call(bf16[384,1280]{1,0:T(8,128)(2,1)} %copy-done.26, bf16[1280,1280]{1,0:T(8,128)(2,1)} %place_rows.3.refs_2_.refs_1_, ...), custom_call_target="tpu_custom_call", output_to_operand_aliasing={{0}: (4, {}), {1}: (5, {})} | custom-call | flops 1000000 | bytes 100000 | tf_op jit(solution)/shard_map/mlp_up/pallas_call | solution.py:477
  274.1 3.9 pair_sum.3
  278.0 9.4 %convolution_convert_fusion.1 = bf16[1280,1280]{1,0:T(8,128)(2,1)} fusion(bf16[1536,1280]{1,0:T(8,128)(2,1)S(1)} %copy-done.38, bf16[1536,1280]{1,0:T(8,128)(2,1)} %get-tuple-element.175), kind=kOutput, calls=%fused_computation.1 | convolution fusion | flops 5034803200 | bytes 11141120 | tf_op jit(solution)/shard_map/dot_general | solution.py:43
  289.1 9.3 %convolution_convert_fusion = bf16[1280,1280]{1,0:T(8,128)(2,1)} fusion(bf16[1536,1280]{1,0:T(8,128)(2,1)} %get-tuple-element.155, bf16[384,1280]{1,0:T(8,128)(2,1)} %copy-done.29, bf16[384,1280]{1,0:T(8,128)(2,1)S(1)} %copy-done.27, bf16[384,1280]{1,0:T(8,128)(2,1)} %copy-done.28, bf16[384,1280]{1,0:T(8,128)(2,1)S(1)} %copy-done.25), kind=kOutput, calls=%fused_computation | convolution fusion | flops 5050531840 | bytes 11141120 | tf_op jit(solution)/shard_map/dot_general | solution.py:43
  298.5 14.2 %collective-permute-done.36.refs_2_ = bf16[384,1280]{1,0:T(8,128)(2,1)} collective-permute-done((bf16[384,1280]{1,0:T(8,128)(2,1)}, bf16[384,1280]{1,0:T(8,128)(2,1)}, u32[]{:S(2)}, u32[]{:S(2)}) %collective-permute-start.36) | collective-permute-done | bytes 983072 | tf_op jit(solution)/shard_map/ppermute | solution.py:68
  312.7 6.2 %second_back.1 = (f32[384,1280]{1,0:T(8,128)}, bf16[384,1280]{1,0:T(8,128)(2,1)}, f32[8,1280]{1,0:T(8,128)}) custom-call(f32[384,1280]{1,0:T(8,128)} %get-tuple-element.131.refs_0_, bf16[384,1280]{1,0:T(8,128)(2,1)} %get-tuple-element.136.refs_1_, bf16[384,1280]{1,0:T(8,128)(2,1)} %collective-permute-done.36.refs_2_, bf16[384,1280]{1,0:T(8,128)(2,1)} %refs_3_.1, ...), custom_call_target="tpu_custom_call" | custom-call | flops 1000000 | bytes 100000 | tf_op jit(solution)/shard_map/second_back/pallas_call | solution.py:565
  323.1 22.3 %attn_bwd.2 = (bf16[1536,1024]{1,0:T(8,128)(2,1)}, f32[8,384]{1,0:T(8,128)}, f32[1536,384]{1,0:T(8,128)}, f32[1536,384]{1,0:T(8,128)}) custom-call(bf16[768,1280]{1,0:T(8,128)(2,1)} %copy-done.9, bf16[1280,384]{1,0:T(8,128)(2,1)} %get-tuple-element.114.wo_ref, bf16[1536,384]{1,0:T(8,128)(2,1)} %get-tuple-element.161.att_ref, ...), custom_call_target="tpu_custom_call" | custom-call | flops 1000000 | bytes 100000 | tf_op jit(solution)/shard_map/attn_bwd/pallas_call | solution.py:405
  353.0 23.5 %attn_bwd.3 = (bf16[1536,1024]{1,0:T(8,128)(2,1)}, f32[8,384]{1,0:T(8,128)}) custom-call(bf16[768,1280]{1,0:T(8,128)(2,1)} %copy-done.11, bf16[1280,384]{1,0:T(8,128)(2,1)} %get-tuple-element.114.wo_ref, bf16[1536,384]{1,0:T(8,128)(2,1)} %get-tuple-element.161.att_ref, ...), custom_call_target="tpu_custom_call", output_to_operand_aliasing={{0}: (10, {})} | custom-call | flops 1000000 | bytes 100000 | tf_op jit(solution)/shard_map/attn_bwd/pallas_call | solution.py:405
  376.5 6.8 %convolution_convert_fusion.2 = bf16[1280,1024]{1,0:T(8,128)(2,1)S(1)} fusion(bf16[1536,1280]{1,0:T(8,128)(2,1)S(1)} %copy-done.66, bf16[1536,1024]{1,0:T(8,128)(2,1)} %get-tuple-element.171), kind=kOutput, calls=%fused_computation.10 | convolution fusion | flops 4027842560 | bytes 9699328 | tf_op jit(solution)/shard_map/dot_general | solution.py:43
  389.3 11.6 %collective-permute-done.44 = bf16[160,1408]{1,0:T(8,128)(2,1)S(1)} collective-permute-done((bf16[160,1408]{1,0:T(8,128)(2,1)S(1)}, bf16[160,1408]{1,0:T(8,128)(2,1)S(1)}, u32[]{:S(2)}, u32[]{:S(2)}) %collective-permute-start.44) | collective-permute-done | bytes 450592 | tf_op jit(solution)/shard_map/ppermute | solution.py:68
  405.3 2.7 convolution_convert_fusion.3
  412.1 16.4 %collective-permute-done.49.refs_2_ = bf16[384,1280]{1,0:T(8,128)(2,1)} collective-permute-done((bf16[384,1280]{1,0:T(8,128)(2,1)S(1)}, bf16[384,1280]{1,0:T(8,128)(2,1)}, u32[]{:S(2)}, u32[]{:S(2)}) %collective-permute-start.49) | collective-permute-done | bytes 983072 | tf_op jit(solution)/shard_map/ppermute | solution.py:68
  428.5 6.6 %first_back.1 = (f32[384,1280]{1,0:T(8,128)}, f32[8,1280]{1,0:T(8,128)}) custom-call(bf16[384,1280]{1,0:T(8,128)(2,1)} %refs_0_.3, bf16[384,1280]{1,0:T(8,128)(2,1)} %slice.210.refs_1_, bf16[384,1280]{1,0:T(8,128)(2,1)} %collective-permute-done.49.refs_2_, f32[384,1280]{1,0:T(8,128)} %get-tuple-element.176.refs_3_, bf16[96,1280]{1,0:T(8,128)(2,1)} %copy-done.40, ...), custom_call_target="tpu_custom_call" | custom-call | flops 1000000 | bytes 100000 | tf_op jit(solution)/shard_map/first_back/pallas_call | solution.py:565
  436.0 4.7 convolution_convert_fusion.4
  446.5 8.1 %collective-permute-done.57 = bf16[160,1408]{1,0:T(8,128)(2,1)S(1)} collective-permute-done((bf16[160,1408]{1,0:T(8,128)(2,1)S(1)}, bf16[160,1408]{1,0:T(8,128)(2,1)S(1)}, u32[]{:S(2)}, u32[]{:S(2)}) %collective-permute-start.57) | collective-permute-done | bytes 450592 | tf_op jit(solution)/shard_map/ppermute | solution.py:68
  458.7 8.2 %collective-permute-done.59 = bf16[160,1408]{1,0:T(8,128)(2,1)S(1)} collective-permute-done((bf16[160,1408]{1,0:T(8,128)(2,1)S(1)}, bf16[160,1408]{1,0:T(8,128)(2,1)S(1)}, u32[]{:S(2)}, u32[]{:S(2)}) %collective-permute-start.59) | collective-permute-done | bytes 450592 | tf_op jit(solution)/shard_map/ppermute | solution.py:68
  472.8 7.5 %collective-permute-done.67 = f32[9,1280]{1,0:T(8,128)S(1)} collective-permute-done((f32[9,1280]{1,0:T(8,128)S(1)}, f32[9,1280]{1,0:T(8,128)S(1)}, u32[]{:S(2)}, u32[]{:S(2)}) %collective-permute-start.67) | collective-permute-done | bytes 46112 | tf_op jit(solution)/shard_map/ppermute | solution.py:68
  482.2 8.2 %collective-permute-done.68 = f32[9,1280]{1,0:T(8,128)S(1)} collective-permute-done((f32[9,1280]{1,0:T(8,128)S(1)}, f32[9,1280]{1,0:T(8,128)S(1)}, u32[]{:S(2)}, u32[]{:S(2)}) %collective-permute-start.68) | collective-permute-done | bytes 46112 | tf_op jit(solution)/shard_map/ppermute | solution.py:68
  499.0 4.0 collective-permute-done.61
  503.7 6.8 %polar.2 = f32[1,160,160]{2,1,0:T(8,128)} custom-call(f32[1,160,160]{2,1,0:T(8,128)} %add.238.gram_ref), custom_call_target="tpu_custom_call" | custom-call | tf_op jit(solution)/shard_map/polar/pallas_call | solution.py:618
  510.5 2.7 fusion.8
  520.8 3.4 add_add_fusion
  524.2 9.7 %collective-permute-done.63 = f32[3,160,160]{2,1,0:T(8,128)S(1)} collective-permute-done((f32[3,160,160]{2,1,0:T(8,128)S(1)}, f32[3,160,160]{2,1,0:T(8,128)S(1)}, u32[]{:S(2)}, u32[]{:S(2)}) %collective-permute-start.63) | collective-permute-done | bytes 307232 | tf_op jit(solution)/shard_map/ppermute | solution.py:68
  534.8 8.9 %polar.3 = f32[3,160,160]{2,1,0:T(8,128)} custom-call(f32[3,160,160]{2,1,0:T(8,128)} %fusion.58.gram_ref), custom_call_target="tpu_custom_call" | custom-call | tf_op jit(solution)/shard_map/polar/pallas_call | solution.py:618
  547.7 2.7 convolution_subtract_fusion
  (361 shorter events, 113.2 us)
Async XLA Ops:
  7.2 200.8 %all-gather.2.cloned.1.call-start = ((), (), s32[]{:S(2)}) async-start(), calls=%async_computation.2 | async-start | bytes 3686400 | tf_op jit(solution)/shard_map/all_gather | solution.py:799
  7.2 31.5 %collective-permute-start.3 = (bf16[384,1280]{1,0:T(8,128)(2,1)}, bf16[384,1280]{1,0:T(8,128)(2,1)}, u32[]{:S(2)}, u32[]{:S(2)}) collective-permute-start(bf16[384,1280]{1,0:T(8,128)(2,1)} %refs_0_.3), channel_id=1, source_target_pairs={{0,2},{1,3},{2,0},{3,1},{4,6},{5,7},{6,4},{7,5},{8,10},{9,11},{10,... | collective-permute-start | bytes 2949128 | tf_op jit(solution)/shard_map/ppermute | solution.py:68
  14.9 12.4 %collective-permute-start.4 = (bf16[160,1408]{1,0:T(8,128)(2,1)S(1)}, bf16[160,1408]{1,0:T(8,128)(2,1)}, u32[]{:S(2)}, u32[]{:S(2)}) collective-permute-start(bf16[160,1408]{1,0:T(8,128)(2,1)S(1)} %concatenate.52.refs_0_), channel_id=1, source_target_pairs={{0,8},{4,12},{8,0},{12,4},{16,24},{20,28},{24,16},{28,20},{1,9},{5... | collective-permute-start | bytes 1351688 | tf_op jit(solution)/shard_map/ppermute | solution.py:68
  16.6 11.5 %collective-permute-start.5 = (bf16[160,1408]{1,0:T(8,128)(2,1)S(1)}, bf16[160,1408]{1,0:T(8,128)(2,1)S(1)}, u32[]{:S(2)}, u32[]{:S(2)}) collective-permute-start(bf16[160,1408]{1,0:T(8,128)(2,1)S(1)} %concatenate.52.refs_0_), channel_id=1, source_target_pairs={{0,4},{4,0},{8,12},{12,8},{16,20},{20,16},{24,28},{28,24},{1,5},{5... | collective-permute-start | bytes 1351688 | tf_op jit(solution)/shard_map/ppermute | solution.py:68
  18.1 20.6 %collective-permute-start = (bf16[160,1408]{1,0:T(8,128)(2,1)S(1)}, bf16[160,1408]{1,0:T(8,128)(2,1)}, u32[]{:S(2)}, u32[]{:S(2)}) collective-permute-start(bf16[160,1408]{1,0:T(8,128)(2,1)S(1)} %concatenate.52.refs_0_), channel_id=1, source_target_pairs={{0,24},{4,28},{8,16},{12,20},{16,8},{20,12},{24,0},{28,4},{1,25},{... | collective-permute-start | bytes 1351688 | tf_op jit(solution)/shard_map/ppermute | solution.py:68
  20.6 44.1 %collective-permute-start.2 = (bf16[384,1280]{1,0:T(8,128)(2,1)S(1)}, bf16[384,1280]{1,0:T(8,128)(2,1)}, u32[]{:S(2)}, u32[]{:S(2)}) collective-permute-start(bf16[384,1280]{1,0:T(8,128)(2,1)S(1)} %copy-done.4), channel_id=1, source_target_pairs={{0,1},{1,0},{2,3},{3,2},{4,5},{5,4},{6,7},{7,6},{8,9},{9,8},{10,11... | collective-permute-start | bytes 2949128 | tf_op jit(solution)/shard_map/ppermute | solution.py:68
  38.7 26.0 %collective-permute-start.6 = (bf16[384,1280]{1,0:T(8,128)(2,1)}, bf16[384,1280]{1,0:T(8,128)(2,1)}, u32[]{:S(2)}, u32[]{:S(2)}) collective-permute-start(bf16[384,1280]{1,0:T(8,128)(2,1)} %collective-permute-done.3), channel_id=1, source_target_pairs={{0,1},{1,0},{2,3},{3,2},{4,5},{5,4},{6,7},{7,6},{8,9},{9,8},{10,11... | collective-permute-start | bytes 2949128 | tf_op jit(solution)/shard_map/ppermute | solution.py:68
  38.7 23.7 %collective-permute-start.8 = (bf16[160,1408]{1,0:T(8,128)(2,1)S(1)}, bf16[160,1408]{1,0:T(8,128)(2,1)}, u32[]{:S(2)}, u32[]{:S(2)}) collective-permute-start(bf16[160,1408]{1,0:T(8,128)(2,1)S(1)} %concatenate.52.refs_0_), channel_id=1, source_target_pairs={{0,16},{4,20},{8,24},{12,28},{16,0},{20,4},{24,8},{28,12},{1,17},{... | collective-permute-start | bytes 1351688 | tf_op jit(solution)/shard_map/ppermute | solution.py:68
  41.8 20.7 %collective-permute-start.1 = (bf16[160,1408]{1,0:T(8,128)(2,1)}, bf16[160,1408]{1,0:T(8,128)(2,1)}, u32[]{:S(2)}, u32[]{:S(2)}) collective-permute-start(bf16[160,1408]{1,0:T(8,128)(2,1)} %collective-permute-done.refs_6_), channel_id=1, source_target_pairs={{0,4},{4,0},{8,12},{12,8},{16,20},{20,16},{24,28},{28,24},{1,5},{5... | collective-permute-start | bytes 1351688 | tf_op jit(solution)/shard_map/ppermute | solution.py:68
  42.3 21.8 %collective-permute-start.7 = (bf16[160,1408]{1,0:T(8,128)(2,1)}, bf16[160,1408]{1,0:T(8,128)(2,1)}, u32[]{:S(2)}, u32[]{:S(2)}) collective-permute-start(bf16[160,1408]{1,0:T(8,128)(2,1)} %collective-permute-done.4.refs_2_), channel_id=1, source_target_pairs={{0,4},{4,0},{8,12},{12,8},{16,20},{20,16},{24,28},{28,24},{1,5},{5... | collective-permute-start | bytes 1351688 | tf_op jit(solution)/shard_map/ppermute | solution.py:68
  64.1 11.9 %collective-permute-start.9 = (bf16[160,1408]{1,0:T(8,128)(2,1)}, bf16[160,1408]{1,0:T(8,128)(2,1)}, u32[]{:S(2)}, u32[]{:S(2)}) collective-permute-start(bf16[160,1408]{1,0:T(8,128)(2,1)} %collective-permute-done.8.refs_4_), channel_id=1, source_target_pairs={{0,4},{4,0},{8,12},{12,8},{16,20},{20,16},{24,28},{28,24},{1,5},{5... | collective-permute-start | bytes 1351688 | tf_op jit(solution)/shard_map/ppermute | solution.py:68
  76.0 415.0 %reduce-scatter.3.cloned.1.call-start = ((), (), s32[]{:S(2)}) async-start(), calls=%async_computation.3 | async-start | bytes 3686400 | tf_op jit(solution)/shard_map/reduce_scatter | solution.py:724
  76.1 101.2 %collective-permute-start.28 = (bf16[384,1280]{1,0:T(8,128)(2,1)S(1)}, bf16[384,1280]{1,0:T(8,128)(2,1)}, u32[]{:S(2)}, u32[]{:S(2)}) collective-permute-start(bf16[384,1280]{1,0:T(8,128)(2,1)S(1)} %copy-done.12), channel_id=1, source_target_pairs={{0,1},{1,0},{2,3},{3,2},{4,5},{5,4},{6,7},{7,6},{8,9},{9,8},{10,11... | collective-permute-start | bytes 2949128 | tf_op jit(solution)/shard_map/ppermute | solution.py:68
  76.2 83.2 %collective-permute-start.29 = (bf16[384,1280]{1,0:T(8,128)(2,1)S(1)}, bf16[384,1280]{1,0:T(8,128)(2,1)S(1)}, u32[]{:S(2)}, u32[]{:S(2)}) collective-permute-start(bf16[384,1280]{1,0:T(8,128)(2,1)S(1)} %copy-done.12), channel_id=1, source_target_pairs={{0,2},{1,3},{2,0},{3,1},{4,6},{5,7},{6,4},{7,5},{8,10},{9,11},{10,... | collective-permute-start | bytes 2949128 | tf_op jit(solution)/shard_map/ppermute | solution.py:68
  90.7 68.7 %collective-permute-start.10 = (bf16[160,1280]{1,0:T(8,128)(2,1)S(1)}, bf16[160,1280]{1,0:T(8,128)(2,1)}, u32[]{:S(2)}, u32[]{:S(2)}) collective-permute-start(bf16[160,1280]{1,0:T(8,128)(2,1)S(1)} %convert_element_type.134.refs_0_), channel_id=1, source_target_pairs={{0,24},{4,28},{8,16},{12,20},{16,8},{20,12},{24,0},{28,4},{1,25},{... | collective-permute-start | bytes 1228808 | tf_op jit(solution)/shard_map/ppermute | solution.py:68
  91.8 58.9 %collective-permute-start.11 = (bf16[160,1280]{1,0:T(8,128)(2,1)S(1)}, bf16[160,1280]{1,0:T(8,128)(2,1)}, u32[]{:S(2)}, u32[]{:S(2)}) collective-permute-start(bf16[160,1280]{1,0:T(8,128)(2,1)S(1)} %convert_element_type.134.refs_0_), channel_id=1, source_target_pairs={{0,16},{4,20},{8,24},{12,28},{16,0},{20,4},{24,8},{28,12},{1,17},{... | collective-permute-start | bytes 1228808 | tf_op jit(solution)/shard_map/ppermute | solution.py:68
  159.4 37.8 %collective-permute-start.30 = (bf16[384,1280]{1,0:T(8,128)(2,1)S(1)}, bf16[384,1280]{1,0:T(8,128)(2,1)S(1)}, u32[]{:S(2)}, u32[]{:S(2)}) collective-permute-start(bf16[384,1280]{1,0:T(8,128)(2,1)S(1)} %collective-permute-done.29), channel_id=1, source_target_pairs={{0,1},{1,0},{2,3},{3,2},{4,5},{5,4},{6,7},{7,6},{8,9},{9,8},{10,11... | collective-permute-start | bytes 2949128 | tf_op jit(solution)/shard_map/ppermute | solution.py:68
  159.4 20.1 %collective-permute-start.16 = (bf16[160,1280]{1,0:T(8,128)(2,1)S(1)}, bf16[160,1280]{1,0:T(8,128)(2,1)}, u32[]{:S(2)}, u32[]{:S(2)}) collective-permute-start(bf16[160,1280]{1,0:T(8,128)(2,1)S(1)} %convert_element_type.134.refs_0_), channel_id=1, source_target_pairs={{0,8},{4,12},{8,0},{12,4},{16,24},{20,28},{24,16},{28,20},{1,9},{5... | collective-permute-start | bytes 1228808 | tf_op jit(solution)/shard_map/ppermute | solution.py:68
  175.9 25.6 %collective-permute-start.17 = (bf16[384,1280]{1,0:T(8,128)(2,1)}, bf16[384,1280]{1,0:T(8,128)(2,1)S(1)}, u32[]{:S(2)}, u32[]{:S(2)}) collective-permute-start(bf16[384,1280]{1,0:T(8,128)(2,1)} %pair_sum.2), channel_id=1, source_target_pairs={{0,2},{1,3},{2,0},{3,1},{4,6},{5,7},{6,4},{7,5},{8,10},{9,11},{10,... | collective-permute-start | bytes 2949128 | tf_op jit(solution)/shard_map/ppermute | solution.py:68
  194.9 13.1 %collective-permute-start.27 = (bf16[160,1280]{1,0:T(8,128)(2,1)}, bf16[160,1280]{1,0:T(8,128)(2,1)}, u32[]{:S(2)}, u32[]{:S(2)}) collective-permute-start(bf16[160,1280]{1,0:T(8,128)(2,1)} %collective-permute-done.10.refs_6_), channel_id=1, source_target_pairs={{0,4},{4,0},{8,12},{12,8},{16,20},{20,16},{24,28},{28,24},{1,5},{5... | collective-permute-start | bytes 1228808 | tf_op jit(solution)/shard_map/ppermute | solution.py:68
  198.9 19.0 %collective-permute-start.24 = (bf16[160,1280]{1,0:T(8,128)(2,1)S(1)}, bf16[160,1280]{1,0:T(8,128)(2,1)}, u32[]{:S(2)}, u32[]{:S(2)}) collective-permute-start(bf16[160,1280]{1,0:T(8,128)(2,1)S(1)} %convert_element_type.134.refs_0_), channel_id=1, source_target_pairs={{0,4},{4,0},{8,12},{12,8},{16,20},{20,16},{24,28},{28,24},{1,5},{5... | collective-permute-start | bytes 1228808 | tf_op jit(solution)/shard_map/ppermute | solution.py:68
  199.4 25.6 %collective-permute-start.25 = (bf16[160,1280]{1,0:T(8,128)(2,1)}, bf16[160,1280]{1,0:T(8,128)(2,1)}, u32[]{:S(2)}, u32[]{:S(2)}) collective-permute-start(bf16[160,1280]{1,0:T(8,128)(2,1)} %collective-permute-done.16.refs_2_), channel_id=1, source_target_pairs={{0,4},{4,0},{8,12},{12,8},{16,20},{20,16},{24,28},{28,24},{1,5},{5... | collective-permute-start | bytes 1228808 | tf_op jit(solution)/shard_map/ppermute | solution.py:68
  201.0 32.4 %collective-permute-start.26 = (bf16[160,1280]{1,0:T(8,128)(2,1)}, bf16[160,1280]{1,0:T(8,128)(2,1)}, u32[]{:S(2)}, u32[]{:S(2)}) collective-permute-start(bf16[160,1280]{1,0:T(8,128)(2,1)} %collective-permute-done.11.refs_4_), channel_id=1, source_target_pairs={{0,4},{4,0},{8,12},{12,8},{16,20},{20,16},{24,28},{28,24},{1,5},{5... | collective-permute-start | bytes 1228808 | tf_op jit(solution)/shard_map/ppermute | solution.py:68
  207.4 45.0 %collective-permute-start.22 = (bf16[384,1280]{1,0:T(8,128)(2,1)}, bf16[384,1280]{1,0:T(8,128)(2,1)S(1)}, u32[]{:S(2)}, u32[]{:S(2)}) collective-permute-start(bf16[384,1280]{1,0:T(8,128)(2,1)} %get-tuple-element.132.refs_0_), channel_id=1, source_target_pairs={{0,2},{1,3},{2,0},{3,1},{4,6},{5,7},{6,4},{7,5},{8,10},{9,11},{10,... | collective-permute-start | bytes 2949128 | tf_op jit(solution)/shard_map/ppermute | solution.py:68
  208.0 29.2 %collective-permute-start.23 = (bf16[384,1280]{1,0:T(8,128)(2,1)}, bf16[384,1280]{1,0:T(8,128)(2,1)S(1)}, u32[]{:S(2)}, u32[]{:S(2)}) collective-permute-start(bf16[384,1280]{1,0:T(8,128)(2,1)} %get-tuple-element.132.refs_0_), channel_id=1, source_target_pairs={{0,1},{1,0},{2,3},{3,2},{4,5},{5,4},{6,7},{7,6},{8,9},{9,8},{10,11... | collective-permute-start | bytes 2949128 | tf_op jit(solution)/shard_map/ppermute | solution.py:68
  287.4 207.5 %reduce-scatter.5.cloned.1.call-start = ((), (), s32[]{:S(2)}) async-start(), calls=%async_computation.4 | async-start | bytes 3686400 | tf_op jit(solution)/shard_map/reduce_scatter | solution.py:724
  287.5 11.0 %collective-permute-start.37 = (bf16[96,1280]{1,0:T(8,128)(2,1)}, bf16[96,1280]{1,0:T(8,128)(2,1)S(1)}, u32[]{:S(2)}, u32[]{:S(2)}) collective-permute-start(bf16[96,1280]{1,0:T(8,128)(2,1)} %get-tuple-element.148), channel_id=1, source_target_pairs={{0,1},{1,0},{2,3},{3,2},{4,5},{5,4},{6,7},{7,6},{8,9},{9,8},{10,11... | collective-permute-start | bytes 737288 | tf_op jit(solution)/shard_map/ppermute | solution.py:68
  287.7 10.8 %collective-permute-start.38 = (bf16[96,1280]{1,0:T(8,128)(2,1)}, bf16[96,1280]{1,0:T(8,128)(2,1)S(1)}, u32[]{:S(2)}, u32[]{:S(2)}) collective-permute-start(bf16[96,1280]{1,0:T(8,128)(2,1)} %get-tuple-element.149), channel_id=1, source_target_pairs={{0,1},{1,0},{2,3},{3,2},{4,5},{5,4},{6,7},{7,6},{8,9},{9,8},{10,11... | collective-permute-start | bytes 737288 | tf_op jit(solution)/shard_map/ppermute | solution.py:68
  288.0 10.4 %collective-permute-start.39 = (bf16[96,1280]{1,0:T(8,128)(2,1)}, bf16[96,1280]{1,0:T(8,128)(2,1)S(1)}, u32[]{:S(2)}, u32[]{:S(2)}) collective-permute-start(bf16[96,1280]{1,0:T(8,128)(2,1)} %get-tuple-element.150), channel_id=1, source_target_pairs={{0,1},{1,0},{2,3},{3,2},{4,5},{5,4},{6,7},{7,6},{8,9},{9,8},{10,11... | collective-permute-start | bytes 737288 | tf_op jit(solution)/shard_map/ppermute | solution.py:68
  288.2 10.3 %collective-permute-start.40 = (bf16[96,1280]{1,0:T(8,128)(2,1)}, bf16[96,1280]{1,0:T(8,128)(2,1)}, u32[]{:S(2)}, u32[]{:S(2)}) collective-permute-start(bf16[96,1280]{1,0:T(8,128)(2,1)} %get-tuple-element.151), channel_id=1, source_target_pairs={{0,1},{1,0},{2,3},{3,2},{4,5},{5,4},{6,7},{7,6},{8,9},{9,8},{10,11... | collective-permute-start | bytes 737288 | tf_op jit(solution)/shard_map/ppermute | solution.py:68
  288.5 24.1 %collective-permute-start.36 = (bf16[384,1280]{1,0:T(8,128)(2,1)}, bf16[384,1280]{1,0:T(8,128)(2,1)}, u32[]{:S(2)}, u32[]{:S(2)}) collective-permute-start(bf16[384,1280]{1,0:T(8,128)(2,1)} %pair_sum.3), channel_id=1, source_target_pairs={{0,2},{1,3},{2,0},{3,1},{4,6},{5,7},{6,4},{7,5},{8,10},{9,11},{10,... | collective-permute-start | bytes 2949128 | tf_op jit(solution)/shard_map/ppermute | solution.py:68
  319.0 26.4 %collective-permute-start.41 = (bf16[384,1280]{1,0:T(8,128)(2,1)}, bf16[384,1280]{1,0:T(8,128)(2,1)S(1)}, u32[]{:S(2)}, u32[]{:S(2)}) collective-permute-start(bf16[384,1280]{1,0:T(8,128)(2,1)} %get-tuple-element.160), channel_id=1, source_target_pairs={{0,2},{1,3},{2,0},{3,1},{4,6},{5,7},{6,4},{7,5},{8,10},{9,11},{10,... | collective-permute-start | bytes 2949128 | tf_op jit(solution)/shard_map/ppermute | solution.py:68
  384.0 16.8 %collective-permute-start.44 = (bf16[160,1408]{1,0:T(8,128)(2,1)S(1)}, bf16[160,1408]{1,0:T(8,128)(2,1)S(1)}, u32[]{:S(2)}, u32[]{:S(2)}) collective-permute-start(bf16[160,1408]{1,0:T(8,128)(2,1)S(1)} %constant_dynamic-slice_fusion.3), channel_id=1, source_target_pairs={{0,4},{4,0},{8,12},{12,8},{16,20},{20,16},{24,28},{28,24},{1,5},{5... | collective-permute-start | bytes 1351688 | tf_op jit(solution)/shard_map/ppermute | solution.py:68
  388.4 15.9 %collective-permute-start.48 = (bf16[384,1280]{1,0:T(8,128)(2,1)S(1)}, bf16[384,1280]{1,0:T(8,128)(2,1)S(1)}, u32[]{:S(2)}, u32[]{:S(2)}) collective-permute-start(bf16[384,1280]{1,0:T(8,128)(2,1)S(1)} %slice.212), channel_id=1, source_target_pairs={{0,1},{1,0},{2,3},{3,2},{4,5},{5,4},{6,7},{7,6},{8,9},{9,8},{10,11... | collective-permute-start | bytes 2949128 | tf_op jit(solution)/shard_map/ppermute | solution.py:68
  404.5 23.9 %collective-permute-start.49 = (bf16[384,1280]{1,0:T(8,128)(2,1)S(1)}, bf16[384,1280]{1,0:T(8,128)(2,1)}, u32[]{:S(2)}, u32[]{:S(2)}) collective-permute-start(bf16[384,1280]{1,0:T(8,128)(2,1)S(1)} %add_convert_fusion), channel_id=1, source_target_pairs={{0,2},{1,3},{2,0},{3,1},{4,6},{5,7},{6,4},{7,5},{8,10},{9,11},{10,... | collective-permute-start | bytes 2949128 | tf_op jit(solution)/shard_map/ppermute | solution.py:68
  410.5 59.5 %collective-permute-start.46 = (bf16[384,1280]{1,0:T(8,128)(2,1)S(1)}, bf16[384,1280]{1,0:T(8,128)(2,1)}, u32[]{:S(2)}, u32[]{:S(2)}) collective-permute-start(bf16[384,1280]{1,0:T(8,128)(2,1)S(1)} %slice.208), channel_id=1, source_target_pairs={{0,1},{1,0},{2,3},{3,2},{4,5},{5,4},{6,7},{7,6},{8,9},{9,8},{10,11... | collective-permute-start | bytes 2949128 | tf_op jit(solution)/shard_map/ppermute | solution.py:68
  410.6 31.9 %collective-permute-start.55 = (bf16[160,1408]{1,0:T(8,128)(2,1)}, bf16[160,1408]{1,0:T(8,128)(2,1)}, u32[]{:S(2)}, u32[]{:S(2)}) collective-permute-start(bf16[160,1408]{1,0:T(8,128)(2,1)} %get-tuple-element.204), channel_id=1, source_target_pairs={{0,4},{4,0},{8,12},{12,8},{16,20},{20,16},{24,28},{28,24},{1,5},{5... | collective-permute-start | bytes 1351688 | tf_op jit(solution)/shard_map/ppermute | solution.py:68
  441.8 53.2 %collective-permute-start.45 = (bf16[384,1280]{1,0:T(8,128)(2,1)}, bf16[384,1280]{1,0:T(8,128)(2,1)}, u32[]{:S(2)}, u32[]{:S(2)}) collective-permute-start(bf16[384,1280]{1,0:T(8,128)(2,1)} %slice.206), channel_id=1, source_target_pairs={{0,1},{1,0},{2,3},{3,2},{4,5},{5,4},{6,7},{7,6},{8,9},{9,8},{10,11... | collective-permute-start | bytes 2949128 | tf_op jit(solution)/shard_map/ppermute | solution.py:68
  442.2 48.8 %collective-permute-start.54 = (bf16[160,1408]{1,0:T(8,128)(2,1)S(1)}, bf16[160,1408]{1,0:T(8,128)(2,1)}, u32[]{:S(2)}, u32[]{:S(2)}) collective-permute-start(bf16[160,1408]{1,0:T(8,128)(2,1)S(1)} %get-tuple-element.205), channel_id=1, source_target_pairs={{0,16},{4,20},{8,24},{12,28},{16,0},{20,4},{24,8},{28,12},{1,17},{... | collective-permute-start | bytes 1351688 | tf_op jit(solution)/shard_map/ppermute | solution.py:68
  442.4 12.2 %collective-permute-start.57 = (bf16[160,1408]{1,0:T(8,128)(2,1)S(1)}, bf16[160,1408]{1,0:T(8,128)(2,1)S(1)}, u32[]{:S(2)}, u32[]{:S(2)}) collective-permute-start(bf16[160,1408]{1,0:T(8,128)(2,1)S(1)} %copy-done.36), channel_id=1, source_target_pairs={{0,4},{4,0},{8,12},{12,8},{16,20},{20,16},{24,28},{28,24},{1,5},{5... | collective-permute-start | bytes 1351688 | tf_op jit(solution)/shard_map/ppermute | solution.py:68
  443.8 12.0 %collective-permute-start.65 = (f32[8,1280]{1,0:T(8,128)S(1)}, f32[8,1280]{1,0:T(8,128)S(1)}, u32[]{:S(2)}, u32[]{:S(2)}) collective-permute-start(f32[8,1280]{1,0:T(8,128)S(1)} %add.251), channel_id=1, source_target_pairs={{0,2},{1,3},{2,0},{3,1},{4,6},{5,7},{6,4},{7,5},{8,10},{9,11},{10,... | collective-permute-start | bytes 122888 | tf_op jit(solution)/shard_map/ppermute | solution.py:68
  454.6 12.3 %collective-permute-start.59 = (bf16[160,1408]{1,0:T(8,128)(2,1)S(1)}, bf16[160,1408]{1,0:T(8,128)(2,1)S(1)}, u32[]{:S(2)}, u32[]{:S(2)}) collective-permute-start(bf16[160,1408]{1,0:T(8,128)(2,1)S(1)} %copy-done.35), channel_id=1, source_target_pairs={{0,4},{4,0},{8,12},{12,8},{16,20},{20,16},{24,28},{28,24},{1,5},{5... | collective-permute-start | bytes 1351688 | tf_op jit(solution)/shard_map/ppermute | solution.py:68
  455.9 13.3 %collective-permute-start.66 = (f32[9,1280]{1,0:T(8,128)S(1)}, f32[9,1280]{1,0:T(8,128)S(1)}, u32[]{:S(2)}, u32[]{:S(2)}) collective-permute-start(f32[9,1280]{1,0:T(8,128)S(1)} %select_maximum_fusion), channel_id=1, source_target_pairs={{0,4},{4,0},{8,12},{12,8},{16,20},{20,16},{24,28},{28,24},{1,5},{5... | collective-permute-start | bytes 138248 | tf_op jit(solution)/shard_map/ppermute | solution.py:68
  466.9 28.0 %collective-permute-start.56 = (bf16[160,1408]{1,0:T(8,128)(2,1)}, bf16[160,1408]{1,0:T(8,128)(2,1)}, u32[]{:S(2)}, u32[]{:S(2)}) collective-permute-start(bf16[160,1408]{1,0:T(8,128)(2,1)} %convert_add_fusion.7), channel_id=1, source_target_pairs={{0,24},{4,28},{8,16},{12,20},{16,8},{20,12},{24,0},{28,4},{1,25},{... | collective-permute-start | bytes 1351688 | tf_op jit(solution)/shard_map/ppermute | solution.py:68
  469.2 11.1 %collective-permute-start.67 = (f32[9,1280]{1,0:T(8,128)S(1)}, f32[9,1280]{1,0:T(8,128)S(1)}, u32[]{:S(2)}, u32[]{:S(2)}) collective-permute-start(f32[9,1280]{1,0:T(8,128)S(1)} %fusion.38), channel_id=1, source_target_pairs={{0,8},{4,12},{8,0},{12,4},{16,24},{20,28},{24,16},{28,20},{1,9},{5... | collective-permute-start | bytes 138248 | tf_op jit(solution)/shard_map/ppermute | solution.py:68
  472.4 22.5 %collective-permute-start.47 = (bf16[384,1280]{1,0:T(8,128)(2,1)}, bf16[384,1280]{1,0:T(8,128)(2,1)}, u32[]{:S(2)}, u32[]{:S(2)}) collective-permute-start(bf16[384,1280]{1,0:T(8,128)(2,1)} %add_convert_fusion.1), channel_id=1, source_target_pairs={{0,2},{1,3},{2,0},{3,1},{4,6},{5,7},{6,4},{7,5},{8,10},{9,11},{10,... | collective-permute-start | bytes 2949128 | tf_op jit(solution)/shard_map/ppermute | solution.py:68
  490.3 22.9 %collective-permute-start.58 = (bf16[160,1408]{1,0:T(8,128)(2,1)}, bf16[160,1408]{1,0:T(8,128)(2,1)}, u32[]{:S(2)}, u32[]{:S(2)}) collective-permute-start(bf16[160,1408]{1,0:T(8,128)(2,1)} %convert_add_fusion.6), channel_id=1, source_target_pairs={{0,8},{4,12},{8,0},{12,4},{16,24},{20,28},{24,16},{28,20},{1,9},{5... | collective-permute-start | bytes 1351688 | tf_op jit(solution)/shard_map/ppermute | solution.py:68
  520.2 13.7 %collective-permute-start.63 = (f32[3,160,160]{2,1,0:T(8,128)S(1)}, f32[3,160,160]{2,1,0:T(8,128)S(1)}, u32[]{:S(2)}, u32[]{:S(2)}) collective-permute-start(f32[3,160,160]{2,1,0:T(8,128)S(1)} %fusion.39), channel_id=1, source_target_pairs={{0,2},{1,3},{2,0},{3,1},{4,6},{5,7},{6,4},{7,5},{8,10},{9,11},{10,... | collective-permute-start | bytes 921608 | tf_op jit(solution)/shard_map/ppermute | solution.py:68
  (92 other events, 1046.7 us)
Sparse Core Ops, SparseCore 0:
  76.2 84.7 all-gather.1
  287.5 73.8 reduce-scatter.2
  365.4 81.7 reduce-scatter.4

commit v3 on v2

--- a/solution.py
+++ b/solution.py
@@ -636,25 +636,30 @@
     return weight - rate * jnp.dot(factor, update, precision=HIGHEST)
 
 
-def place_body(splits, me_ref, *refs):
+def place_body(splits, narrow, me_ref, *refs):
     slots, outs = refs[:8], refs[8:]
     rows = slots[0].shape[0]
     for mask, slot in enumerate(slots):
         start = pl.multiple_of((me_ref[0] ^ mask) * rows, rows)
         for (low, high), out in zip(splits, outs):
             out[pl.ds(start, rows), :] = slot[:, low:high]
-
-
-def place_rows(slots, splits):
+    if narrow is not None:
+        tile = narrow // LANES * LANES
+        turned = jnp.transpose(outs[0][:, tile : tile + LANES].astype(F32))
+        outs[-1][...] = turned[narrow - tile : narrow - tile + 16]
+
+
+def place_rows(slots, splits, narrow):
     rows = slots[0].shape[0]
+    shapes = [jax.ShapeDtypeStruct((8 * rows, high - low), slots[0].dtype) for low, high in splits]
+    if narrow is not None:
+        shapes.append(jax.ShapeDtypeStruct((16, 8 * rows), F32))
     return pl.pallas_call(
-        partial(place_body, splits),
+        partial(place_body, splits, narrow),
         in_specs=[pl.BlockSpec(memory_space=pltpu.SMEM)]
         + [pl.BlockSpec(memory_space=pltpu.VMEM)] * 8,
-        out_specs=[pl.BlockSpec(memory_space=pltpu.VMEM)] * len(splits),
-        out_shape=[
-            jax.ShapeDtypeStruct((8 * rows, high - low), slots[0].dtype) for low, high in splits
-        ],
+        out_specs=[pl.BlockSpec(memory_space=pltpu.VMEM)] * len(shapes),
+        out_shape=shapes,
         compiler_params=params(),
         cost_estimate=LITTLE,
         name="place_rows",
@@ -680,10 +685,13 @@
     return dp_slots(own, ordered)
 
 
-def dp_place(slots, splits):
-    if len(slots) == 1:
-        return [slots[0][:, low:high] for low, high in splits]
-    return place_rows(slots, splits)
+def dp_place(slots, splits, narrow=None):
+    if len(slots) > 1:
+        return place_rows(slots, splits, narrow)
+    parts = [slots[0][:, low:high] for low, high in splits]
+    if narrow is not None:
+        parts.append(jnp.transpose(slots[0][:, narrow : narrow + 16].astype(F32)))
+    return parts
 
 
 LINE = (4, 6, 2, 0)
@@ -792,14 +800,17 @@
     x_rows = jnp.concatenate(
         [inputs, swap(inputs, "tensor", 1), x_far, swap(x_far, "tensor", 1)], axis=0
     )
-    first_slots[-1], x_rows = tie([first_slots[-1], x_rows])
-    cot_rows = tensor_gather(cotangent)
-    wq, wo = dp_place(first_slots, ((0, packed), (packed, packed + padded)))
-    w_down_low = after(w_down.astype(BF16), *first_slots)
-    wd = lax.all_gather(w_down_low, "dp", axis=0, tiled=True)
+    cot_far = after(swap(cotangent, "tensor", 2), *first_slots[4:5])
+    cot_rows = jnp.concatenate(
+        [cotangent, swap(cotangent, "tensor", 1), cot_far, swap(cot_far, "tensor", 1)], axis=0
+    )
+    first_slots[-1], x_rows, cot_rows = tie([first_slots[-1], x_rows, cot_rows])
+    wq, wo, smalls = dp_place(
+        first_slots, ((0, packed), (packed, packed + padded)), head_width
+    )
+    wd = lax.all_gather(w_down.astype(BF16), "dp", axis=0, tiled=True)
     w_up_low = after(w_up.astype(BF16), *first_slots)
     up_slots = dp_send(w_up_low)
-    smalls = jnp.transpose(wq[:, head_width : head_width + 16].astype(F32))
     vec_rows = smalls[:8]
     bu = smalls[6:7]
     bq = smalls[7:9].reshape(2, dp_size, own_rows)[:, :, :own_bias].reshape(2, head_width)
@@ -814,17 +825,17 @@
     attn_in, qkv = qkv_call(x_rows, vec_rows, wq, qkv_bias, tok)
     up_line = up_slots[4:8:2] + up_slots[2:3] if len(up_slots) == 8 else up_slots * 3
     att, lse, *sent = attn_call(
-        heads, ("pieces",), after(qkv, up_line[0]), key_bias, wo, tok, 3 * tok
+        heads, ("pieces",), qkv, key_bias, wo, tok, 3 * tok
     )
     att, lse, part_two = attn_call(
-        heads, ("own",), after(qkv, up_line[1]), key_bias, wo, tok, 2 * tok, (att, lse)
-    )
-    total = pair_pieces(part_two, swap_all(sent, "tensor", 1))
+        heads, ("own",), after(qkv, up_line[0]), key_bias, wo, tok, 2 * tok, (att, lse)
+    )
+    total = pair_pieces(after(part_two, up_line[1]), swap_all(sent, "tensor", 1))
     far = swap(total, "tensor", 2)
     att, lse, mine, *sent = attn_call(
         heads,
         ("own", "pieces"),
-        after(qkv, total, up_line[2]),
+        after(qkv, total),
         key_bias,
         wo,
         tok,
@@ -833,7 +844,7 @@
     )
     near = swap_all(sent, "tensor", 1)
     residual, mlp_in = row_call(
-        residual_body, (inputs, mine, far), near, vec_rows, (F32, BF16), 0, "residual"
+        residual_body, (inputs, mine, after(far, up_line[2], wd, *up_slots[1:6:4])), near, vec_rows, (F32, BF16), 0, "residual"
     )
 
     near = swap(mlp_in, "tensor", 1)
@@ -859,7 +870,10 @@
     hidden_later, d_pre_later = tie([hidden, d_pre], total)
     raw_wd = mm(cot_rows, hidden_later, TN).astype(BF16)
     raw_wu = mm(jnp.concatenate(slots, axis=0), after(d_pre_later, raw_wd), TN).astype(BF16)
-    near_parts = tie(near_parts, raw_wd, raw_wu)
+    hidden = after(hidden, raw_wu)
+    down_far = mm(hidden[half:], wd, NT).astype(BF16)
+    down_mine = mm(hidden[:half], wd, NT).astype(BF16)
+    near_parts = tie(near_parts, raw_wd, raw_wu, down_far, down_mine)
     grad_wd, grad_wu = dp_scatter_plain(raw_wd), dp_scatter_plain(raw_wu)
     d_residual, d_out, sums_two = row_call(
         second_back_body,
@@ -878,30 +892,31 @@
         heads, out_mine, wo, att, qkv, key_bias, lse, block, 0
     )
     far = after(far, carried[1])
+    output_far = swap(after(pair_sum(down_far[:tok], down_far[tok:]), far), "tensor", 2)
+    output_near = swap(down_mine[tok:], "tensor", 1)
     out_far = jnp.concatenate([far, swap(far, "tensor", 1)], axis=0)
     raw_wo = (mm(out_mine, att[:half], TN) + mm(out_far, att[half:], TN)).astype(BF16)
     out_later = after(out_far, raw_wo)
     d_qkv, bias_sums = attn_back_call(
         heads, out_later, wo, att, qkv, key_bias, lse, block, half, carried
     )
-    raw_wq = mm(attn_in, d_qkv, TN).astype(BF16)
+    raw_wq = mm(attn_in, after(d_qkv, grad_wd, output_far, output_near), TN).astype(BF16)
     d_qkv, raw_wq, raw_wo = tie([d_qkv, raw_wq, raw_wo])
     raw_first = jnp.concatenate([raw_wq, raw_wo], axis=1)
     owns, crossed = dp_cross(raw_first)
     first_far = mm(d_qkv[half:], wq, NT).astype(BF16)
     far = swap(pair_sum(first_far[:tok], first_far[tok:]), "tensor", 2)
-    first_mine = mm(after(d_qkv[:half], first_far, crossed[0]), wq, NT).astype(BF16)
-    hidden = after(hidden, first_mine)
-    down_far = mm(hidden[half:], wd, NT).astype(BF16)
-    output_far = swap(pair_sum(down_far[:tok], down_far[tok:]), "tensor", 2)
-    down_mine = mm(hidden[:half], wd, NT).astype(BF16)
-    output_near = swap(down_mine[tok:], "tensor", 1)
+    lined = dp_line(owns, crossed)
+    grad_wd = after(grad_wd, first_far, *crossed[:2])
+    mom_down_new, update_down = momentum(mom_down, grad_wd.astype(F32))
+    early = polar_call(tensor_sum(gram_of(update_down)[None]))
+    new_w_down = applied(w_down, early[0], update_down, STEP_DOWN)
+    first_gate = (first_far, far, new_w_down, grad_wu, *crossed, *lined[:1])
+    first_mine = mm(after(d_qkv[:half], *first_gate), wq, NT).astype(BF16)
     quarter = tok // PIECES
     sent = [first_mine[tok + k * quarter : tok + k * quarter + quarter] for k in range(PIECES)]
     near = swap_all(sent, "tensor", 1)
-    lined = dp_line(owns, crossed)
-    grad_wd = after(grad_wd, first_mine, lined[0], far)
-    grad_wu = after(grad_wu, *lined[:2], output_far, output_near)
+    grad_wu = after(grad_wu, first_mine, lined[0])
     output = (
         residual
         + (down_mine[:tok].astype(F32) + output_near.astype(F32) + output_far.astype(F32))
@@ -934,12 +949,9 @@
         lax.dynamic_slice(rows_of, (7, dp_index * own_bias), (2, own_bias))
     )
 
-    mom_down_new, update_down = momentum(mom_down, grad_wd.astype(F32))
     mom_up_new, update_up = momentum(mom_up, grad_wu.astype(F32))
-    early = polar_call(tensor_sum(gram_of(update_down)[None]))
-    new_w_down = applied(w_down, early[0], update_down, STEP_DOWN)
     gram_up = gram_of(update_up)
-    lined = tie(lined, new_w_down, gram_up, input_grad)
+    lined = tie(lined, gram_up, input_grad)
     grad_first = dp_total(lined)
     grad_wq, grad_wo = grad_first[:, :packed], grad_first[:, packed : packed + head_width]
     mom_out_new, update_out = momentum(mom_out, grad_wo)

time: 563 us -> 537 us (0.954)
  waiting for transfers between devices: 204 us -> 166 us
  starting transfers between devices: 43.5 us -> 51.2 us
  local copies, waits for them, and re-layouts: 26.8 us -> 33 us
    ppermute x69, waiting for transfers between devices: 204 us -> 166 us  [swap(): return lax.ppermute(value, axis, [(i, i ^ mask) for i in range(size)])]
    ppermute x69, starting transfers between devices: 43.4 us -> 51.1 us  [swap(): return lax.ppermute(value, axis, [(i, i ^ mask) for i in range(size)])]
    unnamed x142 -> x155, local copies, waits for them, and re-layouts: 13.6 us -> 16.8 us
  transfers between devices with their start and end apart: 72 -> 72, of which waited for: 23 -> 23; matrix products, arithmetic and copies ran while one was open for 18% -> 19% of each run, Pallas kernels for 26% -> 27%
where the time goes in v3:
time: 537 us; the launch traced here: 533 us
  waiting for transfers between devices  166 us (31%)
  Pallas kernels  166 us (31%)
  matrix products  67.5 us (13%)
  starting transfers between devices  51.2 us (10%)
  other arithmetic  34.5 us (6%)
  local copies, waits for them, and re-layouts  33 us (6%)
  between operations  15.8 us (3%)
    ppermute x69, waiting for transfers between devices, swap(): return lax.ppermute(value, axis, [(i, i ^ mask) for i in range(size)])  166 us
    dot_general x10, matrix products, mm(): return lax.dot_general(left, right, dims, preferred_element_type=F32)  55.3 us
    ppermute x69, starting transfers between devices, swap(): return lax.ppermute(value, axis, [(i, i ^ mask) for i in range(size)])  51.1 us
    pallas_call x2, Pallas kernels, attn_back_call(): pl.pallas_call(partial(attn_back_body, heads, last_part, first), grid=(co...  46.3 us
    pallas_call x3, Pallas kernels, attn_call(): pl.pallas_call(partial(attn_body, heads, emits, len(held)), grid=(count /...  30.6 us
    pallas_call x3, Pallas kernels, mlp_call(): pl.pallas_call(partial(mlp_body, min(256, hidden_width), emits, len(held)...  30.4 us
    pallas_call x3, Pallas kernels, row_call(): pl.pallas_call(partial(row_body, body, len(rows_in)), grid=(PIECES,), in_...  17.1 us
    unnamed x155, local copies, waits for them, and re-layouts  16.8 us
  transfers between devices with their start and end apart: 72, of which 23 were waited for; matrix products, arithmetic and copies ran while one was open for 19% of the time, Pallas kernels for 27%

profile of v3, /device:TPU:0, one launch (start us, length us, event | category | flops | bytes accessed | tf_op | source)
XLA Modules:
  0.0 533.4 jit_solution(1141525611984688856)
XLA Ops:
  9.4 3.0 collective-permute-start.3
  18.4 3.7 collective-permute-start
  24.3 15.8 %collective-permute-done.refs_6_ = bf16[160,1408]{1,0:T(8,128)(2,1)S(1)} collective-permute-done((bf16[160,1408]{1,0:T(8,128)(2,1)S(1)}, bf16[160,1408]{1,0:T(8,128)(2,1)S(1)}, u32[]{:S(2)}, u32[]{:S(2)}) %collective-permute-start) | collective-permute-done | bytes 450592 | tf_op jit(solution)/shard_map/ppermute | solution.py:68
  42.1 13.9 %collective-permute-done.4.refs_2_ = bf16[160,1408]{1,0:T(8,128)(2,1)} collective-permute-done((bf16[160,1408]{1,0:T(8,128)(2,1)S(1)}, bf16[160,1408]{1,0:T(8,128)(2,1)}, u32[]{:S(2)}, u32[]{:S(2)}) %collective-permute-start.4) | collective-permute-done | bytes 450592 | tf_op jit(solution)/shard_map/ppermute | solution.py:68
  58.1 30.9 %collective-permute-done.9.refs_4_ = bf16[160,1408]{1,0:T(8,128)(2,1)} collective-permute-done((bf16[160,1408]{1,0:T(8,128)(2,1)S(1)}, bf16[160,1408]{1,0:T(8,128)(2,1)}, u32[]{:S(2)}, u32[]{:S(2)}) %collective-permute-start.9) | collective-permute-done | bytes 450592 | tf_op jit(solution)/shard_map/ppermute | solution.py:68
  90.7 5.6 %collective-permute-done.10.refs_3_ = bf16[160,1408]{1,0:T(8,128)(2,1)} collective-permute-done((bf16[160,1408]{1,0:T(8,128)(2,1)}, bf16[160,1408]{1,0:T(8,128)(2,1)}, u32[]{:S(2)}, u32[]{:S(2)}) %collective-permute-start.10) | collective-permute-done | bytes 450592 | tf_op jit(solution)/shard_map/ppermute | solution.py:68
  99.7 3.6 pad_maximum_fusion.x_ref
  103.3 3.4 pad_maximum_fusion.1
  106.7 4.4 collective-permute-done.12.refs_5_
  111.9 4.0 place_rows.2
  118.1 3.4 collective-permute-start.13
  124.1 9.7 %norm_qkv.1 = (bf16[1536,1280]{1,0:T(8,128)(2,1)}, bf16[1536,1024]{1,0:T(8,128)(2,1)}) custom-call(bf16[1536,1280]{1,0:T(8,128)(2,1)} %pad_maximum_fusion.x_ref, f32[8,1280]{1,0:T(8,128)} %slice.149.vec_ref.refs_7_.refs_8_, bf16[1280,1024]{1,0:T(8,128)(2,1)} %get-tuple-element.117.w_ref, f32[1,1024]{1,0:T(1,128)} %pad_maximum_fusion.7.bias_ref), custom_call_target="tpu_custom_call" | custom-call | flops 1000000 | bytes 100000 | tf_op jit(solution)/shard_map/norm_qkv/pallas_call | solution.py:109
  133.8 8.1 %attn_fwd.3 = (bf16[1536,384]{1,0:T(8,128)(2,1)}, f32[8,1536]{1,0:T(8,128)}, bf16[96,1280]{1,0:T(8,128)(2,1)}, bf16[96,1280]{1,0:T(8,128)(2,1)}, bf16[96,1280]{1,0:T(8,128)(2,1)}, /*index=5*/bf16[96,1280]{1,0:T(8,128)(2,1)}) custom-call(bf16[1536,1024]{1,0:T(8,128)(2,1)} %get-tuple-element.130.q_ref.qkv_ref, ...), custom_call_target="tpu_custom_call" | custom-call | flops 1000000 | bytes 100000 | tf_op jit(solution)/shard_map/attn_fwd/pallas_call | solution.py:272
  142.4 7.2 %collective-permute-done.13.refs_4_ = bf16[160,1280]{1,0:T(8,128)(2,1)S(1)} collective-permute-done((bf16[160,1280]{1,0:T(8,128)(2,1)}, bf16[160,1280]{1,0:T(8,128)(2,1)S(1)}, u32[]{:S(2)}, u32[]{:S(2)}) %collective-permute-start.13) | collective-permute-done | bytes 409632 | tf_op jit(solution)/shard_map/ppermute | solution.py:68
  149.6 8.3 %attn_fwd.4 = (bf16[1536,384]{1,0:T(8,128)(2,1)}, f32[8,1536]{1,0:T(8,128)}, bf16[384,1280]{1,0:T(8,128)(2,1)}) custom-call(bf16[1536,1024]{1,0:T(8,128)(2,1)} %get-tuple-element.130.q_ref.qkv_ref, bf16[1536,1024]{1,0:T(8,128)(2,1)} %get-tuple-element.130.q_ref.qkv_ref, ...), custom_call_target="tpu_custom_call", output_to_operand_aliasing={{0}: (4, {}), {1}: (5, {})} | custom-call | flops 1000000 | bytes 100000 | tf_op jit(solution)/shard_map/attn_fwd/pallas_call | solution.py:272
  159.5 4.1 pair_sum.2
  166.5 14.2 %attn_fwd.5 = (bf16[1536,384]{1,0:T(8,128)(2,1)}, f32[8,1536]{1,0:T(8,128)}, bf16[384,1280]{1,0:T(8,128)(2,1)}, bf16[96,1280]{1,0:T(8,128)(2,1)}, bf16[96,1280]{...) custom-call(bf16[1536,1024]{1,0:T(8,128)(2,1)} %get-tuple-element.13, ...), custom_call_target="tpu_custom_call", output_to_operand_aliasing={{0}: (4, {}), {1}: (5, {})} | custom-call | flops 1000000 | bytes 100000 | tf_op jit(solution)/shard_map/attn_fwd/pallas_call | solution.py:272
  181.4 3.4 collective-permute-done.22.refs_5_
  190.8 5.0 residual.1
  196.6 9.3 %fusion.43.refs_4_.refs_3_ = f32[1536,1280]{1,0:T(8,128)} fusion(bf16[1536,1280]{1,0:T(8,128)(2,1)S(1)} %copy-done.13, bf16[1280,1280]{1,0:T(8,128)(2,1)} %all-gather.2.cloned.1.call-done), kind=kOutput, calls=%fused_computation.122 | convolution fusion | flops 5033164800 | bytes 15073280 | tf_op jit(solution)/shard_map/dot_general | solution.py:43
  207.8 3.8 place_rows.3.refs_2_.refs_1_
  212.5 14.4 %mlp_up.3 = (bf16[1536,1280]{1,0:T(8,128)(2,1)}, bf16[1536,1280]{1,0:T(8,128)(2,1)}, f32[8,1280]{1,0:T(8,128)}, bf16[384,1280]{1,0:T(8,128)(2,1)}, bf16[96,1280]...) custom-call(bf16[384,1280]{1,0:T(8,128)(2,1)} %get-tuple-element.140.refs_0_, ...), custom_call_target="tpu_custom_call" | custom-call | flops 1000000 | bytes 100000 | tf_op jit(solution)/shard_map/mlp_up/pallas_call | solution.py:477
  230.6 8.0 %mlp_up.4 = (bf16[1536,1280]{1,0:T(8,128)(2,1)}, bf16[1536,1280]{1,0:T(8,128)(2,1)}, f32[8,1280]{1,0:T(8,128)}, bf16[96,1280]{1,0:T(8,128)(2,1)}, bf16[96,1280]{...) custom-call(bf16[384,1280]{1,0:T(8,128)(2,1)} %copy-done.34, ...), custom_call_target="tpu_custom_call", output_to_operand_aliasing={{0}: (4, {}), {1}: (5, {})} | custom-call | flops 1000000 | bytes 100000 | tf_op jit(solution)/shard_map/mlp_up/pallas_call | solution.py:477
  239.6 8.1 %mlp_up.5 = (bf16[1536,1280]{1,0:T(8,128)(2,1)}, bf16[1536,1280]{1,0:T(8,128)(2,1)}, f32[8,1280]{1,0:T(8,128)}, bf16[384,1280]{1,0:T(8,128)(2,1)}) custom-call(bf16[384,1280]{1,0:T(8,128)(2,1)} %copy-done.30, bf16[1280,1280]{1,0:T(8,128)(2,1)} %place_rows.3.refs_2_.refs_1_, ...), custom_call_target="tpu_custom_call", output_to_operand_aliasing={{0}: (4, {}), {1}: (5, {})} | custom-call | flops 1000000 | bytes 100000 | tf_op jit(solution)/shard_map/mlp_up/pallas_call | solution.py:477
  248.6 3.9 pair_sum.3
  252.5 9.1 %convolution_convert_fusion.1 = bf16[1280,1280]{1,0:T(8,128)(2,1)} fusion(bf16[1536,1280]{1,0:T(8,128)(2,1)S(1)} %copy-done.13, bf16[1536,1280]{1,0:T(8,128)(2,1)} %get-tuple-element.160), kind=kOutput, calls=%fused_computation.1 | convolution fusion | flops 5034803200 | bytes 11141120 | tf_op jit(solution)/shard_map/dot_general | solution.py:43
  264.1 9.1 %convolution_convert_fusion = bf16[1280,1280]{1,0:T(8,128)(2,1)} fusion(bf16[1536,1280]{1,0:T(8,128)(2,1)} %get-tuple-element.159, bf16[384,1280]{1,0:T(8,128)(2,1)} %copy-done.34, bf16[384,1280]{1,0:T(8,128)(2,1)S(1)} %copy-done.31, bf16[384,1280]{1,0:T(8,128)(2,1)S(1)} %copy-done.33, bf16[384,1280]{1,0:T(8,128)(2,1)S(1)} %copy-done.29), kind=kOutput, calls=%fused_computation | convolution fusion | flops 5050531840 | bytes 11141120 | tf_op jit(solution)/shard_map/dot_general | solution.py:43
  273.2 5.4 %convolution_convert_fusion.3 = bf16[768,1280]{1,0:T(8,128)(2,1)S(1)} fusion(bf16[1280,1280]{1,0:T(8,128)(2,1)} %all-gather.2.cloned.1.call-done, bf16[1536,1280]{1,0:T(8,128)(2,1)} %get-tuple-element.160), kind=kOutput, calls=%fused_computation.12 | convolution fusion | flops 2517565440 | bytes 7208960 | tf_op jit(solution)/shard_map/dot_general | solution.py:43
  278.7 2.7 convolution_convert_fusion.4
  281.5 5.4 %collective-permute-done.38.refs_2_ = bf16[384,1280]{1,0:T(8,128)(2,1)} collective-permute-done((bf16[384,1280]{1,0:T(8,128)(2,1)}, bf16[384,1280]{1,0:T(8,128)(2,1)}, u32[]{:S(2)}, u32[]{:S(2)}) %collective-permute-start.38) | collective-permute-done | bytes 983072 | tf_op jit(solution)/shard_map/ppermute | solution.py:68
  286.9 6.2 %second_back.1 = (f32[384,1280]{1,0:T(8,128)}, bf16[384,1280]{1,0:T(8,128)(2,1)}, f32[8,1280]{1,0:T(8,128)}) custom-call(f32[384,1280]{1,0:T(8,128)} %get-tuple-element.139.refs_0_, bf16[384,1280]{1,0:T(8,128)(2,1)} %get-tuple-element.144.refs_1_, bf16[384,1280]{1,0:T(8,128)(2,1)} %collective-permute-done.38.refs_2_, bf16[384,1280]{1,0:T(8,128)(2,1)} %refs_3_.1, ...), custom_call_target="tpu_custom_call" | custom-call | flops 1000000 | bytes 100000 | tf_op jit(solution)/shard_map/second_back/pallas_call | solution.py:565
  298.3 22.4 %attn_bwd.2 = (bf16[1536,1024]{1,0:T(8,128)(2,1)}, f32[8,384]{1,0:T(8,128)}, f32[1536,384]{1,0:T(8,128)}, f32[1536,384]{1,0:T(8,128)}) custom-call(bf16[768,1280]{1,0:T(8,128)(2,1)} %copy-done.10, bf16[1280,384]{1,0:T(8,128)(2,1)} %get-tuple-element.121.wo_ref, bf16[1536,384]{1,0:T(8,128)(2,1)} %get-tuple-element.170.att_ref, ...), custom_call_target="tpu_custom_call" | custom-call | flops 1000000 | bytes 100000 | tf_op jit(solution)/shard_map/attn_bwd/pallas_call | solution.py:405
  333.0 23.8 %attn_bwd.3 = (bf16[1536,1024]{1,0:T(8,128)(2,1)}, f32[8,384]{1,0:T(8,128)}) custom-call(bf16[768,1280]{1,0:T(8,128)(2,1)} %copy-done.12, bf16[1280,384]{1,0:T(8,128)(2,1)} %get-tuple-element.121.wo_ref, bf16[1536,384]{1,0:T(8,128)(2,1)} %get-tuple-element.170.att_ref, ...), custom_call_target="tpu_custom_call", output_to_operand_aliasing={{0}: (10, {})} | custom-call | flops 1000000 | bytes 100000 | tf_op jit(solution)/shard_map/attn_bwd/pallas_call | solution.py:405
  356.9 7.8 %convolution_convert_fusion.2 = bf16[1280,1024]{1,0:T(8,128)(2,1)S(1)} fusion(bf16[1536,1280]{1,0:T(8,128)(2,1)} %get-tuple-element.180, bf16[1536,1024]{1,0:T(8,128)(2,1)} %get-tuple-element.182), kind=kOutput, calls=%fused_computation.11 | convolution fusion | flops 4027842560 | bytes 9699328 | tf_op jit(solution)/shard_map/dot_general | solution.py:43
  371.0 14.7 %collective-permute-done.49 = bf16[160,1408]{1,0:T(8,128)(2,1)} collective-permute-done((bf16[160,1408]{1,0:T(8,128)(2,1)}, bf16[160,1408]{1,0:T(8,128)(2,1)}, u32[]{:S(2)}, u32[]{:S(2)}) %collective-permute-start.49) | collective-permute-done | bytes 450592 | tf_op jit(solution)/shard_map/ppermute | solution.py:68
  389.4 4.0 convolution_convert_fusion.6
  393.6 9.1 %collective-permute-done.50 = bf16[160,1408]{1,0:T(8,128)(2,1)S(1)} collective-permute-done((bf16[160,1408]{1,0:T(8,128)(2,1)S(1)}, bf16[160,1408]{1,0:T(8,128)(2,1)S(1)}, u32[]{:S(2)}, u32[]{:S(2)}) %collective-permute-start.50) | collective-permute-done | bytes 450592 | tf_op jit(solution)/shard_map/ppermute | solution.py:68
  409.7 12.1 %collective-permute-done.53 = bf16[160,1408]{1,0:T(8,128)(2,1)S(1)} collective-permute-done((bf16[160,1408]{1,0:T(8,128)(2,1)S(1)}, bf16[160,1408]{1,0:T(8,128)(2,1)S(1)}, u32[]{:S(2)}, u32[]{:S(2)}) %collective-permute-start.53) | collective-permute-done | bytes 450592 | tf_op jit(solution)/shard_map/ppermute | solution.py:68
  431.6 3.5 collective-permute-done.52
  435.9 7.0 %polar.2 = f32[1,160,160]{2,1,0:T(8,128)} custom-call(f32[1,160,160]{2,1,0:T(8,128)} %add.228.gram_ref), custom_call_target="tpu_custom_call" | custom-call | tf_op jit(solution)/shard_map/polar/pallas_call | solution.py:618
  448.6 12.6 %collective-permute-done.55 = bf16[160,1408]{1,0:T(8,128)(2,1)} collective-permute-done((bf16[160,1408]{1,0:T(8,128)(2,1)}, bf16[160,1408]{1,0:T(8,128)(2,1)}, u32[]{:S(2)}, u32[]{:S(2)}) %collective-permute-start.55) | collective-permute-done | bytes 450592 | tf_op jit(solution)/shard_map/ppermute | solution.py:68
  461.2 4.5 convolution_convert_fusion.5
  470.6 6.0 %first_back.1 = (f32[384,1280]{1,0:T(8,128)}, f32[8,1280]{1,0:T(8,128)}) custom-call(bf16[384,1280]{1,0:T(8,128)(2,1)} %refs_0_.3, bf16[384,1280]{1,0:T(8,128)(2,1)} %slice.203.refs_1_, bf16[384,1280]{1,0:T(8,128)(2,1)} %collective-permute-done.48.refs_2_, f32[384,1280]{1,0:T(8,128)} %get-tuple-element.187.refs_3_, bf16[96,1280]{1,0:T(8,128)(2,1)} %copy-done.53, ...), custom_call_target="tpu_custom_call" | custom-call | flops 1000000 | bytes 100000 | tf_op jit(solution)/shard_map/first_back/pallas_call | solution.py:565
  485.1 3.7 collective-permute-done.66
  489.0 4.3 collective-permute-done.67
  493.8 3.0 add_add_fusion
  501.9 7.4 %collective-permute-done.63 = f32[3,160,160]{2,1,0:T(8,128)S(1)} collective-permute-done((f32[3,160,160]{2,1,0:T(8,128)S(1)}, f32[3,160,160]{2,1,0:T(8,128)S(1)}, u32[]{:S(2)}, u32[]{:S(2)}) %collective-permute-start.63) | collective-permute-done | bytes 307232 | tf_op jit(solution)/shard_map/ppermute | solution.py:68
  510.2 8.9 %polar.3 = f32[3,160,160]{2,1,0:T(8,128)} custom-call(f32[3,160,160]{2,1,0:T(8,128)} %fusion.58.gram_ref), custom_call_target="tpu_custom_call" | custom-call | tf_op jit(solution)/shard_map/polar/pallas_call | solution.py:618
  (372 shorter events, 125.8 us)
Async XLA Ops:
  7.2 181.6 %all-gather.2.cloned.1.call-start = ((), (), s32[]{:S(2)}) async-start(), calls=%async_computation.2 | async-start | bytes 3686400 | tf_op jit(solution)/shard_map/all_gather | solution.py:811
  9.4 347.5 %reduce-scatter.3.cloned.1.call-start = ((), (), s32[]{:S(2)}) async-start(), calls=%async_computation.3 | async-start | bytes 3686400 | tf_op jit(solution)/shard_map/reduce_scatter | solution.py:732
  9.4 48.1 %collective-permute-start.3 = (bf16[384,1280]{1,0:T(8,128)(2,1)}, bf16[384,1280]{1,0:T(8,128)(2,1)}, u32[]{:S(2)}, u32[]{:S(2)}) collective-permute-start(bf16[384,1280]{1,0:T(8,128)(2,1)} %refs_0_.3), channel_id=1, source_target_pairs={{0,2},{1,3},{2,0},{3,1},{4,6},{5,7},{6,4},{7,5},{8,10},{9,11},{10,... | collective-permute-start | bytes 2949128 | tf_op jit(solution)/shard_map/ppermute | solution.py:68
  18.4 21.8 %collective-permute-start = (bf16[160,1408]{1,0:T(8,128)(2,1)S(1)}, bf16[160,1408]{1,0:T(8,128)(2,1)S(1)}, u32[]{:S(2)}, u32[]{:S(2)}) collective-permute-start(bf16[160,1408]{1,0:T(8,128)(2,1)S(1)} %concatenate.52.refs_0_), channel_id=1, source_target_pairs={{0,24},{4,28},{8,16},{12,20},{16,8},{20,12},{24,0},{28,4},{1,25},{... | collective-permute-start | bytes 1351688 | tf_op jit(solution)/shard_map/ppermute | solution.py:68
  22.1 33.9 %collective-permute-start.4 = (bf16[160,1408]{1,0:T(8,128)(2,1)S(1)}, bf16[160,1408]{1,0:T(8,128)(2,1)}, u32[]{:S(2)}, u32[]{:S(2)}) collective-permute-start(bf16[160,1408]{1,0:T(8,128)(2,1)S(1)} %concatenate.52.refs_0_), channel_id=1, source_target_pairs={{0,8},{4,12},{8,0},{12,4},{16,24},{20,28},{24,16},{28,20},{1,9},{5... | collective-permute-start | bytes 1351688 | tf_op jit(solution)/shard_map/ppermute | solution.py:68
  22.1 34.0 %collective-permute-start.5 = (bf16[160,1408]{1,0:T(8,128)(2,1)S(1)}, bf16[160,1408]{1,0:T(8,128)(2,1)}, u32[]{:S(2)}, u32[]{:S(2)}) collective-permute-start(bf16[160,1408]{1,0:T(8,128)(2,1)S(1)} %concatenate.52.refs_0_), channel_id=1, source_target_pairs={{0,4},{4,0},{8,12},{12,8},{16,20},{20,16},{24,28},{28,24},{1,5},{5... | collective-permute-start | bytes 1351688 | tf_op jit(solution)/shard_map/ppermute | solution.py:68
  23.6 65.5 %collective-permute-start.9 = (bf16[160,1408]{1,0:T(8,128)(2,1)S(1)}, bf16[160,1408]{1,0:T(8,128)(2,1)}, u32[]{:S(2)}, u32[]{:S(2)}) collective-permute-start(bf16[160,1408]{1,0:T(8,128)(2,1)S(1)} %concatenate.52.refs_0_), channel_id=1, source_target_pairs={{0,16},{4,20},{8,24},{12,28},{16,0},{20,4},{24,8},{28,12},{1,17},{... | collective-permute-start | bytes 1351688 | tf_op jit(solution)/shard_map/ppermute | solution.py:68
  41.0 55.3 %collective-permute-start.8 = (bf16[384,1280]{1,0:T(8,128)(2,1)S(1)}, bf16[384,1280]{1,0:T(8,128)(2,1)}, u32[]{:S(2)}, u32[]{:S(2)}) collective-permute-start(bf16[384,1280]{1,0:T(8,128)(2,1)S(1)} %copy-done.14), channel_id=1, source_target_pairs={{0,2},{1,3},{2,0},{3,1},{4,6},{5,7},{6,4},{7,5},{8,10},{9,11},{10,... | collective-permute-start | bytes 2949128 | tf_op jit(solution)/shard_map/ppermute | solution.py:68
  56.0 43.7 %collective-permute-start.2 = (bf16[384,1280]{1,0:T(8,128)(2,1)S(1)}, bf16[384,1280]{1,0:T(8,128)(2,1)}, u32[]{:S(2)}, u32[]{:S(2)}) collective-permute-start(bf16[384,1280]{1,0:T(8,128)(2,1)S(1)} %copy-done.4), channel_id=1, source_target_pairs={{0,1},{1,0},{2,3},{3,2},{4,5},{5,4},{6,7},{7,6},{8,9},{9,8},{10,11... | collective-permute-start | bytes 2949128 | tf_op jit(solution)/shard_map/ppermute | solution.py:68
  56.0 34.1 %collective-permute-start.1 = (bf16[160,1408]{1,0:T(8,128)(2,1)}, bf16[160,1408]{1,0:T(8,128)(2,1)}, u32[]{:S(2)}, u32[]{:S(2)}) collective-permute-start(bf16[160,1408]{1,0:T(8,128)(2,1)} %copy-done.42), channel_id=1, source_target_pairs={{0,4},{4,0},{8,12},{12,8},{16,20},{20,16},{24,28},{28,24},{1,5},{5... | collective-permute-start | bytes 1351688 | tf_op jit(solution)/shard_map/ppermute | solution.py:68
  57.6 38.7 %collective-permute-start.10 = (bf16[160,1408]{1,0:T(8,128)(2,1)}, bf16[160,1408]{1,0:T(8,128)(2,1)}, u32[]{:S(2)}, u32[]{:S(2)}) collective-permute-start(bf16[160,1408]{1,0:T(8,128)(2,1)} %collective-permute-done.4.refs_2_), channel_id=1, source_target_pairs={{0,4},{4,0},{8,12},{12,8},{16,20},{20,16},{24,28},{28,24},{1,5},{5... | collective-permute-start | bytes 1351688 | tf_op jit(solution)/shard_map/ppermute | solution.py:68
  89.0 10.7 %collective-permute-start.6 = (bf16[384,1280]{1,0:T(8,128)(2,1)}, bf16[384,1280]{1,0:T(8,128)(2,1)}, u32[]{:S(2)}, u32[]{:S(2)}) collective-permute-start(bf16[384,1280]{1,0:T(8,128)(2,1)} %collective-permute-done.3), channel_id=1, source_target_pairs={{0,1},{1,0},{2,3},{3,2},{4,5},{5,4},{6,7},{7,6},{8,9},{9,8},{10,11... | collective-permute-start | bytes 2949128 | tf_op jit(solution)/shard_map/ppermute | solution.py:68
  90.2 13.1 %collective-permute-start.7 = (bf16[384,1280]{1,0:T(8,128)(2,1)S(1)}, bf16[384,1280]{1,0:T(8,128)(2,1)}, u32[]{:S(2)}, u32[]{:S(2)}) collective-permute-start(bf16[384,1280]{1,0:T(8,128)(2,1)S(1)} %copy-done.14), channel_id=1, source_target_pairs={{0,1},{1,0},{2,3},{3,2},{4,5},{5,4},{6,7},{7,6},{8,9},{9,8},{10,11... | collective-permute-start | bytes 2949128 | tf_op jit(solution)/shard_map/ppermute | solution.py:68
  98.1 13.0 %collective-permute-start.12 = (bf16[160,1408]{1,0:T(8,128)(2,1)}, bf16[160,1408]{1,0:T(8,128)(2,1)S(1)}, u32[]{:S(2)}, u32[]{:S(2)}) collective-permute-start(bf16[160,1408]{1,0:T(8,128)(2,1)} %collective-permute-done.9.refs_4_), channel_id=1, source_target_pairs={{0,4},{4,0},{8,12},{12,8},{16,20},{20,16},{24,28},{28,24},{1,5},{5... | collective-permute-start | bytes 1351688 | tf_op jit(solution)/shard_map/ppermute | solution.py:68
  118.1 31.5 %collective-permute-start.13 = (bf16[160,1280]{1,0:T(8,128)(2,1)}, bf16[160,1280]{1,0:T(8,128)(2,1)S(1)}, u32[]{:S(2)}, u32[]{:S(2)}) collective-permute-start(bf16[160,1280]{1,0:T(8,128)(2,1)} %convert_element_type.133.refs_0_), channel_id=1, source_target_pairs={{0,16},{4,20},{8,24},{12,28},{16,0},{20,4},{24,8},{28,12},{1,17},{... | collective-permute-start | bytes 1228808 | tf_op jit(solution)/shard_map/ppermute | solution.py:68
  121.5 36.4 %collective-permute-start.14 = (bf16[160,1280]{1,0:T(8,128)(2,1)}, bf16[160,1280]{1,0:T(8,128)(2,1)}, u32[]{:S(2)}, u32[]{:S(2)}) collective-permute-start(bf16[160,1280]{1,0:T(8,128)(2,1)} %convert_element_type.133.refs_0_), channel_id=1, source_target_pairs={{0,24},{4,28},{8,16},{12,20},{16,8},{20,12},{24,0},{28,4},{1,25},{... | collective-permute-start | bytes 1228808 | tf_op jit(solution)/shard_map/ppermute | solution.py:68
  141.9 16.1 %collective-permute-start.15 = (bf16[96,1280]{1,0:T(8,128)(2,1)}, bf16[96,1280]{1,0:T(8,128)(2,1)S(1)}, u32[]{:S(2)}, u32[]{:S(2)}) collective-permute-start(bf16[96,1280]{1,0:T(8,128)(2,1)} %get-tuple-element.126), channel_id=1, source_target_pairs={{0,1},{1,0},{2,3},{3,2},{4,5},{5,4},{6,7},{7,6},{8,9},{9,8},{10,11... | collective-permute-start | bytes 737288 | tf_op jit(solution)/shard_map/ppermute | solution.py:68
  141.9 16.1 %collective-permute-start.16 = (bf16[96,1280]{1,0:T(8,128)(2,1)}, bf16[96,1280]{1,0:T(8,128)(2,1)S(1)}, u32[]{:S(2)}, u32[]{:S(2)}) collective-permute-start(bf16[96,1280]{1,0:T(8,128)(2,1)} %get-tuple-element.127), channel_id=1, source_target_pairs={{0,1},{1,0},{2,3},{3,2},{4,5},{5,4},{6,7},{7,6},{8,9},{9,8},{10,11... | collective-permute-start | bytes 737288 | tf_op jit(solution)/shard_map/ppermute | solution.py:68
  142.4 15.6 %collective-permute-start.17 = (bf16[96,1280]{1,0:T(8,128)(2,1)}, bf16[96,1280]{1,0:T(8,128)(2,1)S(1)}, u32[]{:S(2)}, u32[]{:S(2)}) collective-permute-start(bf16[96,1280]{1,0:T(8,128)(2,1)} %get-tuple-element.128), channel_id=1, source_target_pairs={{0,1},{1,0},{2,3},{3,2},{4,5},{5,4},{6,7},{7,6},{8,9},{9,8},{10,11... | collective-permute-start | bytes 737288 | tf_op jit(solution)/shard_map/ppermute | solution.py:68
  163.6 24.2 %collective-permute-start.19 = (bf16[384,1280]{1,0:T(8,128)(2,1)}, bf16[384,1280]{1,0:T(8,128)(2,1)S(1)}, u32[]{:S(2)}, u32[]{:S(2)}) collective-permute-start(bf16[384,1280]{1,0:T(8,128)(2,1)} %pair_sum.2), channel_id=1, source_target_pairs={{0,2},{1,3},{2,0},{3,1},{4,6},{5,7},{6,4},{7,5},{8,10},{9,11},{10,... | collective-permute-start | bytes 2949128 | tf_op jit(solution)/shard_map/ppermute | solution.py:68
  164.4 16.4 %collective-permute-start.20 = (bf16[160,1280]{1,0:T(8,128)(2,1)}, bf16[160,1280]{1,0:T(8,128)(2,1)}, u32[]{:S(2)}, u32[]{:S(2)}) collective-permute-start(bf16[160,1280]{1,0:T(8,128)(2,1)} %convert_element_type.133.refs_0_), channel_id=1, source_target_pairs={{0,8},{4,12},{8,0},{12,4},{16,24},{20,28},{24,16},{28,20},{1,9},{5... | collective-permute-start | bytes 1228808 | tf_op jit(solution)/shard_map/ppermute | solution.py:68
  164.5 16.8 %collective-permute-start.21 = (bf16[160,1280]{1,0:T(8,128)(2,1)}, bf16[160,1280]{1,0:T(8,128)(2,1)S(1)}, u32[]{:S(2)}, u32[]{:S(2)}) collective-permute-start(bf16[160,1280]{1,0:T(8,128)(2,1)} %convert_element_type.133.refs_0_), channel_id=1, source_target_pairs={{0,4},{4,0},{8,12},{12,8},{16,20},{20,16},{24,28},{28,24},{1,5},{5... | collective-permute-start | bytes 1228808 | tf_op jit(solution)/shard_map/ppermute | solution.py:68
  165.9 18.9 %collective-permute-start.22 = (bf16[160,1280]{1,0:T(8,128)(2,1)S(1)}, bf16[160,1280]{1,0:T(8,128)(2,1)S(1)}, u32[]{:S(2)}, u32[]{:S(2)}) collective-permute-start(bf16[160,1280]{1,0:T(8,128)(2,1)S(1)} %collective-permute-done.13.refs_4_), channel_id=1, source_target_pairs={{0,4},{4,0},{8,12},{12,8},{16,20},{20,16},{24,28},{28,24},{1,5},{5... | collective-permute-start | bytes 1228808 | tf_op jit(solution)/shard_map/ppermute | solution.py:68
  187.8 20.0 %collective-permute-start.29 = (bf16[160,1280]{1,0:T(8,128)(2,1)}, bf16[160,1280]{1,0:T(8,128)(2,1)}, u32[]{:S(2)}, u32[]{:S(2)}) collective-permute-start(bf16[160,1280]{1,0:T(8,128)(2,1)} %collective-permute-done.20.refs_2_), channel_id=1, source_target_pairs={{0,4},{4,0},{8,12},{12,8},{16,20},{20,16},{24,28},{28,24},{1,5},{5... | collective-permute-start | bytes 1228808 | tf_op jit(solution)/shard_map/ppermute | solution.py:68
  188.9 18.9 %collective-permute-start.30 = (bf16[160,1280]{1,0:T(8,128)(2,1)}, bf16[160,1280]{1,0:T(8,128)(2,1)}, u32[]{:S(2)}, u32[]{:S(2)}) collective-permute-start(bf16[160,1280]{1,0:T(8,128)(2,1)} %collective-permute-done.14.refs_6_), channel_id=1, source_target_pairs={{0,4},{4,0},{8,12},{12,8},{16,20},{20,16},{24,28},{28,24},{1,5},{5... | collective-permute-start | bytes 1228808 | tf_op jit(solution)/shard_map/ppermute | solution.py:68
  195.8 31.2 %collective-permute-start.27 = (bf16[384,1280]{1,0:T(8,128)(2,1)}, bf16[384,1280]{1,0:T(8,128)(2,1)S(1)}, u32[]{:S(2)}, u32[]{:S(2)}) collective-permute-start(bf16[384,1280]{1,0:T(8,128)(2,1)} %get-tuple-element.140.refs_0_), channel_id=1, source_target_pairs={{0,2},{1,3},{2,0},{3,1},{4,6},{5,7},{6,4},{7,5},{8,10},{9,11},{10,... | collective-permute-start | bytes 2949128 | tf_op jit(solution)/shard_map/ppermute | solution.py:68
  196.6 15.0 %collective-permute-start.28 = (bf16[384,1280]{1,0:T(8,128)(2,1)}, bf16[384,1280]{1,0:T(8,128)(2,1)S(1)}, u32[]{:S(2)}, u32[]{:S(2)}) collective-permute-start(bf16[384,1280]{1,0:T(8,128)(2,1)} %get-tuple-element.140.refs_0_), channel_id=1, source_target_pairs={{0,1},{1,0},{2,3},{3,2},{4,5},{5,4},{6,7},{7,6},{8,9},{9,8},{10,11... | collective-permute-start | bytes 2949128 | tf_op jit(solution)/shard_map/ppermute | solution.py:68
  261.7 186.9 %reduce-scatter.5.cloned.1.call-start = ((), (), s32[]{:S(2)}) async-start(), calls=%async_computation.4 | async-start | bytes 3686400 | tf_op jit(solution)/shard_map/reduce_scatter | solution.py:732
  261.7 19.7 %collective-permute-start.39 = (bf16[96,1280]{1,0:T(8,128)(2,1)}, bf16[96,1280]{1,0:T(8,128)(2,1)S(1)}, u32[]{:S(2)}, u32[]{:S(2)}) collective-permute-start(bf16[96,1280]{1,0:T(8,128)(2,1)} %get-tuple-element.161), channel_id=1, source_target_pairs={{0,1},{1,0},{2,3},{3,2},{4,5},{5,4},{6,7},{7,6},{8,9},{9,8},{10,11... | collective-permute-start | bytes 737288 | tf_op jit(solution)/shard_map/ppermute | solution.py:68
  261.9 19.6 %collective-permute-start.40 = (bf16[96,1280]{1,0:T(8,128)(2,1)}, bf16[96,1280]{1,0:T(8,128)(2,1)S(1)}, u32[]{:S(2)}, u32[]{:S(2)}) collective-permute-start(bf16[96,1280]{1,0:T(8,128)(2,1)} %get-tuple-element.162), channel_id=1, source_target_pairs={{0,1},{1,0},{2,3},{3,2},{4,5},{5,4},{6,7},{7,6},{8,9},{9,8},{10,11... | collective-permute-start | bytes 737288 | tf_op jit(solution)/shard_map/ppermute | solution.py:68
  262.3 19.2 %collective-permute-start.41 = (bf16[96,1280]{1,0:T(8,128)(2,1)}, bf16[96,1280]{1,0:T(8,128)(2,1)}, u32[]{:S(2)}, u32[]{:S(2)}) collective-permute-start(bf16[96,1280]{1,0:T(8,128)(2,1)} %get-tuple-element.163), channel_id=1, source_target_pairs={{0,1},{1,0},{2,3},{3,2},{4,5},{5,4},{6,7},{7,6},{8,9},{9,8},{10,11... | collective-permute-start | bytes 737288 | tf_op jit(solution)/shard_map/ppermute | solution.py:68
  262.4 19.1 %collective-permute-start.42 = (bf16[96,1280]{1,0:T(8,128)(2,1)}, bf16[96,1280]{1,0:T(8,128)(2,1)}, u32[]{:S(2)}, u32[]{:S(2)}) collective-permute-start(bf16[96,1280]{1,0:T(8,128)(2,1)} %get-tuple-element.164), channel_id=1, source_target_pairs={{0,1},{1,0},{2,3},{3,2},{4,5},{5,4},{6,7},{7,6},{8,9},{9,8},{10,11... | collective-permute-start | bytes 737288 | tf_op jit(solution)/shard_map/ppermute | solution.py:68
  262.8 24.1 %collective-permute-start.38 = (bf16[384,1280]{1,0:T(8,128)(2,1)}, bf16[384,1280]{1,0:T(8,128)(2,1)}, u32[]{:S(2)}, u32[]{:S(2)}) collective-permute-start(bf16[384,1280]{1,0:T(8,128)(2,1)} %pair_sum.3), channel_id=1, source_target_pairs={{0,2},{1,3},{2,0},{3,1},{4,6},{5,7},{6,4},{7,5},{8,10},{9,11},{10,... | collective-permute-start | bytes 2949128 | tf_op jit(solution)/shard_map/ppermute | solution.py:68
  293.1 27.6 %collective-permute-start.43 = (bf16[384,1280]{1,0:T(8,128)(2,1)}, bf16[384,1280]{1,0:T(8,128)(2,1)}, u32[]{:S(2)}, u32[]{:S(2)}) collective-permute-start(bf16[384,1280]{1,0:T(8,128)(2,1)} %get-tuple-element.169), channel_id=1, source_target_pairs={{0,2},{1,3},{2,0},{3,1},{4,6},{5,7},{6,4},{7,5},{8,10},{9,11},{10,... | collective-permute-start | bytes 2949128 | tf_op jit(solution)/shard_map/ppermute | solution.py:68
  295.5 27.0 %collective-permute-start.37 = (bf16[384,1280]{1,0:T(8,128)(2,1)}, bf16[384,1280]{1,0:T(8,128)(2,1)}, u32[]{:S(2)}, u32[]{:S(2)}) collective-permute-start(bf16[384,1280]{1,0:T(8,128)(2,1)} %slice.200), channel_id=1, source_target_pairs={{0,1},{1,0},{2,3},{3,2},{4,5},{5,4},{6,7},{7,6},{8,9},{9,8},{10,11... | collective-permute-start | bytes 2949128 | tf_op jit(solution)/shard_map/ppermute | solution.py:68
  322.2 34.7 %collective-permute-start.36 = (bf16[384,1280]{1,0:T(8,128)(2,1)}, bf16[384,1280]{1,0:T(8,128)(2,1)S(1)}, u32[]{:S(2)}, u32[]{:S(2)}) collective-permute-start(bf16[384,1280]{1,0:T(8,128)(2,1)} %slice.198), channel_id=1, source_target_pairs={{0,1},{1,0},{2,3},{3,2},{4,5},{5,4},{6,7},{7,6},{8,9},{9,8},{10,11... | collective-permute-start | bytes 2949128 | tf_op jit(solution)/shard_map/ppermute | solution.py:68
  325.2 31.7 %collective-permute-start.45 = (bf16[384,1280]{1,0:T(8,128)(2,1)S(1)}, bf16[384,1280]{1,0:T(8,128)(2,1)}, u32[]{:S(2)}, u32[]{:S(2)}) collective-permute-start(bf16[384,1280]{1,0:T(8,128)(2,1)S(1)} %add_convert_fusion.1), channel_id=1, source_target_pairs={{0,2},{1,3},{2,0},{3,1},{4,6},{5,7},{6,4},{7,5},{8,10},{9,11},{10,... | collective-permute-start | bytes 2949128 | tf_op jit(solution)/shard_map/ppermute | solution.py:68
  368.8 16.9 %collective-permute-start.49 = (bf16[160,1408]{1,0:T(8,128)(2,1)}, bf16[160,1408]{1,0:T(8,128)(2,1)}, u32[]{:S(2)}, u32[]{:S(2)}) collective-permute-start(bf16[160,1408]{1,0:T(8,128)(2,1)} %constant_dynamic-slice_fusion.3), channel_id=1, source_target_pairs={{0,4},{4,0},{8,12},{12,8},{16,20},{20,16},{24,28},{28,24},{1,5},{5... | collective-permute-start | bytes 1351688 | tf_op jit(solution)/shard_map/ppermute | solution.py:68
  387.8 14.8 %collective-permute-start.50 = (bf16[160,1408]{1,0:T(8,128)(2,1)S(1)}, bf16[160,1408]{1,0:T(8,128)(2,1)S(1)}, u32[]{:S(2)}, u32[]{:S(2)}) collective-permute-start(bf16[160,1408]{1,0:T(8,128)(2,1)S(1)} %get-tuple-element.217), channel_id=1, source_target_pairs={{0,4},{4,0},{8,12},{12,8},{16,20},{20,16},{24,28},{28,24},{1,5},{5... | collective-permute-start | bytes 1351688 | tf_op jit(solution)/shard_map/ppermute | solution.py:68
  393.5 12.9 %collective-permute-start.47 = (bf16[384,1280]{1,0:T(8,128)(2,1)S(1)}, bf16[384,1280]{1,0:T(8,128)(2,1)S(1)}, u32[]{:S(2)}, u32[]{:S(2)}) collective-permute-start(bf16[384,1280]{1,0:T(8,128)(2,1)S(1)} %slice.202), channel_id=1, source_target_pairs={{0,1},{1,0},{2,3},{3,2},{4,5},{5,4},{6,7},{7,6},{8,9},{9,8},{10,11... | collective-permute-start | bytes 2949128 | tf_op jit(solution)/shard_map/ppermute | solution.py:68
  404.7 17.1 %collective-permute-start.53 = (bf16[160,1408]{1,0:T(8,128)(2,1)S(1)}, bf16[160,1408]{1,0:T(8,128)(2,1)S(1)}, u32[]{:S(2)}, u32[]{:S(2)}) collective-permute-start(bf16[160,1408]{1,0:T(8,128)(2,1)S(1)} %get-tuple-element.215), channel_id=1, source_target_pairs={{0,4},{4,0},{8,12},{12,8},{16,20},{20,16},{24,28},{28,24},{1,5},{5... | collective-permute-start | bytes 1351688 | tf_op jit(solution)/shard_map/ppermute | solution.py:68
  407.6 53.6 %collective-permute-start.48 = (bf16[384,1280]{1,0:T(8,128)(2,1)}, bf16[384,1280]{1,0:T(8,128)(2,1)}, u32[]{:S(2)}, u32[]{:S(2)}) collective-permute-start(bf16[384,1280]{1,0:T(8,128)(2,1)} %add_convert_fusion), channel_id=1, source_target_pairs={{0,2},{1,3},{2,0},{3,1},{4,6},{5,7},{6,4},{7,5},{8,10},{9,11},{10,... | collective-permute-start | bytes 2949128 | tf_op jit(solution)/shard_map/ppermute | solution.py:68
  408.3 26.8 %collective-permute-start.52 = (f32[1,160,160]{2,1,0:T(8,128)S(1)}, f32[1,160,160]{2,1,0:T(8,128)S(1)}, u32[]{:S(2)}, u32[]{:S(2)}) collective-permute-start(f32[1,160,160]{2,1,0:T(8,128)S(1)} %add.227), channel_id=1, source_target_pairs={{0,2},{1,3},{2,0},{3,1},{4,6},{5,7},{6,4},{7,5},{8,10},{9,11},{10,... | collective-permute-start | bytes 307208 | tf_op jit(solution)/shard_map/ppermute | solution.py:68
  422.8 24.6 %collective-permute-start.54 = (bf16[160,1408]{1,0:T(8,128)(2,1)}, bf16[160,1408]{1,0:T(8,128)(2,1)}, u32[]{:S(2)}, u32[]{:S(2)}) collective-permute-start(bf16[160,1408]{1,0:T(8,128)(2,1)} %get-tuple-element.213), channel_id=1, source_target_pairs={{0,4},{4,0},{8,12},{12,8},{16,20},{20,16},{24,28},{28,24},{1,5},{5... | collective-permute-start | bytes 1351688 | tf_op jit(solution)/shard_map/ppermute | solution.py:68
  427.4 33.8 %collective-permute-start.55 = (bf16[160,1408]{1,0:T(8,128)(2,1)}, bf16[160,1408]{1,0:T(8,128)(2,1)}, u32[]{:S(2)}, u32[]{:S(2)}) collective-permute-start(bf16[160,1408]{1,0:T(8,128)(2,1)} %get-tuple-element.216), channel_id=1, source_target_pairs={{0,16},{4,20},{8,24},{12,28},{16,0},{20,4},{24,8},{28,12},{1,17},{... | collective-permute-start | bytes 1351688 | tf_op jit(solution)/shard_map/ppermute | solution.py:68
  429.6 46.9 %collective-permute-start.60 = (bf16[160,1408]{1,0:T(8,128)(2,1)}, bf16[160,1408]{1,0:T(8,128)(2,1)}, u32[]{:S(2)}, u32[]{:S(2)}) collective-permute-start(bf16[160,1408]{1,0:T(8,128)(2,1)} %get-tuple-element.214), channel_id=1, source_target_pairs={{0,24},{4,28},{8,16},{12,20},{16,8},{20,12},{24,0},{28,4},{1,25},{... | collective-permute-start | bytes 1351688 | tf_op jit(solution)/shard_map/ppermute | solution.py:68
  445.5 31.0 %collective-permute-start.61 = (bf16[160,1408]{1,0:T(8,128)(2,1)}, bf16[160,1408]{1,0:T(8,128)(2,1)S(1)}, u32[]{:S(2)}, u32[]{:S(2)}) collective-permute-start(bf16[160,1408]{1,0:T(8,128)(2,1)} %get-tuple-element.212), channel_id=1, source_target_pairs={{0,8},{4,12},{8,0},{12,4},{16,24},{20,28},{24,16},{28,20},{1,9},{5... | collective-permute-start | bytes 1351688 | tf_op jit(solution)/shard_map/ppermute | solution.py:68
  488.9 10.8 %collective-permute-start.62 = (f32[3,160,160]{2,1,0:T(8,128)S(1)}, f32[3,160,160]{2,1,0:T(8,128)S(1)}, u32[]{:S(2)}, u32[]{:S(2)}) collective-permute-start(f32[3,160,160]{2,1,0:T(8,128)S(1)} %pad_maximum_fusion.4), channel_id=1, source_target_pairs={{0,1},{1,0},{2,3},{3,2},{4,5},{5,4},{6,7},{7,6},{8,9},{9,8},{10,11... | collective-permute-start | bytes 921608 | tf_op jit(solution)/shard_map/ppermute | solution.py:68
  (100 other events, 1008.0 us)
Sparse Core Ops, SparseCore 0:
  10.8 97.8 all-gather.1
  261.8 75.5 reduce-scatter.2
  341.5 87.6 reduce-scatter.4

commit v4 on v3

--- a/solution.py
+++ b/solution.py
@@ -160,23 +160,17 @@
 
 def pair_body(own_ref, *rest):
     pieces, out_ref = rest[:-1], rest[-1]
+    rows = pieces[0].shape[0]
     for index, piece in enumerate(pieces):
-
-        @pl.when(pl.program_id(0) == index)
-        def _():
-            out_ref[...] = (own_ref[...].astype(F32) + piece[...].astype(F32)).astype(BF16)
+        part = slice(index * rows, index * rows + rows)
+        out_ref[part, :] = (own_ref[part, :].astype(F32) + piece[...].astype(F32)).astype(BF16)
 
 
 def pair_pieces(own, pieces):
-    rows, width = own.shape
-    spec = pl.BlockSpec((rows // PIECES, width), lambda i: (i, 0))
     return pl.pallas_call(
         pair_body,
-        grid=(PIECES,),
-        in_specs=[spec] + [pl.BlockSpec(pieces[0].shape, lambda i: (0, 0))] * PIECES,
-        out_specs=spec,
         out_shape=jax.ShapeDtypeStruct(own.shape, BF16),
-        compiler_params=params("arbitrary"),
+        compiler_params=params(),
         cost_estimate=LITTLE,
         name="pair_sum",
     )(own, *pieces)
@@ -713,9 +707,8 @@
 def dp_line(owns, arrivals):
     if not owns:
         return arrivals
-    sums, pair = [], None
+    sums = []
     for mask, own, arrived in zip(LINE, owns, arrivals):
-        arrived = arrived if pair is None else after(arrived, pair)
         pair = own.astype(F32) + arrived.astype(F32)
         sums.append(swap(pair.astype(BF16), "dp", mask) if mask else pair)
     return sums
@@ -809,8 +802,7 @@
         first_slots, ((0, packed), (packed, packed + padded)), head_width
     )
     wd = lax.all_gather(w_down.astype(BF16), "dp", axis=0, tiled=True)
-    w_up_low = after(w_up.astype(BF16), *first_slots)
-    up_slots = dp_send(w_up_low)
+    wu = lax.all_gather(w_up.astype(BF16), "dp", axis=0, tiled=True)
     vec_rows = smalls[:8]
     bu = smalls[6:7]
     bq = smalls[7:9].reshape(2, dp_size, own_rows)[:, :, :own_bias].reshape(2, head_width)
@@ -823,14 +815,13 @@
     key_bias = jnp.where(place < lengths[0], 0.0, MASKED).astype(F32)[:, None]
 
     attn_in, qkv = qkv_call(x_rows, vec_rows, wq, qkv_bias, tok)
-    up_line = up_slots[4:8:2] + up_slots[2:3] if len(up_slots) == 8 else up_slots * 3
     att, lse, *sent = attn_call(
         heads, ("pieces",), qkv, key_bias, wo, tok, 3 * tok
     )
     att, lse, part_two = attn_call(
-        heads, ("own",), after(qkv, up_line[0]), key_bias, wo, tok, 2 * tok, (att, lse)
-    )
-    total = pair_pieces(after(part_two, up_line[1]), swap_all(sent, "tensor", 1))
+        heads, ("own",), qkv, key_bias, wo, tok, 2 * tok, (att, lse)
+    )
+    total = pair_pieces(part_two, swap_all(sent, "tensor", 1))
     far = swap(total, "tensor", 2)
     att, lse, mine, *sent = attn_call(
         heads,
@@ -844,13 +835,12 @@
     )
     near = swap_all(sent, "tensor", 1)
     residual, mlp_in = row_call(
-        residual_body, (inputs, mine, after(far, up_line[2], wd, *up_slots[1:6:4])), near, vec_rows, (F32, BF16), 0, "residual"
+        residual_body, (inputs, mine, after(far, wd)), near, vec_rows, (F32, BF16), 0, "residual"
     )
 
     near = swap(mlp_in, "tensor", 1)
     far = swap(mlp_in, "tensor", 2)
-    d_hidden = mm(after(cot_rows, mlp_in), wd)
-    (wu,) = dp_place([*up_slots[:-1], after(up_slots[-1], d_hidden)], ((0, w_up.shape[1]),))
+    d_hidden = mm(after(cot_rows, mlp_in, wu), wd)
     hidden, d_pre, bu_sums, mine, *sent = mlp_call(
         ("own", "pieces"), [mlp_in, near], wu, bu, d_hidden, 0, frames
     )
@@ -907,16 +897,15 @@
     first_far = mm(d_qkv[half:], wq, NT).astype(BF16)
     far = swap(pair_sum(first_far[:tok], first_far[tok:]), "tensor", 2)
     lined = dp_line(owns, crossed)
-    grad_wd = after(grad_wd, first_far, *crossed[:2])
+    first_mine = mm(after(d_qkv[:half], first_far), wq, NT).astype(BF16)
+    grad_wd = after(grad_wd, first_mine, *crossed)
     mom_down_new, update_down = momentum(mom_down, grad_wd.astype(F32))
     early = polar_call(tensor_sum(gram_of(update_down)[None]))
     new_w_down = applied(w_down, early[0], update_down, STEP_DOWN)
-    first_gate = (first_far, far, new_w_down, grad_wu, *crossed, *lined[:1])
-    first_mine = mm(after(d_qkv[:half], *first_gate), wq, NT).astype(BF16)
     quarter = tok // PIECES
     sent = [first_mine[tok + k * quarter : tok + k * quarter + quarter] for k in range(PIECES)]
     near = swap_all(sent, "tensor", 1)
-    grad_wu = after(grad_wu, first_mine, lined[0])
+    grad_wu = after(after(grad_wu, first_mine, *crossed), *lined[:2])
     output = (
         residual
         + (down_mine[:tok].astype(F32) + output_near.astype(F32) + output_far.astype(F32))
@@ -950,8 +939,9 @@
     )
 
     mom_up_new, update_up = momentum(mom_up, grad_wu.astype(F32))
-    gram_up = gram_of(update_up)
-    lined = tie(lined, gram_up, input_grad)
+    middle = polar_call(tensor_sum(gram_of(update_up)[None]))
+    new_w_up = applied(w_up, middle[0], update_up, STEP_UP)
+    lined = tie(lined, new_w_up, new_w_down, rows_of)
     grad_first = dp_total(lined)
     grad_wq, grad_wo = grad_first[:, :packed], grad_first[:, packed : packed + head_width]
     mom_out_new, update_out = momentum(mom_out, grad_wo)
@@ -961,10 +951,9 @@
     flat = jnp.concatenate(
         [update_qkv[:, 0], jnp.zeros((own_rows, extra), F32), update_qkv[:, 1], update_qkv[:, 2]], axis=1
     )
-    late = tensor_sum(jnp.stack([gram_of(update_out), gram_of(flat), gram_up]))
-    late = polar_call(after(late, vec_sums))
+    late = tensor_sum(jnp.stack([gram_of(update_out), gram_of(flat)]))
+    late = polar_call(late)
     new_w_out = applied(w_out, late[0], update_out, STEP_OUT)
-    new_w_up = applied(w_up, late[2], update_up, STEP_UP)
     polar_qkv = jnp.dot(late[1], flat, precision=HIGHEST)
     new_w_qkv = w_qkv - STEP_QKV * jnp.stack(
         [polar_qkv[:, spot : spot + head_width] for spot in spots], axis=1

time: 537 us -> 537 us (level)
  waiting for transfers between devices: 166 us -> 173 us
  local copies, waits for them, and re-layouts: 33 us -> 26.3 us
    ppermute x69 -> x64, waiting for transfers between devices: 166 us -> 173 us  [swap(): return lax.ppermute(value, axis, [(i, i ^ mask) for i in range(size)])]
    pallas_call x2 -> x3, Pallas kernels: 15.9 us -> 21.6 us  [polar_call(): pl.pallas_call(polar_body, out_shape=jax.ShapeDtypeStruct(grams.shape, F3...]
    unnamed x155 -> x139, local copies, waits for them, and re-layouts: 16.8 us -> 13.9 us
    ppermute x69 -> x64, starting transfers between devices: 51.1 us -> 52.1 us  [swap(): return lax.ppermute(value, axis, [(i, i ^ mask) for i in range(size)])]
  transfers between devices with their start and end apart: 72 -> 68, of which waited for: 23 -> 18; matrix products, arithmetic and copies ran while one was open for 19% -> 17% of each run, Pallas kernels for 27% -> 28%
where the time goes in v4:
time: 537 us; the launch traced here: 532 us
  waiting for transfers between devices  173 us (32%)
  Pallas kernels  167 us (31%)
  matrix products  63.3 us (12%)
  starting transfers between devices  52.2 us (10%)
  other arithmetic  34 us (6%)
  local copies, waits for them, and re-layouts  26.3 us (5%)
  between operations  16.2 us (3%)
    ppermute x64, waiting for transfers between devices, swap(): return lax.ppermute(value, axis, [(i, i ^ mask) for i in range(size)])  173 us
    ppermute x64, starting transfers between devices, swap(): return lax.ppermute(value, axis, [(i, i ^ mask) for i in range(size)])  52.1 us
    dot_general x10, matrix products, mm(): return lax.dot_general(left, right, dims, preferred_element_type=F32)  50.9 us
    pallas_call x2, Pallas kernels, attn_back_call(): pl.pallas_call(partial(attn_back_body, heads, last_part, first), grid=(co...  46.5 us
    pallas_call x3, Pallas kernels, attn_call(): pl.pallas_call(partial(attn_body, heads, emits, len(held)), grid=(count /...  31.2 us
    pallas_call x3, Pallas kernels, mlp_call(): pl.pallas_call(partial(mlp_body, min(256, hidden_width), emits, len(held)...  30.6 us
    pallas_call x3, Pallas kernels, polar_call(): pl.pallas_call(polar_body, out_shape=jax.ShapeDtypeStruct(grams.shape, F3...  21.6 us
    pallas_call x3, Pallas kernels, row_call(): pl.pallas_call(partial(row_body, body, len(rows_in)), grid=(PIECES,), in_...  17.4 us
  transfers between devices with their start and end apart: 68, of which 18 were waited for; matrix products, arithmetic and copies ran while one was open for 17% of the time, Pallas kernels for 28%

profile of v4, /device:TPU:0, one launch (start us, length us, event | category | flops | bytes accessed | tf_op | source)
XLA Modules:
  0.0 532.1 jit_solution(13777591383769889831)
XLA Ops:
  11.5 3.0 collective-permute-start.3
  15.1 3.7 collective-permute-start
  21.1 15.6 %collective-permute-done.refs_6_ = bf16[160,1408]{1,0:T(8,128)(2,1)S(1)} collective-permute-done((bf16[160,1408]{1,0:T(8,128)(2,1)S(1)}, bf16[160,1408]{1,0:T(8,128)(2,1)S(1)}, u32[]{:S(2)}, u32[]{:S(2)}) %collective-permute-start) | collective-permute-done | bytes 450592 | tf_op jit(solution)/shard_map/ppermute | solution.py:68
  37.5 15.2 %collective-permute-done.4.refs_2_ = bf16[160,1408]{1,0:T(8,128)(2,1)} collective-permute-done((bf16[160,1408]{1,0:T(8,128)(2,1)S(1)}, bf16[160,1408]{1,0:T(8,128)(2,1)}, u32[]{:S(2)}, u32[]{:S(2)}) %collective-permute-start.4) | collective-permute-done | bytes 450592 | tf_op jit(solution)/shard_map/ppermute | solution.py:68
  54.7 31.1 %collective-permute-done.9.refs_4_ = bf16[160,1408]{1,0:T(8,128)(2,1)} collective-permute-done((bf16[160,1408]{1,0:T(8,128)(2,1)S(1)}, bf16[160,1408]{1,0:T(8,128)(2,1)}, u32[]{:S(2)}, u32[]{:S(2)}) %collective-permute-start.9) | collective-permute-done | bytes 450592 | tf_op jit(solution)/shard_map/ppermute | solution.py:68
  88.0 4.2 collective-permute-done.10.refs_3_
  96.5 3.5 pad_maximum_fusion.x_ref
  99.9 3.3 pad_maximum_fusion.1
  103.2 4.5 collective-permute-done.12.refs_5_
  108.5 4.0 place_rows.1
  115.7 9.8 %norm_qkv.1 = (bf16[1536,1280]{1,0:T(8,128)(2,1)}, bf16[1536,1024]{1,0:T(8,128)(2,1)}) custom-call(bf16[1536,1280]{1,0:T(8,128)(2,1)} %pad_maximum_fusion.x_ref, f32[8,1280]{1,0:T(8,128)} %slice.146.vec_ref.refs_7_.refs_8_, bf16[1280,1024]{1,0:T(8,128)(2,1)} %get-tuple-element.110.w_ref, f32[1,1024]{1,0:T(1,128)} %pad_maximum_fusion.7.bias_ref), custom_call_target="tpu_custom_call" | custom-call | flops 1000000 | bytes 100000 | tf_op jit(solution)/shard_map/norm_qkv/pallas_call | solution.py:109
  125.5 8.1 %attn_fwd.3 = (bf16[1536,384]{1,0:T(8,128)(2,1)}, f32[8,1536]{1,0:T(8,128)}, bf16[96,1280]{1,0:T(8,128)(2,1)}, bf16[96,1280]{1,0:T(8,128)(2,1)}, bf16[96,1280]{1,0:T(8,128)(2,1)}, /*index=5*/bf16[96,1280]{1,0:T(8,128)(2,1)}) custom-call(bf16[1536,1024]{1,0:T(8,128)(2,1)} %get-tuple-element.120.q_ref.qkv_ref, ...), custom_call_target="tpu_custom_call" | custom-call | flops 1000000 | bytes 100000 | tf_op jit(solution)/shard_map/attn_fwd/pallas_call | solution.py:266
  134.7 8.6 %attn_fwd.4 = (bf16[1536,384]{1,0:T(8,128)(2,1)}, f32[8,1536]{1,0:T(8,128)}, bf16[384,1280]{1,0:T(8,128)(2,1)}) custom-call(bf16[1536,1024]{1,0:T(8,128)(2,1)} %get-tuple-element.120.q_ref.qkv_ref, bf16[1536,1024]{1,0:T(8,128)(2,1)} %get-tuple-element.120.q_ref.qkv_ref, ...), custom_call_target="tpu_custom_call", output_to_operand_aliasing={{0}: (4, {}), {1}: (5, {})} | custom-call | flops 1000000 | bytes 100000 | tf_op jit(solution)/shard_map/attn_fwd/pallas_call | solution.py:266
  144.2 2.7 pair_sum.2
  147.0 14.5 %attn_fwd.5 = (bf16[1536,384]{1,0:T(8,128)(2,1)}, f32[8,1536]{1,0:T(8,128)}, bf16[384,1280]{1,0:T(8,128)(2,1)}, bf16[96,1280]{1,0:T(8,128)(2,1)}, bf16[96,1280]{...) custom-call(bf16[1536,1024]{1,0:T(8,128)(2,1)} %get-tuple-element.12, ...), custom_call_target="tpu_custom_call", output_to_operand_aliasing={{0}: (4, {}), {1}: (5, {})} | custom-call | flops 1000000 | bytes 100000 | tf_op jit(solution)/shard_map/attn_fwd/pallas_call | solution.py:266
  164.0 6.9 %collective-permute-done.17.refs_2_ = bf16[384,1280]{1,0:T(8,128)(2,1)S(1)} collective-permute-done((bf16[384,1280]{1,0:T(8,128)(2,1)}, bf16[384,1280]{1,0:T(8,128)(2,1)S(1)}, u32[]{:S(2)}, u32[]{:S(2)}) %collective-permute-start.17) | collective-permute-done | bytes 983072 | tf_op jit(solution)/shard_map/ppermute | solution.py:68
  172.1 4.9 residual.1
  177.3 9.9 %fusion.43.refs_4_.refs_3_ = f32[1536,1280]{1,0:T(8,128)} fusion(bf16[1536,1280]{1,0:T(8,128)(2,1)} %pad_maximum_fusion.1, bf16[1280,1280]{1,0:T(8,128)(2,1)} %all-gather.3.cloned.1.call-done), kind=kOutput, calls=%fused_computation.123 | convolution fusion | flops 5033164800 | bytes 15073280 | tf_op jit(solution)/shard_map/dot_general | solution.py:43
  188.2 14.5 %mlp_up.3 = (bf16[1536,1280]{1,0:T(8,128)(2,1)}, bf16[1536,1280]{1,0:T(8,128)(2,1)}, f32[8,1280]{1,0:T(8,128)}, bf16[384,1280]{1,0:T(8,128)(2,1)}, bf16[96,1280]...) custom-call(bf16[384,1280]{1,0:T(8,128)(2,1)} %get-tuple-element.130.refs_0_, ...), custom_call_target="tpu_custom_call" | custom-call | flops 1000000 | bytes 100000 | tf_op jit(solution)/shard_map/mlp_up/pallas_call | solution.py:471
  206.4 8.0 %mlp_up.4 = (bf16[1536,1280]{1,0:T(8,128)(2,1)}, bf16[1536,1280]{1,0:T(8,128)(2,1)}, f32[8,1280]{1,0:T(8,128)}, bf16[96,1280]{1,0:T(8,128)(2,1)}, bf16[96,1280]{...) custom-call(bf16[384,1280]{1,0:T(8,128)(2,1)} %copy-done.32, ...), custom_call_target="tpu_custom_call", output_to_operand_aliasing={{0}: (4, {}), {1}: (5, {})} | custom-call | flops 1000000 | bytes 100000 | tf_op jit(solution)/shard_map/mlp_up/pallas_call | solution.py:471
  215.4 8.2 %mlp_up.5 = (bf16[1536,1280]{1,0:T(8,128)(2,1)}, bf16[1536,1280]{1,0:T(8,128)(2,1)}, f32[8,1280]{1,0:T(8,128)}, bf16[384,1280]{1,0:T(8,128)(2,1)}) custom-call(bf16[384,1280]{1,0:T(8,128)(2,1)} %copy-done.28, bf16[1280,1280]{1,0:T(8,128)(2,1)} %all-gather.5.cloned.1.call-done.refs_2_.refs_1_, ...), custom_call_target="tpu_custom_call", output_to_operand_aliasing={{0}: (4, {}), {1}: (5, {})} | custom-call | flops 1000000 | bytes 100000 | tf_op jit(solution)/shard_map/mlp_up/pallas_call | solution.py:471
  224.5 2.8 pair_sum.3
  227.3 9.1 %convolution_convert_fusion.1 = bf16[1280,1280]{1,0:T(8,128)(2,1)} fusion(bf16[1536,1280]{1,0:T(8,128)(2,1)S(1)} %copy-done.10, bf16[1536,1280]{1,0:T(8,128)(2,1)} %get-tuple-element.149), kind=kOutput, calls=%fused_computation.1 | convolution fusion | flops 5034803200 | bytes 11141120 | tf_op jit(solution)/shard_map/dot_general | solution.py:43
  239.4 9.0 %convolution_convert_fusion = bf16[1280,1280]{1,0:T(8,128)(2,1)} fusion(bf16[1536,1280]{1,0:T(8,128)(2,1)} %get-tuple-element.148, bf16[384,1280]{1,0:T(8,128)(2,1)} %copy-done.32, bf16[384,1280]{1,0:T(8,128)(2,1)S(1)} %copy-done.29, bf16[384,1280]{1,0:T(8,128)(2,1)S(1)} %copy-done.31, bf16[384,1280]{1,0:T(8,128)(2,1)S(1)} %copy-done.27), kind=kOutput, calls=%fused_computation | convolution fusion | flops 5050531840 | bytes 11141120 | tf_op jit(solution)/shard_map/dot_general | solution.py:43
  248.4 5.4 %convolution_convert_fusion.3 = bf16[768,1280]{1,0:T(8,128)(2,1)S(1)} fusion(bf16[1280,1280]{1,0:T(8,128)(2,1)} %all-gather.3.cloned.1.call-done, bf16[1536,1280]{1,0:T(8,128)(2,1)} %get-tuple-element.149), kind=kOutput, calls=%fused_computation.12 | convolution fusion | flops 2517565440 | bytes 7208960 | tf_op jit(solution)/shard_map/dot_general | solution.py:43
  253.9 2.7 convolution_convert_fusion.4
  256.7 5.3 collective-permute-done.31.refs_2_
  261.9 6.2 %second_back.1 = (f32[384,1280]{1,0:T(8,128)}, bf16[384,1280]{1,0:T(8,128)(2,1)}, f32[8,1280]{1,0:T(8,128)}) custom-call(f32[384,1280]{1,0:T(8,128)} %get-tuple-element.129.refs_0_, bf16[384,1280]{1,0:T(8,128)(2,1)} %get-tuple-element.133.refs_1_, bf16[384,1280]{1,0:T(8,128)(2,1)} %collective-permute-done.31.refs_2_, bf16[384,1280]{1,0:T(8,128)(2,1)} %refs_3_.1, ...), custom_call_target="tpu_custom_call" | custom-call | flops 1000000 | bytes 100000 | tf_op jit(solution)/shard_map/second_back/pallas_call | solution.py:559
  273.9 22.6 %attn_bwd.2 = (bf16[1536,1024]{1,0:T(8,128)(2,1)}, f32[8,384]{1,0:T(8,128)}, f32[1536,384]{1,0:T(8,128)}, f32[1536,384]{1,0:T(8,128)}) custom-call(bf16[768,1280]{1,0:T(8,128)(2,1)} %copy-done.7, bf16[1280,384]{1,0:T(8,128)(2,1)} %get-tuple-element.112.wo_ref, bf16[1536,384]{1,0:T(8,128)(2,1)} %get-tuple-element.159.att_ref, ...), custom_call_target="tpu_custom_call" | custom-call | flops 1000000 | bytes 100000 | tf_op jit(solution)/shard_map/attn_bwd/pallas_call | solution.py:399
  307.5 23.9 %attn_bwd.3 = (bf16[1536,1024]{1,0:T(8,128)(2,1)}, f32[8,384]{1,0:T(8,128)}) custom-call(bf16[768,1280]{1,0:T(8,128)(2,1)} %copy-done.9, bf16[1280,384]{1,0:T(8,128)(2,1)} %get-tuple-element.112.wo_ref, bf16[1536,384]{1,0:T(8,128)(2,1)} %get-tuple-element.159.att_ref, ...), custom_call_target="tpu_custom_call", output_to_operand_aliasing={{0}: (10, {})} | custom-call | flops 1000000 | bytes 100000 | tf_op jit(solution)/shard_map/attn_bwd/pallas_call | solution.py:399
  331.5 7.8 %convolution_convert_fusion.2 = bf16[1280,1024]{1,0:T(8,128)(2,1)S(1)} fusion(bf16[1536,1280]{1,0:T(8,128)(2,1)} %get-tuple-element.169, bf16[1536,1024]{1,0:T(8,128)(2,1)} %get-tuple-element.171), kind=kOutput, calls=%fused_computation.11 | convolution fusion | flops 4027842560 | bytes 9699328 | tf_op jit(solution)/shard_map/dot_general | solution.py:43
  348.8 9.4 %collective-permute-done.52 = bf16[160,1408]{1,0:T(8,128)(2,1)S(1)} collective-permute-done((bf16[160,1408]{1,0:T(8,128)(2,1)S(1)}, bf16[160,1408]{1,0:T(8,128)(2,1)S(1)}, u32[]{:S(2)}, u32[]{:S(2)}) %collective-permute-start.52) | collective-permute-done | bytes 450592 | tf_op jit(solution)/shard_map/ppermute | solution.py:68
  358.2 14.9 %collective-permute-done.50 = bf16[160,1408]{1,0:T(8,128)(2,1)S(1)} collective-permute-done((bf16[160,1408]{1,0:T(8,128)(2,1)S(1)}, bf16[160,1408]{1,0:T(8,128)(2,1)S(1)}, u32[]{:S(2)}, u32[]{:S(2)}) %collective-permute-start.50) | collective-permute-done | bytes 450592 | tf_op jit(solution)/shard_map/ppermute | solution.py:68
  373.2 10.6 %collective-permute-done.48 = bf16[160,1408]{1,0:T(8,128)(2,1)S(1)} collective-permute-done((bf16[160,1408]{1,0:T(8,128)(2,1)S(1)}, bf16[160,1408]{1,0:T(8,128)(2,1)S(1)}, u32[]{:S(2)}, u32[]{:S(2)}) %collective-permute-start.48) | collective-permute-done | bytes 450592 | tf_op jit(solution)/shard_map/ppermute | solution.py:68
  383.7 13.6 %collective-permute-done.46 = bf16[160,1408]{1,0:T(8,128)(2,1)S(1)} collective-permute-done((bf16[160,1408]{1,0:T(8,128)(2,1)S(1)}, bf16[160,1408]{1,0:T(8,128)(2,1)S(1)}, u32[]{:S(2)}, u32[]{:S(2)}) %collective-permute-start.46) | collective-permute-done | bytes 450592 | tf_op jit(solution)/shard_map/ppermute | solution.py:68
  398.6 4.5 collective-permute-start.47
  403.1 3.0 collective-permute-start.49
  410.5 24.0 %collective-permute-done.47 = bf16[160,1408]{1,0:T(8,128)(2,1)} collective-permute-done((bf16[160,1408]{1,0:T(8,128)(2,1)S(1)}, bf16[160,1408]{1,0:T(8,128)(2,1)}, u32[]{:S(2)}, u32[]{:S(2)}) %collective-permute-start.47) | collective-permute-done | bytes 450592 | tf_op jit(solution)/shard_map/ppermute | solution.py:68
  441.2 6.2 %first_back.1 = (f32[384,1280]{1,0:T(8,128)}, f32[8,1280]{1,0:T(8,128)}) custom-call(bf16[384,1280]{1,0:T(8,128)(2,1)} %refs_0_.3, bf16[384,1280]{1,0:T(8,128)(2,1)} %slice.197.refs_1_, bf16[384,1280]{1,0:T(8,128)(2,1)} %copy-done.33, f32[384,1280]{1,0:T(8,128)} %get-tuple-element.173.refs_3_, bf16[96,1280]{1,0:T(8,128)(2,1)} %copy-done.42, ...), custom_call_target="tpu_custom_call" | custom-call | flops 1000000 | bytes 100000 | tf_op jit(solution)/shard_map/first_back/pallas_call | solution.py:559
  455.1 3.0 add_add_fusion
  458.1 9.6 %collective-permute-start.51 = (bf16[160,1408]{1,0:T(8,128)(2,1)}, bf16[160,1408]{1,0:T(8,128)(2,1)S(1)}, u32[]{:S(2)}, u32[]{:S(2)}) collective-permute-start(bf16[160,1408]{1,0:T(8,128)(2,1)} %get-tuple-element.199), channel_id=1, source_target_pairs={{0,8},{4,12},{8,0},{12,4},{16,24},{20,28},{24,16},{28,20},{1,9},{5... | collective-permute-start | bytes 1351688 | tf_op jit(solution)/shard_map/ppermute | solution.py:68
  469.3 6.8 %polar.4 = f32[1,160,160]{2,1,0:T(8,128)} custom-call(f32[1,160,160]{2,1,0:T(8,128)} %add.248.gram_ref), custom_call_target="tpu_custom_call" | custom-call | tf_op jit(solution)/shard_map/polar/pallas_call | solution.py:612
  477.8 2.7 fusion.8
  483.1 6.8 %polar.3 = f32[1,160,160]{2,1,0:T(8,128)} custom-call(f32[1,160,160]{2,1,0:T(8,128)} %add.244.gram_ref), custom_call_target="tpu_custom_call" | custom-call | tf_op jit(solution)/shard_map/polar/pallas_call | solution.py:612
  490.0 2.7 convolution_subtract_fusion
  492.7 3.0 collective-permute-done.61
  503.4 8.1 %collective-permute-done.63 = f32[2,160,160]{2,1,0:T(8,128)S(1)} collective-permute-done((f32[2,160,160]{2,1,0:T(8,128)S(1)}, f32[2,160,160]{2,1,0:T(8,128)S(1)}, u32[]{:S(2)}, u32[]{:S(2)}) %collective-permute-start.63) | collective-permute-done | bytes 204832 | tf_op jit(solution)/shard_map/ppermute | solution.py:68
  512.3 8.0 %polar.5 = f32[2,160,160]{2,1,0:T(8,128)} custom-call(f32[2,160,160]{2,1,0:T(8,128)} %fusion.58.gram_ref), custom_call_target="tpu_custom_call" | custom-call | tf_op jit(solution)/shard_map/polar/pallas_call | solution.py:612
  (348 shorter events, 100.1 us)
Async XLA Ops:
  7.3 163.6 %all-gather.3.cloned.1.call-start = ((), (), s32[]{:S(2)}) async-start(), calls=%async_computation.2 | async-start | bytes 3686400 | tf_op jit(solution)/shard_map/all_gather | solution.py:804
  9.4 167.9 %all-gather.5.cloned.1.call-start = ((), (), s32[]{:S(2)}) async-start(), calls=%async_computation.3 | async-start | bytes 3686400 | tf_op jit(solution)/shard_map/all_gather | solution.py:805
  11.4 320.0 %reduce-scatter.3.cloned.1.call-start = ((), (), s32[]{:S(2)}) async-start(), calls=%async_computation.4 | async-start | bytes 3686400 | tf_op jit(solution)/shard_map/reduce_scatter | solution.py:725
  11.5 42.7 %collective-permute-start.3 = (bf16[384,1280]{1,0:T(8,128)(2,1)S(1)}, bf16[384,1280]{1,0:T(8,128)(2,1)}, u32[]{:S(2)}, u32[]{:S(2)}) collective-permute-start(bf16[384,1280]{1,0:T(8,128)(2,1)S(1)} %copy-done.2), channel_id=1, source_target_pairs={{0,2},{1,3},{2,0},{3,1},{4,6},{5,7},{6,4},{7,5},{8,10},{9,11},{10,... | collective-permute-start | bytes 2949128 | tf_op jit(solution)/shard_map/ppermute | solution.py:68
  15.1 21.6 %collective-permute-start = (bf16[160,1408]{1,0:T(8,128)(2,1)S(1)}, bf16[160,1408]{1,0:T(8,128)(2,1)S(1)}, u32[]{:S(2)}, u32[]{:S(2)}) collective-permute-start(bf16[160,1408]{1,0:T(8,128)(2,1)S(1)} %concatenate.52.refs_0_), channel_id=1, source_target_pairs={{0,24},{4,28},{8,16},{12,20},{16,8},{20,12},{24,0},{28,4},{1,25},{... | collective-permute-start | bytes 1351688 | tf_op jit(solution)/shard_map/ppermute | solution.py:68
  18.8 33.9 %collective-permute-start.4 = (bf16[160,1408]{1,0:T(8,128)(2,1)S(1)}, bf16[160,1408]{1,0:T(8,128)(2,1)}, u32[]{:S(2)}, u32[]{:S(2)}) collective-permute-start(bf16[160,1408]{1,0:T(8,128)(2,1)S(1)} %concatenate.52.refs_0_), channel_id=1, source_target_pairs={{0,8},{4,12},{8,0},{12,4},{16,24},{20,28},{24,16},{28,20},{1,9},{5... | collective-permute-start | bytes 1351688 | tf_op jit(solution)/shard_map/ppermute | solution.py:68
  18.8 33.9 %collective-permute-start.5 = (bf16[160,1408]{1,0:T(8,128)(2,1)S(1)}, bf16[160,1408]{1,0:T(8,128)(2,1)}, u32[]{:S(2)}, u32[]{:S(2)}) collective-permute-start(bf16[160,1408]{1,0:T(8,128)(2,1)S(1)} %concatenate.52.refs_0_), channel_id=1, source_target_pairs={{0,4},{4,0},{8,12},{12,8},{16,20},{20,16},{24,28},{28,24},{1,5},{5... | collective-permute-start | bytes 1351688 | tf_op jit(solution)/shard_map/ppermute | solution.py:68
  20.3 65.5 %collective-permute-start.9 = (bf16[160,1408]{1,0:T(8,128)(2,1)S(1)}, bf16[160,1408]{1,0:T(8,128)(2,1)}, u32[]{:S(2)}, u32[]{:S(2)}) collective-permute-start(bf16[160,1408]{1,0:T(8,128)(2,1)S(1)} %concatenate.52.refs_0_), channel_id=1, source_target_pairs={{0,16},{4,20},{8,24},{12,28},{16,0},{20,4},{24,8},{28,12},{1,17},{... | collective-permute-start | bytes 1351688 | tf_op jit(solution)/shard_map/ppermute | solution.py:68
  37.5 54.7 %collective-permute-start.8 = (bf16[384,1280]{1,0:T(8,128)(2,1)S(1)}, bf16[384,1280]{1,0:T(8,128)(2,1)S(1)}, u32[]{:S(2)}, u32[]{:S(2)}) collective-permute-start(bf16[384,1280]{1,0:T(8,128)(2,1)S(1)} %copy-done.11), channel_id=1, source_target_pairs={{0,2},{1,3},{2,0},{3,1},{4,6},{5,7},{6,4},{7,5},{8,10},{9,11},{10,... | collective-permute-start | bytes 2949128 | tf_op jit(solution)/shard_map/ppermute | solution.py:68
  52.7 43.8 %collective-permute-start.2 = (bf16[384,1280]{1,0:T(8,128)(2,1)S(1)}, bf16[384,1280]{1,0:T(8,128)(2,1)}, u32[]{:S(2)}, u32[]{:S(2)}) collective-permute-start(bf16[384,1280]{1,0:T(8,128)(2,1)S(1)} %copy-done.2), channel_id=1, source_target_pairs={{0,1},{1,0},{2,3},{3,2},{4,5},{5,4},{6,7},{7,6},{8,9},{9,8},{10,11... | collective-permute-start | bytes 2949128 | tf_op jit(solution)/shard_map/ppermute | solution.py:68
  52.7 34.8 %collective-permute-start.1 = (bf16[160,1408]{1,0:T(8,128)(2,1)}, bf16[160,1408]{1,0:T(8,128)(2,1)}, u32[]{:S(2)}, u32[]{:S(2)}) collective-permute-start(bf16[160,1408]{1,0:T(8,128)(2,1)} %copy-done.39), channel_id=1, source_target_pairs={{0,4},{4,0},{8,12},{12,8},{16,20},{20,16},{24,28},{28,24},{1,5},{5... | collective-permute-start | bytes 1351688 | tf_op jit(solution)/shard_map/ppermute | solution.py:68
  54.2 38.0 %collective-permute-start.10 = (bf16[160,1408]{1,0:T(8,128)(2,1)}, bf16[160,1408]{1,0:T(8,128)(2,1)}, u32[]{:S(2)}, u32[]{:S(2)}) collective-permute-start(bf16[160,1408]{1,0:T(8,128)(2,1)} %collective-permute-done.4.refs_2_), channel_id=1, source_target_pairs={{0,4},{4,0},{8,12},{12,8},{16,20},{20,16},{24,28},{28,24},{1,5},{5... | collective-permute-start | bytes 1351688 | tf_op jit(solution)/shard_map/ppermute | solution.py:68
  85.8 10.7 %collective-permute-start.6 = (bf16[384,1280]{1,0:T(8,128)(2,1)}, bf16[384,1280]{1,0:T(8,128)(2,1)}, u32[]{:S(2)}, u32[]{:S(2)}) collective-permute-start(bf16[384,1280]{1,0:T(8,128)(2,1)} %collective-permute-done.3), channel_id=1, source_target_pairs={{0,1},{1,0},{2,3},{3,2},{4,5},{5,4},{6,7},{7,6},{8,9},{9,8},{10,11... | collective-permute-start | bytes 2949128 | tf_op jit(solution)/shard_map/ppermute | solution.py:68
  87.5 12.4 %collective-permute-start.7 = (bf16[384,1280]{1,0:T(8,128)(2,1)S(1)}, bf16[384,1280]{1,0:T(8,128)(2,1)}, u32[]{:S(2)}, u32[]{:S(2)}) collective-permute-start(bf16[384,1280]{1,0:T(8,128)(2,1)S(1)} %copy-done.11), channel_id=1, source_target_pairs={{0,1},{1,0},{2,3},{3,2},{4,5},{5,4},{6,7},{7,6},{8,9},{9,8},{10,11... | collective-permute-start | bytes 2949128 | tf_op jit(solution)/shard_map/ppermute | solution.py:68
  94.2 13.5 %collective-permute-start.12 = (bf16[160,1408]{1,0:T(8,128)(2,1)}, bf16[160,1408]{1,0:T(8,128)(2,1)S(1)}, u32[]{:S(2)}, u32[]{:S(2)}) collective-permute-start(bf16[160,1408]{1,0:T(8,128)(2,1)} %collective-permute-done.9.refs_4_), channel_id=1, source_target_pairs={{0,4},{4,0},{8,12},{12,8},{16,20},{20,16},{24,28},{28,24},{1,5},{5... | collective-permute-start | bytes 1351688 | tf_op jit(solution)/shard_map/ppermute | solution.py:68
  133.7 9.6 %collective-permute-start.13 = (bf16[96,1280]{1,0:T(8,128)(2,1)}, bf16[96,1280]{1,0:T(8,128)(2,1)S(1)}, u32[]{:S(2)}, u32[]{:S(2)}) collective-permute-start(bf16[96,1280]{1,0:T(8,128)(2,1)} %get-tuple-element.116), channel_id=1, source_target_pairs={{0,1},{1,0},{2,3},{3,2},{4,5},{5,4},{6,7},{7,6},{8,9},{9,8},{10,11... | collective-permute-start | bytes 737288 | tf_op jit(solution)/shard_map/ppermute | solution.py:68
  133.7 9.6 %collective-permute-start.14 = (bf16[96,1280]{1,0:T(8,128)(2,1)}, bf16[96,1280]{1,0:T(8,128)(2,1)S(1)}, u32[]{:S(2)}, u32[]{:S(2)}) collective-permute-start(bf16[96,1280]{1,0:T(8,128)(2,1)} %get-tuple-element.117), channel_id=1, source_target_pairs={{0,1},{1,0},{2,3},{3,2},{4,5},{5,4},{6,7},{7,6},{8,9},{9,8},{10,11... | collective-permute-start | bytes 737288 | tf_op jit(solution)/shard_map/ppermute | solution.py:68
  147.0 23.9 %collective-permute-start.17 = (bf16[384,1280]{1,0:T(8,128)(2,1)}, bf16[384,1280]{1,0:T(8,128)(2,1)S(1)}, u32[]{:S(2)}, u32[]{:S(2)}) collective-permute-start(bf16[384,1280]{1,0:T(8,128)(2,1)} %pair_sum.2), channel_id=1, source_target_pairs={{0,2},{1,3},{2,0},{3,1},{4,6},{5,7},{6,4},{7,5},{8,10},{9,11},{10,... | collective-permute-start | bytes 2949128 | tf_op jit(solution)/shard_map/ppermute | solution.py:68
  161.4 9.4 %collective-permute-start.18 = (bf16[96,1280]{1,0:T(8,128)(2,1)}, bf16[96,1280]{1,0:T(8,128)(2,1)S(1)}, u32[]{:S(2)}, u32[]{:S(2)}) collective-permute-start(bf16[96,1280]{1,0:T(8,128)(2,1)} %get-tuple-element.125), channel_id=1, source_target_pairs={{0,1},{1,0},{2,3},{3,2},{4,5},{5,4},{6,7},{7,6},{8,9},{9,8},{10,11... | collective-permute-start | bytes 737288 | tf_op jit(solution)/shard_map/ppermute | solution.py:68
  161.5 9.3 %collective-permute-start.19 = (bf16[96,1280]{1,0:T(8,128)(2,1)}, bf16[96,1280]{1,0:T(8,128)(2,1)S(1)}, u32[]{:S(2)}, u32[]{:S(2)}) collective-permute-start(bf16[96,1280]{1,0:T(8,128)(2,1)} %get-tuple-element.126), channel_id=1, source_target_pairs={{0,1},{1,0},{2,3},{3,2},{4,5},{5,4},{6,7},{7,6},{8,9},{9,8},{10,11... | collective-permute-start | bytes 737288 | tf_op jit(solution)/shard_map/ppermute | solution.py:68
  177.1 25.6 %collective-permute-start.22 = (bf16[384,1280]{1,0:T(8,128)(2,1)}, bf16[384,1280]{1,0:T(8,128)(2,1)S(1)}, u32[]{:S(2)}, u32[]{:S(2)}) collective-permute-start(bf16[384,1280]{1,0:T(8,128)(2,1)} %get-tuple-element.130.refs_0_), channel_id=1, source_target_pairs={{0,2},{1,3},{2,0},{3,1},{4,6},{5,7},{6,4},{7,5},{8,10},{9,11},{10,... | collective-permute-start | bytes 2949128 | tf_op jit(solution)/shard_map/ppermute | solution.py:68
  177.3 9.9 %collective-permute-start.23 = (bf16[384,1280]{1,0:T(8,128)(2,1)}, bf16[384,1280]{1,0:T(8,128)(2,1)S(1)}, u32[]{:S(2)}, u32[]{:S(2)}) collective-permute-start(bf16[384,1280]{1,0:T(8,128)(2,1)} %get-tuple-element.130.refs_0_), channel_id=1, source_target_pairs={{0,1},{1,0},{2,3},{3,2},{4,5},{5,4},{6,7},{7,6},{8,9},{9,8},{10,11... | collective-permute-start | bytes 2949128 | tf_op jit(solution)/shard_map/ppermute | solution.py:68
  236.5 201.2 %reduce-scatter.5.cloned.1.call-start = ((), (), s32[]{:S(2)}) async-start(), calls=%async_computation.5 | async-start | bytes 3686400 | tf_op jit(solution)/shard_map/reduce_scatter | solution.py:725
  236.5 20.1 %collective-permute-start.32 = (bf16[96,1280]{1,0:T(8,128)(2,1)}, bf16[96,1280]{1,0:T(8,128)(2,1)S(1)}, u32[]{:S(2)}, u32[]{:S(2)}) collective-permute-start(bf16[96,1280]{1,0:T(8,128)(2,1)} %get-tuple-element.150), channel_id=1, source_target_pairs={{0,1},{1,0},{2,3},{3,2},{4,5},{5,4},{6,7},{7,6},{8,9},{9,8},{10,11... | collective-permute-start | bytes 737288 | tf_op jit(solution)/shard_map/ppermute | solution.py:68
  236.9 19.7 %collective-permute-start.33 = (bf16[96,1280]{1,0:T(8,128)(2,1)}, bf16[96,1280]{1,0:T(8,128)(2,1)S(1)}, u32[]{:S(2)}, u32[]{:S(2)}) collective-permute-start(bf16[96,1280]{1,0:T(8,128)(2,1)} %get-tuple-element.151), channel_id=1, source_target_pairs={{0,1},{1,0},{2,3},{3,2},{4,5},{5,4},{6,7},{7,6},{8,9},{9,8},{10,11... | collective-permute-start | bytes 737288 | tf_op jit(solution)/shard_map/ppermute | solution.py:68
  237.1 19.6 %collective-permute-start.34 = (bf16[96,1280]{1,0:T(8,128)(2,1)}, bf16[96,1280]{1,0:T(8,128)(2,1)}, u32[]{:S(2)}, u32[]{:S(2)}) collective-permute-start(bf16[96,1280]{1,0:T(8,128)(2,1)} %get-tuple-element.152), channel_id=1, source_target_pairs={{0,1},{1,0},{2,3},{3,2},{4,5},{5,4},{6,7},{7,6},{8,9},{9,8},{10,11... | collective-permute-start | bytes 737288 | tf_op jit(solution)/shard_map/ppermute | solution.py:68
  237.5 19.2 %collective-permute-start.35 = (bf16[96,1280]{1,0:T(8,128)(2,1)}, bf16[96,1280]{1,0:T(8,128)(2,1)}, u32[]{:S(2)}, u32[]{:S(2)}) collective-permute-start(bf16[96,1280]{1,0:T(8,128)(2,1)} %get-tuple-element.153), channel_id=1, source_target_pairs={{0,1},{1,0},{2,3},{3,2},{4,5},{5,4},{6,7},{7,6},{8,9},{9,8},{10,11... | collective-permute-start | bytes 737288 | tf_op jit(solution)/shard_map/ppermute | solution.py:68
  237.6 24.4 %collective-permute-start.31 = (bf16[384,1280]{1,0:T(8,128)(2,1)}, bf16[384,1280]{1,0:T(8,128)(2,1)}, u32[]{:S(2)}, u32[]{:S(2)}) collective-permute-start(bf16[384,1280]{1,0:T(8,128)(2,1)} %pair_sum.3), channel_id=1, source_target_pairs={{0,2},{1,3},{2,0},{3,1},{4,6},{5,7},{6,4},{7,5},{8,10},{9,11},{10,... | collective-permute-start | bytes 2949128 | tf_op jit(solution)/shard_map/ppermute | solution.py:68
  268.2 28.3 %collective-permute-start.36 = (bf16[384,1280]{1,0:T(8,128)(2,1)}, bf16[384,1280]{1,0:T(8,128)(2,1)}, u32[]{:S(2)}, u32[]{:S(2)}) collective-permute-start(bf16[384,1280]{1,0:T(8,128)(2,1)} %get-tuple-element.158), channel_id=1, source_target_pairs={{0,2},{1,3},{2,0},{3,1},{4,6},{5,7},{6,4},{7,5},{8,10},{9,11},{10,... | collective-permute-start | bytes 2949128 | tf_op jit(solution)/shard_map/ppermute | solution.py:68
  271.1 27.1 %collective-permute-start.30 = (bf16[384,1280]{1,0:T(8,128)(2,1)}, bf16[384,1280]{1,0:T(8,128)(2,1)}, u32[]{:S(2)}, u32[]{:S(2)}) collective-permute-start(bf16[384,1280]{1,0:T(8,128)(2,1)} %slice.196), channel_id=1, source_target_pairs={{0,1},{1,0},{2,3},{3,2},{4,5},{5,4},{6,7},{7,6},{8,9},{9,8},{10,11... | collective-permute-start | bytes 2949128 | tf_op jit(solution)/shard_map/ppermute | solution.py:68
  297.9 33.5 %collective-permute-start.29 = (bf16[384,1280]{1,0:T(8,128)(2,1)}, bf16[384,1280]{1,0:T(8,128)(2,1)S(1)}, u32[]{:S(2)}, u32[]{:S(2)}) collective-permute-start(bf16[384,1280]{1,0:T(8,128)(2,1)} %slice.194), channel_id=1, source_target_pairs={{0,1},{1,0},{2,3},{3,2},{4,5},{5,4},{6,7},{7,6},{8,9},{9,8},{10,11... | collective-permute-start | bytes 2949128 | tf_op jit(solution)/shard_map/ppermute | solution.py:68
  300.8 30.6 %collective-permute-start.38 = (bf16[384,1280]{1,0:T(8,128)(2,1)S(1)}, bf16[384,1280]{1,0:T(8,128)(2,1)}, u32[]{:S(2)}, u32[]{:S(2)}) collective-permute-start(bf16[384,1280]{1,0:T(8,128)(2,1)S(1)} %add_convert_fusion.1), channel_id=1, source_target_pairs={{0,2},{1,3},{2,0},{3,1},{4,6},{5,7},{6,4},{7,5},{8,10},{9,11},{10,... | collective-permute-start | bytes 2949128 | tf_op jit(solution)/shard_map/ppermute | solution.py:68
  341.8 64.4 %collective-permute-start.40 = (bf16[384,1280]{1,0:T(8,128)(2,1)S(1)}, bf16[384,1280]{1,0:T(8,128)(2,1)S(1)}, u32[]{:S(2)}, u32[]{:S(2)}) collective-permute-start(bf16[384,1280]{1,0:T(8,128)(2,1)S(1)} %slice.199), channel_id=1, source_target_pairs={{0,1},{1,0},{2,3},{3,2},{4,5},{5,4},{6,7},{7,6},{8,9},{9,8},{10,11... | collective-permute-start | bytes 2949128 | tf_op jit(solution)/shard_map/ppermute | solution.py:68
  342.4 15.8 %collective-permute-start.52 = (bf16[160,1408]{1,0:T(8,128)(2,1)S(1)}, bf16[160,1408]{1,0:T(8,128)(2,1)S(1)}, u32[]{:S(2)}, u32[]{:S(2)}) collective-permute-start(bf16[160,1408]{1,0:T(8,128)(2,1)S(1)} %get-tuple-element.202), channel_id=1, source_target_pairs={{0,4},{4,0},{8,12},{12,8},{16,20},{20,16},{24,28},{28,24},{1,5},{5... | collective-permute-start | bytes 1351688 | tf_op jit(solution)/shard_map/ppermute | solution.py:68
  344.1 29.0 %collective-permute-start.50 = (bf16[160,1408]{1,0:T(8,128)(2,1)S(1)}, bf16[160,1408]{1,0:T(8,128)(2,1)S(1)}, u32[]{:S(2)}, u32[]{:S(2)}) collective-permute-start(bf16[160,1408]{1,0:T(8,128)(2,1)S(1)} %get-tuple-element.203), channel_id=1, source_target_pairs={{0,4},{4,0},{8,12},{12,8},{16,20},{20,16},{24,28},{28,24},{1,5},{5... | collective-permute-start | bytes 1351688 | tf_op jit(solution)/shard_map/ppermute | solution.py:68
  344.5 39.2 %collective-permute-start.48 = (bf16[160,1408]{1,0:T(8,128)(2,1)S(1)}, bf16[160,1408]{1,0:T(8,128)(2,1)S(1)}, u32[]{:S(2)}, u32[]{:S(2)}) collective-permute-start(bf16[160,1408]{1,0:T(8,128)(2,1)S(1)} %get-tuple-element.204), channel_id=1, source_target_pairs={{0,4},{4,0},{8,12},{12,8},{16,20},{20,16},{24,28},{28,24},{1,5},{5... | collective-permute-start | bytes 1351688 | tf_op jit(solution)/shard_map/ppermute | solution.py:68
  346.2 51.2 %collective-permute-start.46 = (bf16[160,1408]{1,0:T(8,128)(2,1)S(1)}, bf16[160,1408]{1,0:T(8,128)(2,1)S(1)}, u32[]{:S(2)}, u32[]{:S(2)}) collective-permute-start(bf16[160,1408]{1,0:T(8,128)(2,1)S(1)} %get-tuple-element.205), channel_id=1, source_target_pairs={{0,4},{4,0},{8,12},{12,8},{16,20},{20,16},{24,28},{28,24},{1,5},{5... | collective-permute-start | bytes 1351688 | tf_op jit(solution)/shard_map/ppermute | solution.py:68
  398.6 36.0 %collective-permute-start.47 = (bf16[160,1408]{1,0:T(8,128)(2,1)S(1)}, bf16[160,1408]{1,0:T(8,128)(2,1)}, u32[]{:S(2)}, u32[]{:S(2)}) collective-permute-start(bf16[160,1408]{1,0:T(8,128)(2,1)S(1)} %get-tuple-element.201), channel_id=1, source_target_pairs={{0,16},{4,20},{8,24},{12,28},{16,0},{20,4},{24,8},{28,12},{1,17},{... | collective-permute-start | bytes 1351688 | tf_op jit(solution)/shard_map/ppermute | solution.py:68
  403.1 31.5 %collective-permute-start.49 = (bf16[160,1408]{1,0:T(8,128)(2,1)S(1)}, bf16[160,1408]{1,0:T(8,128)(2,1)}, u32[]{:S(2)}, u32[]{:S(2)}) collective-permute-start(bf16[160,1408]{1,0:T(8,128)(2,1)S(1)} %get-tuple-element.200), channel_id=1, source_target_pairs={{0,24},{4,28},{8,16},{12,20},{16,8},{20,12},{24,0},{28,4},{1,25},{... | collective-permute-start | bytes 1351688 | tf_op jit(solution)/shard_map/ppermute | solution.py:68
  407.4 32.9 %collective-permute-start.41 = (bf16[384,1280]{1,0:T(8,128)(2,1)}, bf16[384,1280]{1,0:T(8,128)(2,1)S(1)}, u32[]{:S(2)}, u32[]{:S(2)}) collective-permute-start(bf16[384,1280]{1,0:T(8,128)(2,1)} %add_convert_fusion), channel_id=1, source_target_pairs={{0,2},{1,3},{2,0},{3,1},{4,6},{5,7},{6,4},{7,5},{8,10},{9,11},{10,... | collective-permute-start | bytes 2949128 | tf_op jit(solution)/shard_map/ppermute | solution.py:68
  410.0 28.7 %collective-permute-start.42 = (bf16[96,1280]{1,0:T(8,128)(2,1)}, bf16[96,1280]{1,0:T(8,128)(2,1)S(1)}, u32[]{:S(2)}, u32[]{:S(2)}) collective-permute-start(bf16[96,1280]{1,0:T(8,128)(2,1)} %get-tuple-element.209), channel_id=1, source_target_pairs={{0,1},{1,0},{2,3},{3,2},{4,5},{5,4},{6,7},{7,6},{8,9},{9,8},{10,11... | collective-permute-start | bytes 737288 | tf_op jit(solution)/shard_map/ppermute | solution.py:68
  410.5 29.8 %collective-permute-start.43 = (bf16[96,1280]{1,0:T(8,128)(2,1)}, bf16[96,1280]{1,0:T(8,128)(2,1)}, u32[]{:S(2)}, u32[]{:S(2)}) collective-permute-start(bf16[96,1280]{1,0:T(8,128)(2,1)} %get-tuple-element.208), channel_id=1, source_target_pairs={{0,1},{1,0},{2,3},{3,2},{4,5},{5,4},{6,7},{7,6},{8,9},{9,8},{10,11... | collective-permute-start | bytes 737288 | tf_op jit(solution)/shard_map/ppermute | solution.py:68
  438.6 29.0 %collective-permute-start.56 = (f32[1,160,160]{2,1,0:T(8,128)S(1)}, f32[1,160,160]{2,1,0:T(8,128)}, u32[]{:S(2)}, u32[]{:S(2)}) collective-permute-start(f32[1,160,160]{2,1,0:T(8,128)S(1)} %add.247), channel_id=1, source_target_pairs={{0,2},{1,3},{2,0},{3,1},{4,6},{5,7},{6,4},{7,5},{8,10},{9,11},{10,... | collective-permute-start | bytes 307208 | tf_op jit(solution)/shard_map/ppermute | solution.py:68
  451.4 24.7 %collective-permute-start.53 = (f32[1,160,160]{2,1,0:T(8,128)S(1)}, f32[1,160,160]{2,1,0:T(8,128)}, u32[]{:S(2)}, u32[]{:S(2)}) collective-permute-start(f32[1,160,160]{2,1,0:T(8,128)S(1)} %convolution_bitcast_fusion.3), channel_id=1, source_target_pairs={{0,1},{1,0},{2,3},{3,2},{4,5},{5,4},{6,7},{7,6},{8,9},{9,8},{10,11... | collective-permute-start | bytes 307208 | tf_op jit(solution)/shard_map/ppermute | solution.py:68
  454.0 23.7 %collective-permute-start.59 = (f32[9,1280]{1,0:T(8,128)S(1)}, f32[9,1280]{1,0:T(8,128)S(1)}, u32[]{:S(2)}, u32[]{:S(2)}) collective-permute-start(f32[9,1280]{1,0:T(8,128)S(1)} %select_maximum_fusion), channel_id=1, source_target_pairs={{0,4},{4,0},{8,12},{12,8},{16,20},{20,16},{24,28},{28,24},{1,5},{5... | collective-permute-start | bytes 138248 | tf_op jit(solution)/shard_map/ppermute | solution.py:68
  458.1 37.6 %collective-permute-start.51 = (bf16[160,1408]{1,0:T(8,128)(2,1)}, bf16[160,1408]{1,0:T(8,128)(2,1)S(1)}, u32[]{:S(2)}, u32[]{:S(2)}) collective-permute-start(bf16[160,1408]{1,0:T(8,128)(2,1)} %get-tuple-element.199), channel_id=1, source_target_pairs={{0,8},{4,12},{8,0},{12,4},{16,24},{20,28},{24,16},{28,20},{1,9},{5... | collective-permute-start | bytes 1351688 | tf_op jit(solution)/shard_map/ppermute | solution.py:68
  477.7 12.2 %collective-permute-start.60 = (f32[9,1280]{1,0:T(8,128)S(1)}, f32[9,1280]{1,0:T(8,128)S(1)}, u32[]{:S(2)}, u32[]{:S(2)}) collective-permute-start(f32[9,1280]{1,0:T(8,128)S(1)} %fusion.38), channel_id=1, source_target_pairs={{0,8},{4,12},{8,0},{12,4},{16,24},{20,28},{24,16},{28,20},{1,9},{5... | collective-permute-start | bytes 138248 | tf_op jit(solution)/shard_map/ppermute | solution.py:68
  501.6 9.9 %collective-permute-start.63 = (f32[2,160,160]{2,1,0:T(8,128)S(1)}, f32[2,160,160]{2,1,0:T(8,128)S(1)}, u32[]{:S(2)}, u32[]{:S(2)}) collective-permute-start(f32[2,160,160]{2,1,0:T(8,128)S(1)} %fusion.39), channel_id=1, source_target_pairs={{0,2},{1,3},{2,0},{3,1},{4,6},{5,7},{6,4},{7,5},{8,10},{9,11},{10,... | collective-permute-start | bytes 614408 | tf_op jit(solution)/shard_map/ppermute | solution.py:68
  (88 other events, 901.3 us)
Sparse Core Ops, SparseCore 0:
  10.9 94.9 all-gather.2
  108.6 59.2 all-gather.4
  236.6 77.4 reduce-scatter.2
  318.0 89.0 reduce-scatter.4

commit v5 on v4

--- a/solution.py
+++ b/solution.py
@@ -879,7 +879,7 @@
     far = swap(d_out, "tensor", 2)
     out_mine = jnp.concatenate([d_out, near], axis=0)
     carried = attn_back_call(
-        heads, out_mine, wo, att, qkv, key_bias, lse, block, 0
+        heads, out_mine, wo, att, qkv, key_bias, lse, half, 0
     )
     far = after(far, carried[1])
     output_far = swap(after(pair_sum(down_far[:tok], down_far[tok:]), far), "tensor", 2)
@@ -888,24 +888,24 @@
     raw_wo = (mm(out_mine, att[:half], TN) + mm(out_far, att[half:], TN)).astype(BF16)
     out_later = after(out_far, raw_wo)
     d_qkv, bias_sums = attn_back_call(
-        heads, out_later, wo, att, qkv, key_bias, lse, block, half, carried
-    )
-    raw_wq = mm(attn_in, after(d_qkv, grad_wd, output_far, output_near), TN).astype(BF16)
+        heads, out_later, wo, att, qkv, key_bias, lse, half, half, carried
+    )
+    raw_wq = mm(attn_in, after(d_qkv, output_far, output_near), TN).astype(BF16)
     d_qkv, raw_wq, raw_wo = tie([d_qkv, raw_wq, raw_wo])
     raw_first = jnp.concatenate([raw_wq, raw_wo], axis=1)
     owns, crossed = dp_cross(raw_first)
-    first_far = mm(d_qkv[half:], wq, NT).astype(BF16)
+    first_far = mm(after(d_qkv[half:], grad_wd), wq, NT).astype(BF16)
     far = swap(pair_sum(first_far[:tok], first_far[tok:]), "tensor", 2)
     lined = dp_line(owns, crossed)
     first_mine = mm(after(d_qkv[:half], first_far), wq, NT).astype(BF16)
-    grad_wd = after(grad_wd, first_mine, *crossed)
+    grad_wd = after(grad_wd, first_mine, *crossed[:2])
     mom_down_new, update_down = momentum(mom_down, grad_wd.astype(F32))
     early = polar_call(tensor_sum(gram_of(update_down)[None]))
     new_w_down = applied(w_down, early[0], update_down, STEP_DOWN)
     quarter = tok // PIECES
     sent = [first_mine[tok + k * quarter : tok + k * quarter + quarter] for k in range(PIECES)]
     near = swap_all(sent, "tensor", 1)
-    grad_wu = after(after(grad_wu, first_mine, *crossed), *lined[:2])
+    grad_wu = after(after(grad_wu, first_mine, *crossed), *lined[:3])
     output = (
         residual
         + (down_mine[:tok].astype(F32) + output_near.astype(F32) + output_far.astype(F32))
@@ -921,27 +921,9 @@
         "first_back",
     )
 
-    vec_sums = tensor_sum(sums_one + sums_two)
-    rows_of = jnp.concatenate(
-        [
-            vec_sums[:6],
-            bu_sums[0:1],
-            jnp.pad(bias_sums[:2], ((0, 0), (0, width - padded))),
-        ],
-        axis=0,
-    )
-    rows_of = dp_sum(rows_of)
-    own_cols = lax.dynamic_slice(rows_of, (0, dp_index * own_rows), (7, own_rows))
-    vec_grad = jnp.transpose(own_cols[:6])
-    bu_grad = own_cols[6]
-    bq_grad = jnp.transpose(
-        lax.dynamic_slice(rows_of, (7, dp_index * own_bias), (2, own_bias))
-    )
-
     mom_up_new, update_up = momentum(mom_up, grad_wu.astype(F32))
-    middle = polar_call(tensor_sum(gram_of(update_up)[None]))
-    new_w_up = applied(w_up, middle[0], update_up, STEP_UP)
-    lined = tie(lined, new_w_up, new_w_down, rows_of)
+    gram_up = gram_of(update_up)
+    lined = tie(lined, gram_up, new_w_down, input_grad)
     grad_first = dp_total(lined)
     grad_wq, grad_wo = grad_first[:, :packed], grad_first[:, packed : packed + head_width]
     mom_out_new, update_out = momentum(mom_out, grad_wo)
@@ -951,12 +933,33 @@
     flat = jnp.concatenate(
         [update_qkv[:, 0], jnp.zeros((own_rows, extra), F32), update_qkv[:, 1], update_qkv[:, 2]], axis=1
     )
-    late = tensor_sum(jnp.stack([gram_of(update_out), gram_of(flat)]))
-    late = polar_call(late)
+    vec_tail = (sums_one + sums_two).reshape(-1, own_rows)
+    late = tensor_sum(
+        jnp.concatenate([gram_of(update_out), gram_of(flat), gram_up, vec_tail], axis=0)
+    )
+    vec_sums = late[3 * own_rows :].reshape(8, width)
+    late = polar_call(late[: 3 * own_rows].reshape(3, own_rows, own_rows))
+    new_w_up = applied(w_up, late[2], update_up, STEP_UP)
     new_w_out = applied(w_out, late[0], update_out, STEP_OUT)
     polar_qkv = jnp.dot(late[1], flat, precision=HIGHEST)
     new_w_qkv = w_qkv - STEP_QKV * jnp.stack(
         [polar_qkv[:, spot : spot + head_width] for spot in spots], axis=1
+    )
+
+    rows_of = jnp.concatenate(
+        [
+            vec_sums[:6],
+            bu_sums[0:1],
+            jnp.pad(bias_sums[:2], ((0, 0), (0, width - padded))),
+        ],
+        axis=0,
+    )
+    rows_of = dp_sum(rows_of)
+    own_cols = lax.dynamic_slice(rows_of, (0, dp_index * own_rows), (7, own_rows))
+    vec_grad = jnp.transpose(own_cols[:6])
+    bu_grad = own_cols[6]
+    bq_grad = jnp.transpose(
+        lax.dynamic_slice(rows_of, (7, dp_index * own_bias), (2, own_bias))
     )
 
     vec_rate = VEC_RATE / math.sqrt(tokens)

time: 537 us -> 565 us (1.052)
  local copies, waits for them, and re-layouts: 26.3 us -> 42.6 us
  waiting for transfers between devices: 173 us -> 183 us
  Pallas kernels: 167 us -> 159 us
  matrix products: 63.3 us -> 70.7 us
    ppermute x64 -> x60, waiting for transfers between devices: 173 us -> 183 us  [swap(): return lax.ppermute(value, axis, [(i, i ^ mask) for i in range(size)])]
    pallas_call x3 -> x2, Pallas kernels: 21.6 us -> 15.7 us  [polar_call(): pl.pallas_call(polar_body, out_shape=jax.ShapeDtypeStruct(grams.shape, F3...]
    unnamed x139 -> x165, local copies, waits for them, and re-layouts: 13.9 us -> 17.6 us
    ppermute x64 -> x60, starting transfers between devices: 52.1 us -> 53.4 us  [swap(): return lax.ppermute(value, axis, [(i, i ^ mask) for i in range(size)])]
  transfers between devices with their start and end apart: 68 -> 64, of which waited for: 18 -> 20; matrix products, arithmetic and copies ran while one was open for 17% -> 18% of each run, Pallas kernels for 28% -> 24%
where the time goes in v5:
time: 565 us; the launch traced here: 560 us
  waiting for transfers between devices  183 us (32%)
  Pallas kernels  159 us (28%)
  matrix products  70.7 us (13%)
  starting transfers between devices  53.6 us (9%)
  local copies, waits for them, and re-layouts  42.6 us (8%)
  other arithmetic  36 us (6%)
  between operations  15.8 us (3%)
    ppermute x60, waiting for transfers between devices, swap(): return lax.ppermute(value, axis, [(i, i ^ mask) for i in range(size)])  183 us
    dot_general x10, matrix products, mm(): return lax.dot_general(left, right, dims, preferred_element_type=F32)  55 us
    ppermute x60, starting transfers between devices, swap(): return lax.ppermute(value, axis, [(i, i ^ mask) for i in range(size)])  53.4 us
    pallas_call x2, Pallas kernels, attn_back_call(): pl.pallas_call(partial(attn_back_body, heads, last_part, first), grid=(co...  44.5 us
    pallas_call x3, Pallas kernels, attn_call(): pl.pallas_call(partial(attn_body, heads, emits, len(held)), grid=(count /...  31.2 us
    pallas_call x3, Pallas kernels, mlp_call(): pl.pallas_call(partial(mlp_body, min(256, hidden_width), emits, len(held)...  30.5 us
    unnamed x165, local copies, waits for them, and re-layouts  17.6 us
    pallas_call x3, Pallas kernels, row_call(): pl.pallas_call(partial(row_body, body, len(rows_in)), grid=(PIECES,), in_...  17.5 us
  transfers between devices with their start and end apart: 64, of which 20 were waited for; matrix products, arithmetic and copies ran while one was open for 18% of the time, Pallas kernels for 24%

profile of v5, /device:TPU:0, one launch (start us, length us, event | category | flops | bytes accessed | tf_op | source)
XLA Modules:
  0.0 559.9 jit_solution(6260859474402237429)
XLA Ops:
  11.5 3.0 collective-permute-start.3
  15.1 3.7 collective-permute-start
  21.1 15.6 %collective-permute-done.refs_6_ = bf16[160,1408]{1,0:T(8,128)(2,1)S(1)} collective-permute-done((bf16[160,1408]{1,0:T(8,128)(2,1)S(1)}, bf16[160,1408]{1,0:T(8,128)(2,1)S(1)}, u32[]{:S(2)}, u32[]{:S(2)}) %collective-permute-start) | collective-permute-done | bytes 450592 | tf_op jit(solution)/shard_map/ppermute | solution.py:68
  37.5 15.2 %collective-permute-done.4.refs_2_ = bf16[160,1408]{1,0:T(8,128)(2,1)} collective-permute-done((bf16[160,1408]{1,0:T(8,128)(2,1)S(1)}, bf16[160,1408]{1,0:T(8,128)(2,1)}, u32[]{:S(2)}, u32[]{:S(2)}) %collective-permute-start.4) | collective-permute-done | bytes 450592 | tf_op jit(solution)/shard_map/ppermute | solution.py:68
  54.7 31.1 %collective-permute-done.9.refs_4_ = bf16[160,1408]{1,0:T(8,128)(2,1)} collective-permute-done((bf16[160,1408]{1,0:T(8,128)(2,1)S(1)}, bf16[160,1408]{1,0:T(8,128)(2,1)}, u32[]{:S(2)}, u32[]{:S(2)}) %collective-permute-start.9) | collective-permute-done | bytes 450592 | tf_op jit(solution)/shard_map/ppermute | solution.py:68
  88.0 4.2 collective-permute-done.10.refs_3_
  96.5 3.5 pad_maximum_fusion.x_ref
  100.0 3.3 pad_maximum_fusion.1
  103.3 4.5 collective-permute-done.12.refs_5_
  108.5 4.0 place_rows.1
  115.7 9.8 %norm_qkv.1 = (bf16[1536,1280]{1,0:T(8,128)(2,1)}, bf16[1536,1024]{1,0:T(8,128)(2,1)}) custom-call(bf16[1536,1280]{1,0:T(8,128)(2,1)} %pad_maximum_fusion.x_ref, f32[8,1280]{1,0:T(8,128)} %slice.157.vec_ref.refs_7_.refs_8_, bf16[1280,1024]{1,0:T(8,128)(2,1)} %get-tuple-element.111.w_ref, f32[1,1024]{1,0:T(1,128)} %pad_maximum_fusion.7.bias_ref), custom_call_target="tpu_custom_call" | custom-call | flops 1000000 | bytes 100000 | tf_op jit(solution)/shard_map/norm_qkv/pallas_call | solution.py:109
  125.5 8.1 %attn_fwd.3 = (bf16[1536,384]{1,0:T(8,128)(2,1)}, f32[8,1536]{1,0:T(8,128)}, bf16[96,1280]{1,0:T(8,128)(2,1)}, bf16[96,1280]{1,0:T(8,128)(2,1)}, bf16[96,1280]{1,0:T(8,128)(2,1)}, /*index=5*/bf16[96,1280]{1,0:T(8,128)(2,1)}) custom-call(bf16[1536,1024]{1,0:T(8,128)(2,1)} %get-tuple-element.121.q_ref.qkv_ref, ...), custom_call_target="tpu_custom_call" | custom-call | flops 1000000 | bytes 100000 | tf_op jit(solution)/shard_map/attn_fwd/pallas_call | solution.py:266
  134.7 8.6 %attn_fwd.4 = (bf16[1536,384]{1,0:T(8,128)(2,1)}, f32[8,1536]{1,0:T(8,128)}, bf16[384,1280]{1,0:T(8,128)(2,1)}) custom-call(bf16[1536,1024]{1,0:T(8,128)(2,1)} %get-tuple-element.121.q_ref.qkv_ref, bf16[1536,1024]{1,0:T(8,128)(2,1)} %get-tuple-element.121.q_ref.qkv_ref, ...), custom_call_target="tpu_custom_call", output_to_operand_aliasing={{0}: (4, {}), {1}: (5, {})} | custom-call | flops 1000000 | bytes 100000 | tf_op jit(solution)/shard_map/attn_fwd/pallas_call | solution.py:266
  144.2 2.7 pair_sum.2
  146.9 14.4 %attn_fwd.5 = (bf16[1536,384]{1,0:T(8,128)(2,1)}, f32[8,1536]{1,0:T(8,128)}, bf16[384,1280]{1,0:T(8,128)(2,1)}, bf16[96,1280]{1,0:T(8,128)(2,1)}, bf16[96,1280]{...) custom-call(bf16[1536,1024]{1,0:T(8,128)(2,1)} %get-tuple-element.12, ...), custom_call_target="tpu_custom_call", output_to_operand_aliasing={{0}: (4, {}), {1}: (5, {})} | custom-call | flops 1000000 | bytes 100000 | tf_op jit(solution)/shard_map/attn_fwd/pallas_call | solution.py:266
  163.9 6.9 %collective-permute-done.17.refs_2_ = bf16[384,1280]{1,0:T(8,128)(2,1)S(1)} collective-permute-done((bf16[384,1280]{1,0:T(8,128)(2,1)}, bf16[384,1280]{1,0:T(8,128)(2,1)S(1)}, u32[]{:S(2)}, u32[]{:S(2)}) %collective-permute-start.17) | collective-permute-done | bytes 983072 | tf_op jit(solution)/shard_map/ppermute | solution.py:68
  172.1 4.9 residual.1
  177.3 9.9 %fusion.44.refs_4_.refs_3_ = f32[1536,1280]{1,0:T(8,128)} fusion(bf16[1536,1280]{1,0:T(8,128)(2,1)} %pad_maximum_fusion.1, bf16[1280,1280]{1,0:T(8,128)(2,1)} %all-gather.3.cloned.1.call-done), kind=kOutput, calls=%fused_computation.121 | convolution fusion | flops 5033164800 | bytes 15073280 | tf_op jit(solution)/shard_map/dot_general | solution.py:43
  188.2 14.4 %mlp_up.3 = (bf16[1536,1280]{1,0:T(8,128)(2,1)}, bf16[1536,1280]{1,0:T(8,128)(2,1)}, f32[8,1280]{1,0:T(8,128)}, bf16[384,1280]{1,0:T(8,128)(2,1)}, bf16[96,1280]...) custom-call(bf16[384,1280]{1,0:T(8,128)(2,1)} %get-tuple-element.131.refs_0_, ...), custom_call_target="tpu_custom_call" | custom-call | flops 1000000 | bytes 100000 | tf_op jit(solution)/shard_map/mlp_up/pallas_call | solution.py:471
  206.3 8.0 %mlp_up.4 = (bf16[1536,1280]{1,0:T(8,128)(2,1)}, bf16[1536,1280]{1,0:T(8,128)(2,1)}, f32[8,1280]{1,0:T(8,128)}, bf16[96,1280]{1,0:T(8,128)(2,1)}, bf16[96,1280]{...) custom-call(bf16[384,1280]{1,0:T(8,128)(2,1)} %copy-done.40, ...), custom_call_target="tpu_custom_call", output_to_operand_aliasing={{0}: (4, {}), {1}: (5, {})} | custom-call | flops 1000000 | bytes 100000 | tf_op jit(solution)/shard_map/mlp_up/pallas_call | solution.py:471
  215.3 8.2 %mlp_up.5 = (bf16[1536,1280]{1,0:T(8,128)(2,1)}, bf16[1536,1280]{1,0:T(8,128)(2,1)}, f32[8,1280]{1,0:T(8,128)}, bf16[384,1280]{1,0:T(8,128)(2,1)}) custom-call(bf16[384,1280]{1,0:T(8,128)(2,1)} %copy-done.36, bf16[1280,1280]{1,0:T(8,128)(2,1)} %all-gather.5.cloned.1.call-done.refs_2_.refs_1_, ...), custom_call_target="tpu_custom_call", output_to_operand_aliasing={{0}: (4, {}), {1}: (5, {})} | custom-call | flops 1000000 | bytes 100000 | tf_op jit(solution)/shard_map/mlp_up/pallas_call | solution.py:471
  227.2 9.2 %convolution_convert_fusion.1 = bf16[1280,1280]{1,0:T(8,128)(2,1)} fusion(bf16[1536,1280]{1,0:T(8,128)(2,1)S(1)} %copy-done.13, bf16[1536,1280]{1,0:T(8,128)(2,1)} %get-tuple-element.150), kind=kOutput, calls=%fused_computation.1 | convolution fusion | flops 5034803200 | bytes 11141120 | tf_op jit(solution)/shard_map/dot_general | solution.py:43
  239.2 9.0 %convolution_convert_fusion = bf16[1280,1280]{1,0:T(8,128)(2,1)} fusion(bf16[1536,1280]{1,0:T(8,128)(2,1)} %get-tuple-element.149, bf16[384,1280]{1,0:T(8,128)(2,1)} %copy-done.40, bf16[384,1280]{1,0:T(8,128)(2,1)S(1)} %copy-done.37, bf16[384,1280]{1,0:T(8,128)(2,1)S(1)} %copy-done.39, bf16[384,1280]{1,0:T(8,128)(2,1)S(1)} %copy-done.35), kind=kOutput, calls=%fused_computation | convolution fusion | flops 5050531840 | bytes 11141120 | tf_op jit(solution)/shard_map/dot_general | solution.py:43
  248.3 5.4 convolution_convert_fusion.3
  253.8 2.7 convolution_convert_fusion.4
  256.6 5.3 collective-permute-done.31.refs_2_
  261.8 6.4 %second_back.1 = (f32[384,1280]{1,0:T(8,128)}, bf16[384,1280]{1,0:T(8,128)(2,1)}, f32[8,1280]{1,0:T(8,128)}) custom-call(f32[384,1280]{1,0:T(8,128)} %get-tuple-element.130.refs_0_, bf16[384,1280]{1,0:T(8,128)(2,1)} %get-tuple-element.134.refs_1_, bf16[384,1280]{1,0:T(8,128)(2,1)} %collective-permute-done.31.refs_2_, bf16[384,1280]{1,0:T(8,128)(2,1)} %refs_3_.1, ...), custom_call_target="tpu_custom_call" | custom-call | flops 1000000 | bytes 100000 | tf_op jit(solution)/shard_map/second_back/pallas_call | solution.py:559
  275.2 22.0 %attn_bwd.2 = (bf16[1536,1024]{1,0:T(8,128)(2,1)}, f32[8,384]{1,0:T(8,128)}, f32[1536,384]{1,0:T(8,128)}, f32[1536,384]{1,0:T(8,128)}) custom-call(bf16[768,1280]{1,0:T(8,128)(2,1)} %copy-done.10, bf16[1280,384]{1,0:T(8,128)(2,1)} %get-tuple-element.113.wo_ref, bf16[1536,384]{1,0:T(8,128)(2,1)} %get-tuple-element.160.att_ref, ...), custom_call_target="tpu_custom_call" | custom-call | flops 1000000 | bytes 100000 | tf_op jit(solution)/shard_map/attn_bwd/pallas_call | solution.py:399
  306.9 22.4 %attn_bwd.3 = (bf16[1536,1024]{1,0:T(8,128)(2,1)}, f32[8,384]{1,0:T(8,128)}) custom-call(bf16[768,1280]{1,0:T(8,128)(2,1)} %copy-done.12, bf16[1280,384]{1,0:T(8,128)(2,1)} %get-tuple-element.113.wo_ref, bf16[1536,384]{1,0:T(8,128)(2,1)} %get-tuple-element.160.att_ref, ...), custom_call_target="tpu_custom_call", output_to_operand_aliasing={{0}: (10, {})} | custom-call | flops 1000000 | bytes 100000 | tf_op jit(solution)/shard_map/attn_bwd/pallas_call | solution.py:399
  329.4 8.5 %convolution_convert_fusion.2 = bf16[1280,1024]{1,0:T(8,128)(2,1)S(1)} fusion(bf16[1536,1280]{1,0:T(8,128)(2,1)} %get-tuple-element.170, bf16[1536,1024]{1,0:T(8,128)(2,1)} %get-tuple-element.172), kind=kOutput, calls=%fused_computation.11 | convolution fusion | flops 4027842560 | bytes 9699328 | tf_op jit(solution)/shard_map/dot_general | solution.py:43
  348.6 10.4 %collective-permute-done.52 = bf16[160,1408]{1,0:T(8,128)(2,1)} collective-permute-done((bf16[160,1408]{1,0:T(8,128)(2,1)}, bf16[160,1408]{1,0:T(8,128)(2,1)}, u32[]{:S(2)}, u32[]{:S(2)}) %collective-permute-start.52) | collective-permute-done | bytes 450592 | tf_op jit(solution)/shard_map/ppermute | solution.py:68
  359.1 14.7 %collective-permute-done.50 = bf16[160,1408]{1,0:T(8,128)(2,1)} collective-permute-done((bf16[160,1408]{1,0:T(8,128)(2,1)}, bf16[160,1408]{1,0:T(8,128)(2,1)}, u32[]{:S(2)}, u32[]{:S(2)}) %collective-permute-start.50) | collective-permute-done | bytes 450592 | tf_op jit(solution)/shard_map/ppermute | solution.py:68
  373.8 10.3 %collective-permute-done.48 = bf16[160,1408]{1,0:T(8,128)(2,1)} collective-permute-done((bf16[160,1408]{1,0:T(8,128)(2,1)}, bf16[160,1408]{1,0:T(8,128)(2,1)}, u32[]{:S(2)}, u32[]{:S(2)}) %collective-permute-start.48) | collective-permute-done | bytes 450592 | tf_op jit(solution)/shard_map/ppermute | solution.py:68
  384.1 13.1 %collective-permute-done.46 = bf16[160,1408]{1,0:T(8,128)(2,1)} collective-permute-done((bf16[160,1408]{1,0:T(8,128)(2,1)}, bf16[160,1408]{1,0:T(8,128)(2,1)}, u32[]{:S(2)}, u32[]{:S(2)}) %collective-permute-start.46) | collective-permute-done | bytes 450592 | tf_op jit(solution)/shard_map/ppermute | solution.py:68
  397.2 2.8 convert_add_fusion.5
  400.0 4.5 collective-permute-start.47
  404.5 2.9 collective-permute-start.49
  407.5 4.6 convolution_convert_fusion.6
  418.6 16.7 %collective-permute-done.47 = bf16[160,1408]{1,0:T(8,128)(2,1)S(1)} collective-permute-done((bf16[160,1408]{1,0:T(8,128)(2,1)}, bf16[160,1408]{1,0:T(8,128)(2,1)S(1)}, u32[]{:S(2)}, u32[]{:S(2)}) %collective-permute-start.47) | collective-permute-done | bytes 450592 | tf_op jit(solution)/shard_map/ppermute | solution.py:68
  447.5 21.2 %collective-permute-done.54 = f32[1,160,160]{2,1,0:T(8,128)S(1)} collective-permute-done((f32[1,160,160]{2,1,0:T(8,128)S(1)}, f32[1,160,160]{2,1,0:T(8,128)S(1)}, u32[]{:S(2)}, u32[]{:S(2)}) %collective-permute-start.54) | collective-permute-done | bytes 102432 | tf_op jit(solution)/shard_map/ppermute | solution.py:68
  469.4 6.8 %polar.2 = f32[1,160,160]{2,1,0:T(8,128)} custom-call(f32[1,160,160]{2,1,0:T(8,128)} %add.234.gram_ref), custom_call_target="tpu_custom_call" | custom-call | tf_op jit(solution)/shard_map/polar/pallas_call | solution.py:612
  480.1 6.1 %first_back.1 = (f32[384,1280]{1,0:T(8,128)}, f32[8,1280]{1,0:T(8,128)}) custom-call(bf16[384,1280]{1,0:T(8,128)(2,1)} %refs_0_.3, bf16[384,1280]{1,0:T(8,128)(2,1)} %slice.211.refs_1_, bf16[384,1280]{1,0:T(8,128)(2,1)} %copy-done.41, f32[384,1280]{1,0:T(8,128)} %get-tuple-element.175.refs_3_, bf16[96,1280]{1,0:T(8,128)(2,1)} %copy-done.52, ...), custom_call_target="tpu_custom_call" | custom-call | flops 1000000 | bytes 100000 | tf_op jit(solution)/shard_map/first_back/pallas_call | solution.py:559
  504.5 8.0 %collective-permute-done.56 = f32[544,160]{0,1:T(8,128)S(1)} collective-permute-done((f32[544,160]{0,1:T(8,128)S(1)}, f32[544,160]{0,1:T(8,128)S(1)}, u32[]{:S(2)}, u32[]{:S(2)}) %collective-permute-start.56) | collective-permute-done | bytes 348192 | tf_op jit(solution)/shard_map/ppermute | solution.py:68
  514.3 8.9 %polar.3 = f32[3,160,160]{2,1,0:T(8,128)} custom-call(f32[3,160,160]{2,1,0:T(8,128)} %bitcast.67), custom_call_target="tpu_custom_call" | custom-call | tf_op jit(solution)/shard_map/polar/pallas_call | solution.py:612
  523.2 2.9 fusion.21
  526.1 2.7 convolution_subtract_fusion
  534.6 8.5 %collective-permute-start.58 = (f32[9,1280]{1,0:T(8,128)S(1)}, f32[9,1280]{1,0:T(8,128)S(1)}, u32[]{:S(2)}, u32[]{:S(2)}) collective-permute-start(f32[9,1280]{1,0:T(8,128)S(1)} %fusion.39), channel_id=1, source_target_pairs={{0,8},{4,12},{8,0},{12,4},{16,24},{20,28},{24,16},{28,20},{1,9},{5... | collective-permute-start | bytes 138248 | tf_op jit(solution)/shard_map/ppermute | solution.py:68
  545.5 3.3 collective-permute-start.59
  (368 shorter events, 120.6 us)
Async XLA Ops:
  7.3 163.6 %all-gather.3.cloned.1.call-start = ((), (), s32[]{:S(2)}) async-start(), calls=%async_computation.2 | async-start | bytes 3686400 | tf_op jit(solution)/shard_map/all_gather | solution.py:804
  9.4 167.9 %all-gather.5.cloned.1.call-start = ((), (), s32[]{:S(2)}) async-start(), calls=%async_computation.3 | async-start | bytes 3686400 | tf_op jit(solution)/shard_map/all_gather | solution.py:805
  11.4 396.0 %reduce-scatter.3.cloned.1.call-start = ((), (), s32[]{:S(2)}) async-start(), calls=%async_computation.4 | async-start | bytes 3686400 | tf_op jit(solution)/shard_map/reduce_scatter | solution.py:725
  11.5 42.7 %collective-permute-start.3 = (bf16[384,1280]{1,0:T(8,128)(2,1)S(1)}, bf16[384,1280]{1,0:T(8,128)(2,1)}, u32[]{:S(2)}, u32[]{:S(2)}) collective-permute-start(bf16[384,1280]{1,0:T(8,128)(2,1)S(1)} %copy-done.5), channel_id=1, source_target_pairs={{0,2},{1,3},{2,0},{3,1},{4,6},{5,7},{6,4},{7,5},{8,10},{9,11},{10,... | collective-permute-start | bytes 2949128 | tf_op jit(solution)/shard_map/ppermute | solution.py:68
  15.1 21.6 %collective-permute-start = (bf16[160,1408]{1,0:T(8,128)(2,1)S(1)}, bf16[160,1408]{1,0:T(8,128)(2,1)S(1)}, u32[]{:S(2)}, u32[]{:S(2)}) collective-permute-start(bf16[160,1408]{1,0:T(8,128)(2,1)S(1)} %concatenate.55.refs_0_), channel_id=1, source_target_pairs={{0,24},{4,28},{8,16},{12,20},{16,8},{20,12},{24,0},{28,4},{1,25},{... | collective-permute-start | bytes 1351688 | tf_op jit(solution)/shard_map/ppermute | solution.py:68
  18.8 33.9 %collective-permute-start.4 = (bf16[160,1408]{1,0:T(8,128)(2,1)S(1)}, bf16[160,1408]{1,0:T(8,128)(2,1)}, u32[]{:S(2)}, u32[]{:S(2)}) collective-permute-start(bf16[160,1408]{1,0:T(8,128)(2,1)S(1)} %concatenate.55.refs_0_), channel_id=1, source_target_pairs={{0,8},{4,12},{8,0},{12,4},{16,24},{20,28},{24,16},{28,20},{1,9},{5... | collective-permute-start | bytes 1351688 | tf_op jit(solution)/shard_map/ppermute | solution.py:68
  18.8 33.9 %collective-permute-start.5 = (bf16[160,1408]{1,0:T(8,128)(2,1)S(1)}, bf16[160,1408]{1,0:T(8,128)(2,1)}, u32[]{:S(2)}, u32[]{:S(2)}) collective-permute-start(bf16[160,1408]{1,0:T(8,128)(2,1)S(1)} %concatenate.55.refs_0_), channel_id=1, source_target_pairs={{0,4},{4,0},{8,12},{12,8},{16,20},{20,16},{24,28},{28,24},{1,5},{5... | collective-permute-start | bytes 1351688 | tf_op jit(solution)/shard_map/ppermute | solution.py:68
  20.3 65.5 %collective-permute-start.9 = (bf16[160,1408]{1,0:T(8,128)(2,1)S(1)}, bf16[160,1408]{1,0:T(8,128)(2,1)}, u32[]{:S(2)}, u32[]{:S(2)}) collective-permute-start(bf16[160,1408]{1,0:T(8,128)(2,1)S(1)} %concatenate.55.refs_0_), channel_id=1, source_target_pairs={{0,16},{4,20},{8,24},{12,28},{16,0},{20,4},{24,8},{28,12},{1,17},{... | collective-permute-start | bytes 1351688 | tf_op jit(solution)/shard_map/ppermute | solution.py:68
  37.5 54.7 %collective-permute-start.8 = (bf16[384,1280]{1,0:T(8,128)(2,1)S(1)}, bf16[384,1280]{1,0:T(8,128)(2,1)S(1)}, u32[]{:S(2)}, u32[]{:S(2)}) collective-permute-start(bf16[384,1280]{1,0:T(8,128)(2,1)S(1)} %copy-done.14), channel_id=1, source_target_pairs={{0,2},{1,3},{2,0},{3,1},{4,6},{5,7},{6,4},{7,5},{8,10},{9,11},{10,... | collective-permute-start | bytes 2949128 | tf_op jit(solution)/shard_map/ppermute | solution.py:68
  52.7 43.8 %collective-permute-start.2 = (bf16[384,1280]{1,0:T(8,128)(2,1)S(1)}, bf16[384,1280]{1,0:T(8,128)(2,1)}, u32[]{:S(2)}, u32[]{:S(2)}) collective-permute-start(bf16[384,1280]{1,0:T(8,128)(2,1)S(1)} %copy-done.5), channel_id=1, source_target_pairs={{0,1},{1,0},{2,3},{3,2},{4,5},{5,4},{6,7},{7,6},{8,9},{9,8},{10,11... | collective-permute-start | bytes 2949128 | tf_op jit(solution)/shard_map/ppermute | solution.py:68
  52.7 34.8 %collective-permute-start.1 = (bf16[160,1408]{1,0:T(8,128)(2,1)}, bf16[160,1408]{1,0:T(8,128)(2,1)}, u32[]{:S(2)}, u32[]{:S(2)}) collective-permute-start(bf16[160,1408]{1,0:T(8,128)(2,1)} %copy-done.49), channel_id=1, source_target_pairs={{0,4},{4,0},{8,12},{12,8},{16,20},{20,16},{24,28},{28,24},{1,5},{5... | collective-permute-start | bytes 1351688 | tf_op jit(solution)/shard_map/ppermute | solution.py:68
  54.2 38.0 %collective-permute-start.10 = (bf16[160,1408]{1,0:T(8,128)(2,1)}, bf16[160,1408]{1,0:T(8,128)(2,1)}, u32[]{:S(2)}, u32[]{:S(2)}) collective-permute-start(bf16[160,1408]{1,0:T(8,128)(2,1)} %collective-permute-done.4.refs_2_), channel_id=1, source_target_pairs={{0,4},{4,0},{8,12},{12,8},{16,20},{20,16},{24,28},{28,24},{1,5},{5... | collective-permute-start | bytes 1351688 | tf_op jit(solution)/shard_map/ppermute | solution.py:68
  85.8 10.7 %collective-permute-start.6 = (bf16[384,1280]{1,0:T(8,128)(2,1)}, bf16[384,1280]{1,0:T(8,128)(2,1)}, u32[]{:S(2)}, u32[]{:S(2)}) collective-permute-start(bf16[384,1280]{1,0:T(8,128)(2,1)} %collective-permute-done.3), channel_id=1, source_target_pairs={{0,1},{1,0},{2,3},{3,2},{4,5},{5,4},{6,7},{7,6},{8,9},{9,8},{10,11... | collective-permute-start | bytes 2949128 | tf_op jit(solution)/shard_map/ppermute | solution.py:68
  87.5 12.4 %collective-permute-start.7 = (bf16[384,1280]{1,0:T(8,128)(2,1)S(1)}, bf16[384,1280]{1,0:T(8,128)(2,1)}, u32[]{:S(2)}, u32[]{:S(2)}) collective-permute-start(bf16[384,1280]{1,0:T(8,128)(2,1)S(1)} %copy-done.14), channel_id=1, source_target_pairs={{0,1},{1,0},{2,3},{3,2},{4,5},{5,4},{6,7},{7,6},{8,9},{9,8},{10,11... | collective-permute-start | bytes 2949128 | tf_op jit(solution)/shard_map/ppermute | solution.py:68
  94.2 13.5 %collective-permute-start.12 = (bf16[160,1408]{1,0:T(8,128)(2,1)}, bf16[160,1408]{1,0:T(8,128)(2,1)S(1)}, u32[]{:S(2)}, u32[]{:S(2)}) collective-permute-start(bf16[160,1408]{1,0:T(8,128)(2,1)} %collective-permute-done.9.refs_4_), channel_id=1, source_target_pairs={{0,4},{4,0},{8,12},{12,8},{16,20},{20,16},{24,28},{28,24},{1,5},{5... | collective-permute-start | bytes 1351688 | tf_op jit(solution)/shard_map/ppermute | solution.py:68
  133.6 9.6 %collective-permute-start.13 = (bf16[96,1280]{1,0:T(8,128)(2,1)}, bf16[96,1280]{1,0:T(8,128)(2,1)S(1)}, u32[]{:S(2)}, u32[]{:S(2)}) collective-permute-start(bf16[96,1280]{1,0:T(8,128)(2,1)} %get-tuple-element.117), channel_id=1, source_target_pairs={{0,1},{1,0},{2,3},{3,2},{4,5},{5,4},{6,7},{7,6},{8,9},{9,8},{10,11... | collective-permute-start | bytes 737288 | tf_op jit(solution)/shard_map/ppermute | solution.py:68
  133.6 9.6 %collective-permute-start.14 = (bf16[96,1280]{1,0:T(8,128)(2,1)}, bf16[96,1280]{1,0:T(8,128)(2,1)S(1)}, u32[]{:S(2)}, u32[]{:S(2)}) collective-permute-start(bf16[96,1280]{1,0:T(8,128)(2,1)} %get-tuple-element.118), channel_id=1, source_target_pairs={{0,1},{1,0},{2,3},{3,2},{4,5},{5,4},{6,7},{7,6},{8,9},{9,8},{10,11... | collective-permute-start | bytes 737288 | tf_op jit(solution)/shard_map/ppermute | solution.py:68
  146.9 23.9 %collective-permute-start.17 = (bf16[384,1280]{1,0:T(8,128)(2,1)}, bf16[384,1280]{1,0:T(8,128)(2,1)S(1)}, u32[]{:S(2)}, u32[]{:S(2)}) collective-permute-start(bf16[384,1280]{1,0:T(8,128)(2,1)} %pair_sum.2), channel_id=1, source_target_pairs={{0,2},{1,3},{2,0},{3,1},{4,6},{5,7},{6,4},{7,5},{8,10},{9,11},{10,... | collective-permute-start | bytes 2949128 | tf_op jit(solution)/shard_map/ppermute | solution.py:68
  161.4 9.5 %collective-permute-start.18 = (bf16[96,1280]{1,0:T(8,128)(2,1)}, bf16[96,1280]{1,0:T(8,128)(2,1)S(1)}, u32[]{:S(2)}, u32[]{:S(2)}) collective-permute-start(bf16[96,1280]{1,0:T(8,128)(2,1)} %get-tuple-element.126), channel_id=1, source_target_pairs={{0,1},{1,0},{2,3},{3,2},{4,5},{5,4},{6,7},{7,6},{8,9},{9,8},{10,11... | collective-permute-start | bytes 737288 | tf_op jit(solution)/shard_map/ppermute | solution.py:68
  161.4 9.4 %collective-permute-start.19 = (bf16[96,1280]{1,0:T(8,128)(2,1)}, bf16[96,1280]{1,0:T(8,128)(2,1)S(1)}, u32[]{:S(2)}, u32[]{:S(2)}) collective-permute-start(bf16[96,1280]{1,0:T(8,128)(2,1)} %get-tuple-element.127), channel_id=1, source_target_pairs={{0,1},{1,0},{2,3},{3,2},{4,5},{5,4},{6,7},{7,6},{8,9},{9,8},{10,11... | collective-permute-start | bytes 737288 | tf_op jit(solution)/shard_map/ppermute | solution.py:68
  177.0 25.6 %collective-permute-start.22 = (bf16[384,1280]{1,0:T(8,128)(2,1)}, bf16[384,1280]{1,0:T(8,128)(2,1)S(1)}, u32[]{:S(2)}, u32[]{:S(2)}) collective-permute-start(bf16[384,1280]{1,0:T(8,128)(2,1)} %get-tuple-element.131.refs_0_), channel_id=1, source_target_pairs={{0,2},{1,3},{2,0},{3,1},{4,6},{5,7},{6,4},{7,5},{8,10},{9,11},{10,... | collective-permute-start | bytes 2949128 | tf_op jit(solution)/shard_map/ppermute | solution.py:68
  177.3 9.9 %collective-permute-start.23 = (bf16[384,1280]{1,0:T(8,128)(2,1)}, bf16[384,1280]{1,0:T(8,128)(2,1)S(1)}, u32[]{:S(2)}, u32[]{:S(2)}) collective-permute-start(bf16[384,1280]{1,0:T(8,128)(2,1)} %get-tuple-element.131.refs_0_), channel_id=1, source_target_pairs={{0,1},{1,0},{2,3},{3,2},{4,5},{5,4},{6,7},{7,6},{8,9},{9,8},{10,11... | collective-permute-start | bytes 2949128 | tf_op jit(solution)/shard_map/ppermute | solution.py:68
  236.3 182.3 %reduce-scatter.5.cloned.1.call-start = ((), (), s32[]{:S(2)}) async-start(), calls=%async_computation.5 | async-start | bytes 3686400 | tf_op jit(solution)/shard_map/reduce_scatter | solution.py:725
  236.4 20.1 %collective-permute-start.32 = (bf16[96,1280]{1,0:T(8,128)(2,1)}, bf16[96,1280]{1,0:T(8,128)(2,1)S(1)}, u32[]{:S(2)}, u32[]{:S(2)}) collective-permute-start(bf16[96,1280]{1,0:T(8,128)(2,1)} %get-tuple-element.151), channel_id=1, source_target_pairs={{0,1},{1,0},{2,3},{3,2},{4,5},{5,4},{6,7},{7,6},{8,9},{9,8},{10,11... | collective-permute-start | bytes 737288 | tf_op jit(solution)/shard_map/ppermute | solution.py:68
  236.8 19.7 %collective-permute-start.33 = (bf16[96,1280]{1,0:T(8,128)(2,1)}, bf16[96,1280]{1,0:T(8,128)(2,1)S(1)}, u32[]{:S(2)}, u32[]{:S(2)}) collective-permute-start(bf16[96,1280]{1,0:T(8,128)(2,1)} %get-tuple-element.152), channel_id=1, source_target_pairs={{0,1},{1,0},{2,3},{3,2},{4,5},{5,4},{6,7},{7,6},{8,9},{9,8},{10,11... | collective-permute-start | bytes 737288 | tf_op jit(solution)/shard_map/ppermute | solution.py:68
  237.0 19.6 %collective-permute-start.34 = (bf16[96,1280]{1,0:T(8,128)(2,1)}, bf16[96,1280]{1,0:T(8,128)(2,1)}, u32[]{:S(2)}, u32[]{:S(2)}) collective-permute-start(bf16[96,1280]{1,0:T(8,128)(2,1)} %get-tuple-element.153), channel_id=1, source_target_pairs={{0,1},{1,0},{2,3},{3,2},{4,5},{5,4},{6,7},{7,6},{8,9},{9,8},{10,11... | collective-permute-start | bytes 737288 | tf_op jit(solution)/shard_map/ppermute | solution.py:68
  237.4 19.2 %collective-permute-start.35 = (bf16[96,1280]{1,0:T(8,128)(2,1)}, bf16[96,1280]{1,0:T(8,128)(2,1)}, u32[]{:S(2)}, u32[]{:S(2)}) collective-permute-start(bf16[96,1280]{1,0:T(8,128)(2,1)} %get-tuple-element.154), channel_id=1, source_target_pairs={{0,1},{1,0},{2,3},{3,2},{4,5},{5,4},{6,7},{7,6},{8,9},{9,8},{10,11... | collective-permute-start | bytes 737288 | tf_op jit(solution)/shard_map/ppermute | solution.py:68
  237.5 24.4 %collective-permute-start.31 = (bf16[384,1280]{1,0:T(8,128)(2,1)}, bf16[384,1280]{1,0:T(8,128)(2,1)}, u32[]{:S(2)}, u32[]{:S(2)}) collective-permute-start(bf16[384,1280]{1,0:T(8,128)(2,1)} %pair_sum.3), channel_id=1, source_target_pairs={{0,2},{1,3},{2,0},{3,1},{4,6},{5,7},{6,4},{7,5},{8,10},{9,11},{10,... | collective-permute-start | bytes 2949128 | tf_op jit(solution)/shard_map/ppermute | solution.py:68
  268.3 28.9 %collective-permute-start.36 = (bf16[384,1280]{1,0:T(8,128)(2,1)}, bf16[384,1280]{1,0:T(8,128)(2,1)S(1)}, u32[]{:S(2)}, u32[]{:S(2)}) collective-permute-start(bf16[384,1280]{1,0:T(8,128)(2,1)} %get-tuple-element.159), channel_id=1, source_target_pairs={{0,2},{1,3},{2,0},{3,1},{4,6},{5,7},{6,4},{7,5},{8,10},{9,11},{10,... | collective-permute-start | bytes 2949128 | tf_op jit(solution)/shard_map/ppermute | solution.py:68
  271.2 27.7 %collective-permute-start.30 = (bf16[384,1280]{1,0:T(8,128)(2,1)}, bf16[384,1280]{1,0:T(8,128)(2,1)}, u32[]{:S(2)}, u32[]{:S(2)}) collective-permute-start(bf16[384,1280]{1,0:T(8,128)(2,1)} %slice.210), channel_id=1, source_target_pairs={{0,1},{1,0},{2,3},{3,2},{4,5},{5,4},{6,7},{7,6},{8,9},{9,8},{10,11... | collective-permute-start | bytes 2949128 | tf_op jit(solution)/shard_map/ppermute | solution.py:68
  298.6 30.8 %collective-permute-start.29 = (bf16[384,1280]{1,0:T(8,128)(2,1)}, bf16[384,1280]{1,0:T(8,128)(2,1)S(1)}, u32[]{:S(2)}, u32[]{:S(2)}) collective-permute-start(bf16[384,1280]{1,0:T(8,128)(2,1)} %slice.208), channel_id=1, source_target_pairs={{0,1},{1,0},{2,3},{3,2},{4,5},{5,4},{6,7},{7,6},{8,9},{9,8},{10,11... | collective-permute-start | bytes 2949128 | tf_op jit(solution)/shard_map/ppermute | solution.py:68
  300.7 28.7 %collective-permute-start.38 = (bf16[384,1280]{1,0:T(8,128)(2,1)S(1)}, bf16[384,1280]{1,0:T(8,128)(2,1)S(1)}, u32[]{:S(2)}, u32[]{:S(2)}) collective-permute-start(bf16[384,1280]{1,0:T(8,128)(2,1)S(1)} %add_convert_fusion.1), channel_id=1, source_target_pairs={{0,2},{1,3},{2,0},{3,1},{4,6},{5,7},{6,4},{7,5},{8,10},{9,11},{10,... | collective-permute-start | bytes 2949128 | tf_op jit(solution)/shard_map/ppermute | solution.py:68
  342.5 16.5 %collective-permute-start.52 = (bf16[160,1408]{1,0:T(8,128)(2,1)}, bf16[160,1408]{1,0:T(8,128)(2,1)}, u32[]{:S(2)}, u32[]{:S(2)}) collective-permute-start(bf16[160,1408]{1,0:T(8,128)(2,1)} %get-tuple-element.204), channel_id=1, source_target_pairs={{0,4},{4,0},{8,12},{12,8},{16,20},{20,16},{24,28},{28,24},{1,5},{5... | collective-permute-start | bytes 1351688 | tf_op jit(solution)/shard_map/ppermute | solution.py:68
  344.2 29.6 %collective-permute-start.50 = (bf16[160,1408]{1,0:T(8,128)(2,1)}, bf16[160,1408]{1,0:T(8,128)(2,1)}, u32[]{:S(2)}, u32[]{:S(2)}) collective-permute-start(bf16[160,1408]{1,0:T(8,128)(2,1)} %get-tuple-element.205), channel_id=1, source_target_pairs={{0,4},{4,0},{8,12},{12,8},{16,20},{20,16},{24,28},{28,24},{1,5},{5... | collective-permute-start | bytes 1351688 | tf_op jit(solution)/shard_map/ppermute | solution.py:68
  344.6 39.6 %collective-permute-start.48 = (bf16[160,1408]{1,0:T(8,128)(2,1)}, bf16[160,1408]{1,0:T(8,128)(2,1)}, u32[]{:S(2)}, u32[]{:S(2)}) collective-permute-start(bf16[160,1408]{1,0:T(8,128)(2,1)} %get-tuple-element.206), channel_id=1, source_target_pairs={{0,4},{4,0},{8,12},{12,8},{16,20},{20,16},{24,28},{28,24},{1,5},{5... | collective-permute-start | bytes 1351688 | tf_op jit(solution)/shard_map/ppermute | solution.py:68
  346.2 51.0 %collective-permute-start.46 = (bf16[160,1408]{1,0:T(8,128)(2,1)}, bf16[160,1408]{1,0:T(8,128)(2,1)}, u32[]{:S(2)}, u32[]{:S(2)}) collective-permute-start(bf16[160,1408]{1,0:T(8,128)(2,1)} %get-tuple-element.207), channel_id=1, source_target_pairs={{0,4},{4,0},{8,12},{12,8},{16,20},{20,16},{24,28},{28,24},{1,5},{5... | collective-permute-start | bytes 1351688 | tf_op jit(solution)/shard_map/ppermute | solution.py:68
  400.0 35.3 %collective-permute-start.47 = (bf16[160,1408]{1,0:T(8,128)(2,1)}, bf16[160,1408]{1,0:T(8,128)(2,1)S(1)}, u32[]{:S(2)}, u32[]{:S(2)}) collective-permute-start(bf16[160,1408]{1,0:T(8,128)(2,1)} %get-tuple-element.203), channel_id=1, source_target_pairs={{0,16},{4,20},{8,24},{12,28},{16,0},{20,4},{24,8},{28,12},{1,17},{... | collective-permute-start | bytes 1351688 | tf_op jit(solution)/shard_map/ppermute | solution.py:68
  404.5 30.8 %collective-permute-start.49 = (bf16[160,1408]{1,0:T(8,128)(2,1)}, bf16[160,1408]{1,0:T(8,128)(2,1)}, u32[]{:S(2)}, u32[]{:S(2)}) collective-permute-start(bf16[160,1408]{1,0:T(8,128)(2,1)} %get-tuple-element.202), channel_id=1, source_target_pairs={{0,24},{4,28},{8,16},{12,20},{16,8},{20,12},{24,0},{28,4},{1,25},{... | collective-permute-start | bytes 1351688 | tf_op jit(solution)/shard_map/ppermute | solution.py:68
  407.5 28.1 %collective-permute-start.51 = (bf16[160,1408]{1,0:T(8,128)(2,1)}, bf16[160,1408]{1,0:T(8,128)(2,1)}, u32[]{:S(2)}, u32[]{:S(2)}) collective-permute-start(bf16[160,1408]{1,0:T(8,128)(2,1)} %get-tuple-element.201), channel_id=1, source_target_pairs={{0,8},{4,12},{8,0},{12,4},{16,24},{20,28},{24,16},{28,20},{1,9},{5... | collective-permute-start | bytes 1351688 | tf_op jit(solution)/shard_map/ppermute | solution.py:68
  413.7 24.8 %collective-permute-start.40 = (bf16[384,1280]{1,0:T(8,128)(2,1)}, bf16[384,1280]{1,0:T(8,128)(2,1)S(1)}, u32[]{:S(2)}, u32[]{:S(2)}) collective-permute-start(bf16[384,1280]{1,0:T(8,128)(2,1)} %slice.213), channel_id=1, source_target_pairs={{0,1},{1,0},{2,3},{3,2},{4,5},{5,4},{6,7},{7,6},{8,9},{9,8},{10,11... | collective-permute-start | bytes 2949128 | tf_op jit(solution)/shard_map/ppermute | solution.py:68
  418.1 60.7 %collective-permute-start.42 = (bf16[96,1280]{1,0:T(8,128)(2,1)}, bf16[96,1280]{1,0:T(8,128)(2,1)S(1)}, u32[]{:S(2)}, u32[]{:S(2)}) collective-permute-start(bf16[96,1280]{1,0:T(8,128)(2,1)} %get-tuple-element.213), channel_id=1, source_target_pairs={{0,1},{1,0},{2,3},{3,2},{4,5},{5,4},{6,7},{7,6},{8,9},{9,8},{10,11... | collective-permute-start | bytes 737288 | tf_op jit(solution)/shard_map/ppermute | solution.py:68
  440.9 38.0 %collective-permute-start.41 = (bf16[384,1280]{1,0:T(8,128)(2,1)}, bf16[384,1280]{1,0:T(8,128)(2,1)S(1)}, u32[]{:S(2)}, u32[]{:S(2)}) collective-permute-start(bf16[384,1280]{1,0:T(8,128)(2,1)} %add_convert_fusion), channel_id=1, source_target_pairs={{0,2},{1,3},{2,0},{3,1},{4,6},{5,7},{6,4},{7,5},{8,10},{9,11},{10,... | collective-permute-start | bytes 2949128 | tf_op jit(solution)/shard_map/ppermute | solution.py:68
  443.3 25.4 %collective-permute-start.54 = (f32[1,160,160]{2,1,0:T(8,128)S(1)}, f32[1,160,160]{2,1,0:T(8,128)S(1)}, u32[]{:S(2)}, u32[]{:S(2)}) collective-permute-start(f32[1,160,160]{2,1,0:T(8,128)S(1)} %add.233), channel_id=1, source_target_pairs={{0,2},{1,3},{2,0},{3,1},{4,6},{5,7},{6,4},{7,5},{8,10},{9,11},{10,... | collective-permute-start | bytes 307208 | tf_op jit(solution)/shard_map/ppermute | solution.py:68
  447.0 31.9 %collective-permute-start.43 = (bf16[96,1280]{1,0:T(8,128)(2,1)}, bf16[96,1280]{1,0:T(8,128)(2,1)S(1)}, u32[]{:S(2)}, u32[]{:S(2)}) collective-permute-start(bf16[96,1280]{1,0:T(8,128)(2,1)} %get-tuple-element.212), channel_id=1, source_target_pairs={{0,1},{1,0},{2,3},{3,2},{4,5},{5,4},{6,7},{7,6},{8,9},{9,8},{10,11... | collective-permute-start | bytes 737288 | tf_op jit(solution)/shard_map/ppermute | solution.py:68
  447.0 31.9 %collective-permute-start.44 = (bf16[96,1280]{1,0:T(8,128)(2,1)}, bf16[96,1280]{1,0:T(8,128)(2,1)S(1)}, u32[]{:S(2)}, u32[]{:S(2)}) collective-permute-start(bf16[96,1280]{1,0:T(8,128)(2,1)} %get-tuple-element.211), channel_id=1, source_target_pairs={{0,1},{1,0},{2,3},{3,2},{4,5},{5,4},{6,7},{7,6},{8,9},{9,8},{10,11... | collective-permute-start | bytes 737288 | tf_op jit(solution)/shard_map/ppermute | solution.py:68
  468.7 10.2 %collective-permute-start.45 = (bf16[96,1280]{1,0:T(8,128)(2,1)S(1)}, bf16[96,1280]{1,0:T(8,128)(2,1)S(1)}, u32[]{:S(2)}, u32[]{:S(2)}) collective-permute-start(bf16[96,1280]{1,0:T(8,128)(2,1)S(1)} %copy-done.53), channel_id=1, source_target_pairs={{0,1},{1,0},{2,3},{3,2},{4,5},{5,4},{6,7},{7,6},{8,9},{9,8},{10,11... | collective-permute-start | bytes 737288 | tf_op jit(solution)/shard_map/ppermute | solution.py:68
  500.7 11.8 %collective-permute-start.56 = (f32[544,160]{0,1:T(8,128)S(1)}, f32[544,160]{0,1:T(8,128)S(1)}, u32[]{:S(2)}, u32[]{:S(2)}) collective-permute-start(f32[544,160]{0,1:T(8,128)S(1)} %fusion.60), channel_id=1, source_target_pairs={{0,2},{1,3},{2,0},{3,1},{4,6},{5,7},{6,4},{7,5},{8,10},{9,11},{10,... | collective-permute-start | bytes 1044488 | tf_op jit(solution)/shard_map/ppermute | solution.py:68
  534.6 10.9 %collective-permute-start.58 = (f32[9,1280]{1,0:T(8,128)S(1)}, f32[9,1280]{1,0:T(8,128)S(1)}, u32[]{:S(2)}, u32[]{:S(2)}) collective-permute-start(f32[9,1280]{1,0:T(8,128)S(1)} %fusion.39), channel_id=1, source_target_pairs={{0,8},{4,12},{8,0},{12,4},{16,24},{20,28},{24,16},{28,20},{1,9},{5... | collective-permute-start | bytes 138248 | tf_op jit(solution)/shard_map/ppermute | solution.py:68
  (97 other events, 934.3 us)
Sparse Core Ops, SparseCore 0:
  10.9 94.9 all-gather.2
  108.6 59.2 all-gather.4
  236.5 77.4 reduce-scatter.2
  317.9 88.1 reduce-scatter.4

commit v6 on v4

--- a/solution.py
+++ b/solution.py
@@ -874,12 +874,11 @@
         1,
         "second_back",
     )
-    block = tok * 2 // 3
     near = swap(d_out, "tensor", 1)
     far = swap(d_out, "tensor", 2)
     out_mine = jnp.concatenate([d_out, near], axis=0)
     carried = attn_back_call(
-        heads, out_mine, wo, att, qkv, key_bias, lse, block, 0
+        heads, out_mine, wo, att, qkv, key_bias, lse, half, 0
     )
     far = after(far, carried[1])
     output_far = swap(after(pair_sum(down_far[:tok], down_far[tok:]), far), "tensor", 2)
@@ -888,24 +887,19 @@
     raw_wo = (mm(out_mine, att[:half], TN) + mm(out_far, att[half:], TN)).astype(BF16)
     out_later = after(out_far, raw_wo)
     d_qkv, bias_sums = attn_back_call(
-        heads, out_later, wo, att, qkv, key_bias, lse, block, half, carried
-    )
-    raw_wq = mm(attn_in, after(d_qkv, grad_wd, output_far, output_near), TN).astype(BF16)
+        heads, out_later, wo, att, qkv, key_bias, lse, half, half, carried
+    )
+    d_qkv = after(d_qkv, output_far, output_near)
+    first_far = mm(d_qkv[half:], wq, NT).astype(BF16)
+    raw_wq = mm(attn_in, after(d_qkv, grad_wd, first_far), TN).astype(BF16)
+    first_total = pair_sum(first_far[:tok], first_far[tok:])
+    far = swap(first_total, "tensor", 2)
     d_qkv, raw_wq, raw_wo = tie([d_qkv, raw_wq, raw_wo])
-    raw_first = jnp.concatenate([raw_wq, raw_wo], axis=1)
-    owns, crossed = dp_cross(raw_first)
-    first_far = mm(d_qkv[half:], wq, NT).astype(BF16)
-    far = swap(pair_sum(first_far[:tok], first_far[tok:]), "tensor", 2)
-    lined = dp_line(owns, crossed)
-    first_mine = mm(after(d_qkv[:half], first_far), wq, NT).astype(BF16)
-    grad_wd = after(grad_wd, first_mine, *crossed)
-    mom_down_new, update_down = momentum(mom_down, grad_wd.astype(F32))
-    early = polar_call(tensor_sum(gram_of(update_down)[None]))
-    new_w_down = applied(w_down, early[0], update_down, STEP_DOWN)
+    owns, crossed = dp_cross(jnp.concatenate([raw_wq, raw_wo], axis=1))
+    first_mine = mm(after(d_qkv[:half], first_total), wq, NT).astype(BF16)
     quarter = tok // PIECES
     sent = [first_mine[tok + k * quarter : tok + k * quarter + quarter] for k in range(PIECES)]
     near = swap_all(sent, "tensor", 1)
-    grad_wu = after(after(grad_wu, first_mine, *crossed), *lined[:2])
     output = (
         residual
         + (down_mine[:tok].astype(F32) + output_near.astype(F32) + output_far.astype(F32))
@@ -938,10 +932,16 @@
         lax.dynamic_slice(rows_of, (7, dp_index * own_bias), (2, own_bias))
     )
 
+    lined = dp_line(owns, tie(crossed, input_grad))
+    grad_wd = after(grad_wd, first_mine, lined[-1])
+    mom_down_new, update_down = momentum(mom_down, grad_wd.astype(F32))
+    early = polar_call(tensor_sum(gram_of(update_down)[None]))
+    new_w_down = applied(w_down, early[0], update_down, STEP_DOWN)
+    grad_wu = after(after(grad_wu, first_mine, *crossed), *lined[:3])
+
     mom_up_new, update_up = momentum(mom_up, grad_wu.astype(F32))
-    middle = polar_call(tensor_sum(gram_of(update_up)[None]))
-    new_w_up = applied(w_up, middle[0], update_up, STEP_UP)
-    lined = tie(lined, new_w_up, new_w_down, rows_of)
+    gram_up = gram_of(update_up)
+    lined = tie(lined, gram_up, new_w_down, rows_of)
     grad_first = dp_total(lined)
     grad_wq, grad_wo = grad_first[:, :packed], grad_first[:, packed : packed + head_width]
     mom_out_new, update_out = momentum(mom_out, grad_wo)
@@ -951,9 +951,10 @@
     flat = jnp.concatenate(
         [update_qkv[:, 0], jnp.zeros((own_rows, extra), F32), update_qkv[:, 1], update_qkv[:, 2]], axis=1
     )
-    late = tensor_sum(jnp.stack([gram_of(update_out), gram_of(flat)]))
+    late = tensor_sum(jnp.stack([gram_of(update_out), gram_of(flat), gram_up]))
     late = polar_call(late)
     new_w_out = applied(w_out, late[0], update_out, STEP_OUT)
+    new_w_up = applied(w_up, late[2], update_up, STEP_UP)
     polar_qkv = jnp.dot(late[1], flat, precision=HIGHEST)
     new_w_qkv = w_qkv - STEP_QKV * jnp.stack(
         [polar_qkv[:, spot : spot + head_width] for spot in spots], axis=1

time: 537 us -> 534 us (level)
  waiting for transfers between devices: 173 us -> 184 us
  Pallas kernels: 167 us -> 159 us
  starting transfers between devices: 52.2 us -> 44.2 us
    ppermute x64 -> x62, waiting for transfers between devices: 173 us -> 184 us  [swap(): return lax.ppermute(value, axis, [(i, i ^ mask) for i in range(size)])]
    ppermute x64 -> x62, starting transfers between devices: 52.1 us -> 44 us  [swap(): return lax.ppermute(value, axis, [(i, i ^ mask) for i in range(size)])]
    pallas_call x3 -> x2, Pallas kernels: 21.6 us -> 15.9 us  [polar_call(): pl.pallas_call(polar_body, out_shape=jax.ShapeDtypeStruct(grams.shape, F3...]
    unnamed x139 -> x151, local copies, waits for them, and re-layouts: 13.9 us -> 15.2 us
  transfers between devices with their start and end apart: 68 -> 66, of which waited for: 18 -> 17; matrix products, arithmetic and copies ran while one was open for 17% -> 18% of each run, Pallas kernels for 28% -> 27%
where the time goes in v6:
time: 534 us; the launch traced here: 529 us
  waiting for transfers between devices  184 us (34%)
  Pallas kernels  159 us (30%)
  matrix products  65.3 us (12%)
  starting transfers between devices  44.2 us (8%)
  other arithmetic  32.4 us (6%)
  local copies, waits for them, and re-layouts  27 us (5%)
  between operations  15.9 us (3%)
    ppermute x62, waiting for transfers between devices, swap(): return lax.ppermute(value, axis, [(i, i ^ mask) for i in range(size)])  184 us
    dot_general x10, matrix products, mm(): return lax.dot_general(left, right, dims, preferred_element_type=F32)  53.1 us
    pallas_call x2, Pallas kernels, attn_back_call(): pl.pallas_call(partial(attn_back_body, heads, last_part, first), grid=(co...  44.7 us
    ppermute x62, starting transfers between devices, swap(): return lax.ppermute(value, axis, [(i, i ^ mask) for i in range(size)])  44 us
    pallas_call x3, Pallas kernels, attn_call(): pl.pallas_call(partial(attn_body, heads, emits, len(held)), grid=(count /...  31.2 us
    pallas_call x3, Pallas kernels, mlp_call(): pl.pallas_call(partial(mlp_body, min(256, hidden_width), emits, len(held)...  30.3 us
    pallas_call x3, Pallas kernels, row_call(): pl.pallas_call(partial(row_body, body, len(rows_in)), grid=(PIECES,), in_...  17.9 us
    pallas_call x2, Pallas kernels, polar_call(): pl.pallas_call(polar_body, out_shape=jax.ShapeDtypeStruct(grams.shape, F3...  15.9 us
  transfers between devices with their start and end apart: 66, of which 17 were waited for; matrix products, arithmetic and copies ran while one was open for 18% of the time, Pallas kernels for 27%

profile of v6, /device:TPU:0, one launch (start us, length us, event | category | flops | bytes accessed | tf_op | source)
XLA Modules:
  0.0 528.6 jit_solution(14198571466283408325)
XLA Ops:
  11.5 3.0 collective-permute-start.3
  15.1 3.7 collective-permute-start
  21.1 15.6 %collective-permute-done.refs_6_ = bf16[160,1408]{1,0:T(8,128)(2,1)S(1)} collective-permute-done((bf16[160,1408]{1,0:T(8,128)(2,1)S(1)}, bf16[160,1408]{1,0:T(8,128)(2,1)S(1)}, u32[]{:S(2)}, u32[]{:S(2)}) %collective-permute-start) | collective-permute-done | bytes 450592 | tf_op jit(solution)/shard_map/ppermute | solution.py:68
  36.7 16.0 %collective-permute-done.4.refs_2_ = bf16[160,1408]{1,0:T(8,128)(2,1)} collective-permute-done((bf16[160,1408]{1,0:T(8,128)(2,1)S(1)}, bf16[160,1408]{1,0:T(8,128)(2,1)}, u32[]{:S(2)}, u32[]{:S(2)}) %collective-permute-start.4) | collective-permute-done | bytes 450592 | tf_op jit(solution)/shard_map/ppermute | solution.py:68
  54.7 31.1 %collective-permute-done.9.refs_4_ = bf16[160,1408]{1,0:T(8,128)(2,1)} collective-permute-done((bf16[160,1408]{1,0:T(8,128)(2,1)S(1)}, bf16[160,1408]{1,0:T(8,128)(2,1)}, u32[]{:S(2)}, u32[]{:S(2)}) %collective-permute-start.9) | collective-permute-done | bytes 450592 | tf_op jit(solution)/shard_map/ppermute | solution.py:68
  87.6 4.2 collective-permute-done.10.refs_3_
  95.3 3.5 pad_maximum_fusion.x_ref
  98.8 3.5 pad_maximum_fusion.1
  102.3 4.3 collective-permute-done.12.refs_5_
  107.3 4.0 place_rows.1
  114.5 9.9 %norm_qkv.1 = (bf16[1536,1280]{1,0:T(8,128)(2,1)}, bf16[1536,1024]{1,0:T(8,128)(2,1)}) custom-call(bf16[1536,1280]{1,0:T(8,128)(2,1)} %pad_maximum_fusion.x_ref, f32[8,1280]{1,0:T(8,128)} %slice.149.vec_ref.refs_7_.refs_8_, bf16[1280,1024]{1,0:T(8,128)(2,1)} %get-tuple-element.115.w_ref, f32[1,1024]{1,0:T(1,128)} %pad_maximum_fusion.7.bias_ref), custom_call_target="tpu_custom_call" | custom-call | flops 1000000 | bytes 100000 | tf_op jit(solution)/shard_map/norm_qkv/pallas_call | solution.py:109
  124.4 8.1 %attn_fwd.3 = (bf16[1536,384]{1,0:T(8,128)(2,1)}, f32[8,1536]{1,0:T(8,128)}, bf16[96,1280]{1,0:T(8,128)(2,1)}, bf16[96,1280]{1,0:T(8,128)(2,1)}, bf16[96,1280]{1,0:T(8,128)(2,1)}, /*index=5*/bf16[96,1280]{1,0:T(8,128)(2,1)}) custom-call(bf16[1536,1024]{1,0:T(8,128)(2,1)} %get-tuple-element.125.q_ref.qkv_ref, ...), custom_call_target="tpu_custom_call" | custom-call | flops 1000000 | bytes 100000 | tf_op jit(solution)/shard_map/attn_fwd/pallas_call | solution.py:266
  133.6 8.4 %attn_fwd.4 = (bf16[1536,384]{1,0:T(8,128)(2,1)}, f32[8,1536]{1,0:T(8,128)}, bf16[384,1280]{1,0:T(8,128)(2,1)}) custom-call(bf16[1536,1024]{1,0:T(8,128)(2,1)} %get-tuple-element.125.q_ref.qkv_ref, bf16[1536,1024]{1,0:T(8,128)(2,1)} %get-tuple-element.125.q_ref.qkv_ref, ...), custom_call_target="tpu_custom_call", output_to_operand_aliasing={{0}: (4, {}), {1}: (5, {})} | custom-call | flops 1000000 | bytes 100000 | tf_op jit(solution)/shard_map/attn_fwd/pallas_call | solution.py:266
  142.9 2.7 pair_sum.2
  145.7 14.7 %attn_fwd.5 = (bf16[1536,384]{1,0:T(8,128)(2,1)}, f32[8,1536]{1,0:T(8,128)}, bf16[384,1280]{1,0:T(8,128)(2,1)}, bf16[96,1280]{1,0:T(8,128)(2,1)}, bf16[96,1280]{...) custom-call(bf16[1536,1024]{1,0:T(8,128)(2,1)} %get-tuple-element.12, ...), custom_call_target="tpu_custom_call", output_to_operand_aliasing={{0}: (4, {}), {1}: (5, {})} | custom-call | flops 1000000 | bytes 100000 | tf_op jit(solution)/shard_map/attn_fwd/pallas_call | solution.py:266
  163.5 5.9 %collective-permute-done.17.refs_2_ = bf16[384,1280]{1,0:T(8,128)(2,1)S(1)} collective-permute-done((bf16[384,1280]{1,0:T(8,128)(2,1)}, bf16[384,1280]{1,0:T(8,128)(2,1)S(1)}, u32[]{:S(2)}, u32[]{:S(2)}) %collective-permute-start.17) | collective-permute-done | bytes 983072 | tf_op jit(solution)/shard_map/ppermute | solution.py:68
  170.6 5.0 residual.1
  175.8 9.9 %fusion.43.refs_4_.refs_3_ = f32[1536,1280]{1,0:T(8,128)} fusion(bf16[1536,1280]{1,0:T(8,128)(2,1)} %pad_maximum_fusion.1, bf16[1280,1280]{1,0:T(8,128)(2,1)} %all-gather.3.cloned.1.call-done), kind=kOutput, calls=%fused_computation.123 | convolution fusion | flops 5033164800 | bytes 15073280 | tf_op jit(solution)/shard_map/dot_general | solution.py:43
  186.7 14.2 %mlp_up.3 = (bf16[1536,1280]{1,0:T(8,128)(2,1)}, bf16[1536,1280]{1,0:T(8,128)(2,1)}, f32[8,1280]{1,0:T(8,128)}, bf16[384,1280]{1,0:T(8,128)(2,1)}, bf16[96,1280]...) custom-call(bf16[384,1280]{1,0:T(8,128)(2,1)} %get-tuple-element.135.refs_0_, ...), custom_call_target="tpu_custom_call" | custom-call | flops 1000000 | bytes 100000 | tf_op jit(solution)/shard_map/mlp_up/pallas_call | solution.py:471
  204.6 8.0 %mlp_up.4 = (bf16[1536,1280]{1,0:T(8,128)(2,1)}, bf16[1536,1280]{1,0:T(8,128)(2,1)}, f32[8,1280]{1,0:T(8,128)}, bf16[96,1280]{1,0:T(8,128)(2,1)}, bf16[96,1280]{...) custom-call(bf16[384,1280]{1,0:T(8,128)(2,1)} %copy-done.35, ...), custom_call_target="tpu_custom_call", output_to_operand_aliasing={{0}: (4, {}), {1}: (5, {})} | custom-call | flops 1000000 | bytes 100000 | tf_op jit(solution)/shard_map/mlp_up/pallas_call | solution.py:471
  214.0 8.2 %mlp_up.5 = (bf16[1536,1280]{1,0:T(8,128)(2,1)}, bf16[1536,1280]{1,0:T(8,128)(2,1)}, f32[8,1280]{1,0:T(8,128)}, bf16[384,1280]{1,0:T(8,128)(2,1)}) custom-call(bf16[384,1280]{1,0:T(8,128)(2,1)} %copy-done.31, bf16[1280,1280]{1,0:T(8,128)(2,1)} %all-gather.5.cloned.1.call-done.refs_2_.refs_1_, ...), custom_call_target="tpu_custom_call", output_to_operand_aliasing={{0}: (4, {}), {1}: (5, {})} | custom-call | flops 1000000 | bytes 100000 | tf_op jit(solution)/shard_map/mlp_up/pallas_call | solution.py:471
  223.6 2.7 pair_sum.3
  228.1 8.9 %convolution_convert_fusion.1 = bf16[1280,1280]{1,0:T(8,128)(2,1)} fusion(bf16[1536,1280]{1,0:T(8,128)(2,1)S(1)} %copy-done.10, bf16[1536,1280]{1,0:T(8,128)(2,1)} %get-tuple-element.154), kind=kOutput, calls=%fused_computation.1 | convolution fusion | flops 5034803200 | bytes 11141120 | tf_op jit(solution)/shard_map/dot_general | solution.py:43
  238.8 9.4 %convolution_convert_fusion = bf16[1280,1280]{1,0:T(8,128)(2,1)} fusion(bf16[1536,1280]{1,0:T(8,128)(2,1)} %get-tuple-element.153, bf16[384,1280]{1,0:T(8,128)(2,1)} %copy-done.35, bf16[384,1280]{1,0:T(8,128)(2,1)S(1)} %copy-done.32, bf16[384,1280]{1,0:T(8,128)(2,1)S(1)} %copy-done.34, bf16[384,1280]{1,0:T(8,128)(2,1)S(1)} %copy-done.30), kind=kOutput, calls=%fused_computation | convolution fusion | flops 5050531840 | bytes 11141120 | tf_op jit(solution)/shard_map/dot_general | solution.py:43
  248.3 5.4 %convolution_convert_fusion.3 = bf16[768,1280]{1,0:T(8,128)(2,1)S(1)} fusion(bf16[1280,1280]{1,0:T(8,128)(2,1)} %all-gather.3.cloned.1.call-done, bf16[1536,1280]{1,0:T(8,128)(2,1)} %get-tuple-element.154), kind=kOutput, calls=%fused_computation.12 | convolution fusion | flops 2517565440 | bytes 7208960 | tf_op jit(solution)/shard_map/dot_general | solution.py:43
  253.7 2.7 convolution_convert_fusion.4
  256.5 6.8 %second_back.1 = (f32[384,1280]{1,0:T(8,128)}, bf16[384,1280]{1,0:T(8,128)(2,1)}, f32[8,1280]{1,0:T(8,128)}) custom-call(f32[384,1280]{1,0:T(8,128)} %get-tuple-element.134.refs_0_, bf16[384,1280]{1,0:T(8,128)(2,1)} %get-tuple-element.138.refs_1_, bf16[384,1280]{1,0:T(8,128)(2,1)} %collective-permute-done.31.refs_2_, bf16[384,1280]{1,0:T(8,128)(2,1)} %refs_3_.1, ...), custom_call_target="tpu_custom_call" | custom-call | flops 1000000 | bytes 100000 | tf_op jit(solution)/shard_map/second_back/pallas_call | solution.py:559
  267.5 21.9 %attn_bwd.2 = (bf16[1536,1024]{1,0:T(8,128)(2,1)}, f32[8,384]{1,0:T(8,128)}, f32[1536,384]{1,0:T(8,128)}, f32[1536,384]{1,0:T(8,128)}) custom-call(bf16[768,1280]{1,0:T(8,128)(2,1)} %copy-done.7, bf16[1280,384]{1,0:T(8,128)(2,1)} %get-tuple-element.117.wo_ref, bf16[1536,384]{1,0:T(8,128)(2,1)} %get-tuple-element.164.att_ref, ...), custom_call_target="tpu_custom_call" | custom-call | flops 1000000 | bytes 100000 | tf_op jit(solution)/shard_map/attn_bwd/pallas_call | solution.py:399
  301.1 22.8 %attn_bwd.3 = (bf16[1536,1024]{1,0:T(8,128)(2,1)}, f32[8,384]{1,0:T(8,128)}) custom-call(bf16[768,1280]{1,0:T(8,128)(2,1)} %copy-done.9, bf16[1280,384]{1,0:T(8,128)(2,1)} %get-tuple-element.117.wo_ref, bf16[1536,384]{1,0:T(8,128)(2,1)} %get-tuple-element.164.att_ref, ...), custom_call_target="tpu_custom_call", output_to_operand_aliasing={{0}: (10, {})} | custom-call | flops 1000000 | bytes 100000 | tf_op jit(solution)/shard_map/attn_bwd/pallas_call | solution.py:399
  323.9 4.3 convolution_convert_fusion.6
  333.5 2.7 add_convert_fusion
  336.4 6.8 %convolution_convert_fusion.2 = bf16[1280,1024]{1,0:T(8,128)(2,1)S(1)} fusion(bf16[1536,1280]{1,0:T(8,128)(2,1)} %get-tuple-element.175, bf16[1536,1024]{1,0:T(8,128)(2,1)S(1)} %copy-done.6), kind=kOutput, calls=%fused_computation.11 | convolution fusion | flops 4027842560 | bytes 9699328 | tf_op jit(solution)/shard_map/dot_general | solution.py:43
  348.0 12.4 %collective-permute-done.41.refs_2_ = bf16[384,1280]{1,0:T(8,128)(2,1)} collective-permute-done((bf16[384,1280]{1,0:T(8,128)(2,1)}, bf16[384,1280]{1,0:T(8,128)(2,1)}, u32[]{:S(2)}, u32[]{:S(2)}) %collective-permute-start.41) | collective-permute-done | bytes 983072 | tf_op jit(solution)/shard_map/ppermute | solution.py:68
  361.3 6.1 %first_back.1 = (f32[384,1280]{1,0:T(8,128)}, f32[8,1280]{1,0:T(8,128)}) custom-call(bf16[384,1280]{1,0:T(8,128)(2,1)} %refs_0_.3, bf16[384,1280]{1,0:T(8,128)(2,1)} %slice.203.refs_1_, bf16[384,1280]{1,0:T(8,128)(2,1)} %collective-permute-done.41.refs_2_, f32[384,1280]{1,0:T(8,128)} %get-tuple-element.179.refs_3_, bf16[96,1280]{1,0:T(8,128)(2,1)} %copy-done.48, ...), custom_call_target="tpu_custom_call" | custom-call | flops 1000000 | bytes 100000 | tf_op jit(solution)/shard_map/first_back/pallas_call | solution.py:559
  374.0 13.9 %collective-permute-done.46 = bf16[160,1408]{1,0:T(8,128)(2,1)S(1)} collective-permute-done((bf16[160,1408]{1,0:T(8,128)(2,1)S(1)}, bf16[160,1408]{1,0:T(8,128)(2,1)S(1)}, u32[]{:S(2)}, u32[]{:S(2)}) %collective-permute-start.46) | collective-permute-done | bytes 450592 | tf_op jit(solution)/shard_map/ppermute | solution.py:68
  387.9 9.7 %collective-permute-done.47 = bf16[160,1408]{1,0:T(8,128)(2,1)S(1)} collective-permute-done((bf16[160,1408]{1,0:T(8,128)(2,1)S(1)}, bf16[160,1408]{1,0:T(8,128)(2,1)S(1)}, u32[]{:S(2)}, u32[]{:S(2)}) %collective-permute-start.47) | collective-permute-done | bytes 450592 | tf_op jit(solution)/shard_map/ppermute | solution.py:68
  397.5 14.0 %collective-permute-done.48 = bf16[160,1408]{1,0:T(8,128)(2,1)S(1)} collective-permute-done((bf16[160,1408]{1,0:T(8,128)(2,1)S(1)}, bf16[160,1408]{1,0:T(8,128)(2,1)S(1)}, u32[]{:S(2)}, u32[]{:S(2)}) %collective-permute-start.48) | collective-permute-done | bytes 450592 | tf_op jit(solution)/shard_map/ppermute | solution.py:68
  411.6 9.1 %collective-permute-done.49 = bf16[160,1408]{1,0:T(8,128)(2,1)S(1)} collective-permute-done((bf16[160,1408]{1,0:T(8,128)(2,1)S(1)}, bf16[160,1408]{1,0:T(8,128)(2,1)S(1)}, u32[]{:S(2)}, u32[]{:S(2)}) %collective-permute-start.49) | collective-permute-done | bytes 450592 | tf_op jit(solution)/shard_map/ppermute | solution.py:68
  424.2 4.0 collective-permute-start.50
  428.2 3.5 collective-permute-start.51
  434.4 27.2 %collective-permute-done.58 = f32[9,1280]{1,0:T(8,128)S(1)} collective-permute-done((f32[9,1280]{1,0:T(8,128)S(1)}, f32[9,1280]{1,0:T(8,128)S(1)}, u32[]{:S(2)}, u32[]{:S(2)}) %collective-permute-start.58) | collective-permute-done | bytes 46112 | tf_op jit(solution)/shard_map/ppermute | solution.py:68
  461.6 2.5 collective-permute-start.59
  464.8 6.9 %collective-permute-done.59 = f32[9,1280]{1,0:T(8,128)S(1)} collective-permute-done((f32[9,1280]{1,0:T(8,128)S(1)}, f32[9,1280]{1,0:T(8,128)S(1)}, u32[]{:S(2)}, u32[]{:S(2)}) %collective-permute-start.59) | collective-permute-done | bytes 46112 | tf_op jit(solution)/shard_map/ppermute | solution.py:68
  473.3 6.8 %polar.2 = f32[1,160,160]{2,1,0:T(8,128)} custom-call(f32[1,160,160]{2,1,0:T(8,128)} %add.240.gram_ref), custom_call_target="tpu_custom_call" | custom-call | tf_op jit(solution)/shard_map/polar/pallas_call | solution.py:612
  480.1 2.7 fusion.8
  494.3 9.9 %collective-permute-done.61 = f32[3,160,160]{2,1,0:T(8,128)S(1)} collective-permute-done((f32[3,160,160]{2,1,0:T(8,128)S(1)}, f32[3,160,160]{2,1,0:T(8,128)S(1)}, u32[]{:S(2)}, u32[]{:S(2)}) %collective-permute-start.61) | collective-permute-done | bytes 307232 | tf_op jit(solution)/shard_map/ppermute | solution.py:68
  505.1 9.1 %polar.3 = f32[3,160,160]{2,1,0:T(8,128)} custom-call(f32[3,160,160]{2,1,0:T(8,128)} %fusion.58.gram_ref), custom_call_target="tpu_custom_call" | custom-call | tf_op jit(solution)/shard_map/polar/pallas_call | solution.py:612
  518.1 2.7 convolution_subtract_fusion
  (353 shorter events, 94.2 us)
Async XLA Ops:
  7.3 162.1 %all-gather.3.cloned.1.call-start = ((), (), s32[]{:S(2)}) async-start(), calls=%async_computation.2 | async-start | bytes 3686400 | tf_op jit(solution)/shard_map/all_gather | solution.py:804
  9.4 166.4 %all-gather.5.cloned.1.call-start = ((), (), s32[]{:S(2)}) async-start(), calls=%async_computation.3 | async-start | bytes 3686400 | tf_op jit(solution)/shard_map/all_gather | solution.py:805
  11.4 324.9 %reduce-scatter.3.cloned.1.call-start = ((), (), s32[]{:S(2)}) async-start(), calls=%async_computation.4 | async-start | bytes 3686400 | tf_op jit(solution)/shard_map/reduce_scatter | solution.py:725
  11.5 42.7 %collective-permute-start.3 = (bf16[384,1280]{1,0:T(8,128)(2,1)S(1)}, bf16[384,1280]{1,0:T(8,128)(2,1)}, u32[]{:S(2)}, u32[]{:S(2)}) collective-permute-start(bf16[384,1280]{1,0:T(8,128)(2,1)S(1)} %copy-done.2), channel_id=1, source_target_pairs={{0,2},{1,3},{2,0},{3,1},{4,6},{5,7},{6,4},{7,5},{8,10},{9,11},{10,... | collective-permute-start | bytes 2949128 | tf_op jit(solution)/shard_map/ppermute | solution.py:68
  15.1 21.6 %collective-permute-start = (bf16[160,1408]{1,0:T(8,128)(2,1)S(1)}, bf16[160,1408]{1,0:T(8,128)(2,1)S(1)}, u32[]{:S(2)}, u32[]{:S(2)}) collective-permute-start(bf16[160,1408]{1,0:T(8,128)(2,1)S(1)} %concatenate.52.refs_0_), channel_id=1, source_target_pairs={{0,24},{4,28},{8,16},{12,20},{16,8},{20,12},{24,0},{28,4},{1,25},{... | collective-permute-start | bytes 1351688 | tf_op jit(solution)/shard_map/ppermute | solution.py:68
  18.8 33.9 %collective-permute-start.4 = (bf16[160,1408]{1,0:T(8,128)(2,1)S(1)}, bf16[160,1408]{1,0:T(8,128)(2,1)}, u32[]{:S(2)}, u32[]{:S(2)}) collective-permute-start(bf16[160,1408]{1,0:T(8,128)(2,1)S(1)} %concatenate.52.refs_0_), channel_id=1, source_target_pairs={{0,8},{4,12},{8,0},{12,4},{16,24},{20,28},{24,16},{28,20},{1,9},{5... | collective-permute-start | bytes 1351688 | tf_op jit(solution)/shard_map/ppermute | solution.py:68
  18.8 33.9 %collective-permute-start.5 = (bf16[160,1408]{1,0:T(8,128)(2,1)S(1)}, bf16[160,1408]{1,0:T(8,128)(2,1)}, u32[]{:S(2)}, u32[]{:S(2)}) collective-permute-start(bf16[160,1408]{1,0:T(8,128)(2,1)S(1)} %concatenate.52.refs_0_), channel_id=1, source_target_pairs={{0,4},{4,0},{8,12},{12,8},{16,20},{20,16},{24,28},{28,24},{1,5},{5... | collective-permute-start | bytes 1351688 | tf_op jit(solution)/shard_map/ppermute | solution.py:68
  20.3 65.6 %collective-permute-start.9 = (bf16[160,1408]{1,0:T(8,128)(2,1)S(1)}, bf16[160,1408]{1,0:T(8,128)(2,1)}, u32[]{:S(2)}, u32[]{:S(2)}) collective-permute-start(bf16[160,1408]{1,0:T(8,128)(2,1)S(1)} %concatenate.52.refs_0_), channel_id=1, source_target_pairs={{0,16},{4,20},{8,24},{12,28},{16,0},{20,4},{24,8},{28,12},{1,17},{... | collective-permute-start | bytes 1351688 | tf_op jit(solution)/shard_map/ppermute | solution.py:68
  36.7 55.1 %collective-permute-start.8 = (bf16[384,1280]{1,0:T(8,128)(2,1)S(1)}, bf16[384,1280]{1,0:T(8,128)(2,1)}, u32[]{:S(2)}, u32[]{:S(2)}) collective-permute-start(bf16[384,1280]{1,0:T(8,128)(2,1)S(1)} %copy-done.11), channel_id=1, source_target_pairs={{0,2},{1,3},{2,0},{3,1},{4,6},{5,7},{6,4},{7,5},{8,10},{9,11},{10,... | collective-permute-start | bytes 2949128 | tf_op jit(solution)/shard_map/ppermute | solution.py:68
  52.7 42.6 %collective-permute-start.2 = (bf16[384,1280]{1,0:T(8,128)(2,1)S(1)}, bf16[384,1280]{1,0:T(8,128)(2,1)}, u32[]{:S(2)}, u32[]{:S(2)}) collective-permute-start(bf16[384,1280]{1,0:T(8,128)(2,1)S(1)} %copy-done.2), channel_id=1, source_target_pairs={{0,1},{1,0},{2,3},{3,2},{4,5},{5,4},{6,7},{7,6},{8,9},{9,8},{10,11... | collective-permute-start | bytes 2949128 | tf_op jit(solution)/shard_map/ppermute | solution.py:68
  52.7 34.3 %collective-permute-start.1 = (bf16[160,1408]{1,0:T(8,128)(2,1)S(1)}, bf16[160,1408]{1,0:T(8,128)(2,1)}, u32[]{:S(2)}, u32[]{:S(2)}) collective-permute-start(bf16[160,1408]{1,0:T(8,128)(2,1)S(1)} %collective-permute-done.refs_6_), channel_id=1, source_target_pairs={{0,4},{4,0},{8,12},{12,8},{16,20},{20,16},{24,28},{28,24},{1,5},{5... | collective-permute-start | bytes 1351688 | tf_op jit(solution)/shard_map/ppermute | solution.py:68
  54.2 37.6 %collective-permute-start.10 = (bf16[160,1408]{1,0:T(8,128)(2,1)}, bf16[160,1408]{1,0:T(8,128)(2,1)}, u32[]{:S(2)}, u32[]{:S(2)}) collective-permute-start(bf16[160,1408]{1,0:T(8,128)(2,1)} %collective-permute-done.4.refs_2_), channel_id=1, source_target_pairs={{0,4},{4,0},{8,12},{12,8},{16,20},{20,16},{24,28},{28,24},{1,5},{5... | collective-permute-start | bytes 1351688 | tf_op jit(solution)/shard_map/ppermute | solution.py:68
  85.9 9.5 %collective-permute-start.6 = (bf16[384,1280]{1,0:T(8,128)(2,1)}, bf16[384,1280]{1,0:T(8,128)(2,1)}, u32[]{:S(2)}, u32[]{:S(2)}) collective-permute-start(bf16[384,1280]{1,0:T(8,128)(2,1)} %collective-permute-done.3), channel_id=1, source_target_pairs={{0,1},{1,0},{2,3},{3,2},{4,5},{5,4},{6,7},{7,6},{8,9},{9,8},{10,11... | collective-permute-start | bytes 2949128 | tf_op jit(solution)/shard_map/ppermute | solution.py:68
  87.0 11.8 %collective-permute-start.7 = (bf16[384,1280]{1,0:T(8,128)(2,1)S(1)}, bf16[384,1280]{1,0:T(8,128)(2,1)}, u32[]{:S(2)}, u32[]{:S(2)}) collective-permute-start(bf16[384,1280]{1,0:T(8,128)(2,1)S(1)} %copy-done.11), channel_id=1, source_target_pairs={{0,1},{1,0},{2,3},{3,2},{4,5},{5,4},{6,7},{7,6},{8,9},{9,8},{10,11... | collective-permute-start | bytes 2949128 | tf_op jit(solution)/shard_map/ppermute | solution.py:68
  92.8 13.7 %collective-permute-start.12 = (bf16[160,1408]{1,0:T(8,128)(2,1)}, bf16[160,1408]{1,0:T(8,128)(2,1)S(1)}, u32[]{:S(2)}, u32[]{:S(2)}) collective-permute-start(bf16[160,1408]{1,0:T(8,128)(2,1)} %collective-permute-done.9.refs_4_), channel_id=1, source_target_pairs={{0,4},{4,0},{8,12},{12,8},{16,20},{20,16},{24,28},{28,24},{1,5},{5... | collective-permute-start | bytes 1351688 | tf_op jit(solution)/shard_map/ppermute | solution.py:68
  132.5 9.4 %collective-permute-start.13 = (bf16[96,1280]{1,0:T(8,128)(2,1)}, bf16[96,1280]{1,0:T(8,128)(2,1)S(1)}, u32[]{:S(2)}, u32[]{:S(2)}) collective-permute-start(bf16[96,1280]{1,0:T(8,128)(2,1)} %get-tuple-element.121), channel_id=1, source_target_pairs={{0,1},{1,0},{2,3},{3,2},{4,5},{5,4},{6,7},{7,6},{8,9},{9,8},{10,11... | collective-permute-start | bytes 737288 | tf_op jit(solution)/shard_map/ppermute | solution.py:68
  132.6 9.4 %collective-permute-start.14 = (bf16[96,1280]{1,0:T(8,128)(2,1)}, bf16[96,1280]{1,0:T(8,128)(2,1)S(1)}, u32[]{:S(2)}, u32[]{:S(2)}) collective-permute-start(bf16[96,1280]{1,0:T(8,128)(2,1)} %get-tuple-element.122), channel_id=1, source_target_pairs={{0,1},{1,0},{2,3},{3,2},{4,5},{5,4},{6,7},{7,6},{8,9},{9,8},{10,11... | collective-permute-start | bytes 737288 | tf_op jit(solution)/shard_map/ppermute | solution.py:68
  145.7 23.7 %collective-permute-start.17 = (bf16[384,1280]{1,0:T(8,128)(2,1)}, bf16[384,1280]{1,0:T(8,128)(2,1)S(1)}, u32[]{:S(2)}, u32[]{:S(2)}) collective-permute-start(bf16[384,1280]{1,0:T(8,128)(2,1)} %pair_sum.2), channel_id=1, source_target_pairs={{0,2},{1,3},{2,0},{3,1},{4,6},{5,7},{6,4},{7,5},{8,10},{9,11},{10,... | collective-permute-start | bytes 2949128 | tf_op jit(solution)/shard_map/ppermute | solution.py:68
  175.6 25.3 %collective-permute-start.22 = (bf16[384,1280]{1,0:T(8,128)(2,1)}, bf16[384,1280]{1,0:T(8,128)(2,1)S(1)}, u32[]{:S(2)}, u32[]{:S(2)}) collective-permute-start(bf16[384,1280]{1,0:T(8,128)(2,1)} %get-tuple-element.135.refs_0_), channel_id=1, source_target_pairs={{0,2},{1,3},{2,0},{3,1},{4,6},{5,7},{6,4},{7,5},{8,10},{9,11},{10,... | collective-permute-start | bytes 2949128 | tf_op jit(solution)/shard_map/ppermute | solution.py:68
  175.8 9.9 %collective-permute-start.23 = (bf16[384,1280]{1,0:T(8,128)(2,1)}, bf16[384,1280]{1,0:T(8,128)(2,1)S(1)}, u32[]{:S(2)}, u32[]{:S(2)}) collective-permute-start(bf16[384,1280]{1,0:T(8,128)(2,1)} %get-tuple-element.135.refs_0_), channel_id=1, source_target_pairs={{0,1},{1,0},{2,3},{3,2},{4,5},{5,4},{6,7},{7,6},{8,9},{9,8},{10,11... | collective-permute-start | bytes 2949128 | tf_op jit(solution)/shard_map/ppermute | solution.py:68
  212.6 9.6 %collective-permute-start.25 = (bf16[96,1280]{1,0:T(8,128)(2,1)}, bf16[96,1280]{1,0:T(8,128)(2,1)S(1)}, u32[]{:S(2)}, u32[]{:S(2)}) collective-permute-start(bf16[96,1280]{1,0:T(8,128)(2,1)} %get-tuple-element.147), channel_id=1, source_target_pairs={{0,1},{1,0},{2,3},{3,2},{4,5},{5,4},{6,7},{7,6},{8,9},{9,8},{10,11... | collective-permute-start | bytes 737288 | tf_op jit(solution)/shard_map/ppermute | solution.py:68
  213.1 9.6 %collective-permute-start.27 = (bf16[96,1280]{1,0:T(8,128)(2,1)}, bf16[96,1280]{1,0:T(8,128)(2,1)S(1)}, u32[]{:S(2)}, u32[]{:S(2)}) collective-permute-start(bf16[96,1280]{1,0:T(8,128)(2,1)} %get-tuple-element.149), channel_id=1, source_target_pairs={{0,1},{1,0},{2,3},{3,2},{4,5},{5,4},{6,7},{7,6},{8,9},{9,8},{10,11... | collective-permute-start | bytes 737288 | tf_op jit(solution)/shard_map/ppermute | solution.py:68
  213.6 42.8 %collective-permute-start.32 = (bf16[96,1280]{1,0:T(8,128)(2,1)}, bf16[96,1280]{1,0:T(8,128)(2,1)}, u32[]{:S(2)}, u32[]{:S(2)}) collective-permute-start(bf16[96,1280]{1,0:T(8,128)(2,1)} %get-tuple-element.155), channel_id=1, source_target_pairs={{0,1},{1,0},{2,3},{3,2},{4,5},{5,4},{6,7},{7,6},{8,9},{9,8},{10,11... | collective-permute-start | bytes 737288 | tf_op jit(solution)/shard_map/ppermute | solution.py:68
  222.2 34.3 %collective-permute-start.33 = (bf16[96,1280]{1,0:T(8,128)(2,1)}, bf16[96,1280]{1,0:T(8,128)(2,1)}, u32[]{:S(2)}, u32[]{:S(2)}) collective-permute-start(bf16[96,1280]{1,0:T(8,128)(2,1)} %get-tuple-element.156), channel_id=1, source_target_pairs={{0,1},{1,0},{2,3},{3,2},{4,5},{5,4},{6,7},{7,6},{8,9},{9,8},{10,11... | collective-permute-start | bytes 737288 | tf_op jit(solution)/shard_map/ppermute | solution.py:68
  222.4 34.1 %collective-permute-start.34 = (bf16[96,1280]{1,0:T(8,128)(2,1)}, bf16[96,1280]{1,0:T(8,128)(2,1)}, u32[]{:S(2)}, u32[]{:S(2)}) collective-permute-start(bf16[96,1280]{1,0:T(8,128)(2,1)} %get-tuple-element.157), channel_id=1, source_target_pairs={{0,1},{1,0},{2,3},{3,2},{4,5},{5,4},{6,7},{7,6},{8,9},{9,8},{10,11... | collective-permute-start | bytes 737288 | tf_op jit(solution)/shard_map/ppermute | solution.py:68
  222.7 33.7 %collective-permute-start.35 = (bf16[96,1280]{1,0:T(8,128)(2,1)}, bf16[96,1280]{1,0:T(8,128)(2,1)}, u32[]{:S(2)}, u32[]{:S(2)}) collective-permute-start(bf16[96,1280]{1,0:T(8,128)(2,1)} %get-tuple-element.158), channel_id=1, source_target_pairs={{0,1},{1,0},{2,3},{3,2},{4,5},{5,4},{6,7},{7,6},{8,9},{9,8},{10,11... | collective-permute-start | bytes 737288 | tf_op jit(solution)/shard_map/ppermute | solution.py:68
  226.3 30.1 %collective-permute-start.31 = (bf16[384,1280]{1,0:T(8,128)(2,1)}, bf16[384,1280]{1,0:T(8,128)(2,1)}, u32[]{:S(2)}, u32[]{:S(2)}) collective-permute-start(bf16[384,1280]{1,0:T(8,128)(2,1)} %pair_sum.3), channel_id=1, source_target_pairs={{0,2},{1,3},{2,0},{3,1},{4,6},{5,7},{6,4},{7,5},{8,10},{9,11},{10,... | collective-permute-start | bytes 2949128 | tf_op jit(solution)/shard_map/ppermute | solution.py:68
  237.1 227.7 %reduce-scatter.5.cloned.1.call-start = ((), (), s32[]{:S(2)}) async-start(), calls=%async_computation.5 | async-start | bytes 3686400 | tf_op jit(solution)/shard_map/reduce_scatter | solution.py:725
  263.6 25.8 %collective-permute-start.36 = (bf16[384,1280]{1,0:T(8,128)(2,1)}, bf16[384,1280]{1,0:T(8,128)(2,1)}, u32[]{:S(2)}, u32[]{:S(2)}) collective-permute-start(bf16[384,1280]{1,0:T(8,128)(2,1)} %get-tuple-element.163), channel_id=1, source_target_pairs={{0,2},{1,3},{2,0},{3,1},{4,6},{5,7},{6,4},{7,5},{8,10},{9,11},{10,... | collective-permute-start | bytes 2949128 | tf_op jit(solution)/shard_map/ppermute | solution.py:68
  264.9 26.1 %collective-permute-start.30 = (bf16[384,1280]{1,0:T(8,128)(2,1)}, bf16[384,1280]{1,0:T(8,128)(2,1)}, u32[]{:S(2)}, u32[]{:S(2)}) collective-permute-start(bf16[384,1280]{1,0:T(8,128)(2,1)} %slice.200), channel_id=1, source_target_pairs={{0,1},{1,0},{2,3},{3,2},{4,5},{5,4},{6,7},{7,6},{8,9},{9,8},{10,11... | collective-permute-start | bytes 2949128 | tf_op jit(solution)/shard_map/ppermute | solution.py:68
  291.0 32.9 %collective-permute-start.29 = (bf16[384,1280]{1,0:T(8,128)(2,1)}, bf16[384,1280]{1,0:T(8,128)(2,1)S(1)}, u32[]{:S(2)}, u32[]{:S(2)}) collective-permute-start(bf16[384,1280]{1,0:T(8,128)(2,1)} %slice.198), channel_id=1, source_target_pairs={{0,1},{1,0},{2,3},{3,2},{4,5},{5,4},{6,7},{7,6},{8,9},{9,8},{10,11... | collective-permute-start | bytes 2949128 | tf_op jit(solution)/shard_map/ppermute | solution.py:68
  293.5 30.4 %collective-permute-start.38 = (bf16[384,1280]{1,0:T(8,128)(2,1)}, bf16[384,1280]{1,0:T(8,128)(2,1)S(1)}, u32[]{:S(2)}, u32[]{:S(2)}) collective-permute-start(bf16[384,1280]{1,0:T(8,128)(2,1)} %add_convert_fusion.1), channel_id=1, source_target_pairs={{0,2},{1,3},{2,0},{3,1},{4,6},{5,7},{6,4},{7,5},{8,10},{9,11},{10,... | collective-permute-start | bytes 2949128 | tf_op jit(solution)/shard_map/ppermute | solution.py:68
  336.2 24.2 %collective-permute-start.41 = (bf16[384,1280]{1,0:T(8,128)(2,1)}, bf16[384,1280]{1,0:T(8,128)(2,1)}, u32[]{:S(2)}, u32[]{:S(2)}) collective-permute-start(bf16[384,1280]{1,0:T(8,128)(2,1)} %add_convert_fusion), channel_id=1, source_target_pairs={{0,2},{1,3},{2,0},{3,1},{4,6},{5,7},{6,4},{7,5},{8,10},{9,11},{10,... | collective-permute-start | bytes 2949128 | tf_op jit(solution)/shard_map/ppermute | solution.py:68
  346.6 13.7 %collective-permute-start.42 = (bf16[96,1280]{1,0:T(8,128)(2,1)S(1)}, bf16[96,1280]{1,0:T(8,128)(2,1)S(1)}, u32[]{:S(2)}, u32[]{:S(2)}) collective-permute-start(bf16[96,1280]{1,0:T(8,128)(2,1)S(1)} %get-tuple-element.219), channel_id=1, source_target_pairs={{0,1},{1,0},{2,3},{3,2},{4,5},{5,4},{6,7},{7,6},{8,9},{9,8},{10,11... | collective-permute-start | bytes 737288 | tf_op jit(solution)/shard_map/ppermute | solution.py:68
  346.7 13.6 %collective-permute-start.43 = (bf16[96,1280]{1,0:T(8,128)(2,1)S(1)}, bf16[96,1280]{1,0:T(8,128)(2,1)S(1)}, u32[]{:S(2)}, u32[]{:S(2)}) collective-permute-start(bf16[96,1280]{1,0:T(8,128)(2,1)S(1)} %get-tuple-element.218), channel_id=1, source_target_pairs={{0,1},{1,0},{2,3},{3,2},{4,5},{5,4},{6,7},{7,6},{8,9},{9,8},{10,11... | collective-permute-start | bytes 737288 | tf_op jit(solution)/shard_map/ppermute | solution.py:68
  347.2 13.2 %collective-permute-start.44 = (bf16[96,1280]{1,0:T(8,128)(2,1)S(1)}, bf16[96,1280]{1,0:T(8,128)(2,1)S(1)}, u32[]{:S(2)}, u32[]{:S(2)}) collective-permute-start(bf16[96,1280]{1,0:T(8,128)(2,1)S(1)} %get-tuple-element.217), channel_id=1, source_target_pairs={{0,1},{1,0},{2,3},{3,2},{4,5},{5,4},{6,7},{7,6},{8,9},{9,8},{10,11... | collective-permute-start | bytes 737288 | tf_op jit(solution)/shard_map/ppermute | solution.py:68
  347.3 13.1 %collective-permute-start.45 = (bf16[96,1280]{1,0:T(8,128)(2,1)S(1)}, bf16[96,1280]{1,0:T(8,128)(2,1)S(1)}, u32[]{:S(2)}, u32[]{:S(2)}) collective-permute-start(bf16[96,1280]{1,0:T(8,128)(2,1)S(1)} %get-tuple-element.216), channel_id=1, source_target_pairs={{0,1},{1,0},{2,3},{3,2},{4,5},{5,4},{6,7},{7,6},{8,9},{9,8},{10,11... | collective-permute-start | bytes 737288 | tf_op jit(solution)/shard_map/ppermute | solution.py:68
  369.9 18.0 %collective-permute-start.46 = (bf16[160,1408]{1,0:T(8,128)(2,1)S(1)}, bf16[160,1408]{1,0:T(8,128)(2,1)S(1)}, u32[]{:S(2)}, u32[]{:S(2)}) collective-permute-start(bf16[160,1408]{1,0:T(8,128)(2,1)S(1)} %get-tuple-element.215), channel_id=1, source_target_pairs={{0,4},{4,0},{8,12},{12,8},{16,20},{20,16},{24,28},{28,24},{1,5},{5... | collective-permute-start | bytes 1351688 | tf_op jit(solution)/shard_map/ppermute | solution.py:68
  371.6 25.9 %collective-permute-start.47 = (bf16[160,1408]{1,0:T(8,128)(2,1)S(1)}, bf16[160,1408]{1,0:T(8,128)(2,1)S(1)}, u32[]{:S(2)}, u32[]{:S(2)}) collective-permute-start(bf16[160,1408]{1,0:T(8,128)(2,1)S(1)} %get-tuple-element.214), channel_id=1, source_target_pairs={{0,4},{4,0},{8,12},{12,8},{16,20},{20,16},{24,28},{28,24},{1,5},{5... | collective-permute-start | bytes 1351688 | tf_op jit(solution)/shard_map/ppermute | solution.py:68
  372.0 39.6 %collective-permute-start.48 = (bf16[160,1408]{1,0:T(8,128)(2,1)S(1)}, bf16[160,1408]{1,0:T(8,128)(2,1)S(1)}, u32[]{:S(2)}, u32[]{:S(2)}) collective-permute-start(bf16[160,1408]{1,0:T(8,128)(2,1)S(1)} %get-tuple-element.213), channel_id=1, source_target_pairs={{0,4},{4,0},{8,12},{12,8},{16,20},{20,16},{24,28},{28,24},{1,5},{5... | collective-permute-start | bytes 1351688 | tf_op jit(solution)/shard_map/ppermute | solution.py:68
  373.7 47.0 %collective-permute-start.49 = (bf16[160,1408]{1,0:T(8,128)(2,1)S(1)}, bf16[160,1408]{1,0:T(8,128)(2,1)S(1)}, u32[]{:S(2)}, u32[]{:S(2)}) collective-permute-start(bf16[160,1408]{1,0:T(8,128)(2,1)S(1)} %get-tuple-element.212), channel_id=1, source_target_pairs={{0,4},{4,0},{8,12},{12,8},{16,20},{20,16},{24,28},{28,24},{1,5},{5... | collective-permute-start | bytes 1351688 | tf_op jit(solution)/shard_map/ppermute | solution.py:68
  424.2 58.6 %collective-permute-start.50 = (bf16[160,1408]{1,0:T(8,128)(2,1)}, bf16[160,1408]{1,0:T(8,128)(2,1)}, u32[]{:S(2)}, u32[]{:S(2)}) collective-permute-start(bf16[160,1408]{1,0:T(8,128)(2,1)} %get-tuple-element.211), channel_id=1, source_target_pairs={{0,16},{4,20},{8,24},{12,28},{16,0},{20,4},{24,8},{28,12},{1,17},{... | collective-permute-start | bytes 1351688 | tf_op jit(solution)/shard_map/ppermute | solution.py:68
  428.2 54.6 %collective-permute-start.51 = (bf16[160,1408]{1,0:T(8,128)(2,1)}, bf16[160,1408]{1,0:T(8,128)(2,1)}, u32[]{:S(2)}, u32[]{:S(2)}) collective-permute-start(bf16[160,1408]{1,0:T(8,128)(2,1)} %get-tuple-element.210), channel_id=1, source_target_pairs={{0,24},{4,28},{8,16},{12,20},{16,8},{20,12},{24,0},{28,4},{1,25},{... | collective-permute-start | bytes 1351688 | tf_op jit(solution)/shard_map/ppermute | solution.py:68
  431.6 51.2 %collective-permute-start.52 = (bf16[160,1408]{1,0:T(8,128)(2,1)}, bf16[160,1408]{1,0:T(8,128)(2,1)}, u32[]{:S(2)}, u32[]{:S(2)}) collective-permute-start(bf16[160,1408]{1,0:T(8,128)(2,1)} %get-tuple-element.209), channel_id=1, source_target_pairs={{0,8},{4,12},{8,0},{12,4},{16,24},{20,28},{24,16},{28,20},{1,9},{5... | collective-permute-start | bytes 1351688 | tf_op jit(solution)/shard_map/ppermute | solution.py:68
  431.7 40.0 %collective-permute-start.54 = (f32[1,160,160]{2,1,0:T(8,128)S(1)}, f32[1,160,160]{2,1,0:T(8,128)}, u32[]{:S(2)}, u32[]{:S(2)}) collective-permute-start(f32[1,160,160]{2,1,0:T(8,128)S(1)} %add.239), channel_id=1, source_target_pairs={{0,2},{1,3},{2,0},{3,1},{4,6},{5,7},{6,4},{7,5},{8,10},{9,11},{10,... | collective-permute-start | bytes 307208 | tf_op jit(solution)/shard_map/ppermute | solution.py:68
  432.3 29.3 %collective-permute-start.58 = (f32[9,1280]{1,0:T(8,128)S(1)}, f32[9,1280]{1,0:T(8,128)S(1)}, u32[]{:S(2)}, u32[]{:S(2)}) collective-permute-start(f32[9,1280]{1,0:T(8,128)S(1)} %fusion.38), channel_id=1, source_target_pairs={{0,8},{4,12},{8,0},{12,4},{16,24},{20,28},{24,16},{28,20},{1,9},{5... | collective-permute-start | bytes 138248 | tf_op jit(solution)/shard_map/ppermute | solution.py:68
  461.6 10.1 %collective-permute-start.59 = (f32[9,1280]{1,0:T(8,128)S(1)}, f32[9,1280]{1,0:T(8,128)S(1)}, u32[]{:S(2)}, u32[]{:S(2)}) collective-permute-start(f32[9,1280]{1,0:T(8,128)S(1)} %add.247), channel_id=1, source_target_pairs={{0,16},{4,20},{8,24},{12,28},{16,0},{20,4},{24,8},{28,12},{1,17},{... | collective-permute-start | bytes 138248 | tf_op jit(solution)/shard_map/ppermute | solution.py:68
  491.1 13.2 %collective-permute-start.61 = (f32[3,160,160]{2,1,0:T(8,128)S(1)}, f32[3,160,160]{2,1,0:T(8,128)S(1)}, u32[]{:S(2)}, u32[]{:S(2)}) collective-permute-start(f32[3,160,160]{2,1,0:T(8,128)S(1)} %fusion.39), channel_id=1, source_target_pairs={{0,2},{1,3},{2,0},{3,1},{4,6},{5,7},{6,4},{7,5},{8,10},{9,11},{10,... | collective-permute-start | bytes 921608 | tf_op jit(solution)/shard_map/ppermute | solution.py:68
  (92 other events, 941.4 us)
Sparse Core Ops, SparseCore 0:
  10.9 94.5 all-gather.2
  108.2 59.4 all-gather.4
  237.2 77.6 reduce-scatter.2
  330.9 88.5 reduce-scatter.4

commit v7 on v6

--- a/solution.py
+++ b/solution.py
@@ -896,7 +896,9 @@
     far = swap(first_total, "tensor", 2)
     d_qkv, raw_wq, raw_wo = tie([d_qkv, raw_wq, raw_wo])
     owns, crossed = dp_cross(jnp.concatenate([raw_wq, raw_wo], axis=1))
-    first_mine = mm(after(d_qkv[:half], first_total), wq, NT).astype(BF16)
+    first_mine = mm(after(d_qkv[:half], first_total, *crossed[:1]), wq, NT).astype(BF16)
+    lined = dp_line(owns, tie(crossed, far))
+    far = after(far, lined[-1])
     quarter = tok // PIECES
     sent = [first_mine[tok + k * quarter : tok + k * quarter + quarter] for k in range(PIECES)]
     near = swap_all(sent, "tensor", 1)
@@ -916,6 +918,13 @@
     )
 
     vec_sums = tensor_sum(sums_one + sums_two)
+    grad_wd = after(grad_wd, first_mine, lined[-1])
+    mom_down_new, update_down = momentum(mom_down, grad_wd.astype(F32))
+    early = polar_call(tensor_sum(gram_of(update_down)[None]))
+    early = after(early, *lined[:2])
+    new_w_down = applied(w_down, early[0], update_down, STEP_DOWN)
+    grad_wu = after(after(grad_wu, first_mine, *crossed), *lined[:3])
+
     rows_of = jnp.concatenate(
         [
             vec_sums[:6],
@@ -924,20 +933,13 @@
         ],
         axis=0,
     )
-    rows_of = dp_sum(rows_of)
+    rows_of = dp_sum(after(rows_of, new_w_down))
     own_cols = lax.dynamic_slice(rows_of, (0, dp_index * own_rows), (7, own_rows))
     vec_grad = jnp.transpose(own_cols[:6])
     bu_grad = own_cols[6]
     bq_grad = jnp.transpose(
         lax.dynamic_slice(rows_of, (7, dp_index * own_bias), (2, own_bias))
     )
-
-    lined = dp_line(owns, tie(crossed, input_grad))
-    grad_wd = after(grad_wd, first_mine, lined[-1])
-    mom_down_new, update_down = momentum(mom_down, grad_wd.astype(F32))
-    early = polar_call(tensor_sum(gram_of(update_down)[None]))
-    new_w_down = applied(w_down, early[0], update_down, STEP_DOWN)
-    grad_wu = after(after(grad_wu, first_mine, *crossed), *lined[:3])
 
     mom_up_new, update_up = momentum(mom_up, grad_wu.astype(F32))
     gram_up = gram_of(update_up)

time: 534 us -> 539 us (level)
  waiting for transfers between devices: 184 us -> 168 us
  starting transfers between devices: 44.2 us -> 57.7 us
    ppermute x62, waiting for transfers between devices: 184 us -> 167 us  [swap(): return lax.ppermute(value, axis, [(i, i ^ mask) for i in range(size)])]
    ppermute x62, starting transfers between devices: 44 us -> 57.5 us  [swap(): return lax.ppermute(value, axis, [(i, i ^ mask) for i in range(size)])]
    unnamed x151 -> x145, local copies, waits for them, and re-layouts: 15.2 us -> 19.4 us
  transfers between devices with their start and end apart: 66 -> 66, of which waited for: 17 -> 17; matrix products, arithmetic and copies ran while one was open for 18% -> 19% of each run, Pallas kernels for 27% -> 27%
where the time goes in v7:
time: 539 us; the launch traced here: 534 us
  waiting for transfers between devices  168 us (31%)
  Pallas kernels  159 us (29%)
  matrix products  68.3 us (13%)
  starting transfers between devices  57.7 us (11%)
  other arithmetic  33.5 us (6%)
  local copies, waits for them, and re-layouts  31.7 us (6%)
  between operations  15.8 us (3%)
    ppermute x62, waiting for transfers between devices, swap(): return lax.ppermute(value, axis, [(i, i ^ mask) for i in range(size)])  167 us
    ppermute x62, starting transfers between devices, swap(): return lax.ppermute(value, axis, [(i, i ^ mask) for i in range(size)])  57.5 us
    dot_general x10, matrix products, mm(): return lax.dot_general(left, right, dims, preferred_element_type=F32)  55 us
    pallas_call x2, Pallas kernels, attn_back_call(): pl.pallas_call(partial(attn_back_body, heads, last_part, first), grid=(co...  44.7 us
    pallas_call x3, Pallas kernels, attn_call(): pl.pallas_call(partial(attn_body, heads, emits, len(held)), grid=(count /...  31.4 us
    pallas_call x3, Pallas kernels, mlp_call(): pl.pallas_call(partial(mlp_body, min(256, hidden_width), emits, len(held)...  30.3 us
    unnamed x145, local copies, waits for them, and re-layouts  19.4 us
    pallas_call x3, Pallas kernels, row_call(): pl.pallas_call(partial(row_body, body, len(rows_in)), grid=(PIECES,), in_...  17.5 us
  transfers between devices with their start and end apart: 66, of which 17 were waited for; matrix products, arithmetic and copies ran while one was open for 19% of the time, Pallas kernels for 27%

profile of v7, /device:TPU:0, one launch (start us, length us, event | category | flops | bytes accessed | tf_op | source)
XLA Modules:
  0.0 533.8 jit_solution(6398847694668773065)
XLA Ops:
  11.5 3.0 collective-permute-start.3
  15.1 3.7 collective-permute-start
  21.1 15.6 %collective-permute-done.refs_6_ = bf16[160,1408]{1,0:T(8,128)(2,1)S(1)} collective-permute-done((bf16[160,1408]{1,0:T(8,128)(2,1)S(1)}, bf16[160,1408]{1,0:T(8,128)(2,1)S(1)}, u32[]{:S(2)}, u32[]{:S(2)}) %collective-permute-start) | collective-permute-done | bytes 450592 | tf_op jit(solution)/shard_map/ppermute | solution.py:68
  37.5 15.2 %collective-permute-done.4.refs_2_ = bf16[160,1408]{1,0:T(8,128)(2,1)} collective-permute-done((bf16[160,1408]{1,0:T(8,128)(2,1)S(1)}, bf16[160,1408]{1,0:T(8,128)(2,1)}, u32[]{:S(2)}, u32[]{:S(2)}) %collective-permute-start.4) | collective-permute-done | bytes 450592 | tf_op jit(solution)/shard_map/ppermute | solution.py:68
  54.7 31.1 %collective-permute-done.9.refs_4_ = bf16[160,1408]{1,0:T(8,128)(2,1)} collective-permute-done((bf16[160,1408]{1,0:T(8,128)(2,1)S(1)}, bf16[160,1408]{1,0:T(8,128)(2,1)}, u32[]{:S(2)}, u32[]{:S(2)}) %collective-permute-start.9) | collective-permute-done | bytes 450592 | tf_op jit(solution)/shard_map/ppermute | solution.py:68
  88.0 4.2 collective-permute-done.10.refs_3_
  96.5 3.5 pad_maximum_fusion.x_ref
  100.0 3.3 pad_maximum_fusion.1
  103.3 4.4 collective-permute-done.12.refs_5_
  108.5 4.0 place_rows.1
  115.7 9.9 %norm_qkv.1 = (bf16[1536,1280]{1,0:T(8,128)(2,1)}, bf16[1536,1024]{1,0:T(8,128)(2,1)}) custom-call(bf16[1536,1280]{1,0:T(8,128)(2,1)} %pad_maximum_fusion.x_ref, f32[8,1280]{1,0:T(8,128)} %slice.149.vec_ref.refs_7_.refs_8_, bf16[1280,1024]{1,0:T(8,128)(2,1)} %get-tuple-element.118.w_ref, f32[1,1024]{1,0:T(1,128)} %pad_maximum_fusion.7.bias_ref), custom_call_target="tpu_custom_call" | custom-call | flops 1000000 | bytes 100000 | tf_op jit(solution)/shard_map/norm_qkv/pallas_call | solution.py:109
  125.6 8.2 %attn_fwd.3 = (bf16[1536,384]{1,0:T(8,128)(2,1)}, f32[8,1536]{1,0:T(8,128)}, bf16[96,1280]{1,0:T(8,128)(2,1)}, bf16[96,1280]{1,0:T(8,128)(2,1)}, bf16[96,1280]{1,0:T(8,128)(2,1)}, /*index=5*/bf16[96,1280]{1,0:T(8,128)(2,1)}) custom-call(bf16[1536,1024]{1,0:T(8,128)(2,1)} %get-tuple-element.128.q_ref.qkv_ref, ...), custom_call_target="tpu_custom_call" | custom-call | flops 1000000 | bytes 100000 | tf_op jit(solution)/shard_map/attn_fwd/pallas_call | solution.py:266
  134.7 8.6 %attn_fwd.4 = (bf16[1536,384]{1,0:T(8,128)(2,1)}, f32[8,1536]{1,0:T(8,128)}, bf16[384,1280]{1,0:T(8,128)(2,1)}) custom-call(bf16[1536,1024]{1,0:T(8,128)(2,1)} %get-tuple-element.128.q_ref.qkv_ref, bf16[1536,1024]{1,0:T(8,128)(2,1)} %get-tuple-element.128.q_ref.qkv_ref, ...), custom_call_target="tpu_custom_call", output_to_operand_aliasing={{0}: (4, {}), {1}: (5, {})} | custom-call | flops 1000000 | bytes 100000 | tf_op jit(solution)/shard_map/attn_fwd/pallas_call | solution.py:266
  144.3 2.7 pair_sum.2
  147.0 14.7 %attn_fwd.5 = (bf16[1536,384]{1,0:T(8,128)(2,1)}, f32[8,1536]{1,0:T(8,128)}, bf16[384,1280]{1,0:T(8,128)(2,1)}, bf16[96,1280]{1,0:T(8,128)(2,1)}, bf16[96,1280]{...) custom-call(bf16[1536,1024]{1,0:T(8,128)(2,1)} %get-tuple-element.12, ...), custom_call_target="tpu_custom_call", output_to_operand_aliasing={{0}: (4, {}), {1}: (5, {})} | custom-call | flops 1000000 | bytes 100000 | tf_op jit(solution)/shard_map/attn_fwd/pallas_call | solution.py:266
  164.2 6.7 %collective-permute-done.17.refs_2_ = bf16[384,1280]{1,0:T(8,128)(2,1)S(1)} collective-permute-done((bf16[384,1280]{1,0:T(8,128)(2,1)}, bf16[384,1280]{1,0:T(8,128)(2,1)S(1)}, u32[]{:S(2)}, u32[]{:S(2)}) %collective-permute-start.17) | collective-permute-done | bytes 983072 | tf_op jit(solution)/shard_map/ppermute | solution.py:68
  172.2 5.0 residual.1
  177.4 9.9 %fusion.42.refs_4_.refs_3_ = f32[1536,1280]{1,0:T(8,128)} fusion(bf16[1536,1280]{1,0:T(8,128)(2,1)} %pad_maximum_fusion.1, bf16[1280,1280]{1,0:T(8,128)(2,1)} %all-gather.3.cloned.1.call-done), kind=kOutput, calls=%fused_computation.122 | convolution fusion | flops 5033164800 | bytes 15073280 | tf_op jit(solution)/shard_map/dot_general | solution.py:43
  188.3 14.2 %mlp_up.3 = (bf16[1536,1280]{1,0:T(8,128)(2,1)}, bf16[1536,1280]{1,0:T(8,128)(2,1)}, f32[8,1280]{1,0:T(8,128)}, bf16[384,1280]{1,0:T(8,128)(2,1)}, bf16[96,1280]...) custom-call(bf16[384,1280]{1,0:T(8,128)(2,1)} %get-tuple-element.138.refs_0_, ...), custom_call_target="tpu_custom_call" | custom-call | flops 1000000 | bytes 100000 | tf_op jit(solution)/shard_map/mlp_up/pallas_call | solution.py:471
  206.2 8.0 %mlp_up.4 = (bf16[1536,1280]{1,0:T(8,128)(2,1)}, bf16[1536,1280]{1,0:T(8,128)(2,1)}, f32[8,1280]{1,0:T(8,128)}, bf16[96,1280]{1,0:T(8,128)(2,1)}, bf16[96,1280]{...) custom-call(bf16[384,1280]{1,0:T(8,128)(2,1)} %copy-done.35, ...), custom_call_target="tpu_custom_call", output_to_operand_aliasing={{0}: (4, {}), {1}: (5, {})} | custom-call | flops 1000000 | bytes 100000 | tf_op jit(solution)/shard_map/mlp_up/pallas_call | solution.py:471
  215.6 8.2 %mlp_up.5 = (bf16[1536,1280]{1,0:T(8,128)(2,1)}, bf16[1536,1280]{1,0:T(8,128)(2,1)}, f32[8,1280]{1,0:T(8,128)}, bf16[384,1280]{1,0:T(8,128)(2,1)}) custom-call(bf16[384,1280]{1,0:T(8,128)(2,1)} %copy-done.31, bf16[1280,1280]{1,0:T(8,128)(2,1)} %all-gather.5.cloned.1.call-done.refs_2_.refs_1_, ...), custom_call_target="tpu_custom_call", output_to_operand_aliasing={{0}: (4, {}), {1}: (5, {})} | custom-call | flops 1000000 | bytes 100000 | tf_op jit(solution)/shard_map/mlp_up/pallas_call | solution.py:471
  225.2 2.7 pair_sum.3
  229.7 8.9 %convolution_convert_fusion.1 = bf16[1280,1280]{1,0:T(8,128)(2,1)} fusion(bf16[1536,1280]{1,0:T(8,128)(2,1)S(1)} %copy-done.12, bf16[1536,1280]{1,0:T(8,128)(2,1)} %get-tuple-element.157), kind=kOutput, calls=%fused_computation.1 | convolution fusion | flops 5034803200 | bytes 11141120 | tf_op jit(solution)/shard_map/dot_general | solution.py:43
  240.4 9.4 %convolution_convert_fusion = bf16[1280,1280]{1,0:T(8,128)(2,1)} fusion(bf16[1536,1280]{1,0:T(8,128)(2,1)} %get-tuple-element.156, bf16[384,1280]{1,0:T(8,128)(2,1)} %copy-done.35, bf16[384,1280]{1,0:T(8,128)(2,1)S(1)} %copy-done.32, bf16[384,1280]{1,0:T(8,128)(2,1)S(1)} %copy-done.34, bf16[384,1280]{1,0:T(8,128)(2,1)S(1)} %copy-done.30), kind=kOutput, calls=%fused_computation | convolution fusion | flops 5050531840 | bytes 11141120 | tf_op jit(solution)/shard_map/dot_general | solution.py:43
  249.8 5.4 %convolution_convert_fusion.3 = bf16[768,1280]{1,0:T(8,128)(2,1)S(1)} fusion(bf16[1280,1280]{1,0:T(8,128)(2,1)} %all-gather.3.cloned.1.call-done, bf16[1536,1280]{1,0:T(8,128)(2,1)} %get-tuple-element.157), kind=kOutput, calls=%fused_computation.12 | convolution fusion | flops 2517565440 | bytes 7208960 | tf_op jit(solution)/shard_map/dot_general | solution.py:43
  255.2 2.7 convolution_convert_fusion.4
  258.8 6.4 %second_back.1 = (f32[384,1280]{1,0:T(8,128)}, bf16[384,1280]{1,0:T(8,128)(2,1)}, f32[8,1280]{1,0:T(8,128)}) custom-call(f32[384,1280]{1,0:T(8,128)} %get-tuple-element.137.refs_0_, bf16[384,1280]{1,0:T(8,128)(2,1)} %get-tuple-element.141.refs_1_, bf16[384,1280]{1,0:T(8,128)(2,1)} %collective-permute-done.31.refs_2_, bf16[384,1280]{1,0:T(8,128)(2,1)} %refs_3_.1, ...), custom_call_target="tpu_custom_call" | custom-call | flops 1000000 | bytes 100000 | tf_op jit(solution)/shard_map/second_back/pallas_call | solution.py:559
  269.3 21.9 %attn_bwd.2 = (bf16[1536,1024]{1,0:T(8,128)(2,1)}, f32[8,384]{1,0:T(8,128)}, f32[1536,384]{1,0:T(8,128)}, f32[1536,384]{1,0:T(8,128)}) custom-call(bf16[768,1280]{1,0:T(8,128)(2,1)} %copy-done.9, bf16[1280,384]{1,0:T(8,128)(2,1)} %get-tuple-element.120.wo_ref, bf16[1536,384]{1,0:T(8,128)(2,1)} %get-tuple-element.167.att_ref, ...), custom_call_target="tpu_custom_call" | custom-call | flops 1000000 | bytes 100000 | tf_op jit(solution)/shard_map/attn_bwd/pallas_call | solution.py:399
  302.9 22.8 %attn_bwd.3 = (bf16[1536,1024]{1,0:T(8,128)(2,1)}, f32[8,384]{1,0:T(8,128)}) custom-call(bf16[768,1280]{1,0:T(8,128)(2,1)} %copy-done.11, bf16[1280,384]{1,0:T(8,128)(2,1)} %get-tuple-element.120.wo_ref, bf16[1536,384]{1,0:T(8,128)(2,1)} %get-tuple-element.167.att_ref, ...), custom_call_target="tpu_custom_call", output_to_operand_aliasing={{0}: (10, {})} | custom-call | flops 1000000 | bytes 100000 | tf_op jit(solution)/shard_map/attn_bwd/pallas_call | solution.py:399
  325.8 4.3 convolution_convert_fusion.6
  332.5 2.9 collective-permute-done.40
  338.5 6.6 %convolution_convert_fusion.2 = bf16[1280,1024]{1,0:T(8,128)(2,1)S(1)} fusion(bf16[1536,1280]{1,0:T(8,128)(2,1)} %get-tuple-element.178, bf16[1536,1024]{1,0:T(8,128)(2,1)S(1)} %copy-done.8), kind=kOutput, calls=%fused_computation.11 | convolution fusion | flops 4027842560 | bytes 9699328 | tf_op jit(solution)/shard_map/dot_general | solution.py:43
  353.8 13.7 %collective-permute-done.41 = bf16[160,1408]{1,0:T(8,128)(2,1)} collective-permute-done((bf16[160,1408]{1,0:T(8,128)(2,1)}, bf16[160,1408]{1,0:T(8,128)(2,1)}, u32[]{:S(2)}, u32[]{:S(2)}) %collective-permute-start.41) | collective-permute-done | bytes 450592 | tf_op jit(solution)/shard_map/ppermute | solution.py:68
  367.5 13.7 %collective-permute-done.43 = bf16[160,1408]{1,0:T(8,128)(2,1)} collective-permute-done((bf16[160,1408]{1,0:T(8,128)(2,1)}, bf16[160,1408]{1,0:T(8,128)(2,1)}, u32[]{:S(2)}, u32[]{:S(2)}) %collective-permute-start.43) | collective-permute-done | bytes 450592 | tf_op jit(solution)/shard_map/ppermute | solution.py:68
  381.2 14.1 %collective-permute-done.44 = bf16[160,1408]{1,0:T(8,128)(2,1)} collective-permute-done((bf16[160,1408]{1,0:T(8,128)(2,1)}, bf16[160,1408]{1,0:T(8,128)(2,1)}, u32[]{:S(2)}, u32[]{:S(2)}) %collective-permute-start.44) | collective-permute-done | bytes 450592 | tf_op jit(solution)/shard_map/ppermute | solution.py:68
  395.3 8.8 %collective-permute-done.45 = bf16[160,1408]{1,0:T(8,128)(2,1)} collective-permute-done((bf16[160,1408]{1,0:T(8,128)(2,1)}, bf16[160,1408]{1,0:T(8,128)(2,1)}, u32[]{:S(2)}, u32[]{:S(2)}) %collective-permute-start.45) | collective-permute-done | bytes 450592 | tf_op jit(solution)/shard_map/ppermute | solution.py:68
  404.1 4.2 convolution_convert_fusion.5
  409.6 2.8 add_convert_fusion.2
  415.5 6.2 %first_back.1 = (f32[384,1280]{1,0:T(8,128)}, f32[8,1280]{1,0:T(8,128)}) custom-call(bf16[384,1280]{1,0:T(8,128)(2,1)} %refs_0_.3, bf16[384,1280]{1,0:T(8,128)(2,1)} %slice.203.refs_1_, bf16[384,1280]{1,0:T(8,128)(2,1)} %collective-permute-done.42.refs_2_, f32[384,1280]{1,0:T(8,128)} %get-tuple-element.186.refs_3_, bf16[96,1280]{1,0:T(8,128)(2,1)} %copy-done.47, ...), custom_call_target="tpu_custom_call" | custom-call | flops 1000000 | bytes 100000 | tf_op jit(solution)/shard_map/first_back/pallas_call | solution.py:559
  427.0 4.5 collective-permute-start.50
  431.5 3.7 collective-permute-start.51
  435.9 6.8 %polar.2 = f32[1,160,160]{2,1,0:T(8,128)} custom-call(f32[1,160,160]{2,1,0:T(8,128)} %add.240.gram_ref), custom_call_target="tpu_custom_call" | custom-call | tf_op jit(solution)/shard_map/polar/pallas_call | solution.py:612
  443.4 18.9 %collective-permute-done.50 = bf16[160,1408]{1,0:T(8,128)(2,1)S(1)} collective-permute-done((bf16[160,1408]{1,0:T(8,128)(2,1)}, bf16[160,1408]{1,0:T(8,128)(2,1)S(1)}, u32[]{:S(2)}, u32[]{:S(2)}) %collective-permute-start.50) | collective-permute-done | bytes 450592 | tf_op jit(solution)/shard_map/ppermute | solution.py:68
  462.3 2.7 fusion.8
  471.2 9.1 %collective-permute-start.58 = (f32[9,1280]{1,0:T(8,128)S(1)}, f32[9,1280]{1,0:T(8,128)S(1)}, u32[]{:S(2)}, u32[]{:S(2)}) collective-permute-start(f32[9,1280]{1,0:T(8,128)S(1)} %add.246), channel_id=1, source_target_pairs={{0,8},{4,12},{8,0},{12,4},{16,24},{20,28},{24,16},{28,20},{1,9},{5... | collective-permute-start | bytes 138248 | tf_op jit(solution)/shard_map/ppermute | solution.py:68
  482.7 4.3 collective-permute-start.59
  498.9 10.6 %collective-permute-done.61 = f32[3,160,160]{2,1,0:T(8,128)S(1)} collective-permute-done((f32[3,160,160]{2,1,0:T(8,128)S(1)}, f32[3,160,160]{2,1,0:T(8,128)S(1)}, u32[]{:S(2)}, u32[]{:S(2)}) %collective-permute-start.61) | collective-permute-done | bytes 307232 | tf_op jit(solution)/shard_map/ppermute | solution.py:68
  510.3 9.1 %polar.3 = f32[3,160,160]{2,1,0:T(8,128)} custom-call(f32[3,160,160]{2,1,0:T(8,128)} %fusion.57.gram_ref), custom_call_target="tpu_custom_call" | custom-call | tf_op jit(solution)/shard_map/polar/pallas_call | solution.py:612
  (347 shorter events, 106.7 us)
Async XLA Ops:
  7.3 163.7 %all-gather.3.cloned.1.call-start = ((), (), s32[]{:S(2)}) async-start(), calls=%async_computation.2 | async-start | bytes 3686400 | tf_op jit(solution)/shard_map/all_gather | solution.py:804
  9.4 168.0 %all-gather.5.cloned.1.call-start = ((), (), s32[]{:S(2)}) async-start(), calls=%async_computation.3 | async-start | bytes 3686400 | tf_op jit(solution)/shard_map/all_gather | solution.py:805
  11.4 327.0 %reduce-scatter.3.cloned.1.call-start = ((), (), s32[]{:S(2)}) async-start(), calls=%async_computation.4 | async-start | bytes 3686400 | tf_op jit(solution)/shard_map/reduce_scatter | solution.py:725
  11.5 42.7 %collective-permute-start.3 = (bf16[384,1280]{1,0:T(8,128)(2,1)S(1)}, bf16[384,1280]{1,0:T(8,128)(2,1)}, u32[]{:S(2)}, u32[]{:S(2)}) collective-permute-start(bf16[384,1280]{1,0:T(8,128)(2,1)S(1)} %copy-done.4), channel_id=1, source_target_pairs={{0,2},{1,3},{2,0},{3,1},{4,6},{5,7},{6,4},{7,5},{8,10},{9,11},{10,... | collective-permute-start | bytes 2949128 | tf_op jit(solution)/shard_map/ppermute | solution.py:68
  15.1 21.6 %collective-permute-start = (bf16[160,1408]{1,0:T(8,128)(2,1)S(1)}, bf16[160,1408]{1,0:T(8,128)(2,1)S(1)}, u32[]{:S(2)}, u32[]{:S(2)}) collective-permute-start(bf16[160,1408]{1,0:T(8,128)(2,1)S(1)} %concatenate.52.refs_0_), channel_id=1, source_target_pairs={{0,24},{4,28},{8,16},{12,20},{16,8},{20,12},{24,0},{28,4},{1,25},{... | collective-permute-start | bytes 1351688 | tf_op jit(solution)/shard_map/ppermute | solution.py:68
  18.8 33.9 %collective-permute-start.4 = (bf16[160,1408]{1,0:T(8,128)(2,1)S(1)}, bf16[160,1408]{1,0:T(8,128)(2,1)}, u32[]{:S(2)}, u32[]{:S(2)}) collective-permute-start(bf16[160,1408]{1,0:T(8,128)(2,1)S(1)} %concatenate.52.refs_0_), channel_id=1, source_target_pairs={{0,8},{4,12},{8,0},{12,4},{16,24},{20,28},{24,16},{28,20},{1,9},{5... | collective-permute-start | bytes 1351688 | tf_op jit(solution)/shard_map/ppermute | solution.py:68
  18.8 33.9 %collective-permute-start.5 = (bf16[160,1408]{1,0:T(8,128)(2,1)S(1)}, bf16[160,1408]{1,0:T(8,128)(2,1)}, u32[]{:S(2)}, u32[]{:S(2)}) collective-permute-start(bf16[160,1408]{1,0:T(8,128)(2,1)S(1)} %concatenate.52.refs_0_), channel_id=1, source_target_pairs={{0,4},{4,0},{8,12},{12,8},{16,20},{20,16},{24,28},{28,24},{1,5},{5... | collective-permute-start | bytes 1351688 | tf_op jit(solution)/shard_map/ppermute | solution.py:68
  20.3 65.5 %collective-permute-start.9 = (bf16[160,1408]{1,0:T(8,128)(2,1)S(1)}, bf16[160,1408]{1,0:T(8,128)(2,1)}, u32[]{:S(2)}, u32[]{:S(2)}) collective-permute-start(bf16[160,1408]{1,0:T(8,128)(2,1)S(1)} %concatenate.52.refs_0_), channel_id=1, source_target_pairs={{0,16},{4,20},{8,24},{12,28},{16,0},{20,4},{24,8},{28,12},{1,17},{... | collective-permute-start | bytes 1351688 | tf_op jit(solution)/shard_map/ppermute | solution.py:68
  37.5 54.7 %collective-permute-start.8 = (bf16[384,1280]{1,0:T(8,128)(2,1)S(1)}, bf16[384,1280]{1,0:T(8,128)(2,1)S(1)}, u32[]{:S(2)}, u32[]{:S(2)}) collective-permute-start(bf16[384,1280]{1,0:T(8,128)(2,1)S(1)} %copy-done.13), channel_id=1, source_target_pairs={{0,2},{1,3},{2,0},{3,1},{4,6},{5,7},{6,4},{7,5},{8,10},{9,11},{10,... | collective-permute-start | bytes 2949128 | tf_op jit(solution)/shard_map/ppermute | solution.py:68
  52.7 43.8 %collective-permute-start.2 = (bf16[384,1280]{1,0:T(8,128)(2,1)S(1)}, bf16[384,1280]{1,0:T(8,128)(2,1)}, u32[]{:S(2)}, u32[]{:S(2)}) collective-permute-start(bf16[384,1280]{1,0:T(8,128)(2,1)S(1)} %copy-done.4), channel_id=1, source_target_pairs={{0,1},{1,0},{2,3},{3,2},{4,5},{5,4},{6,7},{7,6},{8,9},{9,8},{10,11... | collective-permute-start | bytes 2949128 | tf_op jit(solution)/shard_map/ppermute | solution.py:68
  52.7 34.8 %collective-permute-start.1 = (bf16[160,1408]{1,0:T(8,128)(2,1)}, bf16[160,1408]{1,0:T(8,128)(2,1)}, u32[]{:S(2)}, u32[]{:S(2)}) collective-permute-start(bf16[160,1408]{1,0:T(8,128)(2,1)} %copy-done.43), channel_id=1, source_target_pairs={{0,4},{4,0},{8,12},{12,8},{16,20},{20,16},{24,28},{28,24},{1,5},{5... | collective-permute-start | bytes 1351688 | tf_op jit(solution)/shard_map/ppermute | solution.py:68
  54.2 38.0 %collective-permute-start.10 = (bf16[160,1408]{1,0:T(8,128)(2,1)}, bf16[160,1408]{1,0:T(8,128)(2,1)}, u32[]{:S(2)}, u32[]{:S(2)}) collective-permute-start(bf16[160,1408]{1,0:T(8,128)(2,1)} %collective-permute-done.4.refs_2_), channel_id=1, source_target_pairs={{0,4},{4,0},{8,12},{12,8},{16,20},{20,16},{24,28},{28,24},{1,5},{5... | collective-permute-start | bytes 1351688 | tf_op jit(solution)/shard_map/ppermute | solution.py:68
  85.8 10.7 %collective-permute-start.6 = (bf16[384,1280]{1,0:T(8,128)(2,1)}, bf16[384,1280]{1,0:T(8,128)(2,1)}, u32[]{:S(2)}, u32[]{:S(2)}) collective-permute-start(bf16[384,1280]{1,0:T(8,128)(2,1)} %collective-permute-done.3), channel_id=1, source_target_pairs={{0,1},{1,0},{2,3},{3,2},{4,5},{5,4},{6,7},{7,6},{8,9},{9,8},{10,11... | collective-permute-start | bytes 2949128 | tf_op jit(solution)/shard_map/ppermute | solution.py:68
  87.5 12.4 %collective-permute-start.7 = (bf16[384,1280]{1,0:T(8,128)(2,1)S(1)}, bf16[384,1280]{1,0:T(8,128)(2,1)}, u32[]{:S(2)}, u32[]{:S(2)}) collective-permute-start(bf16[384,1280]{1,0:T(8,128)(2,1)S(1)} %copy-done.13), channel_id=1, source_target_pairs={{0,1},{1,0},{2,3},{3,2},{4,5},{5,4},{6,7},{7,6},{8,9},{9,8},{10,11... | collective-permute-start | bytes 2949128 | tf_op jit(solution)/shard_map/ppermute | solution.py:68
  94.2 13.5 %collective-permute-start.12 = (bf16[160,1408]{1,0:T(8,128)(2,1)}, bf16[160,1408]{1,0:T(8,128)(2,1)S(1)}, u32[]{:S(2)}, u32[]{:S(2)}) collective-permute-start(bf16[160,1408]{1,0:T(8,128)(2,1)} %collective-permute-done.9.refs_4_), channel_id=1, source_target_pairs={{0,4},{4,0},{8,12},{12,8},{16,20},{20,16},{24,28},{28,24},{1,5},{5... | collective-permute-start | bytes 1351688 | tf_op jit(solution)/shard_map/ppermute | solution.py:68
  133.7 9.6 %collective-permute-start.13 = (bf16[96,1280]{1,0:T(8,128)(2,1)}, bf16[96,1280]{1,0:T(8,128)(2,1)S(1)}, u32[]{:S(2)}, u32[]{:S(2)}) collective-permute-start(bf16[96,1280]{1,0:T(8,128)(2,1)} %get-tuple-element.124), channel_id=1, source_target_pairs={{0,1},{1,0},{2,3},{3,2},{4,5},{5,4},{6,7},{7,6},{8,9},{9,8},{10,11... | collective-permute-start | bytes 737288 | tf_op jit(solution)/shard_map/ppermute | solution.py:68
  133.7 9.6 %collective-permute-start.14 = (bf16[96,1280]{1,0:T(8,128)(2,1)}, bf16[96,1280]{1,0:T(8,128)(2,1)S(1)}, u32[]{:S(2)}, u32[]{:S(2)}) collective-permute-start(bf16[96,1280]{1,0:T(8,128)(2,1)} %get-tuple-element.125), channel_id=1, source_target_pairs={{0,1},{1,0},{2,3},{3,2},{4,5},{5,4},{6,7},{7,6},{8,9},{9,8},{10,11... | collective-permute-start | bytes 737288 | tf_op jit(solution)/shard_map/ppermute | solution.py:68
  147.0 23.9 %collective-permute-start.17 = (bf16[384,1280]{1,0:T(8,128)(2,1)}, bf16[384,1280]{1,0:T(8,128)(2,1)S(1)}, u32[]{:S(2)}, u32[]{:S(2)}) collective-permute-start(bf16[384,1280]{1,0:T(8,128)(2,1)} %pair_sum.2), channel_id=1, source_target_pairs={{0,2},{1,3},{2,0},{3,1},{4,6},{5,7},{6,4},{7,5},{8,10},{9,11},{10,... | collective-permute-start | bytes 2949128 | tf_op jit(solution)/shard_map/ppermute | solution.py:68
  161.7 9.2 %collective-permute-start.18 = (bf16[96,1280]{1,0:T(8,128)(2,1)}, bf16[96,1280]{1,0:T(8,128)(2,1)S(1)}, u32[]{:S(2)}, u32[]{:S(2)}) collective-permute-start(bf16[96,1280]{1,0:T(8,128)(2,1)} %get-tuple-element.133), channel_id=1, source_target_pairs={{0,1},{1,0},{2,3},{3,2},{4,5},{5,4},{6,7},{7,6},{8,9},{9,8},{10,11... | collective-permute-start | bytes 737288 | tf_op jit(solution)/shard_map/ppermute | solution.py:68
  177.1 25.3 %collective-permute-start.22 = (bf16[384,1280]{1,0:T(8,128)(2,1)}, bf16[384,1280]{1,0:T(8,128)(2,1)S(1)}, u32[]{:S(2)}, u32[]{:S(2)}) collective-permute-start(bf16[384,1280]{1,0:T(8,128)(2,1)} %get-tuple-element.138.refs_0_), channel_id=1, source_target_pairs={{0,2},{1,3},{2,0},{3,1},{4,6},{5,7},{6,4},{7,5},{8,10},{9,11},{10,... | collective-permute-start | bytes 2949128 | tf_op jit(solution)/shard_map/ppermute | solution.py:68
  177.4 9.9 %collective-permute-start.23 = (bf16[384,1280]{1,0:T(8,128)(2,1)}, bf16[384,1280]{1,0:T(8,128)(2,1)S(1)}, u32[]{:S(2)}, u32[]{:S(2)}) collective-permute-start(bf16[384,1280]{1,0:T(8,128)(2,1)} %get-tuple-element.138.refs_0_), channel_id=1, source_target_pairs={{0,1},{1,0},{2,3},{3,2},{4,5},{5,4},{6,7},{7,6},{8,9},{9,8},{10,11... | collective-permute-start | bytes 2949128 | tf_op jit(solution)/shard_map/ppermute | solution.py:68
  214.2 9.6 %collective-permute-start.25 = (bf16[96,1280]{1,0:T(8,128)(2,1)}, bf16[96,1280]{1,0:T(8,128)(2,1)S(1)}, u32[]{:S(2)}, u32[]{:S(2)}) collective-permute-start(bf16[96,1280]{1,0:T(8,128)(2,1)} %get-tuple-element.150), channel_id=1, source_target_pairs={{0,1},{1,0},{2,3},{3,2},{4,5},{5,4},{6,7},{7,6},{8,9},{9,8},{10,11... | collective-permute-start | bytes 737288 | tf_op jit(solution)/shard_map/ppermute | solution.py:68
  214.5 9.4 %collective-permute-start.26 = (bf16[96,1280]{1,0:T(8,128)(2,1)}, bf16[96,1280]{1,0:T(8,128)(2,1)S(1)}, u32[]{:S(2)}, u32[]{:S(2)}) collective-permute-start(bf16[96,1280]{1,0:T(8,128)(2,1)} %get-tuple-element.151), channel_id=1, source_target_pairs={{0,1},{1,0},{2,3},{3,2},{4,5},{5,4},{6,7},{7,6},{8,9},{9,8},{10,11... | collective-permute-start | bytes 737288 | tf_op jit(solution)/shard_map/ppermute | solution.py:68
  214.7 9.6 %collective-permute-start.27 = (bf16[96,1280]{1,0:T(8,128)(2,1)}, bf16[96,1280]{1,0:T(8,128)(2,1)S(1)}, u32[]{:S(2)}, u32[]{:S(2)}) collective-permute-start(bf16[96,1280]{1,0:T(8,128)(2,1)} %get-tuple-element.152), channel_id=1, source_target_pairs={{0,1},{1,0},{2,3},{3,2},{4,5},{5,4},{6,7},{7,6},{8,9},{9,8},{10,11... | collective-permute-start | bytes 737288 | tf_op jit(solution)/shard_map/ppermute | solution.py:68
  215.0 9.4 %collective-permute-start.28 = (bf16[96,1280]{1,0:T(8,128)(2,1)}, bf16[96,1280]{1,0:T(8,128)(2,1)S(1)}, u32[]{:S(2)}, u32[]{:S(2)}) collective-permute-start(bf16[96,1280]{1,0:T(8,128)(2,1)} %get-tuple-element.153), channel_id=1, source_target_pairs={{0,1},{1,0},{2,3},{3,2},{4,5},{5,4},{6,7},{7,6},{8,9},{9,8},{10,11... | collective-permute-start | bytes 737288 | tf_op jit(solution)/shard_map/ppermute | solution.py:68
  215.2 42.8 %collective-permute-start.32 = (bf16[96,1280]{1,0:T(8,128)(2,1)}, bf16[96,1280]{1,0:T(8,128)(2,1)S(1)}, u32[]{:S(2)}, u32[]{:S(2)}) collective-permute-start(bf16[96,1280]{1,0:T(8,128)(2,1)} %get-tuple-element.158), channel_id=1, source_target_pairs={{0,1},{1,0},{2,3},{3,2},{4,5},{5,4},{6,7},{7,6},{8,9},{9,8},{10,11... | collective-permute-start | bytes 737288 | tf_op jit(solution)/shard_map/ppermute | solution.py:68
  223.7 34.3 %collective-permute-start.33 = (bf16[96,1280]{1,0:T(8,128)(2,1)}, bf16[96,1280]{1,0:T(8,128)(2,1)}, u32[]{:S(2)}, u32[]{:S(2)}) collective-permute-start(bf16[96,1280]{1,0:T(8,128)(2,1)} %get-tuple-element.159), channel_id=1, source_target_pairs={{0,1},{1,0},{2,3},{3,2},{4,5},{5,4},{6,7},{7,6},{8,9},{9,8},{10,11... | collective-permute-start | bytes 737288 | tf_op jit(solution)/shard_map/ppermute | solution.py:68
  223.9 34.1 %collective-permute-start.34 = (bf16[96,1280]{1,0:T(8,128)(2,1)}, bf16[96,1280]{1,0:T(8,128)(2,1)}, u32[]{:S(2)}, u32[]{:S(2)}) collective-permute-start(bf16[96,1280]{1,0:T(8,128)(2,1)} %get-tuple-element.160), channel_id=1, source_target_pairs={{0,1},{1,0},{2,3},{3,2},{4,5},{5,4},{6,7},{7,6},{8,9},{9,8},{10,11... | collective-permute-start | bytes 737288 | tf_op jit(solution)/shard_map/ppermute | solution.py:68
  224.3 33.7 %collective-permute-start.35 = (bf16[96,1280]{1,0:T(8,128)(2,1)}, bf16[96,1280]{1,0:T(8,128)(2,1)}, u32[]{:S(2)}, u32[]{:S(2)}) collective-permute-start(bf16[96,1280]{1,0:T(8,128)(2,1)} %get-tuple-element.161), channel_id=1, source_target_pairs={{0,1},{1,0},{2,3},{3,2},{4,5},{5,4},{6,7},{7,6},{8,9},{9,8},{10,11... | collective-permute-start | bytes 737288 | tf_op jit(solution)/shard_map/ppermute | solution.py:68
  227.9 30.2 %collective-permute-start.31 = (bf16[384,1280]{1,0:T(8,128)(2,1)}, bf16[384,1280]{1,0:T(8,128)(2,1)}, u32[]{:S(2)}, u32[]{:S(2)}) collective-permute-start(bf16[384,1280]{1,0:T(8,128)(2,1)} %pair_sum.3), channel_id=1, source_target_pairs={{0,2},{1,3},{2,0},{3,1},{4,6},{5,7},{6,4},{7,5},{8,10},{9,11},{10,... | collective-permute-start | bytes 2949128 | tf_op jit(solution)/shard_map/ppermute | solution.py:68
  238.6 229.0 %reduce-scatter.5.cloned.1.call-start = ((), (), s32[]{:S(2)}) async-start(), calls=%async_computation.5 | async-start | bytes 3686400 | tf_op jit(solution)/shard_map/reduce_scatter | solution.py:725
  265.1 26.1 %collective-permute-start.36 = (bf16[384,1280]{1,0:T(8,128)(2,1)}, bf16[384,1280]{1,0:T(8,128)(2,1)}, u32[]{:S(2)}, u32[]{:S(2)}) collective-permute-start(bf16[384,1280]{1,0:T(8,128)(2,1)} %get-tuple-element.166), channel_id=1, source_target_pairs={{0,2},{1,3},{2,0},{3,1},{4,6},{5,7},{6,4},{7,5},{8,10},{9,11},{10,... | collective-permute-start | bytes 2949128 | tf_op jit(solution)/shard_map/ppermute | solution.py:68
  266.4 26.4 %collective-permute-start.30 = (bf16[384,1280]{1,0:T(8,128)(2,1)}, bf16[384,1280]{1,0:T(8,128)(2,1)}, u32[]{:S(2)}, u32[]{:S(2)}) collective-permute-start(bf16[384,1280]{1,0:T(8,128)(2,1)} %slice.200), channel_id=1, source_target_pairs={{0,1},{1,0},{2,3},{3,2},{4,5},{5,4},{6,7},{7,6},{8,9},{9,8},{10,11... | collective-permute-start | bytes 2949128 | tf_op jit(solution)/shard_map/ppermute | solution.py:68
  292.6 33.1 %collective-permute-start.29 = (bf16[384,1280]{1,0:T(8,128)(2,1)}, bf16[384,1280]{1,0:T(8,128)(2,1)S(1)}, u32[]{:S(2)}, u32[]{:S(2)}) collective-permute-start(bf16[384,1280]{1,0:T(8,128)(2,1)} %slice.198), channel_id=1, source_target_pairs={{0,1},{1,0},{2,3},{3,2},{4,5},{5,4},{6,7},{7,6},{8,9},{9,8},{10,11... | collective-permute-start | bytes 2949128 | tf_op jit(solution)/shard_map/ppermute | solution.py:68
  295.3 30.4 %collective-permute-start.38 = (bf16[384,1280]{1,0:T(8,128)(2,1)}, bf16[384,1280]{1,0:T(8,128)(2,1)S(1)}, u32[]{:S(2)}, u32[]{:S(2)}) collective-permute-start(bf16[384,1280]{1,0:T(8,128)(2,1)} %add_convert_fusion.1), channel_id=1, source_target_pairs={{0,2},{1,3},{2,0},{3,1},{4,6},{5,7},{6,4},{7,5},{8,10},{9,11},{10,... | collective-permute-start | bytes 2949128 | tf_op jit(solution)/shard_map/ppermute | solution.py:68
  338.0 29.5 %collective-permute-start.42 = (bf16[384,1280]{1,0:T(8,128)(2,1)}, bf16[384,1280]{1,0:T(8,128)(2,1)}, u32[]{:S(2)}, u32[]{:S(2)}) collective-permute-start(bf16[384,1280]{1,0:T(8,128)(2,1)} %add_convert_fusion), channel_id=1, source_target_pairs={{0,2},{1,3},{2,0},{3,1},{4,6},{5,7},{6,4},{7,5},{8,10},{9,11},{10,... | collective-permute-start | bytes 2949128 | tf_op jit(solution)/shard_map/ppermute | solution.py:68
  349.6 17.9 %collective-permute-start.41 = (bf16[160,1408]{1,0:T(8,128)(2,1)}, bf16[160,1408]{1,0:T(8,128)(2,1)}, u32[]{:S(2)}, u32[]{:S(2)}) collective-permute-start(bf16[160,1408]{1,0:T(8,128)(2,1)} %get-tuple-element.221), channel_id=1, source_target_pairs={{0,4},{4,0},{8,12},{12,8},{16,20},{20,16},{24,28},{28,24},{1,5},{5... | collective-permute-start | bytes 1351688 | tf_op jit(solution)/shard_map/ppermute | solution.py:68
  351.2 29.9 %collective-permute-start.43 = (bf16[160,1408]{1,0:T(8,128)(2,1)}, bf16[160,1408]{1,0:T(8,128)(2,1)}, u32[]{:S(2)}, u32[]{:S(2)}) collective-permute-start(bf16[160,1408]{1,0:T(8,128)(2,1)} %get-tuple-element.220), channel_id=1, source_target_pairs={{0,4},{4,0},{8,12},{12,8},{16,20},{20,16},{24,28},{28,24},{1,5},{5... | collective-permute-start | bytes 1351688 | tf_op jit(solution)/shard_map/ppermute | solution.py:68
  351.6 43.7 %collective-permute-start.44 = (bf16[160,1408]{1,0:T(8,128)(2,1)}, bf16[160,1408]{1,0:T(8,128)(2,1)}, u32[]{:S(2)}, u32[]{:S(2)}) collective-permute-start(bf16[160,1408]{1,0:T(8,128)(2,1)} %get-tuple-element.219), channel_id=1, source_target_pairs={{0,4},{4,0},{8,12},{12,8},{16,20},{20,16},{24,28},{28,24},{1,5},{5... | collective-permute-start | bytes 1351688 | tf_op jit(solution)/shard_map/ppermute | solution.py:68
  353.3 50.9 %collective-permute-start.45 = (bf16[160,1408]{1,0:T(8,128)(2,1)}, bf16[160,1408]{1,0:T(8,128)(2,1)}, u32[]{:S(2)}, u32[]{:S(2)}) collective-permute-start(bf16[160,1408]{1,0:T(8,128)(2,1)} %get-tuple-element.218), channel_id=1, source_target_pairs={{0,4},{4,0},{8,12},{12,8},{16,20},{20,16},{24,28},{28,24},{1,5},{5... | collective-permute-start | bytes 1351688 | tf_op jit(solution)/shard_map/ppermute | solution.py:68
  413.4 9.6 %collective-permute-start.53 = (f32[1,160,160]{2,1,0:T(8,128)S(1)}, f32[1,160,160]{2,1,0:T(8,128)S(1)}, u32[]{:S(2)}, u32[]{:S(2)}) collective-permute-start(f32[1,160,160]{2,1,0:T(8,128)S(1)} %convolution_bitcast_fusion.2), channel_id=1, source_target_pairs={{0,1},{1,0},{2,3},{3,2},{4,5},{5,4},{6,7},{7,6},{8,9},{9,8},{10,11... | collective-permute-start | bytes 307208 | tf_op jit(solution)/shard_map/ppermute | solution.py:68
  423.0 12.2 %collective-permute-start.54 = (f32[1,160,160]{2,1,0:T(8,128)S(1)}, f32[1,160,160]{2,1,0:T(8,128)S(1)}, u32[]{:S(2)}, u32[]{:S(2)}) collective-permute-start(f32[1,160,160]{2,1,0:T(8,128)S(1)} %add.239), channel_id=1, source_target_pairs={{0,2},{1,3},{2,0},{3,1},{4,6},{5,7},{6,4},{7,5},{8,10},{9,11},{10,... | collective-permute-start | bytes 307208 | tf_op jit(solution)/shard_map/ppermute | solution.py:68
  424.7 18.0 %collective-permute-start.56 = (f32[8,1280]{1,0:T(8,128)S(1)}, f32[8,1280]{1,0:T(8,128)S(1)}, u32[]{:S(2)}, u32[]{:S(2)}) collective-permute-start(f32[8,1280]{1,0:T(8,128)S(1)} %add.242), channel_id=1, source_target_pairs={{0,2},{1,3},{2,0},{3,1},{4,6},{5,7},{6,4},{7,5},{8,10},{9,11},{10,... | collective-permute-start | bytes 122888 | tf_op jit(solution)/shard_map/ppermute | solution.py:68
  427.0 35.3 %collective-permute-start.50 = (bf16[160,1408]{1,0:T(8,128)(2,1)}, bf16[160,1408]{1,0:T(8,128)(2,1)S(1)}, u32[]{:S(2)}, u32[]{:S(2)}) collective-permute-start(bf16[160,1408]{1,0:T(8,128)(2,1)} %get-tuple-element.216), channel_id=1, source_target_pairs={{0,16},{4,20},{8,24},{12,28},{16,0},{20,4},{24,8},{28,12},{1,17},{... | collective-permute-start | bytes 1351688 | tf_op jit(solution)/shard_map/ppermute | solution.py:68
  431.5 30.8 %collective-permute-start.51 = (bf16[160,1408]{1,0:T(8,128)(2,1)}, bf16[160,1408]{1,0:T(8,128)(2,1)S(1)}, u32[]{:S(2)}, u32[]{:S(2)}) collective-permute-start(bf16[160,1408]{1,0:T(8,128)(2,1)} %get-tuple-element.215), channel_id=1, source_target_pairs={{0,24},{4,28},{8,16},{12,20},{16,8},{20,12},{24,0},{28,4},{1,25},{... | collective-permute-start | bytes 1351688 | tf_op jit(solution)/shard_map/ppermute | solution.py:68
  435.2 32.3 %collective-permute-start.52 = (bf16[160,1408]{1,0:T(8,128)(2,1)S(1)}, bf16[160,1408]{1,0:T(8,128)(2,1)S(1)}, u32[]{:S(2)}, u32[]{:S(2)}) collective-permute-start(bf16[160,1408]{1,0:T(8,128)(2,1)S(1)} %get-tuple-element.214), channel_id=1, source_target_pairs={{0,8},{4,12},{8,0},{12,4},{16,24},{20,28},{24,16},{28,20},{1,9},{5... | collective-permute-start | bytes 1351688 | tf_op jit(solution)/shard_map/ppermute | solution.py:68
  471.2 11.5 %collective-permute-start.58 = (f32[9,1280]{1,0:T(8,128)S(1)}, f32[9,1280]{1,0:T(8,128)S(1)}, u32[]{:S(2)}, u32[]{:S(2)}) collective-permute-start(f32[9,1280]{1,0:T(8,128)S(1)} %add.246), channel_id=1, source_target_pairs={{0,8},{4,12},{8,0},{12,4},{16,24},{20,28},{24,16},{28,20},{1,9},{5... | collective-permute-start | bytes 138248 | tf_op jit(solution)/shard_map/ppermute | solution.py:68
  496.3 13.2 %collective-permute-start.61 = (f32[3,160,160]{2,1,0:T(8,128)S(1)}, f32[3,160,160]{2,1,0:T(8,128)S(1)}, u32[]{:S(2)}, u32[]{:S(2)}) collective-permute-start(f32[3,160,160]{2,1,0:T(8,128)S(1)} %fusion.38), channel_id=1, source_target_pairs={{0,2},{1,3},{2,0},{3,1},{4,6},{5,7},{6,4},{7,5},{8,10},{9,11},{10,... | collective-permute-start | bytes 921608 | tf_op jit(solution)/shard_map/ppermute | solution.py:68
  (89 other events, 844.7 us)
Sparse Core Ops, SparseCore 0:
  10.8 94.9 all-gather.2
  108.6 59.2 all-gather.4
  238.7 77.1 reduce-scatter.2
  332.6 89.5 reduce-scatter.4

commit v8 on v7

--- a/solution.py
+++ b/solution.py
@@ -943,7 +943,7 @@
 
     mom_up_new, update_up = momentum(mom_up, grad_wu.astype(F32))
     gram_up = gram_of(update_up)
-    lined = tie(lined, gram_up, new_w_down, rows_of)
+    lined = tie(lined, gram_up, new_w_down, vec_sums)
     grad_first = dp_total(lined)
     grad_wq, grad_wo = grad_first[:, :packed], grad_first[:, packed : packed + head_width]
     mom_out_new, update_out = momentum(mom_out, grad_wo)

time: 539 us -> 530 us (0.983)
  transfers between devices with their start and end apart: 66 -> 66, of which waited for: 17 -> 19; matrix products, arithmetic and copies ran while one was open for 19% -> 19% of each run, Pallas kernels for 27% -> 27%
where the time goes in v8:
time: 530 us; the launch traced here: 525 us
  waiting for transfers between devices  163 us (31%)
  Pallas kernels  159 us (30%)
  matrix products  66.3 us (13%)
  starting transfers between devices  56.4 us (11%)
  other arithmetic  33.6 us (6%)
  local copies, waits for them, and re-layouts  31.2 us (6%)
  between operations  15.9 us (3%)
    ppermute x62, waiting for transfers between devices, swap(): return lax.ppermute(value, axis, [(i, i ^ mask) for i in range(size)])  162 us
    ppermute x62, starting transfers between devices, swap(): return lax.ppermute(value, axis, [(i, i ^ mask) for i in range(size)])  56.3 us
    dot_general x10, matrix products, mm(): return lax.dot_general(left, right, dims, preferred_element_type=F32)  55 us
    pallas_call x2, Pallas kernels, attn_back_call(): pl.pallas_call(partial(attn_back_body, heads, last_part, first), grid=(co...  44.7 us
    pallas_call x3, Pallas kernels, attn_call(): pl.pallas_call(partial(attn_body, heads, emits, len(held)), grid=(count /...  31.4 us
    pallas_call x3, Pallas kernels, mlp_call(): pl.pallas_call(partial(mlp_body, min(256, hidden_width), emits, len(held)...  30.3 us
    unnamed x145, local copies, waits for them, and re-layouts  18.8 us
    pallas_call x3, Pallas kernels, row_call(): pl.pallas_call(partial(row_body, body, len(rows_in)), grid=(PIECES,), in_...  17.4 us
  transfers between devices with their start and end apart: 66, of which 19 were waited for; matrix products, arithmetic and copies ran while one was open for 19% of the time, Pallas kernels for 27%

profile of v8, /device:TPU:0, one launch (start us, length us, event | category | flops | bytes accessed | tf_op | source)
XLA Modules:
  0.0 524.9 jit_solution(930073317232251562)
XLA Ops:
  11.5 3.0 collective-permute-start.3
  15.1 3.7 collective-permute-start
  21.1 15.6 %collective-permute-done.refs_6_ = bf16[160,1408]{1,0:T(8,128)(2,1)S(1)} collective-permute-done((bf16[160,1408]{1,0:T(8,128)(2,1)S(1)}, bf16[160,1408]{1,0:T(8,128)(2,1)S(1)}, u32[]{:S(2)}, u32[]{:S(2)}) %collective-permute-start) | collective-permute-done | bytes 450592 | tf_op jit(solution)/shard_map/ppermute | solution.py:68
  37.5 15.2 %collective-permute-done.4.refs_2_ = bf16[160,1408]{1,0:T(8,128)(2,1)} collective-permute-done((bf16[160,1408]{1,0:T(8,128)(2,1)S(1)}, bf16[160,1408]{1,0:T(8,128)(2,1)}, u32[]{:S(2)}, u32[]{:S(2)}) %collective-permute-start.4) | collective-permute-done | bytes 450592 | tf_op jit(solution)/shard_map/ppermute | solution.py:68
  54.7 31.1 %collective-permute-done.9.refs_4_ = bf16[160,1408]{1,0:T(8,128)(2,1)} collective-permute-done((bf16[160,1408]{1,0:T(8,128)(2,1)S(1)}, bf16[160,1408]{1,0:T(8,128)(2,1)}, u32[]{:S(2)}, u32[]{:S(2)}) %collective-permute-start.9) | collective-permute-done | bytes 450592 | tf_op jit(solution)/shard_map/ppermute | solution.py:68
  88.0 4.2 collective-permute-done.10.refs_3_
  96.5 3.5 pad_maximum_fusion.x_ref
  100.0 3.3 pad_maximum_fusion.1
  103.3 4.4 collective-permute-done.12.refs_5_
  108.5 4.0 place_rows.1
  115.7 9.8 %norm_qkv.1 = (bf16[1536,1280]{1,0:T(8,128)(2,1)}, bf16[1536,1024]{1,0:T(8,128)(2,1)}) custom-call(bf16[1536,1280]{1,0:T(8,128)(2,1)} %pad_maximum_fusion.x_ref, f32[8,1280]{1,0:T(8,128)} %slice.149.vec_ref.refs_7_.refs_8_, bf16[1280,1024]{1,0:T(8,128)(2,1)} %get-tuple-element.118.w_ref, f32[1,1024]{1,0:T(1,128)} %pad_maximum_fusion.7.bias_ref), custom_call_target="tpu_custom_call" | custom-call | flops 1000000 | bytes 100000 | tf_op jit(solution)/shard_map/norm_qkv/pallas_call | solution.py:109
  125.5 8.2 %attn_fwd.3 = (bf16[1536,384]{1,0:T(8,128)(2,1)}, f32[8,1536]{1,0:T(8,128)}, bf16[96,1280]{1,0:T(8,128)(2,1)}, bf16[96,1280]{1,0:T(8,128)(2,1)}, bf16[96,1280]{1,0:T(8,128)(2,1)}, /*index=5*/bf16[96,1280]{1,0:T(8,128)(2,1)}) custom-call(bf16[1536,1024]{1,0:T(8,128)(2,1)} %get-tuple-element.128.q_ref.qkv_ref, ...), custom_call_target="tpu_custom_call" | custom-call | flops 1000000 | bytes 100000 | tf_op jit(solution)/shard_map/attn_fwd/pallas_call | solution.py:266
  134.7 8.6 %attn_fwd.4 = (bf16[1536,384]{1,0:T(8,128)(2,1)}, f32[8,1536]{1,0:T(8,128)}, bf16[384,1280]{1,0:T(8,128)(2,1)}) custom-call(bf16[1536,1024]{1,0:T(8,128)(2,1)} %get-tuple-element.128.q_ref.qkv_ref, bf16[1536,1024]{1,0:T(8,128)(2,1)} %get-tuple-element.128.q_ref.qkv_ref, ...), custom_call_target="tpu_custom_call", output_to_operand_aliasing={{0}: (4, {}), {1}: (5, {})} | custom-call | flops 1000000 | bytes 100000 | tf_op jit(solution)/shard_map/attn_fwd/pallas_call | solution.py:266
  144.3 2.7 pair_sum.2
  147.0 14.6 %attn_fwd.5 = (bf16[1536,384]{1,0:T(8,128)(2,1)}, f32[8,1536]{1,0:T(8,128)}, bf16[384,1280]{1,0:T(8,128)(2,1)}, bf16[96,1280]{1,0:T(8,128)(2,1)}, bf16[96,1280]{...) custom-call(bf16[1536,1024]{1,0:T(8,128)(2,1)} %get-tuple-element.12, ...), custom_call_target="tpu_custom_call", output_to_operand_aliasing={{0}: (4, {}), {1}: (5, {})} | custom-call | flops 1000000 | bytes 100000 | tf_op jit(solution)/shard_map/attn_fwd/pallas_call | solution.py:266
  164.2 6.7 %collective-permute-done.17.refs_2_ = bf16[384,1280]{1,0:T(8,128)(2,1)S(1)} collective-permute-done((bf16[384,1280]{1,0:T(8,128)(2,1)}, bf16[384,1280]{1,0:T(8,128)(2,1)S(1)}, u32[]{:S(2)}, u32[]{:S(2)}) %collective-permute-start.17) | collective-permute-done | bytes 983072 | tf_op jit(solution)/shard_map/ppermute | solution.py:68
  172.1 5.0 residual.1
  177.4 9.9 %fusion.42.refs_4_.refs_3_ = f32[1536,1280]{1,0:T(8,128)} fusion(bf16[1536,1280]{1,0:T(8,128)(2,1)} %pad_maximum_fusion.1, bf16[1280,1280]{1,0:T(8,128)(2,1)} %all-gather.3.cloned.1.call-done), kind=kOutput, calls=%fused_computation.121 | convolution fusion | flops 5033164800 | bytes 15073280 | tf_op jit(solution)/shard_map/dot_general | solution.py:43
  188.2 14.2 %mlp_up.3 = (bf16[1536,1280]{1,0:T(8,128)(2,1)}, bf16[1536,1280]{1,0:T(8,128)(2,1)}, f32[8,1280]{1,0:T(8,128)}, bf16[384,1280]{1,0:T(8,128)(2,1)}, bf16[96,1280]...) custom-call(bf16[384,1280]{1,0:T(8,128)(2,1)} %get-tuple-element.138.refs_0_, ...), custom_call_target="tpu_custom_call" | custom-call | flops 1000000 | bytes 100000 | tf_op jit(solution)/shard_map/mlp_up/pallas_call | solution.py:471
  206.1 8.0 %mlp_up.4 = (bf16[1536,1280]{1,0:T(8,128)(2,1)}, bf16[1536,1280]{1,0:T(8,128)(2,1)}, f32[8,1280]{1,0:T(8,128)}, bf16[96,1280]{1,0:T(8,128)(2,1)}, bf16[96,1280]{...) custom-call(bf16[384,1280]{1,0:T(8,128)(2,1)} %copy-done.35, ...), custom_call_target="tpu_custom_call", output_to_operand_aliasing={{0}: (4, {}), {1}: (5, {})} | custom-call | flops 1000000 | bytes 100000 | tf_op jit(solution)/shard_map/mlp_up/pallas_call | solution.py:471
  215.5 8.2 %mlp_up.5 = (bf16[1536,1280]{1,0:T(8,128)(2,1)}, bf16[1536,1280]{1,0:T(8,128)(2,1)}, f32[8,1280]{1,0:T(8,128)}, bf16[384,1280]{1,0:T(8,128)(2,1)}) custom-call(bf16[384,1280]{1,0:T(8,128)(2,1)} %copy-done.31, bf16[1280,1280]{1,0:T(8,128)(2,1)} %all-gather.5.cloned.1.call-done.refs_2_.refs_1_, ...), custom_call_target="tpu_custom_call", output_to_operand_aliasing={{0}: (4, {}), {1}: (5, {})} | custom-call | flops 1000000 | bytes 100000 | tf_op jit(solution)/shard_map/mlp_up/pallas_call | solution.py:471
  225.1 2.7 pair_sum.3
  229.6 8.9 %convolution_convert_fusion.1 = bf16[1280,1280]{1,0:T(8,128)(2,1)} fusion(bf16[1536,1280]{1,0:T(8,128)(2,1)S(1)} %copy-done.12, bf16[1536,1280]{1,0:T(8,128)(2,1)} %get-tuple-element.157), kind=kOutput, calls=%fused_computation.1 | convolution fusion | flops 5034803200 | bytes 11141120 | tf_op jit(solution)/shard_map/dot_general | solution.py:43
  240.3 9.4 %convolution_convert_fusion = bf16[1280,1280]{1,0:T(8,128)(2,1)} fusion(bf16[1536,1280]{1,0:T(8,128)(2,1)} %get-tuple-element.156, bf16[384,1280]{1,0:T(8,128)(2,1)} %copy-done.35, bf16[384,1280]{1,0:T(8,128)(2,1)S(1)} %copy-done.32, bf16[384,1280]{1,0:T(8,128)(2,1)S(1)} %copy-done.34, bf16[384,1280]{1,0:T(8,128)(2,1)S(1)} %copy-done.30), kind=kOutput, calls=%fused_computation | convolution fusion | flops 5050531840 | bytes 11141120 | tf_op jit(solution)/shard_map/dot_general | solution.py:43
  249.8 5.4 %convolution_convert_fusion.3 = bf16[768,1280]{1,0:T(8,128)(2,1)S(1)} fusion(bf16[1280,1280]{1,0:T(8,128)(2,1)} %all-gather.3.cloned.1.call-done, bf16[1536,1280]{1,0:T(8,128)(2,1)} %get-tuple-element.157), kind=kOutput, calls=%fused_computation.12 | convolution fusion | flops 2517565440 | bytes 7208960 | tf_op jit(solution)/shard_map/dot_general | solution.py:43
  255.2 2.7 convolution_convert_fusion.4
  258.7 6.3 %second_back.1 = (f32[384,1280]{1,0:T(8,128)}, bf16[384,1280]{1,0:T(8,128)(2,1)}, f32[8,1280]{1,0:T(8,128)}) custom-call(f32[384,1280]{1,0:T(8,128)} %get-tuple-element.137.refs_0_, bf16[384,1280]{1,0:T(8,128)(2,1)} %get-tuple-element.141.refs_1_, bf16[384,1280]{1,0:T(8,128)(2,1)} %collective-permute-done.31.refs_2_, bf16[384,1280]{1,0:T(8,128)(2,1)} %refs_3_.1, ...), custom_call_target="tpu_custom_call" | custom-call | flops 1000000 | bytes 100000 | tf_op jit(solution)/shard_map/second_back/pallas_call | solution.py:559
  269.2 21.9 %attn_bwd.2 = (bf16[1536,1024]{1,0:T(8,128)(2,1)}, f32[8,384]{1,0:T(8,128)}, f32[1536,384]{1,0:T(8,128)}, f32[1536,384]{1,0:T(8,128)}) custom-call(bf16[768,1280]{1,0:T(8,128)(2,1)} %copy-done.9, bf16[1280,384]{1,0:T(8,128)(2,1)} %get-tuple-element.120.wo_ref, bf16[1536,384]{1,0:T(8,128)(2,1)} %get-tuple-element.167.att_ref, ...), custom_call_target="tpu_custom_call" | custom-call | flops 1000000 | bytes 100000 | tf_op jit(solution)/shard_map/attn_bwd/pallas_call | solution.py:399
  302.8 22.8 %attn_bwd.3 = (bf16[1536,1024]{1,0:T(8,128)(2,1)}, f32[8,384]{1,0:T(8,128)}) custom-call(bf16[768,1280]{1,0:T(8,128)(2,1)} %copy-done.11, bf16[1280,384]{1,0:T(8,128)(2,1)} %get-tuple-element.120.wo_ref, bf16[1536,384]{1,0:T(8,128)(2,1)} %get-tuple-element.167.att_ref, ...), custom_call_target="tpu_custom_call", output_to_operand_aliasing={{0}: (10, {})} | custom-call | flops 1000000 | bytes 100000 | tf_op jit(solution)/shard_map/attn_bwd/pallas_call | solution.py:399
  325.7 4.3 convolution_convert_fusion.6
  332.4 2.8 collective-permute-done.40
  338.3 6.6 %convolution_convert_fusion.2 = bf16[1280,1024]{1,0:T(8,128)(2,1)S(1)} fusion(bf16[1536,1280]{1,0:T(8,128)(2,1)} %get-tuple-element.178, bf16[1536,1024]{1,0:T(8,128)(2,1)S(1)} %copy-done.8), kind=kOutput, calls=%fused_computation.11 | convolution fusion | flops 4027842560 | bytes 9699328 | tf_op jit(solution)/shard_map/dot_general | solution.py:43
  353.6 13.7 %collective-permute-done.41 = bf16[160,1408]{1,0:T(8,128)(2,1)} collective-permute-done((bf16[160,1408]{1,0:T(8,128)(2,1)}, bf16[160,1408]{1,0:T(8,128)(2,1)}, u32[]{:S(2)}, u32[]{:S(2)}) %collective-permute-start.41) | collective-permute-done | bytes 450592 | tf_op jit(solution)/shard_map/ppermute | solution.py:68
  367.4 13.7 %collective-permute-done.43 = bf16[160,1408]{1,0:T(8,128)(2,1)} collective-permute-done((bf16[160,1408]{1,0:T(8,128)(2,1)}, bf16[160,1408]{1,0:T(8,128)(2,1)}, u32[]{:S(2)}, u32[]{:S(2)}) %collective-permute-start.43) | collective-permute-done | bytes 450592 | tf_op jit(solution)/shard_map/ppermute | solution.py:68
  381.1 14.0 %collective-permute-done.44 = bf16[160,1408]{1,0:T(8,128)(2,1)} collective-permute-done((bf16[160,1408]{1,0:T(8,128)(2,1)}, bf16[160,1408]{1,0:T(8,128)(2,1)}, u32[]{:S(2)}, u32[]{:S(2)}) %collective-permute-start.44) | collective-permute-done | bytes 450592 | tf_op jit(solution)/shard_map/ppermute | solution.py:68
  395.1 8.9 %collective-permute-done.45 = bf16[160,1408]{1,0:T(8,128)(2,1)} collective-permute-done((bf16[160,1408]{1,0:T(8,128)(2,1)}, bf16[160,1408]{1,0:T(8,128)(2,1)}, u32[]{:S(2)}, u32[]{:S(2)}) %collective-permute-start.45) | collective-permute-done | bytes 450592 | tf_op jit(solution)/shard_map/ppermute | solution.py:68
  404.0 4.3 convolution_convert_fusion.5
  409.5 2.8 add_convert_fusion.2
  415.4 6.1 %first_back.1 = (f32[384,1280]{1,0:T(8,128)}, f32[8,1280]{1,0:T(8,128)}) custom-call(bf16[384,1280]{1,0:T(8,128)(2,1)} %refs_0_.3, bf16[384,1280]{1,0:T(8,128)(2,1)} %slice.203.refs_1_, bf16[384,1280]{1,0:T(8,128)(2,1)} %collective-permute-done.42.refs_2_, f32[384,1280]{1,0:T(8,128)} %get-tuple-element.186.refs_3_, bf16[96,1280]{1,0:T(8,128)(2,1)} %copy-done.47, ...), custom_call_target="tpu_custom_call" | custom-call | flops 1000000 | bytes 100000 | tf_op jit(solution)/shard_map/first_back/pallas_call | solution.py:559
  422.9 4.8 collective-permute-start.50
  427.8 3.7 collective-permute-start.51
  438.3 6.8 %polar.2 = f32[1,160,160]{2,1,0:T(8,128)} custom-call(f32[1,160,160]{2,1,0:T(8,128)} %add.240.gram_ref), custom_call_target="tpu_custom_call" | custom-call | tf_op jit(solution)/shard_map/polar/pallas_call | solution.py:612
  445.2 13.4 %collective-permute-done.50 = bf16[160,1408]{1,0:T(8,128)(2,1)} collective-permute-done((bf16[160,1408]{1,0:T(8,128)(2,1)}, bf16[160,1408]{1,0:T(8,128)(2,1)}, u32[]{:S(2)}, u32[]{:S(2)}) %collective-permute-start.50) | collective-permute-done | bytes 450592 | tf_op jit(solution)/shard_map/ppermute | solution.py:68
  471.3 9.0 %collective-permute-start.60 = (f32[9,1280]{1,0:T(8,128)S(1)}, f32[9,1280]{1,0:T(8,128)S(1)}, u32[]{:S(2)}, u32[]{:S(2)}) collective-permute-start(f32[9,1280]{1,0:T(8,128)S(1)} %add.255), channel_id=1, source_target_pairs={{0,8},{4,12},{8,0},{12,4},{16,24},{20,28},{24,16},{28,20},{1,9},{5... | collective-permute-start | bytes 138248 | tf_op jit(solution)/shard_map/ppermute | solution.py:68
  482.7 4.3 collective-permute-start.61
  492.5 8.0 %collective-permute-done.58 = f32[3,160,160]{2,1,0:T(8,128)S(1)} collective-permute-done((f32[3,160,160]{2,1,0:T(8,128)S(1)}, f32[3,160,160]{2,1,0:T(8,128)S(1)}, u32[]{:S(2)}, u32[]{:S(2)}) %collective-permute-start.58) | collective-permute-done | bytes 307232 | tf_op jit(solution)/shard_map/ppermute | solution.py:68
  501.4 9.1 %polar.3 = f32[3,160,160]{2,1,0:T(8,128)} custom-call(f32[3,160,160]{2,1,0:T(8,128)} %fusion.57.gram_ref), custom_call_target="tpu_custom_call" | custom-call | tf_op jit(solution)/shard_map/polar/pallas_call | solution.py:612
  514.4 2.7 convolution_subtract_fusion
  (347 shorter events, 105.7 us)
Async XLA Ops:
  7.3 163.6 %all-gather.3.cloned.1.call-start = ((), (), s32[]{:S(2)}) async-start(), calls=%async_computation.2 | async-start | bytes 3686400 | tf_op jit(solution)/shard_map/all_gather | solution.py:804
  9.4 168.0 %all-gather.5.cloned.1.call-start = ((), (), s32[]{:S(2)}) async-start(), calls=%async_computation.3 | async-start | bytes 3686400 | tf_op jit(solution)/shard_map/all_gather | solution.py:805
  11.4 326.9 %reduce-scatter.3.cloned.1.call-start = ((), (), s32[]{:S(2)}) async-start(), calls=%async_computation.4 | async-start | bytes 3686400 | tf_op jit(solution)/shard_map/reduce_scatter | solution.py:725
  11.5 42.7 %collective-permute-start.3 = (bf16[384,1280]{1,0:T(8,128)(2,1)S(1)}, bf16[384,1280]{1,0:T(8,128)(2,1)}, u32[]{:S(2)}, u32[]{:S(2)}) collective-permute-start(bf16[384,1280]{1,0:T(8,128)(2,1)S(1)} %copy-done.4), channel_id=1, source_target_pairs={{0,2},{1,3},{2,0},{3,1},{4,6},{5,7},{6,4},{7,5},{8,10},{9,11},{10,... | collective-permute-start | bytes 2949128 | tf_op jit(solution)/shard_map/ppermute | solution.py:68
  15.1 21.6 %collective-permute-start = (bf16[160,1408]{1,0:T(8,128)(2,1)S(1)}, bf16[160,1408]{1,0:T(8,128)(2,1)S(1)}, u32[]{:S(2)}, u32[]{:S(2)}) collective-permute-start(bf16[160,1408]{1,0:T(8,128)(2,1)S(1)} %concatenate.52.refs_0_), channel_id=1, source_target_pairs={{0,24},{4,28},{8,16},{12,20},{16,8},{20,12},{24,0},{28,4},{1,25},{... | collective-permute-start | bytes 1351688 | tf_op jit(solution)/shard_map/ppermute | solution.py:68
  18.8 33.9 %collective-permute-start.4 = (bf16[160,1408]{1,0:T(8,128)(2,1)S(1)}, bf16[160,1408]{1,0:T(8,128)(2,1)}, u32[]{:S(2)}, u32[]{:S(2)}) collective-permute-start(bf16[160,1408]{1,0:T(8,128)(2,1)S(1)} %concatenate.52.refs_0_), channel_id=1, source_target_pairs={{0,8},{4,12},{8,0},{12,4},{16,24},{20,28},{24,16},{28,20},{1,9},{5... | collective-permute-start | bytes 1351688 | tf_op jit(solution)/shard_map/ppermute | solution.py:68
  18.8 33.9 %collective-permute-start.5 = (bf16[160,1408]{1,0:T(8,128)(2,1)S(1)}, bf16[160,1408]{1,0:T(8,128)(2,1)}, u32[]{:S(2)}, u32[]{:S(2)}) collective-permute-start(bf16[160,1408]{1,0:T(8,128)(2,1)S(1)} %concatenate.52.refs_0_), channel_id=1, source_target_pairs={{0,4},{4,0},{8,12},{12,8},{16,20},{20,16},{24,28},{28,24},{1,5},{5... | collective-permute-start | bytes 1351688 | tf_op jit(solution)/shard_map/ppermute | solution.py:68
  20.3 65.5 %collective-permute-start.9 = (bf16[160,1408]{1,0:T(8,128)(2,1)S(1)}, bf16[160,1408]{1,0:T(8,128)(2,1)}, u32[]{:S(2)}, u32[]{:S(2)}) collective-permute-start(bf16[160,1408]{1,0:T(8,128)(2,1)S(1)} %concatenate.52.refs_0_), channel_id=1, source_target_pairs={{0,16},{4,20},{8,24},{12,28},{16,0},{20,4},{24,8},{28,12},{1,17},{... | collective-permute-start | bytes 1351688 | tf_op jit(solution)/shard_map/ppermute | solution.py:68
  37.5 54.7 %collective-permute-start.8 = (bf16[384,1280]{1,0:T(8,128)(2,1)S(1)}, bf16[384,1280]{1,0:T(8,128)(2,1)S(1)}, u32[]{:S(2)}, u32[]{:S(2)}) collective-permute-start(bf16[384,1280]{1,0:T(8,128)(2,1)S(1)} %copy-done.13), channel_id=1, source_target_pairs={{0,2},{1,3},{2,0},{3,1},{4,6},{5,7},{6,4},{7,5},{8,10},{9,11},{10,... | collective-permute-start | bytes 2949128 | tf_op jit(solution)/shard_map/ppermute | solution.py:68
  52.7 43.8 %collective-permute-start.2 = (bf16[384,1280]{1,0:T(8,128)(2,1)S(1)}, bf16[384,1280]{1,0:T(8,128)(2,1)}, u32[]{:S(2)}, u32[]{:S(2)}) collective-permute-start(bf16[384,1280]{1,0:T(8,128)(2,1)S(1)} %copy-done.4), channel_id=1, source_target_pairs={{0,1},{1,0},{2,3},{3,2},{4,5},{5,4},{6,7},{7,6},{8,9},{9,8},{10,11... | collective-permute-start | bytes 2949128 | tf_op jit(solution)/shard_map/ppermute | solution.py:68
  52.7 34.8 %collective-permute-start.1 = (bf16[160,1408]{1,0:T(8,128)(2,1)}, bf16[160,1408]{1,0:T(8,128)(2,1)}, u32[]{:S(2)}, u32[]{:S(2)}) collective-permute-start(bf16[160,1408]{1,0:T(8,128)(2,1)} %copy-done.43), channel_id=1, source_target_pairs={{0,4},{4,0},{8,12},{12,8},{16,20},{20,16},{24,28},{28,24},{1,5},{5... | collective-permute-start | bytes 1351688 | tf_op jit(solution)/shard_map/ppermute | solution.py:68
  54.2 38.0 %collective-permute-start.10 = (bf16[160,1408]{1,0:T(8,128)(2,1)}, bf16[160,1408]{1,0:T(8,128)(2,1)}, u32[]{:S(2)}, u32[]{:S(2)}) collective-permute-start(bf16[160,1408]{1,0:T(8,128)(2,1)} %collective-permute-done.4.refs_2_), channel_id=1, source_target_pairs={{0,4},{4,0},{8,12},{12,8},{16,20},{20,16},{24,28},{28,24},{1,5},{5... | collective-permute-start | bytes 1351688 | tf_op jit(solution)/shard_map/ppermute | solution.py:68
  85.8 10.7 %collective-permute-start.6 = (bf16[384,1280]{1,0:T(8,128)(2,1)}, bf16[384,1280]{1,0:T(8,128)(2,1)}, u32[]{:S(2)}, u32[]{:S(2)}) collective-permute-start(bf16[384,1280]{1,0:T(8,128)(2,1)} %collective-permute-done.3), channel_id=1, source_target_pairs={{0,1},{1,0},{2,3},{3,2},{4,5},{5,4},{6,7},{7,6},{8,9},{9,8},{10,11... | collective-permute-start | bytes 2949128 | tf_op jit(solution)/shard_map/ppermute | solution.py:68
  87.5 12.4 %collective-permute-start.7 = (bf16[384,1280]{1,0:T(8,128)(2,1)S(1)}, bf16[384,1280]{1,0:T(8,128)(2,1)}, u32[]{:S(2)}, u32[]{:S(2)}) collective-permute-start(bf16[384,1280]{1,0:T(8,128)(2,1)S(1)} %copy-done.13), channel_id=1, source_target_pairs={{0,1},{1,0},{2,3},{3,2},{4,5},{5,4},{6,7},{7,6},{8,9},{9,8},{10,11... | collective-permute-start | bytes 2949128 | tf_op jit(solution)/shard_map/ppermute | solution.py:68
  94.2 13.5 %collective-permute-start.12 = (bf16[160,1408]{1,0:T(8,128)(2,1)}, bf16[160,1408]{1,0:T(8,128)(2,1)S(1)}, u32[]{:S(2)}, u32[]{:S(2)}) collective-permute-start(bf16[160,1408]{1,0:T(8,128)(2,1)} %collective-permute-done.9.refs_4_), channel_id=1, source_target_pairs={{0,4},{4,0},{8,12},{12,8},{16,20},{20,16},{24,28},{28,24},{1,5},{5... | collective-permute-start | bytes 1351688 | tf_op jit(solution)/shard_map/ppermute | solution.py:68
  133.7 9.6 %collective-permute-start.13 = (bf16[96,1280]{1,0:T(8,128)(2,1)}, bf16[96,1280]{1,0:T(8,128)(2,1)S(1)}, u32[]{:S(2)}, u32[]{:S(2)}) collective-permute-start(bf16[96,1280]{1,0:T(8,128)(2,1)} %get-tuple-element.124), channel_id=1, source_target_pairs={{0,1},{1,0},{2,3},{3,2},{4,5},{5,4},{6,7},{7,6},{8,9},{9,8},{10,11... | collective-permute-start | bytes 737288 | tf_op jit(solution)/shard_map/ppermute | solution.py:68
  133.7 9.6 %collective-permute-start.14 = (bf16[96,1280]{1,0:T(8,128)(2,1)}, bf16[96,1280]{1,0:T(8,128)(2,1)S(1)}, u32[]{:S(2)}, u32[]{:S(2)}) collective-permute-start(bf16[96,1280]{1,0:T(8,128)(2,1)} %get-tuple-element.125), channel_id=1, source_target_pairs={{0,1},{1,0},{2,3},{3,2},{4,5},{5,4},{6,7},{7,6},{8,9},{9,8},{10,11... | collective-permute-start | bytes 737288 | tf_op jit(solution)/shard_map/ppermute | solution.py:68
  147.0 23.9 %collective-permute-start.17 = (bf16[384,1280]{1,0:T(8,128)(2,1)}, bf16[384,1280]{1,0:T(8,128)(2,1)S(1)}, u32[]{:S(2)}, u32[]{:S(2)}) collective-permute-start(bf16[384,1280]{1,0:T(8,128)(2,1)} %pair_sum.2), channel_id=1, source_target_pairs={{0,2},{1,3},{2,0},{3,1},{4,6},{5,7},{6,4},{7,5},{8,10},{9,11},{10,... | collective-permute-start | bytes 2949128 | tf_op jit(solution)/shard_map/ppermute | solution.py:68
  161.6 9.3 %collective-permute-start.18 = (bf16[96,1280]{1,0:T(8,128)(2,1)}, bf16[96,1280]{1,0:T(8,128)(2,1)S(1)}, u32[]{:S(2)}, u32[]{:S(2)}) collective-permute-start(bf16[96,1280]{1,0:T(8,128)(2,1)} %get-tuple-element.133), channel_id=1, source_target_pairs={{0,1},{1,0},{2,3},{3,2},{4,5},{5,4},{6,7},{7,6},{8,9},{9,8},{10,11... | collective-permute-start | bytes 737288 | tf_op jit(solution)/shard_map/ppermute | solution.py:68
  177.1 25.3 %collective-permute-start.22 = (bf16[384,1280]{1,0:T(8,128)(2,1)}, bf16[384,1280]{1,0:T(8,128)(2,1)S(1)}, u32[]{:S(2)}, u32[]{:S(2)}) collective-permute-start(bf16[384,1280]{1,0:T(8,128)(2,1)} %get-tuple-element.138.refs_0_), channel_id=1, source_target_pairs={{0,2},{1,3},{2,0},{3,1},{4,6},{5,7},{6,4},{7,5},{8,10},{9,11},{10,... | collective-permute-start | bytes 2949128 | tf_op jit(solution)/shard_map/ppermute | solution.py:68
  177.4 9.9 %collective-permute-start.23 = (bf16[384,1280]{1,0:T(8,128)(2,1)}, bf16[384,1280]{1,0:T(8,128)(2,1)S(1)}, u32[]{:S(2)}, u32[]{:S(2)}) collective-permute-start(bf16[384,1280]{1,0:T(8,128)(2,1)} %get-tuple-element.138.refs_0_), channel_id=1, source_target_pairs={{0,1},{1,0},{2,3},{3,2},{4,5},{5,4},{6,7},{7,6},{8,9},{9,8},{10,11... | collective-permute-start | bytes 2949128 | tf_op jit(solution)/shard_map/ppermute | solution.py:68
  214.1 9.6 %collective-permute-start.25 = (bf16[96,1280]{1,0:T(8,128)(2,1)}, bf16[96,1280]{1,0:T(8,128)(2,1)S(1)}, u32[]{:S(2)}, u32[]{:S(2)}) collective-permute-start(bf16[96,1280]{1,0:T(8,128)(2,1)} %get-tuple-element.150), channel_id=1, source_target_pairs={{0,1},{1,0},{2,3},{3,2},{4,5},{5,4},{6,7},{7,6},{8,9},{9,8},{10,11... | collective-permute-start | bytes 737288 | tf_op jit(solution)/shard_map/ppermute | solution.py:68
  214.5 9.4 %collective-permute-start.26 = (bf16[96,1280]{1,0:T(8,128)(2,1)}, bf16[96,1280]{1,0:T(8,128)(2,1)S(1)}, u32[]{:S(2)}, u32[]{:S(2)}) collective-permute-start(bf16[96,1280]{1,0:T(8,128)(2,1)} %get-tuple-element.151), channel_id=1, source_target_pairs={{0,1},{1,0},{2,3},{3,2},{4,5},{5,4},{6,7},{7,6},{8,9},{9,8},{10,11... | collective-permute-start | bytes 737288 | tf_op jit(solution)/shard_map/ppermute | solution.py:68
  214.6 9.6 %collective-permute-start.27 = (bf16[96,1280]{1,0:T(8,128)(2,1)}, bf16[96,1280]{1,0:T(8,128)(2,1)S(1)}, u32[]{:S(2)}, u32[]{:S(2)}) collective-permute-start(bf16[96,1280]{1,0:T(8,128)(2,1)} %get-tuple-element.152), channel_id=1, source_target_pairs={{0,1},{1,0},{2,3},{3,2},{4,5},{5,4},{6,7},{7,6},{8,9},{9,8},{10,11... | collective-permute-start | bytes 737288 | tf_op jit(solution)/shard_map/ppermute | solution.py:68
  215.0 9.4 %collective-permute-start.28 = (bf16[96,1280]{1,0:T(8,128)(2,1)}, bf16[96,1280]{1,0:T(8,128)(2,1)S(1)}, u32[]{:S(2)}, u32[]{:S(2)}) collective-permute-start(bf16[96,1280]{1,0:T(8,128)(2,1)} %get-tuple-element.153), channel_id=1, source_target_pairs={{0,1},{1,0},{2,3},{3,2},{4,5},{5,4},{6,7},{7,6},{8,9},{9,8},{10,11... | collective-permute-start | bytes 737288 | tf_op jit(solution)/shard_map/ppermute | solution.py:68
  215.1 42.8 %collective-permute-start.32 = (bf16[96,1280]{1,0:T(8,128)(2,1)}, bf16[96,1280]{1,0:T(8,128)(2,1)S(1)}, u32[]{:S(2)}, u32[]{:S(2)}) collective-permute-start(bf16[96,1280]{1,0:T(8,128)(2,1)} %get-tuple-element.158), channel_id=1, source_target_pairs={{0,1},{1,0},{2,3},{3,2},{4,5},{5,4},{6,7},{7,6},{8,9},{9,8},{10,11... | collective-permute-start | bytes 737288 | tf_op jit(solution)/shard_map/ppermute | solution.py:68
  223.7 34.3 %collective-permute-start.33 = (bf16[96,1280]{1,0:T(8,128)(2,1)}, bf16[96,1280]{1,0:T(8,128)(2,1)}, u32[]{:S(2)}, u32[]{:S(2)}) collective-permute-start(bf16[96,1280]{1,0:T(8,128)(2,1)} %get-tuple-element.159), channel_id=1, source_target_pairs={{0,1},{1,0},{2,3},{3,2},{4,5},{5,4},{6,7},{7,6},{8,9},{9,8},{10,11... | collective-permute-start | bytes 737288 | tf_op jit(solution)/shard_map/ppermute | solution.py:68
  223.9 34.1 %collective-permute-start.34 = (bf16[96,1280]{1,0:T(8,128)(2,1)}, bf16[96,1280]{1,0:T(8,128)(2,1)}, u32[]{:S(2)}, u32[]{:S(2)}) collective-permute-start(bf16[96,1280]{1,0:T(8,128)(2,1)} %get-tuple-element.160), channel_id=1, source_target_pairs={{0,1},{1,0},{2,3},{3,2},{4,5},{5,4},{6,7},{7,6},{8,9},{9,8},{10,11... | collective-permute-start | bytes 737288 | tf_op jit(solution)/shard_map/ppermute | solution.py:68
  224.3 33.7 %collective-permute-start.35 = (bf16[96,1280]{1,0:T(8,128)(2,1)}, bf16[96,1280]{1,0:T(8,128)(2,1)}, u32[]{:S(2)}, u32[]{:S(2)}) collective-permute-start(bf16[96,1280]{1,0:T(8,128)(2,1)} %get-tuple-element.161), channel_id=1, source_target_pairs={{0,1},{1,0},{2,3},{3,2},{4,5},{5,4},{6,7},{7,6},{8,9},{9,8},{10,11... | collective-permute-start | bytes 737288 | tf_op jit(solution)/shard_map/ppermute | solution.py:68
  227.8 30.2 %collective-permute-start.31 = (bf16[384,1280]{1,0:T(8,128)(2,1)}, bf16[384,1280]{1,0:T(8,128)(2,1)}, u32[]{:S(2)}, u32[]{:S(2)}) collective-permute-start(bf16[384,1280]{1,0:T(8,128)(2,1)} %pair_sum.3), channel_id=1, source_target_pairs={{0,2},{1,3},{2,0},{3,1},{4,6},{5,7},{6,4},{7,5},{8,10},{9,11},{10,... | collective-permute-start | bytes 2949128 | tf_op jit(solution)/shard_map/ppermute | solution.py:68
  238.6 196.6 %reduce-scatter.5.cloned.1.call-start = ((), (), s32[]{:S(2)}) async-start(), calls=%async_computation.5 | async-start | bytes 3686400 | tf_op jit(solution)/shard_map/reduce_scatter | solution.py:725
  265.1 26.1 %collective-permute-start.36 = (bf16[384,1280]{1,0:T(8,128)(2,1)}, bf16[384,1280]{1,0:T(8,128)(2,1)}, u32[]{:S(2)}, u32[]{:S(2)}) collective-permute-start(bf16[384,1280]{1,0:T(8,128)(2,1)} %get-tuple-element.166), channel_id=1, source_target_pairs={{0,2},{1,3},{2,0},{3,1},{4,6},{5,7},{6,4},{7,5},{8,10},{9,11},{10,... | collective-permute-start | bytes 2949128 | tf_op jit(solution)/shard_map/ppermute | solution.py:68
  266.4 26.4 %collective-permute-start.30 = (bf16[384,1280]{1,0:T(8,128)(2,1)}, bf16[384,1280]{1,0:T(8,128)(2,1)}, u32[]{:S(2)}, u32[]{:S(2)}) collective-permute-start(bf16[384,1280]{1,0:T(8,128)(2,1)} %slice.200), channel_id=1, source_target_pairs={{0,1},{1,0},{2,3},{3,2},{4,5},{5,4},{6,7},{7,6},{8,9},{9,8},{10,11... | collective-permute-start | bytes 2949128 | tf_op jit(solution)/shard_map/ppermute | solution.py:68
  292.5 33.1 %collective-permute-start.29 = (bf16[384,1280]{1,0:T(8,128)(2,1)}, bf16[384,1280]{1,0:T(8,128)(2,1)S(1)}, u32[]{:S(2)}, u32[]{:S(2)}) collective-permute-start(bf16[384,1280]{1,0:T(8,128)(2,1)} %slice.198), channel_id=1, source_target_pairs={{0,1},{1,0},{2,3},{3,2},{4,5},{5,4},{6,7},{7,6},{8,9},{9,8},{10,11... | collective-permute-start | bytes 2949128 | tf_op jit(solution)/shard_map/ppermute | solution.py:68
  295.3 30.4 %collective-permute-start.38 = (bf16[384,1280]{1,0:T(8,128)(2,1)}, bf16[384,1280]{1,0:T(8,128)(2,1)S(1)}, u32[]{:S(2)}, u32[]{:S(2)}) collective-permute-start(bf16[384,1280]{1,0:T(8,128)(2,1)} %add_convert_fusion.1), channel_id=1, source_target_pairs={{0,2},{1,3},{2,0},{3,1},{4,6},{5,7},{6,4},{7,5},{8,10},{9,11},{10,... | collective-permute-start | bytes 2949128 | tf_op jit(solution)/shard_map/ppermute | solution.py:68
  337.9 29.5 %collective-permute-start.42 = (bf16[384,1280]{1,0:T(8,128)(2,1)}, bf16[384,1280]{1,0:T(8,128)(2,1)}, u32[]{:S(2)}, u32[]{:S(2)}) collective-permute-start(bf16[384,1280]{1,0:T(8,128)(2,1)} %add_convert_fusion), channel_id=1, source_target_pairs={{0,2},{1,3},{2,0},{3,1},{4,6},{5,7},{6,4},{7,5},{8,10},{9,11},{10,... | collective-permute-start | bytes 2949128 | tf_op jit(solution)/shard_map/ppermute | solution.py:68
  349.5 17.9 %collective-permute-start.41 = (bf16[160,1408]{1,0:T(8,128)(2,1)}, bf16[160,1408]{1,0:T(8,128)(2,1)}, u32[]{:S(2)}, u32[]{:S(2)}) collective-permute-start(bf16[160,1408]{1,0:T(8,128)(2,1)} %get-tuple-element.221), channel_id=1, source_target_pairs={{0,4},{4,0},{8,12},{12,8},{16,20},{20,16},{24,28},{28,24},{1,5},{5... | collective-permute-start | bytes 1351688 | tf_op jit(solution)/shard_map/ppermute | solution.py:68
  351.2 29.9 %collective-permute-start.43 = (bf16[160,1408]{1,0:T(8,128)(2,1)}, bf16[160,1408]{1,0:T(8,128)(2,1)}, u32[]{:S(2)}, u32[]{:S(2)}) collective-permute-start(bf16[160,1408]{1,0:T(8,128)(2,1)} %get-tuple-element.220), channel_id=1, source_target_pairs={{0,4},{4,0},{8,12},{12,8},{16,20},{20,16},{24,28},{28,24},{1,5},{5... | collective-permute-start | bytes 1351688 | tf_op jit(solution)/shard_map/ppermute | solution.py:68
  351.5 43.6 %collective-permute-start.44 = (bf16[160,1408]{1,0:T(8,128)(2,1)}, bf16[160,1408]{1,0:T(8,128)(2,1)}, u32[]{:S(2)}, u32[]{:S(2)}) collective-permute-start(bf16[160,1408]{1,0:T(8,128)(2,1)} %get-tuple-element.219), channel_id=1, source_target_pairs={{0,4},{4,0},{8,12},{12,8},{16,20},{20,16},{24,28},{28,24},{1,5},{5... | collective-permute-start | bytes 1351688 | tf_op jit(solution)/shard_map/ppermute | solution.py:68
  353.2 50.8 %collective-permute-start.45 = (bf16[160,1408]{1,0:T(8,128)(2,1)}, bf16[160,1408]{1,0:T(8,128)(2,1)}, u32[]{:S(2)}, u32[]{:S(2)}) collective-permute-start(bf16[160,1408]{1,0:T(8,128)(2,1)} %get-tuple-element.218), channel_id=1, source_target_pairs={{0,4},{4,0},{8,12},{12,8},{16,20},{20,16},{24,28},{28,24},{1,5},{5... | collective-permute-start | bytes 1351688 | tf_op jit(solution)/shard_map/ppermute | solution.py:68
  413.3 18.2 %collective-permute-start.53 = (f32[1,160,160]{2,1,0:T(8,128)S(1)}, f32[1,160,160]{2,1,0:T(8,128)S(1)}, u32[]{:S(2)}, u32[]{:S(2)}) collective-permute-start(f32[1,160,160]{2,1,0:T(8,128)S(1)} %convolution_bitcast_fusion.2), channel_id=1, source_target_pairs={{0,1},{1,0},{2,3},{3,2},{4,5},{5,4},{6,7},{7,6},{8,9},{9,8},{10,11... | collective-permute-start | bytes 307208 | tf_op jit(solution)/shard_map/ppermute | solution.py:68
  422.9 35.6 %collective-permute-start.50 = (bf16[160,1408]{1,0:T(8,128)(2,1)}, bf16[160,1408]{1,0:T(8,128)(2,1)}, u32[]{:S(2)}, u32[]{:S(2)}) collective-permute-start(bf16[160,1408]{1,0:T(8,128)(2,1)} %get-tuple-element.216), channel_id=1, source_target_pairs={{0,16},{4,20},{8,24},{12,28},{16,0},{20,4},{24,8},{28,12},{1,17},{... | collective-permute-start | bytes 1351688 | tf_op jit(solution)/shard_map/ppermute | solution.py:68
  427.8 30.8 %collective-permute-start.51 = (bf16[160,1408]{1,0:T(8,128)(2,1)}, bf16[160,1408]{1,0:T(8,128)(2,1)}, u32[]{:S(2)}, u32[]{:S(2)}) collective-permute-start(bf16[160,1408]{1,0:T(8,128)(2,1)} %get-tuple-element.215), channel_id=1, source_target_pairs={{0,24},{4,28},{8,16},{12,20},{16,8},{20,12},{24,0},{28,4},{1,25},{... | collective-permute-start | bytes 1351688 | tf_op jit(solution)/shard_map/ppermute | solution.py:68
  431.5 27.9 %collective-permute-start.52 = (bf16[160,1408]{1,0:T(8,128)(2,1)}, bf16[160,1408]{1,0:T(8,128)(2,1)}, u32[]{:S(2)}, u32[]{:S(2)}) collective-permute-start(bf16[160,1408]{1,0:T(8,128)(2,1)} %get-tuple-element.214), channel_id=1, source_target_pairs={{0,8},{4,12},{8,0},{12,4},{16,24},{20,28},{24,16},{28,20},{1,9},{5... | collective-permute-start | bytes 1351688 | tf_op jit(solution)/shard_map/ppermute | solution.py:68
  431.6 13.5 %collective-permute-start.56 = (f32[8,1280]{1,0:T(8,128)S(1)}, f32[8,1280]{1,0:T(8,128)S(1)}, u32[]{:S(2)}, u32[]{:S(2)}) collective-permute-start(f32[8,1280]{1,0:T(8,128)S(1)} %add.242), channel_id=1, source_target_pairs={{0,2},{1,3},{2,0},{3,1},{4,6},{5,7},{6,4},{7,5},{8,10},{9,11},{10,... | collective-permute-start | bytes 122888 | tf_op jit(solution)/shard_map/ppermute | solution.py:68
  471.3 11.4 %collective-permute-start.60 = (f32[9,1280]{1,0:T(8,128)S(1)}, f32[9,1280]{1,0:T(8,128)S(1)}, u32[]{:S(2)}, u32[]{:S(2)}) collective-permute-start(f32[9,1280]{1,0:T(8,128)S(1)} %add.255), channel_id=1, source_target_pairs={{0,8},{4,12},{8,0},{12,4},{16,24},{20,28},{24,16},{28,20},{1,9},{5... | collective-permute-start | bytes 138248 | tf_op jit(solution)/shard_map/ppermute | solution.py:68
  480.3 10.7 %collective-permute-start.57 = (f32[3,160,160]{2,1,0:T(8,128)S(1)}, f32[3,160,160]{2,1,0:T(8,128)S(1)}, u32[]{:S(2)}, u32[]{:S(2)}) collective-permute-start(f32[3,160,160]{2,1,0:T(8,128)S(1)} %pad_maximum_fusion.4), channel_id=1, source_target_pairs={{0,1},{1,0},{2,3},{3,2},{4,5},{5,4},{6,7},{7,6},{8,9},{9,8},{10,11... | collective-permute-start | bytes 921608 | tf_op jit(solution)/shard_map/ppermute | solution.py:68
  491.1 9.5 %collective-permute-start.58 = (f32[3,160,160]{2,1,0:T(8,128)S(1)}, f32[3,160,160]{2,1,0:T(8,128)S(1)}, u32[]{:S(2)}, u32[]{:S(2)}) collective-permute-start(f32[3,160,160]{2,1,0:T(8,128)S(1)} %fusion.38), channel_id=1, source_target_pairs={{0,2},{1,3},{2,0},{3,1},{4,6},{5,7},{6,4},{7,5},{8,10},{9,11},{10,... | collective-permute-start | bytes 921608 | tf_op jit(solution)/shard_map/ppermute | solution.py:68
  (89 other events, 882.7 us)
Sparse Core Ops, SparseCore 0:
  10.8 94.9 all-gather.2
  108.6 59.2 all-gather.4
  238.7 77.2 reduce-scatter.2
  332.5 89.6 reduce-scatter.4

commit v9 on v8

--- a/solution.py
+++ b/solution.py
@@ -925,22 +925,6 @@
     new_w_down = applied(w_down, early[0], update_down, STEP_DOWN)
     grad_wu = after(after(grad_wu, first_mine, *crossed), *lined[:3])
 
-    rows_of = jnp.concatenate(
-        [
-            vec_sums[:6],
-            bu_sums[0:1],
-            jnp.pad(bias_sums[:2], ((0, 0), (0, width - padded))),
-        ],
-        axis=0,
-    )
-    rows_of = dp_sum(after(rows_of, new_w_down))
-    own_cols = lax.dynamic_slice(rows_of, (0, dp_index * own_rows), (7, own_rows))
-    vec_grad = jnp.transpose(own_cols[:6])
-    bu_grad = own_cols[6]
-    bq_grad = jnp.transpose(
-        lax.dynamic_slice(rows_of, (7, dp_index * own_bias), (2, own_bias))
-    )
-
     mom_up_new, update_up = momentum(mom_up, grad_wu.astype(F32))
     gram_up = gram_of(update_up)
     lined = tie(lined, gram_up, new_w_down, vec_sums)
@@ -954,6 +938,22 @@
         [update_qkv[:, 0], jnp.zeros((own_rows, extra), F32), update_qkv[:, 1], update_qkv[:, 2]], axis=1
     )
     late = tensor_sum(jnp.stack([gram_of(update_out), gram_of(flat), gram_up]))
+    rows_of = jnp.concatenate(
+        [
+            vec_sums[:6],
+            bu_sums[0:1],
+            jnp.pad(bias_sums[:2], ((0, 0), (0, width - padded))),
+        ],
+        axis=0,
+    )
+    rows_of = dp_sum(after(rows_of, late))
+    own_cols = lax.dynamic_slice(rows_of, (0, dp_index * own_rows), (7, own_rows))
+    vec_grad = jnp.transpose(own_cols[:6])
+    bu_grad = own_cols[6]
+    bq_grad = jnp.transpose(
+        lax.dynamic_slice(rows_of, (7, dp_index * own_bias), (2, own_bias))
+    )
+
     late = polar_call(late)
     new_w_out = applied(w_out, late[0], update_out, STEP_OUT)
     new_w_up = applied(w_up, late[2], update_up, STEP_UP)

time: 530 us -> 526 us (level)
  transfers between devices with their start and end apart: 66 -> 66, of which waited for: 19 -> 21; matrix products, arithmetic and copies ran while one was open for 19% -> 19% of each run, Pallas kernels for 27% -> 27%
where the time goes in v9:
time: 526 us; the launch traced here: 521 us
  waiting for transfers between devices  159 us (30%)
  Pallas kernels  159 us (30%)
  matrix products  67.9 us (13%)
  starting transfers between devices  55 us (10%)
  other arithmetic  33.6 us (6%)
  local copies, waits for them, and re-layouts  31.1 us (6%)
  between operations  15.8 us (3%)
    ppermute x62, waiting for transfers between devices, swap(): return lax.ppermute(value, axis, [(i, i ^ mask) for i in range(size)])  159 us
    dot_general x10, matrix products, mm(): return lax.dot_general(left, right, dims, preferred_element_type=F32)  55.1 us
    ppermute x62, starting transfers between devices, swap(): return lax.ppermute(value, axis, [(i, i ^ mask) for i in range(size)])  54.8 us
    pallas_call x2, Pallas kernels, attn_back_call(): pl.pallas_call(partial(attn_back_body, heads, last_part, first), grid=(co...  44.5 us
    pallas_call x3, Pallas kernels, attn_call(): pl.pallas_call(partial(attn_body, heads, emits, len(held)), grid=(count /...  31.4 us
    pallas_call x3, Pallas kernels, mlp_call(): pl.pallas_call(partial(mlp_body, min(256, hidden_width), emits, len(held)...  30.3 us
    unnamed x145, local copies, waits for them, and re-layouts  18.6 us
    pallas_call x3, Pallas kernels, row_call(): pl.pallas_call(partial(row_body, body, len(rows_in)), grid=(PIECES,), in_...  17.4 us
  transfers between devices with their start and end apart: 66, of which 21 were waited for; matrix products, arithmetic and copies ran while one was open for 19% of the time, Pallas kernels for 27%

profile of v9, /device:TPU:0, one launch (start us, length us, event | category | flops | bytes accessed | tf_op | source)
XLA Modules:
  0.0 521.0 jit_solution(13948490035110146811)
XLA Ops:
  11.5 3.0 collective-permute-start.3
  15.1 3.7 collective-permute-start
  21.1 15.6 %collective-permute-done.refs_6_ = bf16[160,1408]{1,0:T(8,128)(2,1)S(1)} collective-permute-done((bf16[160,1408]{1,0:T(8,128)(2,1)S(1)}, bf16[160,1408]{1,0:T(8,128)(2,1)S(1)}, u32[]{:S(2)}, u32[]{:S(2)}) %collective-permute-start) | collective-permute-done | bytes 450592 | tf_op jit(solution)/shard_map/ppermute | solution.py:68
  37.5 15.2 %collective-permute-done.4.refs_2_ = bf16[160,1408]{1,0:T(8,128)(2,1)} collective-permute-done((bf16[160,1408]{1,0:T(8,128)(2,1)S(1)}, bf16[160,1408]{1,0:T(8,128)(2,1)}, u32[]{:S(2)}, u32[]{:S(2)}) %collective-permute-start.4) | collective-permute-done | bytes 450592 | tf_op jit(solution)/shard_map/ppermute | solution.py:68
  54.7 31.1 %collective-permute-done.9.refs_4_ = bf16[160,1408]{1,0:T(8,128)(2,1)} collective-permute-done((bf16[160,1408]{1,0:T(8,128)(2,1)S(1)}, bf16[160,1408]{1,0:T(8,128)(2,1)}, u32[]{:S(2)}, u32[]{:S(2)}) %collective-permute-start.9) | collective-permute-done | bytes 450592 | tf_op jit(solution)/shard_map/ppermute | solution.py:68
  88.0 4.2 collective-permute-done.10.refs_3_
  96.5 3.5 pad_maximum_fusion.x_ref
  100.0 3.3 pad_maximum_fusion.1
  103.3 4.4 collective-permute-done.12.refs_5_
  108.5 4.0 place_rows.1
  115.7 9.9 %norm_qkv.1 = (bf16[1536,1280]{1,0:T(8,128)(2,1)}, bf16[1536,1024]{1,0:T(8,128)(2,1)}) custom-call(bf16[1536,1280]{1,0:T(8,128)(2,1)} %pad_maximum_fusion.x_ref, f32[8,1280]{1,0:T(8,128)} %slice.149.vec_ref.refs_7_.refs_8_, bf16[1280,1024]{1,0:T(8,128)(2,1)} %get-tuple-element.118.w_ref, f32[1,1024]{1,0:T(1,128)} %pad_maximum_fusion.7.bias_ref), custom_call_target="tpu_custom_call" | custom-call | flops 1000000 | bytes 100000 | tf_op jit(solution)/shard_map/norm_qkv/pallas_call | solution.py:109
  125.6 8.2 %attn_fwd.3 = (bf16[1536,384]{1,0:T(8,128)(2,1)}, f32[8,1536]{1,0:T(8,128)}, bf16[96,1280]{1,0:T(8,128)(2,1)}, bf16[96,1280]{1,0:T(8,128)(2,1)}, bf16[96,1280]{1,0:T(8,128)(2,1)}, /*index=5*/bf16[96,1280]{1,0:T(8,128)(2,1)}) custom-call(bf16[1536,1024]{1,0:T(8,128)(2,1)} %get-tuple-element.128.q_ref.qkv_ref, ...), custom_call_target="tpu_custom_call" | custom-call | flops 1000000 | bytes 100000 | tf_op jit(solution)/shard_map/attn_fwd/pallas_call | solution.py:266
  134.7 8.6 %attn_fwd.4 = (bf16[1536,384]{1,0:T(8,128)(2,1)}, f32[8,1536]{1,0:T(8,128)}, bf16[384,1280]{1,0:T(8,128)(2,1)}) custom-call(bf16[1536,1024]{1,0:T(8,128)(2,1)} %get-tuple-element.128.q_ref.qkv_ref, bf16[1536,1024]{1,0:T(8,128)(2,1)} %get-tuple-element.128.q_ref.qkv_ref, ...), custom_call_target="tpu_custom_call", output_to_operand_aliasing={{0}: (4, {}), {1}: (5, {})} | custom-call | flops 1000000 | bytes 100000 | tf_op jit(solution)/shard_map/attn_fwd/pallas_call | solution.py:266
  144.3 2.7 pair_sum.2
  147.0 14.7 %attn_fwd.5 = (bf16[1536,384]{1,0:T(8,128)(2,1)}, f32[8,1536]{1,0:T(8,128)}, bf16[384,1280]{1,0:T(8,128)(2,1)}, bf16[96,1280]{1,0:T(8,128)(2,1)}, bf16[96,1280]{...) custom-call(bf16[1536,1024]{1,0:T(8,128)(2,1)} %get-tuple-element.12, ...), custom_call_target="tpu_custom_call", output_to_operand_aliasing={{0}: (4, {}), {1}: (5, {})} | custom-call | flops 1000000 | bytes 100000 | tf_op jit(solution)/shard_map/attn_fwd/pallas_call | solution.py:266
  164.2 6.7 %collective-permute-done.17.refs_2_ = bf16[384,1280]{1,0:T(8,128)(2,1)S(1)} collective-permute-done((bf16[384,1280]{1,0:T(8,128)(2,1)}, bf16[384,1280]{1,0:T(8,128)(2,1)S(1)}, u32[]{:S(2)}, u32[]{:S(2)}) %collective-permute-start.17) | collective-permute-done | bytes 983072 | tf_op jit(solution)/shard_map/ppermute | solution.py:68
  172.2 5.0 residual.1
  177.4 9.9 %fusion.42.refs_4_.refs_3_ = f32[1536,1280]{1,0:T(8,128)} fusion(bf16[1536,1280]{1,0:T(8,128)(2,1)} %pad_maximum_fusion.1, bf16[1280,1280]{1,0:T(8,128)(2,1)} %all-gather.3.cloned.1.call-done), kind=kOutput, calls=%fused_computation.121 | convolution fusion | flops 5033164800 | bytes 15073280 | tf_op jit(solution)/shard_map/dot_general | solution.py:43
  188.3 14.2 %mlp_up.3 = (bf16[1536,1280]{1,0:T(8,128)(2,1)}, bf16[1536,1280]{1,0:T(8,128)(2,1)}, f32[8,1280]{1,0:T(8,128)}, bf16[384,1280]{1,0:T(8,128)(2,1)}, bf16[96,1280]...) custom-call(bf16[384,1280]{1,0:T(8,128)(2,1)} %get-tuple-element.138.refs_0_, ...), custom_call_target="tpu_custom_call" | custom-call | flops 1000000 | bytes 100000 | tf_op jit(solution)/shard_map/mlp_up/pallas_call | solution.py:471
  206.2 8.0 %mlp_up.4 = (bf16[1536,1280]{1,0:T(8,128)(2,1)}, bf16[1536,1280]{1,0:T(8,128)(2,1)}, f32[8,1280]{1,0:T(8,128)}, bf16[96,1280]{1,0:T(8,128)(2,1)}, bf16[96,1280]{...) custom-call(bf16[384,1280]{1,0:T(8,128)(2,1)} %copy-done.35, ...), custom_call_target="tpu_custom_call", output_to_operand_aliasing={{0}: (4, {}), {1}: (5, {})} | custom-call | flops 1000000 | bytes 100000 | tf_op jit(solution)/shard_map/mlp_up/pallas_call | solution.py:471
  215.6 8.2 %mlp_up.5 = (bf16[1536,1280]{1,0:T(8,128)(2,1)}, bf16[1536,1280]{1,0:T(8,128)(2,1)}, f32[8,1280]{1,0:T(8,128)}, bf16[384,1280]{1,0:T(8,128)(2,1)}) custom-call(bf16[384,1280]{1,0:T(8,128)(2,1)} %copy-done.31, bf16[1280,1280]{1,0:T(8,128)(2,1)} %all-gather.5.cloned.1.call-done.refs_2_.refs_1_, ...), custom_call_target="tpu_custom_call", output_to_operand_aliasing={{0}: (4, {}), {1}: (5, {})} | custom-call | flops 1000000 | bytes 100000 | tf_op jit(solution)/shard_map/mlp_up/pallas_call | solution.py:471
  225.2 2.7 pair_sum.3
  229.7 8.9 %convolution_convert_fusion.1 = bf16[1280,1280]{1,0:T(8,128)(2,1)} fusion(bf16[1536,1280]{1,0:T(8,128)(2,1)S(1)} %copy-done.12, bf16[1536,1280]{1,0:T(8,128)(2,1)} %get-tuple-element.157), kind=kOutput, calls=%fused_computation.1 | convolution fusion | flops 5034803200 | bytes 11141120 | tf_op jit(solution)/shard_map/dot_general | solution.py:43
  240.4 9.4 %convolution_convert_fusion = bf16[1280,1280]{1,0:T(8,128)(2,1)} fusion(bf16[1536,1280]{1,0:T(8,128)(2,1)} %get-tuple-element.156, bf16[384,1280]{1,0:T(8,128)(2,1)} %copy-done.35, bf16[384,1280]{1,0:T(8,128)(2,1)S(1)} %copy-done.32, bf16[384,1280]{1,0:T(8,128)(2,1)S(1)} %copy-done.34, bf16[384,1280]{1,0:T(8,128)(2,1)S(1)} %copy-done.30), kind=kOutput, calls=%fused_computation | convolution fusion | flops 5050531840 | bytes 11141120 | tf_op jit(solution)/shard_map/dot_general | solution.py:43
  249.8 5.4 %convolution_convert_fusion.3 = bf16[768,1280]{1,0:T(8,128)(2,1)S(1)} fusion(bf16[1280,1280]{1,0:T(8,128)(2,1)} %all-gather.3.cloned.1.call-done, bf16[1536,1280]{1,0:T(8,128)(2,1)} %get-tuple-element.157), kind=kOutput, calls=%fused_computation.12 | convolution fusion | flops 2517565440 | bytes 7208960 | tf_op jit(solution)/shard_map/dot_general | solution.py:43
  255.2 2.7 convolution_convert_fusion.4
  258.8 6.4 %second_back.1 = (f32[384,1280]{1,0:T(8,128)}, bf16[384,1280]{1,0:T(8,128)(2,1)}, f32[8,1280]{1,0:T(8,128)}) custom-call(f32[384,1280]{1,0:T(8,128)} %get-tuple-element.137.refs_0_, bf16[384,1280]{1,0:T(8,128)(2,1)} %get-tuple-element.141.refs_1_, bf16[384,1280]{1,0:T(8,128)(2,1)} %collective-permute-done.31.refs_2_, bf16[384,1280]{1,0:T(8,128)(2,1)} %refs_3_.1, ...), custom_call_target="tpu_custom_call" | custom-call | flops 1000000 | bytes 100000 | tf_op jit(solution)/shard_map/second_back/pallas_call | solution.py:559
  269.3 21.9 %attn_bwd.2 = (bf16[1536,1024]{1,0:T(8,128)(2,1)}, f32[8,384]{1,0:T(8,128)}, f32[1536,384]{1,0:T(8,128)}, f32[1536,384]{1,0:T(8,128)}) custom-call(bf16[768,1280]{1,0:T(8,128)(2,1)} %copy-done.9, bf16[1280,384]{1,0:T(8,128)(2,1)} %get-tuple-element.120.wo_ref, bf16[1536,384]{1,0:T(8,128)(2,1)} %get-tuple-element.167.att_ref, ...), custom_call_target="tpu_custom_call" | custom-call | flops 1000000 | bytes 100000 | tf_op jit(solution)/shard_map/attn_bwd/pallas_call | solution.py:399
  302.9 22.6 %attn_bwd.3 = (bf16[1536,1024]{1,0:T(8,128)(2,1)}, f32[8,384]{1,0:T(8,128)}) custom-call(bf16[768,1280]{1,0:T(8,128)(2,1)} %copy-done.11, bf16[1280,384]{1,0:T(8,128)(2,1)} %get-tuple-element.120.wo_ref, bf16[1536,384]{1,0:T(8,128)(2,1)} %get-tuple-element.167.att_ref, ...), custom_call_target="tpu_custom_call", output_to_operand_aliasing={{0}: (10, {})} | custom-call | flops 1000000 | bytes 100000 | tf_op jit(solution)/shard_map/attn_bwd/pallas_call | solution.py:399
  325.6 4.3 convolution_convert_fusion.6
  332.3 2.9 collective-permute-done.40
  338.3 7.0 %convolution_convert_fusion.2 = bf16[1280,1024]{1,0:T(8,128)(2,1)S(1)} fusion(bf16[1536,1280]{1,0:T(8,128)(2,1)} %get-tuple-element.178, bf16[1536,1024]{1,0:T(8,128)(2,1)S(1)} %copy-done.8), kind=kOutput, calls=%fused_computation.11 | convolution fusion | flops 4027842560 | bytes 9699328 | tf_op jit(solution)/shard_map/dot_general | solution.py:43
  354.0 13.7 %collective-permute-done.41 = bf16[160,1408]{1,0:T(8,128)(2,1)} collective-permute-done((bf16[160,1408]{1,0:T(8,128)(2,1)}, bf16[160,1408]{1,0:T(8,128)(2,1)}, u32[]{:S(2)}, u32[]{:S(2)}) %collective-permute-start.41) | collective-permute-done | bytes 450592 | tf_op jit(solution)/shard_map/ppermute | solution.py:68
  367.7 13.9 %collective-permute-done.43 = bf16[160,1408]{1,0:T(8,128)(2,1)} collective-permute-done((bf16[160,1408]{1,0:T(8,128)(2,1)}, bf16[160,1408]{1,0:T(8,128)(2,1)}, u32[]{:S(2)}, u32[]{:S(2)}) %collective-permute-start.43) | collective-permute-done | bytes 450592 | tf_op jit(solution)/shard_map/ppermute | solution.py:68
  381.6 14.1 %collective-permute-done.44 = bf16[160,1408]{1,0:T(8,128)(2,1)} collective-permute-done((bf16[160,1408]{1,0:T(8,128)(2,1)}, bf16[160,1408]{1,0:T(8,128)(2,1)}, u32[]{:S(2)}, u32[]{:S(2)}) %collective-permute-start.44) | collective-permute-done | bytes 450592 | tf_op jit(solution)/shard_map/ppermute | solution.py:68
  395.7 8.6 %collective-permute-done.45 = bf16[160,1408]{1,0:T(8,128)(2,1)} collective-permute-done((bf16[160,1408]{1,0:T(8,128)(2,1)}, bf16[160,1408]{1,0:T(8,128)(2,1)}, u32[]{:S(2)}, u32[]{:S(2)}) %collective-permute-start.45) | collective-permute-done | bytes 450592 | tf_op jit(solution)/shard_map/ppermute | solution.py:68
  404.4 4.0 convolution_convert_fusion.5
  409.1 2.8 add_convert_fusion.2
  413.0 4.9 collective-permute-start.50
  417.9 4.2 collective-permute-start.51
  425.5 6.1 %first_back.1 = (f32[384,1280]{1,0:T(8,128)}, f32[8,1280]{1,0:T(8,128)}) custom-call(bf16[384,1280]{1,0:T(8,128)(2,1)} %refs_0_.3, bf16[384,1280]{1,0:T(8,128)(2,1)} %slice.203.refs_1_, bf16[384,1280]{1,0:T(8,128)(2,1)} %collective-permute-done.42.refs_2_, f32[384,1280]{1,0:T(8,128)} %get-tuple-element.186.refs_3_, bf16[96,1280]{1,0:T(8,128)(2,1)} %copy-done.47, ...), custom_call_target="tpu_custom_call" | custom-call | flops 1000000 | bytes 100000 | tf_op jit(solution)/shard_map/first_back/pallas_call | solution.py:559
  436.5 6.8 %polar.2 = f32[1,160,160]{2,1,0:T(8,128)} custom-call(f32[1,160,160]{2,1,0:T(8,128)} %add.240.gram_ref), custom_call_target="tpu_custom_call" | custom-call | tf_op jit(solution)/shard_map/polar/pallas_call | solution.py:612
  443.3 7.0 %collective-permute-done.50 = bf16[160,1408]{1,0:T(8,128)(2,1)} collective-permute-done((bf16[160,1408]{1,0:T(8,128)(2,1)}, bf16[160,1408]{1,0:T(8,128)(2,1)}, u32[]{:S(2)}, u32[]{:S(2)}) %collective-permute-start.50) | collective-permute-done | bytes 450592 | tf_op jit(solution)/shard_map/ppermute | solution.py:68
  467.1 9.3 %collective-permute-done.58 = f32[3,160,160]{2,1,0:T(8,128)S(1)} collective-permute-done((f32[3,160,160]{2,1,0:T(8,128)S(1)}, f32[3,160,160]{2,1,0:T(8,128)S(1)}, u32[]{:S(2)}, u32[]{:S(2)}) %collective-permute-start.58) | collective-permute-done | bytes 307232 | tf_op jit(solution)/shard_map/ppermute | solution.py:68
  477.3 9.1 %polar.3 = f32[3,160,160]{2,1,0:T(8,128)} custom-call(f32[3,160,160]{2,1,0:T(8,128)} %fusion.57.gram_ref), custom_call_target="tpu_custom_call" | custom-call | tf_op jit(solution)/shard_map/polar/pallas_call | solution.py:612
  488.2 2.7 convolution_subtract_fusion
  492.4 3.0 collective-permute-done.59
  495.4 9.0 %collective-permute-start.60 = (f32[9,1280]{1,0:T(8,128)S(1)}, f32[9,1280]{1,0:T(8,128)S(1)}, u32[]{:S(2)}, u32[]{:S(2)}) collective-permute-start(f32[9,1280]{1,0:T(8,128)S(1)} %add.255), channel_id=1, source_target_pairs={{0,8},{4,12},{8,0},{12,4},{16,24},{20,28},{24,16},{28,20},{1,9},{5... | collective-permute-start | bytes 138248 | tf_op jit(solution)/shard_map/ppermute | solution.py:68
  (347 shorter events, 107.8 us)
Async XLA Ops:
  7.3 163.7 %all-gather.3.cloned.1.call-start = ((), (), s32[]{:S(2)}) async-start(), calls=%async_computation.2 | async-start | bytes 3686400 | tf_op jit(solution)/shard_map/all_gather | solution.py:804
  9.4 168.0 %all-gather.5.cloned.1.call-start = ((), (), s32[]{:S(2)}) async-start(), calls=%async_computation.3 | async-start | bytes 3686400 | tf_op jit(solution)/shard_map/all_gather | solution.py:805
  11.4 326.8 %reduce-scatter.3.cloned.1.call-start = ((), (), s32[]{:S(2)}) async-start(), calls=%async_computation.4 | async-start | bytes 3686400 | tf_op jit(solution)/shard_map/reduce_scatter | solution.py:725
  11.5 42.7 %collective-permute-start.3 = (bf16[384,1280]{1,0:T(8,128)(2,1)S(1)}, bf16[384,1280]{1,0:T(8,128)(2,1)}, u32[]{:S(2)}, u32[]{:S(2)}) collective-permute-start(bf16[384,1280]{1,0:T(8,128)(2,1)S(1)} %copy-done.4), channel_id=1, source_target_pairs={{0,2},{1,3},{2,0},{3,1},{4,6},{5,7},{6,4},{7,5},{8,10},{9,11},{10,... | collective-permute-start | bytes 2949128 | tf_op jit(solution)/shard_map/ppermute | solution.py:68
  15.1 21.6 %collective-permute-start = (bf16[160,1408]{1,0:T(8,128)(2,1)S(1)}, bf16[160,1408]{1,0:T(8,128)(2,1)S(1)}, u32[]{:S(2)}, u32[]{:S(2)}) collective-permute-start(bf16[160,1408]{1,0:T(8,128)(2,1)S(1)} %concatenate.52.refs_0_), channel_id=1, source_target_pairs={{0,24},{4,28},{8,16},{12,20},{16,8},{20,12},{24,0},{28,4},{1,25},{... | collective-permute-start | bytes 1351688 | tf_op jit(solution)/shard_map/ppermute | solution.py:68
  18.8 33.9 %collective-permute-start.4 = (bf16[160,1408]{1,0:T(8,128)(2,1)S(1)}, bf16[160,1408]{1,0:T(8,128)(2,1)}, u32[]{:S(2)}, u32[]{:S(2)}) collective-permute-start(bf16[160,1408]{1,0:T(8,128)(2,1)S(1)} %concatenate.52.refs_0_), channel_id=1, source_target_pairs={{0,8},{4,12},{8,0},{12,4},{16,24},{20,28},{24,16},{28,20},{1,9},{5... | collective-permute-start | bytes 1351688 | tf_op jit(solution)/shard_map/ppermute | solution.py:68
  18.8 33.9 %collective-permute-start.5 = (bf16[160,1408]{1,0:T(8,128)(2,1)S(1)}, bf16[160,1408]{1,0:T(8,128)(2,1)}, u32[]{:S(2)}, u32[]{:S(2)}) collective-permute-start(bf16[160,1408]{1,0:T(8,128)(2,1)S(1)} %concatenate.52.refs_0_), channel_id=1, source_target_pairs={{0,4},{4,0},{8,12},{12,8},{16,20},{20,16},{24,28},{28,24},{1,5},{5... | collective-permute-start | bytes 1351688 | tf_op jit(solution)/shard_map/ppermute | solution.py:68
  20.3 65.5 %collective-permute-start.9 = (bf16[160,1408]{1,0:T(8,128)(2,1)S(1)}, bf16[160,1408]{1,0:T(8,128)(2,1)}, u32[]{:S(2)}, u32[]{:S(2)}) collective-permute-start(bf16[160,1408]{1,0:T(8,128)(2,1)S(1)} %concatenate.52.refs_0_), channel_id=1, source_target_pairs={{0,16},{4,20},{8,24},{12,28},{16,0},{20,4},{24,8},{28,12},{1,17},{... | collective-permute-start | bytes 1351688 | tf_op jit(solution)/shard_map/ppermute | solution.py:68
  37.5 54.7 %collective-permute-start.8 = (bf16[384,1280]{1,0:T(8,128)(2,1)S(1)}, bf16[384,1280]{1,0:T(8,128)(2,1)S(1)}, u32[]{:S(2)}, u32[]{:S(2)}) collective-permute-start(bf16[384,1280]{1,0:T(8,128)(2,1)S(1)} %copy-done.13), channel_id=1, source_target_pairs={{0,2},{1,3},{2,0},{3,1},{4,6},{5,7},{6,4},{7,5},{8,10},{9,11},{10,... | collective-permute-start | bytes 2949128 | tf_op jit(solution)/shard_map/ppermute | solution.py:68
  52.7 43.8 %collective-permute-start.2 = (bf16[384,1280]{1,0:T(8,128)(2,1)S(1)}, bf16[384,1280]{1,0:T(8,128)(2,1)}, u32[]{:S(2)}, u32[]{:S(2)}) collective-permute-start(bf16[384,1280]{1,0:T(8,128)(2,1)S(1)} %copy-done.4), channel_id=1, source_target_pairs={{0,1},{1,0},{2,3},{3,2},{4,5},{5,4},{6,7},{7,6},{8,9},{9,8},{10,11... | collective-permute-start | bytes 2949128 | tf_op jit(solution)/shard_map/ppermute | solution.py:68
  52.7 34.8 %collective-permute-start.1 = (bf16[160,1408]{1,0:T(8,128)(2,1)}, bf16[160,1408]{1,0:T(8,128)(2,1)}, u32[]{:S(2)}, u32[]{:S(2)}) collective-permute-start(bf16[160,1408]{1,0:T(8,128)(2,1)} %copy-done.43), channel_id=1, source_target_pairs={{0,4},{4,0},{8,12},{12,8},{16,20},{20,16},{24,28},{28,24},{1,5},{5... | collective-permute-start | bytes 1351688 | tf_op jit(solution)/shard_map/ppermute | solution.py:68
  54.2 38.0 %collective-permute-start.10 = (bf16[160,1408]{1,0:T(8,128)(2,1)}, bf16[160,1408]{1,0:T(8,128)(2,1)}, u32[]{:S(2)}, u32[]{:S(2)}) collective-permute-start(bf16[160,1408]{1,0:T(8,128)(2,1)} %collective-permute-done.4.refs_2_), channel_id=1, source_target_pairs={{0,4},{4,0},{8,12},{12,8},{16,20},{20,16},{24,28},{28,24},{1,5},{5... | collective-permute-start | bytes 1351688 | tf_op jit(solution)/shard_map/ppermute | solution.py:68
  85.8 10.7 %collective-permute-start.6 = (bf16[384,1280]{1,0:T(8,128)(2,1)}, bf16[384,1280]{1,0:T(8,128)(2,1)}, u32[]{:S(2)}, u32[]{:S(2)}) collective-permute-start(bf16[384,1280]{1,0:T(8,128)(2,1)} %collective-permute-done.3), channel_id=1, source_target_pairs={{0,1},{1,0},{2,3},{3,2},{4,5},{5,4},{6,7},{7,6},{8,9},{9,8},{10,11... | collective-permute-start | bytes 2949128 | tf_op jit(solution)/shard_map/ppermute | solution.py:68
  87.5 12.4 %collective-permute-start.7 = (bf16[384,1280]{1,0:T(8,128)(2,1)S(1)}, bf16[384,1280]{1,0:T(8,128)(2,1)}, u32[]{:S(2)}, u32[]{:S(2)}) collective-permute-start(bf16[384,1280]{1,0:T(8,128)(2,1)S(1)} %copy-done.13), channel_id=1, source_target_pairs={{0,1},{1,0},{2,3},{3,2},{4,5},{5,4},{6,7},{7,6},{8,9},{9,8},{10,11... | collective-permute-start | bytes 2949128 | tf_op jit(solution)/shard_map/ppermute | solution.py:68
  94.2 13.5 %collective-permute-start.12 = (bf16[160,1408]{1,0:T(8,128)(2,1)}, bf16[160,1408]{1,0:T(8,128)(2,1)S(1)}, u32[]{:S(2)}, u32[]{:S(2)}) collective-permute-start(bf16[160,1408]{1,0:T(8,128)(2,1)} %collective-permute-done.9.refs_4_), channel_id=1, source_target_pairs={{0,4},{4,0},{8,12},{12,8},{16,20},{20,16},{24,28},{28,24},{1,5},{5... | collective-permute-start | bytes 1351688 | tf_op jit(solution)/shard_map/ppermute | solution.py:68
  133.7 9.6 %collective-permute-start.13 = (bf16[96,1280]{1,0:T(8,128)(2,1)}, bf16[96,1280]{1,0:T(8,128)(2,1)S(1)}, u32[]{:S(2)}, u32[]{:S(2)}) collective-permute-start(bf16[96,1280]{1,0:T(8,128)(2,1)} %get-tuple-element.124), channel_id=1, source_target_pairs={{0,1},{1,0},{2,3},{3,2},{4,5},{5,4},{6,7},{7,6},{8,9},{9,8},{10,11... | collective-permute-start | bytes 737288 | tf_op jit(solution)/shard_map/ppermute | solution.py:68
  133.7 9.6 %collective-permute-start.14 = (bf16[96,1280]{1,0:T(8,128)(2,1)}, bf16[96,1280]{1,0:T(8,128)(2,1)S(1)}, u32[]{:S(2)}, u32[]{:S(2)}) collective-permute-start(bf16[96,1280]{1,0:T(8,128)(2,1)} %get-tuple-element.125), channel_id=1, source_target_pairs={{0,1},{1,0},{2,3},{3,2},{4,5},{5,4},{6,7},{7,6},{8,9},{9,8},{10,11... | collective-permute-start | bytes 737288 | tf_op jit(solution)/shard_map/ppermute | solution.py:68
  147.0 23.9 %collective-permute-start.17 = (bf16[384,1280]{1,0:T(8,128)(2,1)}, bf16[384,1280]{1,0:T(8,128)(2,1)S(1)}, u32[]{:S(2)}, u32[]{:S(2)}) collective-permute-start(bf16[384,1280]{1,0:T(8,128)(2,1)} %pair_sum.2), channel_id=1, source_target_pairs={{0,2},{1,3},{2,0},{3,1},{4,6},{5,7},{6,4},{7,5},{8,10},{9,11},{10,... | collective-permute-start | bytes 2949128 | tf_op jit(solution)/shard_map/ppermute | solution.py:68
  177.1 25.3 %collective-permute-start.22 = (bf16[384,1280]{1,0:T(8,128)(2,1)}, bf16[384,1280]{1,0:T(8,128)(2,1)S(1)}, u32[]{:S(2)}, u32[]{:S(2)}) collective-permute-start(bf16[384,1280]{1,0:T(8,128)(2,1)} %get-tuple-element.138.refs_0_), channel_id=1, source_target_pairs={{0,2},{1,3},{2,0},{3,1},{4,6},{5,7},{6,4},{7,5},{8,10},{9,11},{10,... | collective-permute-start | bytes 2949128 | tf_op jit(solution)/shard_map/ppermute | solution.py:68
  177.4 9.9 %collective-permute-start.23 = (bf16[384,1280]{1,0:T(8,128)(2,1)}, bf16[384,1280]{1,0:T(8,128)(2,1)S(1)}, u32[]{:S(2)}, u32[]{:S(2)}) collective-permute-start(bf16[384,1280]{1,0:T(8,128)(2,1)} %get-tuple-element.138.refs_0_), channel_id=1, source_target_pairs={{0,1},{1,0},{2,3},{3,2},{4,5},{5,4},{6,7},{7,6},{8,9},{9,8},{10,11... | collective-permute-start | bytes 2949128 | tf_op jit(solution)/shard_map/ppermute | solution.py:68
  214.2 9.6 %collective-permute-start.25 = (bf16[96,1280]{1,0:T(8,128)(2,1)}, bf16[96,1280]{1,0:T(8,128)(2,1)S(1)}, u32[]{:S(2)}, u32[]{:S(2)}) collective-permute-start(bf16[96,1280]{1,0:T(8,128)(2,1)} %get-tuple-element.150), channel_id=1, source_target_pairs={{0,1},{1,0},{2,3},{3,2},{4,5},{5,4},{6,7},{7,6},{8,9},{9,8},{10,11... | collective-permute-start | bytes 737288 | tf_op jit(solution)/shard_map/ppermute | solution.py:68
  214.5 9.4 %collective-permute-start.26 = (bf16[96,1280]{1,0:T(8,128)(2,1)}, bf16[96,1280]{1,0:T(8,128)(2,1)S(1)}, u32[]{:S(2)}, u32[]{:S(2)}) collective-permute-start(bf16[96,1280]{1,0:T(8,128)(2,1)} %get-tuple-element.151), channel_id=1, source_target_pairs={{0,1},{1,0},{2,3},{3,2},{4,5},{5,4},{6,7},{7,6},{8,9},{9,8},{10,11... | collective-permute-start | bytes 737288 | tf_op jit(solution)/shard_map/ppermute | solution.py:68
  214.7 9.6 %collective-permute-start.27 = (bf16[96,1280]{1,0:T(8,128)(2,1)}, bf16[96,1280]{1,0:T(8,128)(2,1)S(1)}, u32[]{:S(2)}, u32[]{:S(2)}) collective-permute-start(bf16[96,1280]{1,0:T(8,128)(2,1)} %get-tuple-element.152), channel_id=1, source_target_pairs={{0,1},{1,0},{2,3},{3,2},{4,5},{5,4},{6,7},{7,6},{8,9},{9,8},{10,11... | collective-permute-start | bytes 737288 | tf_op jit(solution)/shard_map/ppermute | solution.py:68
  215.0 9.4 %collective-permute-start.28 = (bf16[96,1280]{1,0:T(8,128)(2,1)}, bf16[96,1280]{1,0:T(8,128)(2,1)S(1)}, u32[]{:S(2)}, u32[]{:S(2)}) collective-permute-start(bf16[96,1280]{1,0:T(8,128)(2,1)} %get-tuple-element.153), channel_id=1, source_target_pairs={{0,1},{1,0},{2,3},{3,2},{4,5},{5,4},{6,7},{7,6},{8,9},{9,8},{10,11... | collective-permute-start | bytes 737288 | tf_op jit(solution)/shard_map/ppermute | solution.py:68
  215.2 42.8 %collective-permute-start.32 = (bf16[96,1280]{1,0:T(8,128)(2,1)}, bf16[96,1280]{1,0:T(8,128)(2,1)S(1)}, u32[]{:S(2)}, u32[]{:S(2)}) collective-permute-start(bf16[96,1280]{1,0:T(8,128)(2,1)} %get-tuple-element.158), channel_id=1, source_target_pairs={{0,1},{1,0},{2,3},{3,2},{4,5},{5,4},{6,7},{7,6},{8,9},{9,8},{10,11... | collective-permute-start | bytes 737288 | tf_op jit(solution)/shard_map/ppermute | solution.py:68
  223.7 34.3 %collective-permute-start.33 = (bf16[96,1280]{1,0:T(8,128)(2,1)}, bf16[96,1280]{1,0:T(8,128)(2,1)}, u32[]{:S(2)}, u32[]{:S(2)}) collective-permute-start(bf16[96,1280]{1,0:T(8,128)(2,1)} %get-tuple-element.159), channel_id=1, source_target_pairs={{0,1},{1,0},{2,3},{3,2},{4,5},{5,4},{6,7},{7,6},{8,9},{9,8},{10,11... | collective-permute-start | bytes 737288 | tf_op jit(solution)/shard_map/ppermute | solution.py:68
  223.9 34.1 %collective-permute-start.34 = (bf16[96,1280]{1,0:T(8,128)(2,1)}, bf16[96,1280]{1,0:T(8,128)(2,1)}, u32[]{:S(2)}, u32[]{:S(2)}) collective-permute-start(bf16[96,1280]{1,0:T(8,128)(2,1)} %get-tuple-element.160), channel_id=1, source_target_pairs={{0,1},{1,0},{2,3},{3,2},{4,5},{5,4},{6,7},{7,6},{8,9},{9,8},{10,11... | collective-permute-start | bytes 737288 | tf_op jit(solution)/shard_map/ppermute | solution.py:68
  224.3 33.7 %collective-permute-start.35 = (bf16[96,1280]{1,0:T(8,128)(2,1)}, bf16[96,1280]{1,0:T(8,128)(2,1)}, u32[]{:S(2)}, u32[]{:S(2)}) collective-permute-start(bf16[96,1280]{1,0:T(8,128)(2,1)} %get-tuple-element.161), channel_id=1, source_target_pairs={{0,1},{1,0},{2,3},{3,2},{4,5},{5,4},{6,7},{7,6},{8,9},{9,8},{10,11... | collective-permute-start | bytes 737288 | tf_op jit(solution)/shard_map/ppermute | solution.py:68
  227.9 30.2 %collective-permute-start.31 = (bf16[384,1280]{1,0:T(8,128)(2,1)}, bf16[384,1280]{1,0:T(8,128)(2,1)}, u32[]{:S(2)}, u32[]{:S(2)}) collective-permute-start(bf16[384,1280]{1,0:T(8,128)(2,1)} %pair_sum.3), channel_id=1, source_target_pairs={{0,2},{1,3},{2,0},{3,1},{4,6},{5,7},{6,4},{7,5},{8,10},{9,11},{10,... | collective-permute-start | bytes 2949128 | tf_op jit(solution)/shard_map/ppermute | solution.py:68
  238.6 197.2 %reduce-scatter.5.cloned.1.call-start = ((), (), s32[]{:S(2)}) async-start(), calls=%async_computation.5 | async-start | bytes 3686400 | tf_op jit(solution)/shard_map/reduce_scatter | solution.py:725
  265.2 26.1 %collective-permute-start.36 = (bf16[384,1280]{1,0:T(8,128)(2,1)}, bf16[384,1280]{1,0:T(8,128)(2,1)}, u32[]{:S(2)}, u32[]{:S(2)}) collective-permute-start(bf16[384,1280]{1,0:T(8,128)(2,1)} %get-tuple-element.166), channel_id=1, source_target_pairs={{0,2},{1,3},{2,0},{3,1},{4,6},{5,7},{6,4},{7,5},{8,10},{9,11},{10,... | collective-permute-start | bytes 2949128 | tf_op jit(solution)/shard_map/ppermute | solution.py:68
  266.4 26.4 %collective-permute-start.30 = (bf16[384,1280]{1,0:T(8,128)(2,1)}, bf16[384,1280]{1,0:T(8,128)(2,1)}, u32[]{:S(2)}, u32[]{:S(2)}) collective-permute-start(bf16[384,1280]{1,0:T(8,128)(2,1)} %slice.200), channel_id=1, source_target_pairs={{0,1},{1,0},{2,3},{3,2},{4,5},{5,4},{6,7},{7,6},{8,9},{9,8},{10,11... | collective-permute-start | bytes 2949128 | tf_op jit(solution)/shard_map/ppermute | solution.py:68
  292.6 33.0 %collective-permute-start.29 = (bf16[384,1280]{1,0:T(8,128)(2,1)}, bf16[384,1280]{1,0:T(8,128)(2,1)S(1)}, u32[]{:S(2)}, u32[]{:S(2)}) collective-permute-start(bf16[384,1280]{1,0:T(8,128)(2,1)} %slice.198), channel_id=1, source_target_pairs={{0,1},{1,0},{2,3},{3,2},{4,5},{5,4},{6,7},{7,6},{8,9},{9,8},{10,11... | collective-permute-start | bytes 2949128 | tf_op jit(solution)/shard_map/ppermute | solution.py:68
  295.3 30.2 %collective-permute-start.38 = (bf16[384,1280]{1,0:T(8,128)(2,1)}, bf16[384,1280]{1,0:T(8,128)(2,1)S(1)}, u32[]{:S(2)}, u32[]{:S(2)}) collective-permute-start(bf16[384,1280]{1,0:T(8,128)(2,1)} %add_convert_fusion.1), channel_id=1, source_target_pairs={{0,2},{1,3},{2,0},{3,1},{4,6},{5,7},{6,4},{7,5},{8,10},{9,11},{10,... | collective-permute-start | bytes 2949128 | tf_op jit(solution)/shard_map/ppermute | solution.py:68
  337.8 29.9 %collective-permute-start.42 = (bf16[384,1280]{1,0:T(8,128)(2,1)}, bf16[384,1280]{1,0:T(8,128)(2,1)}, u32[]{:S(2)}, u32[]{:S(2)}) collective-permute-start(bf16[384,1280]{1,0:T(8,128)(2,1)} %add_convert_fusion), channel_id=1, source_target_pairs={{0,2},{1,3},{2,0},{3,1},{4,6},{5,7},{6,4},{7,5},{8,10},{9,11},{10,... | collective-permute-start | bytes 2949128 | tf_op jit(solution)/shard_map/ppermute | solution.py:68
  349.8 17.9 %collective-permute-start.41 = (bf16[160,1408]{1,0:T(8,128)(2,1)}, bf16[160,1408]{1,0:T(8,128)(2,1)}, u32[]{:S(2)}, u32[]{:S(2)}) collective-permute-start(bf16[160,1408]{1,0:T(8,128)(2,1)} %get-tuple-element.221), channel_id=1, source_target_pairs={{0,4},{4,0},{8,12},{12,8},{16,20},{20,16},{24,28},{28,24},{1,5},{5... | collective-permute-start | bytes 1351688 | tf_op jit(solution)/shard_map/ppermute | solution.py:68
  351.4 30.2 %collective-permute-start.43 = (bf16[160,1408]{1,0:T(8,128)(2,1)}, bf16[160,1408]{1,0:T(8,128)(2,1)}, u32[]{:S(2)}, u32[]{:S(2)}) collective-permute-start(bf16[160,1408]{1,0:T(8,128)(2,1)} %get-tuple-element.220), channel_id=1, source_target_pairs={{0,4},{4,0},{8,12},{12,8},{16,20},{20,16},{24,28},{28,24},{1,5},{5... | collective-permute-start | bytes 1351688 | tf_op jit(solution)/shard_map/ppermute | solution.py:68
  351.8 43.9 %collective-permute-start.44 = (bf16[160,1408]{1,0:T(8,128)(2,1)}, bf16[160,1408]{1,0:T(8,128)(2,1)}, u32[]{:S(2)}, u32[]{:S(2)}) collective-permute-start(bf16[160,1408]{1,0:T(8,128)(2,1)} %get-tuple-element.219), channel_id=1, source_target_pairs={{0,4},{4,0},{8,12},{12,8},{16,20},{20,16},{24,28},{28,24},{1,5},{5... | collective-permute-start | bytes 1351688 | tf_op jit(solution)/shard_map/ppermute | solution.py:68
  353.5 50.9 %collective-permute-start.45 = (bf16[160,1408]{1,0:T(8,128)(2,1)}, bf16[160,1408]{1,0:T(8,128)(2,1)}, u32[]{:S(2)}, u32[]{:S(2)}) collective-permute-start(bf16[160,1408]{1,0:T(8,128)(2,1)} %get-tuple-element.218), channel_id=1, source_target_pairs={{0,4},{4,0},{8,12},{12,8},{16,20},{20,16},{24,28},{28,24},{1,5},{5... | collective-permute-start | bytes 1351688 | tf_op jit(solution)/shard_map/ppermute | solution.py:68
  408.5 13.7 %collective-permute-start.46 = (bf16[96,1280]{1,0:T(8,128)(2,1)S(1)}, bf16[96,1280]{1,0:T(8,128)(2,1)S(1)}, u32[]{:S(2)}, u32[]{:S(2)}) collective-permute-start(bf16[96,1280]{1,0:T(8,128)(2,1)S(1)} %get-tuple-element.225), channel_id=1, source_target_pairs={{0,1},{1,0},{2,3},{3,2},{4,5},{5,4},{6,7},{7,6},{8,9},{9,8},{10,11... | collective-permute-start | bytes 737288 | tf_op jit(solution)/shard_map/ppermute | solution.py:68
  408.6 13.7 %collective-permute-start.47 = (bf16[96,1280]{1,0:T(8,128)(2,1)S(1)}, bf16[96,1280]{1,0:T(8,128)(2,1)S(1)}, u32[]{:S(2)}, u32[]{:S(2)}) collective-permute-start(bf16[96,1280]{1,0:T(8,128)(2,1)S(1)} %get-tuple-element.224), channel_id=1, source_target_pairs={{0,1},{1,0},{2,3},{3,2},{4,5},{5,4},{6,7},{7,6},{8,9},{9,8},{10,11... | collective-permute-start | bytes 737288 | tf_op jit(solution)/shard_map/ppermute | solution.py:68
  413.0 37.2 %collective-permute-start.50 = (bf16[160,1408]{1,0:T(8,128)(2,1)}, bf16[160,1408]{1,0:T(8,128)(2,1)}, u32[]{:S(2)}, u32[]{:S(2)}) collective-permute-start(bf16[160,1408]{1,0:T(8,128)(2,1)} %get-tuple-element.216), channel_id=1, source_target_pairs={{0,16},{4,20},{8,24},{12,28},{16,0},{20,4},{24,8},{28,12},{1,17},{... | collective-permute-start | bytes 1351688 | tf_op jit(solution)/shard_map/ppermute | solution.py:68
  417.9 32.3 %collective-permute-start.51 = (bf16[160,1408]{1,0:T(8,128)(2,1)}, bf16[160,1408]{1,0:T(8,128)(2,1)}, u32[]{:S(2)}, u32[]{:S(2)}) collective-permute-start(bf16[160,1408]{1,0:T(8,128)(2,1)} %get-tuple-element.215), channel_id=1, source_target_pairs={{0,24},{4,28},{8,16},{12,20},{16,8},{20,12},{24,0},{28,4},{1,25},{... | collective-permute-start | bytes 1351688 | tf_op jit(solution)/shard_map/ppermute | solution.py:68
  422.1 29.4 %collective-permute-start.52 = (bf16[160,1408]{1,0:T(8,128)(2,1)}, bf16[160,1408]{1,0:T(8,128)(2,1)}, u32[]{:S(2)}, u32[]{:S(2)}) collective-permute-start(bf16[160,1408]{1,0:T(8,128)(2,1)} %get-tuple-element.214), channel_id=1, source_target_pairs={{0,8},{4,12},{8,0},{12,4},{16,24},{20,28},{24,16},{28,20},{1,9},{5... | collective-permute-start | bytes 1351688 | tf_op jit(solution)/shard_map/ppermute | solution.py:68
  423.7 12.0 %collective-permute-start.54 = (f32[1,160,160]{2,1,0:T(8,128)S(1)}, f32[1,160,160]{2,1,0:T(8,128)S(1)}, u32[]{:S(2)}, u32[]{:S(2)}) collective-permute-start(f32[1,160,160]{2,1,0:T(8,128)S(1)} %add.239), channel_id=1, source_target_pairs={{0,2},{1,3},{2,0},{3,1},{4,6},{5,7},{6,4},{7,5},{8,10},{9,11},{10,... | collective-permute-start | bytes 307208 | tf_op jit(solution)/shard_map/ppermute | solution.py:68
  433.7 9.6 %collective-permute-start.56 = (f32[8,1280]{1,0:T(8,128)S(1)}, f32[8,1280]{1,0:T(8,128)S(1)}, u32[]{:S(2)}, u32[]{:S(2)}) collective-permute-start(f32[8,1280]{1,0:T(8,128)S(1)} %add.242), channel_id=1, source_target_pairs={{0,2},{1,3},{2,0},{3,1},{4,6},{5,7},{6,4},{7,5},{8,10},{9,11},{10,... | collective-permute-start | bytes 122888 | tf_op jit(solution)/shard_map/ppermute | solution.py:68
  463.1 13.3 %collective-permute-start.58 = (f32[3,160,160]{2,1,0:T(8,128)S(1)}, f32[3,160,160]{2,1,0:T(8,128)S(1)}, u32[]{:S(2)}, u32[]{:S(2)}) collective-permute-start(f32[3,160,160]{2,1,0:T(8,128)S(1)} %fusion.38), channel_id=1, source_target_pairs={{0,2},{1,3},{2,0},{3,1},{4,6},{5,7},{6,4},{7,5},{8,10},{9,11},{10,... | collective-permute-start | bytes 921608 | tf_op jit(solution)/shard_map/ppermute | solution.py:68
  495.4 11.4 %collective-permute-start.60 = (f32[9,1280]{1,0:T(8,128)S(1)}, f32[9,1280]{1,0:T(8,128)S(1)}, u32[]{:S(2)}, u32[]{:S(2)}) collective-permute-start(f32[9,1280]{1,0:T(8,128)S(1)} %add.255), channel_id=1, source_target_pairs={{0,8},{4,12},{8,0},{12,4},{16,24},{20,28},{24,16},{28,20},{1,9},{5... | collective-permute-start | bytes 138248 | tf_op jit(solution)/shard_map/ppermute | solution.py:68
  (89 other events, 817.1 us)
Sparse Core Ops, SparseCore 0:
  10.8 94.9 all-gather.2
  108.6 59.2 all-gather.4
  238.7 77.1 reduce-scatter.2
  332.4 90.5 reduce-scatter.4

commit v10 on v9

--- a/solution.py
+++ b/solution.py
@@ -896,9 +896,8 @@
     far = swap(first_total, "tensor", 2)
     d_qkv, raw_wq, raw_wo = tie([d_qkv, raw_wq, raw_wo])
     owns, crossed = dp_cross(jnp.concatenate([raw_wq, raw_wo], axis=1))
-    first_mine = mm(after(d_qkv[:half], first_total, *crossed[:1]), wq, NT).astype(BF16)
+    first_mine = mm(after(d_qkv[:half], first_total), wq, NT).astype(BF16)
     lined = dp_line(owns, tie(crossed, far))
-    far = after(far, lined[-1])
     quarter = tok // PIECES
     sent = [first_mine[tok + k * quarter : tok + k * quarter + quarter] for k in range(PIECES)]
     near = swap_all(sent, "tensor", 1)

time: 526 us -> 515 us (0.979)
    unnamed x145 -> x143, local copies, waits for them, and re-layouts: 18.6 us -> 15.9 us
  transfers between devices with their start and end apart: 66 -> 66, of which waited for: 21 -> 25; matrix products, arithmetic and copies ran while one was open for 19% -> 17% of each run, Pallas kernels for 27% -> 27%
where the time goes in v10:
time: 515 us; the launch traced here: 510 us
  waiting for transfers between devices  159 us (31%)
  Pallas kernels  159 us (31%)
  matrix products  65.1 us (13%)
  starting transfers between devices  50.3 us (10%)
  other arithmetic  32.2 us (6%)
  local copies, waits for them, and re-layouts  28.5 us (6%)
  between operations  16.1 us (3%)
    ppermute x62, waiting for transfers between devices, swap(): return lax.ppermute(value, axis, [(i, i ^ mask) for i in range(size)])  159 us
    dot_general x10, matrix products, mm(): return lax.dot_general(left, right, dims, preferred_element_type=F32)  52.3 us
    ppermute x62, starting transfers between devices, swap(): return lax.ppermute(value, axis, [(i, i ^ mask) for i in range(size)])  50.1 us
    pallas_call x2, Pallas kernels, attn_back_call(): pl.pallas_call(partial(attn_back_body, heads, last_part, first), grid=(co...  44.8 us
    pallas_call x3, Pallas kernels, attn_call(): pl.pallas_call(partial(attn_body, heads, emits, len(held)), grid=(count /...  31.2 us
    pallas_call x3, Pallas kernels, mlp_call(): pl.pallas_call(partial(mlp_body, min(256, hidden_width), emits, len(held)...  30.6 us
    pallas_call x3, Pallas kernels, row_call(): pl.pallas_call(partial(row_body, body, len(rows_in)), grid=(PIECES,), in_...  17.5 us
    pallas_call x2, Pallas kernels, polar_call(): pl.pallas_call(polar_body, out_shape=jax.ShapeDtypeStruct(grams.shape, F3...  16 us
  transfers between devices with their start and end apart: 66, of which 25 were waited for; matrix products, arithmetic and copies ran while one was open for 17% of the time, Pallas kernels for 27%

profile of v10, /device:TPU:0, one launch (start us, length us, event | category | flops | bytes accessed | tf_op | source)
XLA Modules:
  0.0 510.2 jit_solution(3423635903201052223)
XLA Ops:
  11.5 3.0 collective-permute-start.3
  15.1 3.7 collective-permute-start
  21.1 15.6 %collective-permute-done.refs_6_ = bf16[160,1408]{1,0:T(8,128)(2,1)S(1)} collective-permute-done((bf16[160,1408]{1,0:T(8,128)(2,1)S(1)}, bf16[160,1408]{1,0:T(8,128)(2,1)S(1)}, u32[]{:S(2)}, u32[]{:S(2)}) %collective-permute-start) | collective-permute-done | bytes 450592 | tf_op jit(solution)/shard_map/ppermute | solution.py:68
  37.5 15.2 %collective-permute-done.4.refs_2_ = bf16[160,1408]{1,0:T(8,128)(2,1)} collective-permute-done((bf16[160,1408]{1,0:T(8,128)(2,1)S(1)}, bf16[160,1408]{1,0:T(8,128)(2,1)}, u32[]{:S(2)}, u32[]{:S(2)}) %collective-permute-start.4) | collective-permute-done | bytes 450592 | tf_op jit(solution)/shard_map/ppermute | solution.py:68
  54.7 31.1 %collective-permute-done.9.refs_4_ = bf16[160,1408]{1,0:T(8,128)(2,1)} collective-permute-done((bf16[160,1408]{1,0:T(8,128)(2,1)S(1)}, bf16[160,1408]{1,0:T(8,128)(2,1)}, u32[]{:S(2)}, u32[]{:S(2)}) %collective-permute-start.9) | collective-permute-done | bytes 450592 | tf_op jit(solution)/shard_map/ppermute | solution.py:68
  88.0 4.2 collective-permute-done.10.refs_3_
  96.5 3.5 pad_maximum_fusion.x_ref
  99.9 3.3 pad_maximum_fusion.1
  103.2 4.5 collective-permute-done.12.refs_5_
  108.5 4.0 place_rows.1
  115.7 9.8 %norm_qkv.1 = (bf16[1536,1280]{1,0:T(8,128)(2,1)}, bf16[1536,1024]{1,0:T(8,128)(2,1)}) custom-call(bf16[1536,1280]{1,0:T(8,128)(2,1)} %pad_maximum_fusion.x_ref, f32[8,1280]{1,0:T(8,128)} %slice.149.vec_ref.refs_7_.refs_8_, bf16[1280,1024]{1,0:T(8,128)(2,1)} %get-tuple-element.117.w_ref, f32[1,1024]{1,0:T(1,128)} %pad_maximum_fusion.7.bias_ref), custom_call_target="tpu_custom_call" | custom-call | flops 1000000 | bytes 100000 | tf_op jit(solution)/shard_map/norm_qkv/pallas_call | solution.py:109
  125.5 8.1 %attn_fwd.3 = (bf16[1536,384]{1,0:T(8,128)(2,1)}, f32[8,1536]{1,0:T(8,128)}, bf16[96,1280]{1,0:T(8,128)(2,1)}, bf16[96,1280]{1,0:T(8,128)(2,1)}, bf16[96,1280]{1,0:T(8,128)(2,1)}, /*index=5*/bf16[96,1280]{1,0:T(8,128)(2,1)}) custom-call(bf16[1536,1024]{1,0:T(8,128)(2,1)} %get-tuple-element.127.q_ref.qkv_ref, ...), custom_call_target="tpu_custom_call" | custom-call | flops 1000000 | bytes 100000 | tf_op jit(solution)/shard_map/attn_fwd/pallas_call | solution.py:266
  134.7 8.6 %attn_fwd.4 = (bf16[1536,384]{1,0:T(8,128)(2,1)}, f32[8,1536]{1,0:T(8,128)}, bf16[384,1280]{1,0:T(8,128)(2,1)}) custom-call(bf16[1536,1024]{1,0:T(8,128)(2,1)} %get-tuple-element.127.q_ref.qkv_ref, bf16[1536,1024]{1,0:T(8,128)(2,1)} %get-tuple-element.127.q_ref.qkv_ref, ...), custom_call_target="tpu_custom_call", output_to_operand_aliasing={{0}: (4, {}), {1}: (5, {})} | custom-call | flops 1000000 | bytes 100000 | tf_op jit(solution)/shard_map/attn_fwd/pallas_call | solution.py:266
  144.2 2.7 pair_sum.2
  147.0 14.5 %attn_fwd.5 = (bf16[1536,384]{1,0:T(8,128)(2,1)}, f32[8,1536]{1,0:T(8,128)}, bf16[384,1280]{1,0:T(8,128)(2,1)}, bf16[96,1280]{1,0:T(8,128)(2,1)}, bf16[96,1280]{...) custom-call(bf16[1536,1024]{1,0:T(8,128)(2,1)} %get-tuple-element.12, ...), custom_call_target="tpu_custom_call", output_to_operand_aliasing={{0}: (4, {}), {1}: (5, {})} | custom-call | flops 1000000 | bytes 100000 | tf_op jit(solution)/shard_map/attn_fwd/pallas_call | solution.py:266
  164.0 6.9 %collective-permute-done.17.refs_2_ = bf16[384,1280]{1,0:T(8,128)(2,1)S(1)} collective-permute-done((bf16[384,1280]{1,0:T(8,128)(2,1)}, bf16[384,1280]{1,0:T(8,128)(2,1)S(1)}, u32[]{:S(2)}, u32[]{:S(2)}) %collective-permute-start.17) | collective-permute-done | bytes 983072 | tf_op jit(solution)/shard_map/ppermute | solution.py:68
  172.1 4.9 residual.1
  177.3 9.9 %fusion.42.refs_4_.refs_3_ = f32[1536,1280]{1,0:T(8,128)} fusion(bf16[1536,1280]{1,0:T(8,128)(2,1)} %pad_maximum_fusion.1, bf16[1280,1280]{1,0:T(8,128)(2,1)} %all-gather.3.cloned.1.call-done), kind=kOutput, calls=%fused_computation.121 | convolution fusion | flops 5033164800 | bytes 15073280 | tf_op jit(solution)/shard_map/dot_general | solution.py:43
  188.2 14.5 %mlp_up.3 = (bf16[1536,1280]{1,0:T(8,128)(2,1)}, bf16[1536,1280]{1,0:T(8,128)(2,1)}, f32[8,1280]{1,0:T(8,128)}, bf16[384,1280]{1,0:T(8,128)(2,1)}, bf16[96,1280]...) custom-call(bf16[384,1280]{1,0:T(8,128)(2,1)} %get-tuple-element.137.refs_0_, ...), custom_call_target="tpu_custom_call" | custom-call | flops 1000000 | bytes 100000 | tf_op jit(solution)/shard_map/mlp_up/pallas_call | solution.py:471
  206.4 8.0 %mlp_up.4 = (bf16[1536,1280]{1,0:T(8,128)(2,1)}, bf16[1536,1280]{1,0:T(8,128)(2,1)}, f32[8,1280]{1,0:T(8,128)}, bf16[96,1280]{1,0:T(8,128)(2,1)}, bf16[96,1280]{...) custom-call(bf16[384,1280]{1,0:T(8,128)(2,1)} %copy-done.35, ...), custom_call_target="tpu_custom_call", output_to_operand_aliasing={{0}: (4, {}), {1}: (5, {})} | custom-call | flops 1000000 | bytes 100000 | tf_op jit(solution)/shard_map/mlp_up/pallas_call | solution.py:471
  215.4 8.2 %mlp_up.5 = (bf16[1536,1280]{1,0:T(8,128)(2,1)}, bf16[1536,1280]{1,0:T(8,128)(2,1)}, f32[8,1280]{1,0:T(8,128)}, bf16[384,1280]{1,0:T(8,128)(2,1)}) custom-call(bf16[384,1280]{1,0:T(8,128)(2,1)} %copy-done.31, bf16[1280,1280]{1,0:T(8,128)(2,1)} %all-gather.5.cloned.1.call-done.refs_2_.refs_1_, ...), custom_call_target="tpu_custom_call", output_to_operand_aliasing={{0}: (4, {}), {1}: (5, {})} | custom-call | flops 1000000 | bytes 100000 | tf_op jit(solution)/shard_map/mlp_up/pallas_call | solution.py:471
  224.5 2.8 pair_sum.3
  227.3 9.1 %convolution_convert_fusion.1 = bf16[1280,1280]{1,0:T(8,128)(2,1)} fusion(bf16[1536,1280]{1,0:T(8,128)(2,1)S(1)} %copy-done.10, bf16[1536,1280]{1,0:T(8,128)(2,1)} %get-tuple-element.156), kind=kOutput, calls=%fused_computation.1 | convolution fusion | flops 5034803200 | bytes 11141120 | tf_op jit(solution)/shard_map/dot_general | solution.py:43
  239.4 9.0 %convolution_convert_fusion = bf16[1280,1280]{1,0:T(8,128)(2,1)} fusion(bf16[1536,1280]{1,0:T(8,128)(2,1)} %get-tuple-element.155, bf16[384,1280]{1,0:T(8,128)(2,1)} %copy-done.35, bf16[384,1280]{1,0:T(8,128)(2,1)S(1)} %copy-done.32, bf16[384,1280]{1,0:T(8,128)(2,1)S(1)} %copy-done.34, bf16[384,1280]{1,0:T(8,128)(2,1)S(1)} %copy-done.29), kind=kOutput, calls=%fused_computation | convolution fusion | flops 5050531840 | bytes 11141120 | tf_op jit(solution)/shard_map/dot_general | solution.py:43
  248.4 5.4 %convolution_convert_fusion.3 = bf16[768,1280]{1,0:T(8,128)(2,1)S(1)} fusion(bf16[1280,1280]{1,0:T(8,128)(2,1)} %all-gather.3.cloned.1.call-done, bf16[1536,1280]{1,0:T(8,128)(2,1)} %get-tuple-element.156), kind=kOutput, calls=%fused_computation.12 | convolution fusion | flops 2517565440 | bytes 7208960 | tf_op jit(solution)/shard_map/dot_general | solution.py:43
  253.8 2.7 convolution_convert_fusion.4
  256.7 5.3 %collective-permute-done.31.refs_2_ = bf16[384,1280]{1,0:T(8,128)(2,1)} collective-permute-done((bf16[384,1280]{1,0:T(8,128)(2,1)}, bf16[384,1280]{1,0:T(8,128)(2,1)}, u32[]{:S(2)}, u32[]{:S(2)}) %collective-permute-start.31) | collective-permute-done | bytes 983072 | tf_op jit(solution)/shard_map/ppermute | solution.py:68
  261.9 6.4 %second_back.1 = (f32[384,1280]{1,0:T(8,128)}, bf16[384,1280]{1,0:T(8,128)(2,1)}, f32[8,1280]{1,0:T(8,128)}) custom-call(f32[384,1280]{1,0:T(8,128)} %get-tuple-element.136.refs_0_, bf16[384,1280]{1,0:T(8,128)(2,1)} %get-tuple-element.140.refs_1_, bf16[384,1280]{1,0:T(8,128)(2,1)} %collective-permute-done.31.refs_2_, bf16[384,1280]{1,0:T(8,128)(2,1)} %refs_3_.1, ...), custom_call_target="tpu_custom_call" | custom-call | flops 1000000 | bytes 100000 | tf_op jit(solution)/shard_map/second_back/pallas_call | solution.py:559
  274.1 22.2 %attn_bwd.2 = (bf16[1536,1024]{1,0:T(8,128)(2,1)}, f32[8,384]{1,0:T(8,128)}, f32[1536,384]{1,0:T(8,128)}, f32[1536,384]{1,0:T(8,128)}) custom-call(bf16[768,1280]{1,0:T(8,128)(2,1)} %copy-done.7, bf16[1280,384]{1,0:T(8,128)(2,1)} %get-tuple-element.119.wo_ref, bf16[1536,384]{1,0:T(8,128)(2,1)} %get-tuple-element.166.att_ref, ...), custom_call_target="tpu_custom_call" | custom-call | flops 1000000 | bytes 100000 | tf_op jit(solution)/shard_map/attn_bwd/pallas_call | solution.py:399
  307.8 22.6 %attn_bwd.3 = (bf16[1536,1024]{1,0:T(8,128)(2,1)}, f32[8,384]{1,0:T(8,128)}) custom-call(bf16[768,1280]{1,0:T(8,128)(2,1)} %copy-done.9, bf16[1280,384]{1,0:T(8,128)(2,1)} %get-tuple-element.119.wo_ref, bf16[1536,384]{1,0:T(8,128)(2,1)} %get-tuple-element.166.att_ref, ...), custom_call_target="tpu_custom_call", output_to_operand_aliasing={{0}: (10, {})} | custom-call | flops 1000000 | bytes 100000 | tf_op jit(solution)/shard_map/attn_bwd/pallas_call | solution.py:399
  331.7 3.7 convolution_convert_fusion.6
  337.7 2.9 collective-permute-done.40
  340.6 2.8 add_convert_fusion
  344.9 6.8 %convolution_convert_fusion.2 = bf16[1280,1024]{1,0:T(8,128)(2,1)S(1)} fusion(bf16[1536,1280]{1,0:T(8,128)(2,1)} %get-tuple-element.177, bf16[1536,1024]{1,0:T(8,128)(2,1)S(1)} %copy-done.6), kind=kOutput, calls=%fused_computation.11 | convolution fusion | flops 4027842560 | bytes 9699328 | tf_op jit(solution)/shard_map/dot_general | solution.py:43
  359.9 7.5 %collective-permute-done.41.refs_2_ = bf16[384,1280]{1,0:T(8,128)(2,1)} collective-permute-done((bf16[384,1280]{1,0:T(8,128)(2,1)}, bf16[384,1280]{1,0:T(8,128)(2,1)}, u32[]{:S(2)}, u32[]{:S(2)}) %collective-permute-start.41) | collective-permute-done | bytes 983072 | tf_op jit(solution)/shard_map/ppermute | solution.py:68
  367.4 4.6 collective-permute-done.46
  372.0 9.8 %collective-permute-done.47 = bf16[160,1408]{1,0:T(8,128)(2,1)S(1)} collective-permute-done((bf16[160,1408]{1,0:T(8,128)(2,1)S(1)}, bf16[160,1408]{1,0:T(8,128)(2,1)S(1)}, u32[]{:S(2)}, u32[]{:S(2)}) %collective-permute-start.47) | collective-permute-done | bytes 450592 | tf_op jit(solution)/shard_map/ppermute | solution.py:68
  381.8 14.0 %collective-permute-done.48 = bf16[160,1408]{1,0:T(8,128)(2,1)S(1)} collective-permute-done((bf16[160,1408]{1,0:T(8,128)(2,1)S(1)}, bf16[160,1408]{1,0:T(8,128)(2,1)S(1)}, u32[]{:S(2)}, u32[]{:S(2)}) %collective-permute-start.48) | collective-permute-done | bytes 450592 | tf_op jit(solution)/shard_map/ppermute | solution.py:68
  395.8 9.3 %collective-permute-done.49 = bf16[160,1408]{1,0:T(8,128)(2,1)S(1)} collective-permute-done((bf16[160,1408]{1,0:T(8,128)(2,1)S(1)}, bf16[160,1408]{1,0:T(8,128)(2,1)S(1)}, u32[]{:S(2)}, u32[]{:S(2)}) %collective-permute-start.49) | collective-permute-done | bytes 450592 | tf_op jit(solution)/shard_map/ppermute | solution.py:68
  408.1 3.1 collective-permute-start.51
  417.2 6.2 %first_back.1 = (f32[384,1280]{1,0:T(8,128)}, f32[8,1280]{1,0:T(8,128)}) custom-call(bf16[384,1280]{1,0:T(8,128)(2,1)} %refs_0_.3, bf16[384,1280]{1,0:T(8,128)(2,1)} %slice.203.refs_1_, bf16[384,1280]{1,0:T(8,128)(2,1)} %collective-permute-done.41.refs_2_, f32[384,1280]{1,0:T(8,128)} %get-tuple-element.181.refs_3_, bf16[96,1280]{1,0:T(8,128)(2,1)} %copy-done.45, ...), custom_call_target="tpu_custom_call" | custom-call | flops 1000000 | bytes 100000 | tf_op jit(solution)/shard_map/first_back/pallas_call | solution.py:559
  426.2 3.3 collective-permute-done.56
  430.2 6.8 %polar.2 = f32[1,160,160]{2,1,0:T(8,128)} custom-call(f32[1,160,160]{2,1,0:T(8,128)} %add.240.gram_ref), custom_call_target="tpu_custom_call" | custom-call | tf_op jit(solution)/shard_map/polar/pallas_call | solution.py:612
  437.0 3.1 collective-permute-done.50
  456.1 9.3 %collective-permute-done.58 = f32[3,160,160]{2,1,0:T(8,128)S(1)} collective-permute-done((f32[3,160,160]{2,1,0:T(8,128)S(1)}, f32[3,160,160]{2,1,0:T(8,128)S(1)}, u32[]{:S(2)}, u32[]{:S(2)}) %collective-permute-start.58) | collective-permute-done | bytes 307232 | tf_op jit(solution)/shard_map/ppermute | solution.py:68
  466.2 9.2 %polar.3 = f32[3,160,160]{2,1,0:T(8,128)} custom-call(f32[3,160,160]{2,1,0:T(8,128)} %fusion.57.gram_ref), custom_call_target="tpu_custom_call" | custom-call | tf_op jit(solution)/shard_map/polar/pallas_call | solution.py:612
  480.5 3.9 collective-permute-done.59
  484.4 9.0 %collective-permute-start.60 = (f32[9,1280]{1,0:T(8,128)S(1)}, f32[9,1280]{1,0:T(8,128)S(1)}, u32[]{:S(2)}, u32[]{:S(2)}) collective-permute-start(f32[9,1280]{1,0:T(8,128)S(1)} %add.255), channel_id=1, source_target_pairs={{0,8},{4,12},{8,0},{12,4},{16,24},{20,28},{24,16},{28,20},{1,9},{5... | collective-permute-start | bytes 138248 | tf_op jit(solution)/shard_map/ppermute | solution.py:68
  (345 shorter events, 109.4 us)
Async XLA Ops:
  7.3 163.6 %all-gather.3.cloned.1.call-start = ((), (), s32[]{:S(2)}) async-start(), calls=%async_computation.2 | async-start | bytes 3686400 | tf_op jit(solution)/shard_map/all_gather | solution.py:804
  9.4 167.9 %all-gather.5.cloned.1.call-start = ((), (), s32[]{:S(2)}) async-start(), calls=%async_computation.3 | async-start | bytes 3686400 | tf_op jit(solution)/shard_map/all_gather | solution.py:805
  11.4 333.5 %reduce-scatter.3.cloned.1.call-start = ((), (), s32[]{:S(2)}) async-start(), calls=%async_computation.4 | async-start | bytes 3686400 | tf_op jit(solution)/shard_map/reduce_scatter | solution.py:725
  11.5 42.7 %collective-permute-start.3 = (bf16[384,1280]{1,0:T(8,128)(2,1)S(1)}, bf16[384,1280]{1,0:T(8,128)(2,1)}, u32[]{:S(2)}, u32[]{:S(2)}) collective-permute-start(bf16[384,1280]{1,0:T(8,128)(2,1)S(1)} %copy-done.2), channel_id=1, source_target_pairs={{0,2},{1,3},{2,0},{3,1},{4,6},{5,7},{6,4},{7,5},{8,10},{9,11},{10,... | collective-permute-start | bytes 2949128 | tf_op jit(solution)/shard_map/ppermute | solution.py:68
  15.1 21.6 %collective-permute-start = (bf16[160,1408]{1,0:T(8,128)(2,1)S(1)}, bf16[160,1408]{1,0:T(8,128)(2,1)S(1)}, u32[]{:S(2)}, u32[]{:S(2)}) collective-permute-start(bf16[160,1408]{1,0:T(8,128)(2,1)S(1)} %concatenate.52.refs_0_), channel_id=1, source_target_pairs={{0,24},{4,28},{8,16},{12,20},{16,8},{20,12},{24,0},{28,4},{1,25},{... | collective-permute-start | bytes 1351688 | tf_op jit(solution)/shard_map/ppermute | solution.py:68
  18.8 33.9 %collective-permute-start.4 = (bf16[160,1408]{1,0:T(8,128)(2,1)S(1)}, bf16[160,1408]{1,0:T(8,128)(2,1)}, u32[]{:S(2)}, u32[]{:S(2)}) collective-permute-start(bf16[160,1408]{1,0:T(8,128)(2,1)S(1)} %concatenate.52.refs_0_), channel_id=1, source_target_pairs={{0,8},{4,12},{8,0},{12,4},{16,24},{20,28},{24,16},{28,20},{1,9},{5... | collective-permute-start | bytes 1351688 | tf_op jit(solution)/shard_map/ppermute | solution.py:68
  18.8 33.9 %collective-permute-start.5 = (bf16[160,1408]{1,0:T(8,128)(2,1)S(1)}, bf16[160,1408]{1,0:T(8,128)(2,1)}, u32[]{:S(2)}, u32[]{:S(2)}) collective-permute-start(bf16[160,1408]{1,0:T(8,128)(2,1)S(1)} %concatenate.52.refs_0_), channel_id=1, source_target_pairs={{0,4},{4,0},{8,12},{12,8},{16,20},{20,16},{24,28},{28,24},{1,5},{5... | collective-permute-start | bytes 1351688 | tf_op jit(solution)/shard_map/ppermute | solution.py:68
  20.3 65.5 %collective-permute-start.9 = (bf16[160,1408]{1,0:T(8,128)(2,1)S(1)}, bf16[160,1408]{1,0:T(8,128)(2,1)}, u32[]{:S(2)}, u32[]{:S(2)}) collective-permute-start(bf16[160,1408]{1,0:T(8,128)(2,1)S(1)} %concatenate.52.refs_0_), channel_id=1, source_target_pairs={{0,16},{4,20},{8,24},{12,28},{16,0},{20,4},{24,8},{28,12},{1,17},{... | collective-permute-start | bytes 1351688 | tf_op jit(solution)/shard_map/ppermute | solution.py:68
  37.5 54.7 %collective-permute-start.8 = (bf16[384,1280]{1,0:T(8,128)(2,1)S(1)}, bf16[384,1280]{1,0:T(8,128)(2,1)S(1)}, u32[]{:S(2)}, u32[]{:S(2)}) collective-permute-start(bf16[384,1280]{1,0:T(8,128)(2,1)S(1)} %copy-done.11), channel_id=1, source_target_pairs={{0,2},{1,3},{2,0},{3,1},{4,6},{5,7},{6,4},{7,5},{8,10},{9,11},{10,... | collective-permute-start | bytes 2949128 | tf_op jit(solution)/shard_map/ppermute | solution.py:68
  52.7 43.8 %collective-permute-start.2 = (bf16[384,1280]{1,0:T(8,128)(2,1)S(1)}, bf16[384,1280]{1,0:T(8,128)(2,1)}, u32[]{:S(2)}, u32[]{:S(2)}) collective-permute-start(bf16[384,1280]{1,0:T(8,128)(2,1)S(1)} %copy-done.2), channel_id=1, source_target_pairs={{0,1},{1,0},{2,3},{3,2},{4,5},{5,4},{6,7},{7,6},{8,9},{9,8},{10,11... | collective-permute-start | bytes 2949128 | tf_op jit(solution)/shard_map/ppermute | solution.py:68
  52.7 34.8 %collective-permute-start.1 = (bf16[160,1408]{1,0:T(8,128)(2,1)}, bf16[160,1408]{1,0:T(8,128)(2,1)}, u32[]{:S(2)}, u32[]{:S(2)}) collective-permute-start(bf16[160,1408]{1,0:T(8,128)(2,1)} %copy-done.42), channel_id=1, source_target_pairs={{0,4},{4,0},{8,12},{12,8},{16,20},{20,16},{24,28},{28,24},{1,5},{5... | collective-permute-start | bytes 1351688 | tf_op jit(solution)/shard_map/ppermute | solution.py:68
  54.2 38.0 %collective-permute-start.10 = (bf16[160,1408]{1,0:T(8,128)(2,1)}, bf16[160,1408]{1,0:T(8,128)(2,1)}, u32[]{:S(2)}, u32[]{:S(2)}) collective-permute-start(bf16[160,1408]{1,0:T(8,128)(2,1)} %collective-permute-done.4.refs_2_), channel_id=1, source_target_pairs={{0,4},{4,0},{8,12},{12,8},{16,20},{20,16},{24,28},{28,24},{1,5},{5... | collective-permute-start | bytes 1351688 | tf_op jit(solution)/shard_map/ppermute | solution.py:68
  85.8 10.7 %collective-permute-start.6 = (bf16[384,1280]{1,0:T(8,128)(2,1)}, bf16[384,1280]{1,0:T(8,128)(2,1)}, u32[]{:S(2)}, u32[]{:S(2)}) collective-permute-start(bf16[384,1280]{1,0:T(8,128)(2,1)} %collective-permute-done.3), channel_id=1, source_target_pairs={{0,1},{1,0},{2,3},{3,2},{4,5},{5,4},{6,7},{7,6},{8,9},{9,8},{10,11... | collective-permute-start | bytes 2949128 | tf_op jit(solution)/shard_map/ppermute | solution.py:68
  87.5 12.4 %collective-permute-start.7 = (bf16[384,1280]{1,0:T(8,128)(2,1)S(1)}, bf16[384,1280]{1,0:T(8,128)(2,1)}, u32[]{:S(2)}, u32[]{:S(2)}) collective-permute-start(bf16[384,1280]{1,0:T(8,128)(2,1)S(1)} %copy-done.11), channel_id=1, source_target_pairs={{0,1},{1,0},{2,3},{3,2},{4,5},{5,4},{6,7},{7,6},{8,9},{9,8},{10,11... | collective-permute-start | bytes 2949128 | tf_op jit(solution)/shard_map/ppermute | solution.py:68
  94.2 13.5 %collective-permute-start.12 = (bf16[160,1408]{1,0:T(8,128)(2,1)}, bf16[160,1408]{1,0:T(8,128)(2,1)S(1)}, u32[]{:S(2)}, u32[]{:S(2)}) collective-permute-start(bf16[160,1408]{1,0:T(8,128)(2,1)} %collective-permute-done.9.refs_4_), channel_id=1, source_target_pairs={{0,4},{4,0},{8,12},{12,8},{16,20},{20,16},{24,28},{28,24},{1,5},{5... | collective-permute-start | bytes 1351688 | tf_op jit(solution)/shard_map/ppermute | solution.py:68
  133.7 9.6 %collective-permute-start.13 = (bf16[96,1280]{1,0:T(8,128)(2,1)}, bf16[96,1280]{1,0:T(8,128)(2,1)S(1)}, u32[]{:S(2)}, u32[]{:S(2)}) collective-permute-start(bf16[96,1280]{1,0:T(8,128)(2,1)} %get-tuple-element.123), channel_id=1, source_target_pairs={{0,1},{1,0},{2,3},{3,2},{4,5},{5,4},{6,7},{7,6},{8,9},{9,8},{10,11... | collective-permute-start | bytes 737288 | tf_op jit(solution)/shard_map/ppermute | solution.py:68
  133.7 9.6 %collective-permute-start.14 = (bf16[96,1280]{1,0:T(8,128)(2,1)}, bf16[96,1280]{1,0:T(8,128)(2,1)S(1)}, u32[]{:S(2)}, u32[]{:S(2)}) collective-permute-start(bf16[96,1280]{1,0:T(8,128)(2,1)} %get-tuple-element.124), channel_id=1, source_target_pairs={{0,1},{1,0},{2,3},{3,2},{4,5},{5,4},{6,7},{7,6},{8,9},{9,8},{10,11... | collective-permute-start | bytes 737288 | tf_op jit(solution)/shard_map/ppermute | solution.py:68
  134.2 9.1 %collective-permute-start.15 = (bf16[96,1280]{1,0:T(8,128)(2,1)}, bf16[96,1280]{1,0:T(8,128)(2,1)S(1)}, u32[]{:S(2)}, u32[]{:S(2)}) collective-permute-start(bf16[96,1280]{1,0:T(8,128)(2,1)} %get-tuple-element.125), channel_id=1, source_target_pairs={{0,1},{1,0},{2,3},{3,2},{4,5},{5,4},{6,7},{7,6},{8,9},{9,8},{10,11... | collective-permute-start | bytes 737288 | tf_op jit(solution)/shard_map/ppermute | solution.py:68
  134.2 9.2 %collective-permute-start.16 = (bf16[96,1280]{1,0:T(8,128)(2,1)}, bf16[96,1280]{1,0:T(8,128)(2,1)S(1)}, u32[]{:S(2)}, u32[]{:S(2)}) collective-permute-start(bf16[96,1280]{1,0:T(8,128)(2,1)} %get-tuple-element.126), channel_id=1, source_target_pairs={{0,1},{1,0},{2,3},{3,2},{4,5},{5,4},{6,7},{7,6},{8,9},{9,8},{10,11... | collective-permute-start | bytes 737288 | tf_op jit(solution)/shard_map/ppermute | solution.py:68
  147.0 23.9 %collective-permute-start.17 = (bf16[384,1280]{1,0:T(8,128)(2,1)}, bf16[384,1280]{1,0:T(8,128)(2,1)S(1)}, u32[]{:S(2)}, u32[]{:S(2)}) collective-permute-start(bf16[384,1280]{1,0:T(8,128)(2,1)} %pair_sum.2), channel_id=1, source_target_pairs={{0,2},{1,3},{2,0},{3,1},{4,6},{5,7},{6,4},{7,5},{8,10},{9,11},{10,... | collective-permute-start | bytes 2949128 | tf_op jit(solution)/shard_map/ppermute | solution.py:68
  161.4 9.4 %collective-permute-start.18 = (bf16[96,1280]{1,0:T(8,128)(2,1)}, bf16[96,1280]{1,0:T(8,128)(2,1)S(1)}, u32[]{:S(2)}, u32[]{:S(2)}) collective-permute-start(bf16[96,1280]{1,0:T(8,128)(2,1)} %get-tuple-element.132), channel_id=1, source_target_pairs={{0,1},{1,0},{2,3},{3,2},{4,5},{5,4},{6,7},{7,6},{8,9},{9,8},{10,11... | collective-permute-start | bytes 737288 | tf_op jit(solution)/shard_map/ppermute | solution.py:68
  161.5 9.4 %collective-permute-start.19 = (bf16[96,1280]{1,0:T(8,128)(2,1)}, bf16[96,1280]{1,0:T(8,128)(2,1)S(1)}, u32[]{:S(2)}, u32[]{:S(2)}) collective-permute-start(bf16[96,1280]{1,0:T(8,128)(2,1)} %get-tuple-element.133), channel_id=1, source_target_pairs={{0,1},{1,0},{2,3},{3,2},{4,5},{5,4},{6,7},{7,6},{8,9},{9,8},{10,11... | collective-permute-start | bytes 737288 | tf_op jit(solution)/shard_map/ppermute | solution.py:68
  177.1 25.6 %collective-permute-start.22 = (bf16[384,1280]{1,0:T(8,128)(2,1)}, bf16[384,1280]{1,0:T(8,128)(2,1)S(1)}, u32[]{:S(2)}, u32[]{:S(2)}) collective-permute-start(bf16[384,1280]{1,0:T(8,128)(2,1)} %get-tuple-element.137.refs_0_), channel_id=1, source_target_pairs={{0,2},{1,3},{2,0},{3,1},{4,6},{5,7},{6,4},{7,5},{8,10},{9,11},{10,... | collective-permute-start | bytes 2949128 | tf_op jit(solution)/shard_map/ppermute | solution.py:68
  177.3 9.9 %collective-permute-start.23 = (bf16[384,1280]{1,0:T(8,128)(2,1)}, bf16[384,1280]{1,0:T(8,128)(2,1)S(1)}, u32[]{:S(2)}, u32[]{:S(2)}) collective-permute-start(bf16[384,1280]{1,0:T(8,128)(2,1)} %get-tuple-element.137.refs_0_), channel_id=1, source_target_pairs={{0,1},{1,0},{2,3},{3,2},{4,5},{5,4},{6,7},{7,6},{8,9},{9,8},{10,11... | collective-permute-start | bytes 2949128 | tf_op jit(solution)/shard_map/ppermute | solution.py:68
  214.4 9.2 %collective-permute-start.25 = (bf16[96,1280]{1,0:T(8,128)(2,1)}, bf16[96,1280]{1,0:T(8,128)(2,1)S(1)}, u32[]{:S(2)}, u32[]{:S(2)}) collective-permute-start(bf16[96,1280]{1,0:T(8,128)(2,1)} %get-tuple-element.149), channel_id=1, source_target_pairs={{0,1},{1,0},{2,3},{3,2},{4,5},{5,4},{6,7},{7,6},{8,9},{9,8},{10,11... | collective-permute-start | bytes 737288 | tf_op jit(solution)/shard_map/ppermute | solution.py:68
  236.5 193.1 %reduce-scatter.5.cloned.1.call-start = ((), (), s32[]{:S(2)}) async-start(), calls=%async_computation.5 | async-start | bytes 3686400 | tf_op jit(solution)/shard_map/reduce_scatter | solution.py:725
  236.5 20.1 %collective-permute-start.32 = (bf16[96,1280]{1,0:T(8,128)(2,1)}, bf16[96,1280]{1,0:T(8,128)(2,1)S(1)}, u32[]{:S(2)}, u32[]{:S(2)}) collective-permute-start(bf16[96,1280]{1,0:T(8,128)(2,1)} %get-tuple-element.157), channel_id=1, source_target_pairs={{0,1},{1,0},{2,3},{3,2},{4,5},{5,4},{6,7},{7,6},{8,9},{9,8},{10,11... | collective-permute-start | bytes 737288 | tf_op jit(solution)/shard_map/ppermute | solution.py:68
  236.9 19.7 %collective-permute-start.33 = (bf16[96,1280]{1,0:T(8,128)(2,1)}, bf16[96,1280]{1,0:T(8,128)(2,1)}, u32[]{:S(2)}, u32[]{:S(2)}) collective-permute-start(bf16[96,1280]{1,0:T(8,128)(2,1)} %get-tuple-element.158), channel_id=1, source_target_pairs={{0,1},{1,0},{2,3},{3,2},{4,5},{5,4},{6,7},{7,6},{8,9},{9,8},{10,11... | collective-permute-start | bytes 737288 | tf_op jit(solution)/shard_map/ppermute | solution.py:68
  237.1 19.6 %collective-permute-start.34 = (bf16[96,1280]{1,0:T(8,128)(2,1)}, bf16[96,1280]{1,0:T(8,128)(2,1)}, u32[]{:S(2)}, u32[]{:S(2)}) collective-permute-start(bf16[96,1280]{1,0:T(8,128)(2,1)} %get-tuple-element.159), channel_id=1, source_target_pairs={{0,1},{1,0},{2,3},{3,2},{4,5},{5,4},{6,7},{7,6},{8,9},{9,8},{10,11... | collective-permute-start | bytes 737288 | tf_op jit(solution)/shard_map/ppermute | solution.py:68
  237.5 19.2 %collective-permute-start.35 = (bf16[96,1280]{1,0:T(8,128)(2,1)}, bf16[96,1280]{1,0:T(8,128)(2,1)}, u32[]{:S(2)}, u32[]{:S(2)}) collective-permute-start(bf16[96,1280]{1,0:T(8,128)(2,1)} %get-tuple-element.160), channel_id=1, source_target_pairs={{0,1},{1,0},{2,3},{3,2},{4,5},{5,4},{6,7},{7,6},{8,9},{9,8},{10,11... | collective-permute-start | bytes 737288 | tf_op jit(solution)/shard_map/ppermute | solution.py:68
  237.6 24.4 %collective-permute-start.31 = (bf16[384,1280]{1,0:T(8,128)(2,1)}, bf16[384,1280]{1,0:T(8,128)(2,1)}, u32[]{:S(2)}, u32[]{:S(2)}) collective-permute-start(bf16[384,1280]{1,0:T(8,128)(2,1)} %pair_sum.3), channel_id=1, source_target_pairs={{0,2},{1,3},{2,0},{3,1},{4,6},{5,7},{6,4},{7,5},{8,10},{9,11},{10,... | collective-permute-start | bytes 2949128 | tf_op jit(solution)/shard_map/ppermute | solution.py:68
  268.5 27.8 %collective-permute-start.36 = (bf16[384,1280]{1,0:T(8,128)(2,1)}, bf16[384,1280]{1,0:T(8,128)(2,1)}, u32[]{:S(2)}, u32[]{:S(2)}) collective-permute-start(bf16[384,1280]{1,0:T(8,128)(2,1)} %get-tuple-element.165), channel_id=1, source_target_pairs={{0,2},{1,3},{2,0},{3,1},{4,6},{5,7},{6,4},{7,5},{8,10},{9,11},{10,... | collective-permute-start | bytes 2949128 | tf_op jit(solution)/shard_map/ppermute | solution.py:68
  271.3 26.6 %collective-permute-start.30 = (bf16[384,1280]{1,0:T(8,128)(2,1)}, bf16[384,1280]{1,0:T(8,128)(2,1)}, u32[]{:S(2)}, u32[]{:S(2)}) collective-permute-start(bf16[384,1280]{1,0:T(8,128)(2,1)} %slice.200), channel_id=1, source_target_pairs={{0,1},{1,0},{2,3},{3,2},{4,5},{5,4},{6,7},{7,6},{8,9},{9,8},{10,11... | collective-permute-start | bytes 2949128 | tf_op jit(solution)/shard_map/ppermute | solution.py:68
  297.6 32.8 %collective-permute-start.29 = (bf16[384,1280]{1,0:T(8,128)(2,1)}, bf16[384,1280]{1,0:T(8,128)(2,1)S(1)}, u32[]{:S(2)}, u32[]{:S(2)}) collective-permute-start(bf16[384,1280]{1,0:T(8,128)(2,1)} %slice.198), channel_id=1, source_target_pairs={{0,1},{1,0},{2,3},{3,2},{4,5},{5,4},{6,7},{7,6},{8,9},{9,8},{10,11... | collective-permute-start | bytes 2949128 | tf_op jit(solution)/shard_map/ppermute | solution.py:68
  300.4 30.0 %collective-permute-start.38 = (bf16[384,1280]{1,0:T(8,128)(2,1)}, bf16[384,1280]{1,0:T(8,128)(2,1)S(1)}, u32[]{:S(2)}, u32[]{:S(2)}) collective-permute-start(bf16[384,1280]{1,0:T(8,128)(2,1)} %add_convert_fusion.1), channel_id=1, source_target_pairs={{0,2},{1,3},{2,0},{3,1},{4,6},{5,7},{6,4},{7,5},{8,10},{9,11},{10,... | collective-permute-start | bytes 2949128 | tf_op jit(solution)/shard_map/ppermute | solution.py:68
  343.3 24.1 %collective-permute-start.41 = (bf16[384,1280]{1,0:T(8,128)(2,1)}, bf16[384,1280]{1,0:T(8,128)(2,1)}, u32[]{:S(2)}, u32[]{:S(2)}) collective-permute-start(bf16[384,1280]{1,0:T(8,128)(2,1)} %add_convert_fusion), channel_id=1, source_target_pairs={{0,2},{1,3},{2,0},{3,1},{4,6},{5,7},{6,4},{7,5},{8,10},{9,11},{10,... | collective-permute-start | bytes 2949128 | tf_op jit(solution)/shard_map/ppermute | solution.py:68
  353.5 18.5 %collective-permute-start.46 = (bf16[160,1408]{1,0:T(8,128)(2,1)S(1)}, bf16[160,1408]{1,0:T(8,128)(2,1)S(1)}, u32[]{:S(2)}, u32[]{:S(2)}) collective-permute-start(bf16[160,1408]{1,0:T(8,128)(2,1)S(1)} %get-tuple-element.219), channel_id=1, source_target_pairs={{0,4},{4,0},{8,12},{12,8},{16,20},{20,16},{24,28},{28,24},{1,5},{5... | collective-permute-start | bytes 1351688 | tf_op jit(solution)/shard_map/ppermute | solution.py:68
  355.3 26.5 %collective-permute-start.47 = (bf16[160,1408]{1,0:T(8,128)(2,1)S(1)}, bf16[160,1408]{1,0:T(8,128)(2,1)S(1)}, u32[]{:S(2)}, u32[]{:S(2)}) collective-permute-start(bf16[160,1408]{1,0:T(8,128)(2,1)S(1)} %get-tuple-element.218), channel_id=1, source_target_pairs={{0,4},{4,0},{8,12},{12,8},{16,20},{20,16},{24,28},{28,24},{1,5},{5... | collective-permute-start | bytes 1351688 | tf_op jit(solution)/shard_map/ppermute | solution.py:68
  355.6 40.2 %collective-permute-start.48 = (bf16[160,1408]{1,0:T(8,128)(2,1)S(1)}, bf16[160,1408]{1,0:T(8,128)(2,1)S(1)}, u32[]{:S(2)}, u32[]{:S(2)}) collective-permute-start(bf16[160,1408]{1,0:T(8,128)(2,1)S(1)} %get-tuple-element.217), channel_id=1, source_target_pairs={{0,4},{4,0},{8,12},{12,8},{16,20},{20,16},{24,28},{28,24},{1,5},{5... | collective-permute-start | bytes 1351688 | tf_op jit(solution)/shard_map/ppermute | solution.py:68
  357.3 47.9 %collective-permute-start.49 = (bf16[160,1408]{1,0:T(8,128)(2,1)S(1)}, bf16[160,1408]{1,0:T(8,128)(2,1)S(1)}, u32[]{:S(2)}, u32[]{:S(2)}) collective-permute-start(bf16[160,1408]{1,0:T(8,128)(2,1)S(1)} %get-tuple-element.216), channel_id=1, source_target_pairs={{0,4},{4,0},{8,12},{12,8},{16,20},{20,16},{24,28},{28,24},{1,5},{5... | collective-permute-start | bytes 1351688 | tf_op jit(solution)/shard_map/ppermute | solution.py:68
  367.4 44.8 %collective-permute-start.42 = (bf16[96,1280]{1,0:T(8,128)(2,1)S(1)}, bf16[96,1280]{1,0:T(8,128)(2,1)S(1)}, u32[]{:S(2)}, u32[]{:S(2)}) collective-permute-start(bf16[96,1280]{1,0:T(8,128)(2,1)S(1)} %get-tuple-element.223), channel_id=1, source_target_pairs={{0,1},{1,0},{2,3},{3,2},{4,5},{5,4},{6,7},{7,6},{8,9},{9,8},{10,11... | collective-permute-start | bytes 737288 | tf_op jit(solution)/shard_map/ppermute | solution.py:68
  372.0 40.3 %collective-permute-start.43 = (bf16[96,1280]{1,0:T(8,128)(2,1)S(1)}, bf16[96,1280]{1,0:T(8,128)(2,1)S(1)}, u32[]{:S(2)}, u32[]{:S(2)}) collective-permute-start(bf16[96,1280]{1,0:T(8,128)(2,1)S(1)} %get-tuple-element.222), channel_id=1, source_target_pairs={{0,1},{1,0},{2,3},{3,2},{4,5},{5,4},{6,7},{7,6},{8,9},{9,8},{10,11... | collective-permute-start | bytes 737288 | tf_op jit(solution)/shard_map/ppermute | solution.py:68
  406.5 33.7 %collective-permute-start.50 = (bf16[160,1408]{1,0:T(8,128)(2,1)}, bf16[160,1408]{1,0:T(8,128)(2,1)}, u32[]{:S(2)}, u32[]{:S(2)}) collective-permute-start(bf16[160,1408]{1,0:T(8,128)(2,1)} %get-tuple-element.215), channel_id=1, source_target_pairs={{0,16},{4,20},{8,24},{12,28},{16,0},{20,4},{24,8},{28,12},{1,17},{... | collective-permute-start | bytes 1351688 | tf_op jit(solution)/shard_map/ppermute | solution.py:68
  408.1 32.1 %collective-permute-start.51 = (bf16[160,1408]{1,0:T(8,128)(2,1)}, bf16[160,1408]{1,0:T(8,128)(2,1)}, u32[]{:S(2)}, u32[]{:S(2)}) collective-permute-start(bf16[160,1408]{1,0:T(8,128)(2,1)} %get-tuple-element.214), channel_id=1, source_target_pairs={{0,24},{4,28},{8,16},{12,20},{16,8},{20,12},{24,0},{28,4},{1,25},{... | collective-permute-start | bytes 1351688 | tf_op jit(solution)/shard_map/ppermute | solution.py:68
  411.1 29.3 %collective-permute-start.52 = (bf16[160,1408]{1,0:T(8,128)(2,1)}, bf16[160,1408]{1,0:T(8,128)(2,1)}, u32[]{:S(2)}, u32[]{:S(2)}) collective-permute-start(bf16[160,1408]{1,0:T(8,128)(2,1)} %get-tuple-element.213), channel_id=1, source_target_pairs={{0,8},{4,12},{8,0},{12,4},{16,24},{20,28},{24,16},{28,20},{1,9},{5... | collective-permute-start | bytes 1351688 | tf_op jit(solution)/shard_map/ppermute | solution.py:68
  414.0 15.5 %collective-permute-start.54 = (f32[1,160,160]{2,1,0:T(8,128)S(1)}, f32[1,160,160]{2,1,0:T(8,128)S(1)}, u32[]{:S(2)}, u32[]{:S(2)}) collective-permute-start(f32[1,160,160]{2,1,0:T(8,128)S(1)} %add.239), channel_id=1, source_target_pairs={{0,2},{1,3},{2,0},{3,1},{4,6},{5,7},{6,4},{7,5},{8,10},{9,11},{10,... | collective-permute-start | bytes 307208 | tf_op jit(solution)/shard_map/ppermute | solution.py:68
  452.0 13.3 %collective-permute-start.58 = (f32[3,160,160]{2,1,0:T(8,128)S(1)}, f32[3,160,160]{2,1,0:T(8,128)S(1)}, u32[]{:S(2)}, u32[]{:S(2)}) collective-permute-start(f32[3,160,160]{2,1,0:T(8,128)S(1)} %fusion.38), channel_id=1, source_target_pairs={{0,2},{1,3},{2,0},{3,1},{4,6},{5,7},{6,4},{7,5},{8,10},{9,11},{10,... | collective-permute-start | bytes 921608 | tf_op jit(solution)/shard_map/ppermute | solution.py:68
  484.4 11.4 %collective-permute-start.60 = (f32[9,1280]{1,0:T(8,128)S(1)}, f32[9,1280]{1,0:T(8,128)S(1)}, u32[]{:S(2)}, u32[]{:S(2)}) collective-permute-start(f32[9,1280]{1,0:T(8,128)S(1)} %add.255), channel_id=1, source_target_pairs={{0,8},{4,12},{8,0},{12,4},{16,24},{20,28},{24,16},{28,20},{1,9},{5... | collective-permute-start | bytes 138248 | tf_op jit(solution)/shard_map/ppermute | solution.py:68
  (88 other events, 843.9 us)
Sparse Core Ops, SparseCore 0:
  10.8 94.9 all-gather.2
  108.6 59.2 all-gather.4
  236.6 77.5 reduce-scatter.2
  318.1 87.3 reduce-scatter.4
